TPU v7x, 32 devices: a whole 2x2x4 slice. The times are simulated.
32 devices in a mesh: seq: 8 (over z, x), head: 4 (over y, core).
Axes of the slice: x: 2, y: 2, z: 4, core: 2. Of those that a mesh axis runs over, the one named last changes fastest.
Arguments:
- tokens: bfloat16 [6, 2048, 2048], P(None, 'seq'), may hold values from -6 to 6
- segments: int32 [6, 2048], P(None, 'seq'), may hold values from 0 to 1, as said below
- norm_gain: float32 [2048], replicated, may hold values from 0.1 to 1.9
- w_zx: bfloat16 [2048, 2, 4096], P(None, None, 'head'), may hold values from -0.125 to 0.125
- w_bc: bfloat16 [2048, 256], replicated, may hold values from -0.125 to 0.125
- w_dt: bfloat16 [2048, 64], P(None, 'head'), may hold values from -0.125 to 0.125
- conv_x: float32 [4, 4096], P(None, 'head'), may hold values from -3 to 3
- conv_x_bias: float32 [4096], P('head'), may hold values from -0.5 to 0.5
- conv_bc: float32 [4, 256], replicated, may hold values from -3 to 3
- conv_bc_bias: float32 [256], replicated, may hold values from -0.5 to 0.5
- dt_bias: float32 [64], P('head'), may hold values from -2 to 1
- a_log: float32 [64], P('head'), may hold values from -9 to -2
- d_skip: float32 [64], P('head'), may hold values from 0.5 to 1.5
- gate_gain: float32 [4096], P('head'), may hold values from 0.1 to 1.9
- w_out: bfloat16 [2048, 4096], P(None, 'head'), may hold values from -0.09375 to 0.09375
- cotangent: bfloat16 [6, 2048, 2048], P(None, 'seq', 'head'), may hold values from -6 to 6
Outputs:
- layer_out: bfloat16 [6, 2048, 2048], P(None, 'seq', 'head')
- input_grad: bfloat16 [6, 2048, 2048], P(None, 'seq', 'head')
- norm_gain_grad: float32 [2048], P('head')
- w_zx_grad: float32 [2048, 2, 4096], P('seq', None, 'head')
- w_bc_grad: float32 [2048, 256], P('seq')
- w_dt_grad: float32 [2048, 64], P('seq', 'head')
- conv_x_grad: float32 [4, 4096], P(None, 'head')
- conv_x_bias_grad: float32 [4096], P('head')
- conv_bc_grad: float32 [4, 256], replicated
- conv_bc_bias_grad: float32 [256], replicated
- dt_bias_grad: float32 [64], P('head')
- a_log_grad: float32 [64], P('head')
- d_skip_grad: float32 [64], P('head')
- gate_gain_grad: float32 [4096], P('head')
- w_out_grad: float32 [2048, 4096], P('seq', 'head')
Inputs may be any that keep to these rules, and one draw needn't show every extreme that they name: `segments`: within a sequence the segment numbers start at 0 and rise by 0 or 1 from one position to the next; every sequence holds exactly 2 documents, each of 200 to 2000 positions, and its longest document has exactly min(2000, 1848) positions.
All inputs are finite; a program needn't handle non-finite values.
Results may differ from a plain program's by a relative error of at most 0.03.
The roundings to bfloat16 on the way count: a program that leaves them out, or rounds other values in their place, can miss the bound.
Values may be sent and summed in bfloat16 or wider, within the bound.
No kernel may reach another device: no remote copies, remote signals or barrier semaphores. Data moves between devices by JAX's collectives and lax.ppermute only.
A program may use at most 256 MiB of HBM per device.

v0:
```python
import jax
import jax.numpy as jnp
from jax import lax
from jax.sharding import PartitionSpec as P

HEAD_DIM = 64
BLOCK_LEN = 256


EPS = 1e-05


def from_behind(value, axis, steps):
    count = lax.axis_size(axis)
    leading, last = (max(0, -steps), min(count, count - steps))
    return lax.ppermute(value, axis, [(source, source + steps) for source in range(leading, last)])


def prefix(shard, axis, join, neutral, backward):
    count = lax.axis_size(axis)
    place = lax.axis_index(axis)
    ahead = count - 1 - place if backward else place
    gathered = jax.tree.map(
        lambda a, kind: lax.all_gather(a.astype(kind), axis), shard, (jnp.bfloat16, jnp.bfloat16)
    )
    state = jax.tree.map(lambda a, e: jnp.zeros_like(a) + jnp.asarray(e, a.dtype), shard, neutral)

    def one(lap, state):
        source = count - 1 - lap if backward else lap
        return join(
            state,
            jax.tree.map(
                lambda a, own: lax.dynamic_index_in_dim(a, source, 0, False).astype(own.dtype),
                gathered,
                shard,
            ),
        )

    return lax.fori_loop(0, ahead, one, state)


def silu_grad(value):
    sigmoid_v = jax.nn.sigmoid(value)
    return sigmoid_v * (1.0 + value * (1.0 - sigmoid_v))


def compose(earlier, later):
    return (later[0] * earlier[0], later[0][..., None, None] * earlier[1] + later[1])


def conv_apply(extended, same_taps, weight, bias, span_len):
    running = jnp.zeros((extended.shape[0], span_len, extended.shape[2]), jnp.float32) + bias
    for tap_pos in range(weight.shape[0]):
        window = extended[:, tap_pos : tap_pos + span_len].astype(jnp.float32)
        running = running + weight[tap_pos] * window * same_taps[tap_pos][..., None]
    return running


def conv_back(d_conv, extended, same_taps, weight, span_len):
    edge_rows = weight.shape[0] - 1
    bias_grad = jnp.sum(d_conv, axis=(0, 1))
    tap_grads = []
    d_extended = jnp.zeros(extended.shape, jnp.float32)
    for tap_pos in range(weight.shape[0]):
        masked = d_conv * same_taps[tap_pos][..., None]
        window = extended[:, tap_pos : tap_pos + span_len].astype(jnp.float32)
        tap_grads.append(jnp.sum(masked * window, axis=(0, 1)))
        d_extended = d_extended + jnp.pad(
            masked * weight[tap_pos], ((0, 0), (tap_pos, edge_rows - tap_pos), (0, 0))
        )
    return (jnp.stack(tap_grads), bias_grad, d_extended)


def local(
    tokens,
    segments,
    norm_gain,
    w_zx,
    w_bc,
    w_dt,
    conv_x,
    conv_x_bias,
    conv_bc,
    conv_bc_bias,
    dt_bias,
    a_log,
    d_skip,
    gate_gain,
    w_out,
    cotangent,
):
    seq_count, span_len, model_width = tokens.shape
    head_count = d_skip.shape[0]
    inner_own = head_count * HEAD_DIM
    inner_total = inner_own * lax.axis_size("head")
    state_width = w_bc.shape[1] // 2
    share_cols = model_width // lax.axis_size("head")
    offset = lax.axis_index("head") * share_cols
    blocks = span_len // BLOCK_LEN
    edge_rows = conv_x.shape[0] - 1
    tokens_f = tokens.astype(jnp.float32)
    rstd_in = lax.rsqrt(jnp.mean(tokens_f * tokens_f, axis=-1, keepdims=True) + EPS)
    unit = tokens_f * rstd_in
    normed = (unit * norm_gain).astype(jnp.bfloat16)
    w_in_flat = w_zx.reshape(model_width, 2 * inner_own)
    projected = jnp.dot(normed, w_in_flat, preferred_element_type=jnp.float32)
    gate_z = projected[..., :inner_own]
    x_pre = projected[..., inner_own:].astype(jnp.bfloat16)
    bc_pre = jnp.dot(normed, w_bc, preferred_element_type=jnp.float32).astype(jnp.bfloat16)
    dt_raw = jnp.dot(normed, w_dt, preferred_element_type=jnp.float32)
    parity = (segments % 2).astype(jnp.bfloat16)
    halo_x, halo_bc, halo_par = from_behind(
        (x_pre[:, -edge_rows:], bc_pre[:, -edge_rows:], parity[:, -edge_rows:]), "seq", 1
    )
    ext_x = jnp.concatenate([halo_x, x_pre], axis=1)
    ext_bc = jnp.concatenate([halo_bc, bc_pre], axis=1)
    ext_par = jnp.concatenate([halo_par, parity], axis=1)
    same_taps = [
        (ext_par[:, tap_pos : tap_pos + span_len] == parity).astype(jnp.float32)
        for tap_pos in range(edge_rows + 1)
    ]
    x_conv = conv_apply(ext_x, same_taps, conv_x, conv_x_bias, span_len)
    bc_conv = conv_apply(ext_bc, same_taps, conv_bc, conv_bc_bias, span_len)
    x_ssm = jax.nn.silu(x_conv).astype(jnp.bfloat16)
    bc_ssm = jax.nn.silu(bc_conv).astype(jnp.bfloat16)
    dt_pre = dt_raw + dt_bias
    step_size = jax.nn.softplus(dt_pre)
    decay_rate = jnp.exp(a_log)
    log_decay = -decay_rate * step_size
    x_blocks = x_ssm.reshape(seq_count, blocks, BLOCK_LEN, head_count, HEAD_DIM)
    x_float = x_blocks.astype(jnp.float32)
    b_blocks = bc_ssm[..., :state_width].reshape(seq_count, blocks, BLOCK_LEN, state_width)
    c_blocks = bc_ssm[..., state_width:].reshape(seq_count, blocks, BLOCK_LEN, state_width)
    log_blocks = log_decay.reshape(seq_count, blocks, BLOCK_LEN, head_count)
    dt_blocks = step_size.reshape(seq_count, blocks, BLOCK_LEN, head_count)
    seg_blocks = segments.reshape(seq_count, blocks, BLOCK_LEN)
    par_blocks = parity.reshape(seq_count, blocks, BLOCK_LEN)
    prev_par = jnp.concatenate(
        [halo_par[:, -1:], parity[:, BLOCK_LEN - 1 :: BLOCK_LEN][:, :-1]], axis=1
    )
    first_same = par_blocks[:, :, 0] == prev_par
    start_same = (first_same[..., None] & (seg_blocks == seg_blocks[..., :1])).astype(jnp.float32)
    end_same = (seg_blocks == seg_blocks[..., -1:]).astype(jnp.float32)
    places = jnp.arange(BLOCK_LEN)
    causal = places[None, :] <= places[:, None]
    same_doc = ((seg_blocks[..., :, None] == seg_blocks[..., None, :]) & causal).astype(jnp.float32)
    cum_log = jnp.cumsum(log_blocks, axis=2)
    cum_heads = jnp.swapaxes(cum_log, 2, 3)
    step_heads = jnp.swapaxes(dt_blocks, 2, 3)
    lag_diff = cum_heads[..., :, None] - cum_heads[..., None, :]
    mixing = jnp.exp(jnp.minimum(lag_diff, 0.0)) * same_doc[:, :, None]
    scores = jnp.einsum("sbin,sbjn->sbij", c_blocks, b_blocks, preferred_element_type=jnp.float32)
    weights = (scores[:, :, None] * mixing * step_heads[..., None, :]).astype(jnp.bfloat16)
    inner_y = jnp.einsum(
        "sbhij,sbjhp->sbihp", weights, x_blocks, preferred_element_type=jnp.float32
    )
    tail_decay = jnp.exp(cum_log[:, :, -1:, :] - cum_log) * end_same[..., None]
    tail_step = tail_decay * dt_blocks
    loaded = (x_float * tail_step[..., None]).astype(jnp.bfloat16)
    local_state = jnp.einsum(
        "sbjhp,sbjn->sbhpn", loaded, b_blocks, preferred_element_type=jnp.float32
    )
    block_decay = jnp.exp(cum_log[:, :, -1, :]) * start_same[:, :, -1:]
    dev_decay = jnp.ones((seq_count, head_count), jnp.float32)
    dev_state = jnp.zeros((seq_count, head_count, HEAD_DIM, state_width), jnp.float32)
    block_idx = 0
    dev_state = block_decay[:, block_idx, :, None, None] * dev_state + local_state[:, block_idx]
    dev_decay = block_decay[:, block_idx] * dev_decay
    identity = (jnp.ones_like(dev_decay), jnp.zeros_like(dev_state))
    entering = prefix((dev_decay, dev_state), "seq", compose, identity, False)[1]
    block_idx = 0
    state_list = [entering]
    states_in = jnp.stack(state_list, axis=1)
    states_low = states_in.astype(jnp.bfloat16)
    carried = jnp.einsum(
        "sbin,sbhpn->sbihp", c_blocks, states_low, preferred_element_type=jnp.float32
    )
    entry_decay = jnp.exp(cum_log) * start_same[..., None]
    y_blocks = inner_y + carried * entry_decay[..., None] + d_skip[:, None] * x_float
    y_flat = y_blocks.reshape(seq_count, span_len, inner_own)
    sigmoid_z = jax.nn.sigmoid(gate_z)
    silu_z = gate_z * sigmoid_z
    gated_out = y_flat * silu_z
    part_squares = jnp.sum(gated_out * gated_out, axis=-1)
    scaled = (gated_out * gate_gain).astype(jnp.bfloat16)
    proj_out = lax.dot_general(
        scaled, w_out, (((2,), (1,)), ((), ())), preferred_element_type=jnp.float32
    )
    total_squares = lax.psum(part_squares, "head")
    rstd_gate = lax.rsqrt(total_squares / inner_total + EPS)
    out_term = proj_out * rstd_gate[..., None]
    own_sum = lax.psum_scatter(
        out_term.astype(jnp.bfloat16), "head", scatter_dimension=2, tiled=True
    ).astype(jnp.float32)
    layer_out = (lax.dynamic_slice_in_dim(tokens_f, offset, share_cols, 2) + own_sum).astype(
        jnp.bfloat16
    )
    cot_full = lax.all_gather(cotangent, "head", axis=2, tiled=True)
    cot_float = cot_full.astype(jnp.float32)
    d_proj = (cot_float * rstd_gate[..., None]).astype(jnp.bfloat16)
    d_scaled = lax.dot_general(
        d_proj, w_out, (((2,), (0,)), ((), ())), preferred_element_type=jnp.float32
    )
    g_w_out = lax.dot_general(
        d_proj, scaled, (((0, 1), (0, 1)), ((), ())), preferred_element_type=jnp.float32
    )
    part_dots = jnp.sum(cot_float * proj_out, axis=-1)
    d_rstd = lax.psum(part_dots, "head")
    d_gated = (
        d_scaled * gate_gain
        - (d_rstd * rstd_gate * rstd_gate * rstd_gate / inner_total)[..., None] * gated_out
    )
    g_gate_gain = jnp.sum(d_scaled * gated_out, axis=(0, 1))
    d_y = d_gated * silu_z
    d_z_low = (d_gated * y_flat * silu_grad(gate_z)).astype(jnp.bfloat16)
    d_blocks = d_y.reshape(seq_count, blocks, BLOCK_LEN, head_count, HEAD_DIM)
    dy_low = d_blocks.astype(jnp.bfloat16)
    d_carried = (d_blocks * entry_decay[..., None]).astype(jnp.bfloat16)
    g_skip = jnp.sum(d_blocks * x_float, axis=(0, 1, 2, 4))
    d_entry = jnp.sum(d_blocks * carried, axis=-1)
    d_weights = jnp.einsum(
        "sbihp,sbjhp->sbhij", dy_low, x_blocks, preferred_element_type=jnp.float32
    )
    d_x = d_skip[:, None] * d_blocks + jnp.einsum(
        "sbhij,sbihp->sbjhp", weights, dy_low, preferred_element_type=jnp.float32
    )
    d_mixed = d_weights * mixing
    d_scores_low = jnp.sum(d_mixed * step_heads[..., None, :], axis=2).astype(jnp.bfloat16)
    score_terms = d_mixed * scores[:, :, None]
    d_step_heads = jnp.sum(score_terms, axis=-2)
    shift_terms = score_terms * step_heads[..., None, :]
    d_cum_heads = jnp.sum(shift_terms, axis=-1) - jnp.sum(shift_terms, axis=-2)
    d_c = jnp.einsum("sbij,sbjn->sbin", d_scores_low, b_blocks, preferred_element_type=jnp.float32)
    d_c = d_c + jnp.einsum(
        "sbihp,sbhpn->sbin", d_carried, states_low, preferred_element_type=jnp.float32
    )
    d_b = jnp.einsum("sbij,sbin->sbjn", d_scores_low, c_blocks, preferred_element_type=jnp.float32)
    r_grad = jnp.einsum(
        "sbihp,sbin->sbhpn", d_carried, c_blocks, preferred_element_type=jnp.float32
    )
    dev_grad = jnp.zeros_like(dev_state)
    for block_idx in reversed(range(blocks)):
        dev_grad = block_decay[:, block_idx, :, None, None] * dev_grad + r_grad[:, block_idx]
    leaving = prefix((dev_decay, dev_grad), "seq", compose, identity, True)[1]
    grad_list = [None] * blocks
    running_grad = leaving
    for block_idx in reversed(range(blocks)):
        grad_list[block_idx] = running_grad
        running_grad = (
            block_decay[:, block_idx, :, None, None] * running_grad + r_grad[:, block_idx]
        )
    end_grads = jnp.stack(grad_list, axis=1)
    d_decay = jnp.sum(end_grads * states_in, axis=(-1, -2))
    ends_low = end_grads.astype(jnp.bfloat16)
    d_loaded = jnp.einsum(
        "sbjn,sbhpn->sbjhp", b_blocks, ends_low, preferred_element_type=jnp.float32
    )
    d_b = d_b + jnp.einsum(
        "sbjhp,sbhpn->sbjn", loaded, ends_low, preferred_element_type=jnp.float32
    )
    d_x = d_x + d_loaded * tail_step[..., None]
    d_tail = jnp.sum(d_loaded * x_float, axis=-1)
    end_terms = d_tail * tail_step
    d_cum = jnp.swapaxes(d_cum_heads, 2, 3) - end_terms + d_entry * entry_decay
    d_cum = d_cum.at[:, :, -1, :].add(jnp.sum(end_terms, axis=2) + d_decay * block_decay)
    d_log = lax.cumsum(d_cum, axis=2, reverse=True)
    d_step = jnp.swapaxes(d_step_heads, 2, 3) + d_tail * tail_decay - d_log * decay_rate
    g_a_log = jnp.sum(d_log * log_blocks, axis=(0, 1, 2))
    d_dt_pre = d_step.reshape(seq_count, span_len, head_count) * jax.nn.sigmoid(dt_pre)
    g_dt_bias = jnp.sum(d_dt_pre, axis=(0, 1))
    d_dt_low = d_dt_pre.astype(jnp.bfloat16)
    d_x_flat = d_x.reshape(seq_count, span_len, inner_own)
    d_bc_part = jnp.concatenate([d_b, d_c], axis=-1).reshape(seq_count, span_len, 2 * state_width)
    d_bc_all = lax.psum(d_bc_part.astype(jnp.bfloat16), "head").astype(jnp.float32)
    g_conv_x, g_conv_x_bias, d_ext_x = conv_back(
        d_x_flat * silu_grad(x_conv), ext_x, same_taps, conv_x, span_len
    )
    g_conv_bc, g_conv_bc_bias, d_ext_bc = conv_back(
        d_bc_all * silu_grad(bc_conv), ext_bc, same_taps, conv_bc, span_len
    )
    back_x, back_bc = (
        from_behind(d_ext_x[:, :edge_rows].astype(jnp.bfloat16), "seq", -1).astype(jnp.float32),
        from_behind(d_ext_bc[:, :edge_rows].astype(jnp.bfloat16), "seq", -1).astype(jnp.float32),
    )
    d_x_pre = d_ext_x[:, edge_rows:].at[:, -edge_rows:].add(back_x).astype(jnp.bfloat16)
    d_bc_pre = d_ext_bc[:, edge_rows:].at[:, -edge_rows:].add(back_bc).astype(jnp.bfloat16)
    d_in_low = jnp.concatenate([d_z_low, d_x_pre], axis=-1)
    part_normed = lax.dot_general(
        d_in_low, w_in_flat, (((2,), (1,)), ((), ())), preferred_element_type=jnp.float32
    )
    part_normed = part_normed + lax.dot_general(
        d_dt_low, w_dt, (((2,), (1,)), ((), ())), preferred_element_type=jnp.float32
    )
    g_w_zx = lax.dot_general(
        normed, d_in_low, (((0, 1), (0, 1)), ((), ())), preferred_element_type=jnp.float32
    ).reshape(model_width, 2, inner_own)
    g_w_dt = lax.dot_general(
        normed, d_dt_low, (((0, 1), (0, 1)), ((), ())), preferred_element_type=jnp.float32
    )
    g_w_bc = lax.dot_general(
        normed, d_bc_pre, (((0, 1), (0, 1)), ((), ())), preferred_element_type=jnp.float32
    )
    full_grad = lax.psum(part_normed.astype(jnp.bfloat16), "head").astype(jnp.float32)
    full_grad = full_grad + lax.dot_general(
        d_bc_pre, w_bc, (((2,), (1,)), ((), ())), preferred_element_type=jnp.float32
    )
    d_unit = full_grad * norm_gain
    g_norm_full = jnp.sum(full_grad * unit, axis=(0, 1))
    mean_dot = jnp.mean(d_unit * unit, axis=-1, keepdims=True)
    d_tokens = rstd_in * (d_unit - unit * mean_dot) + cot_float
    input_grad = lax.dynamic_slice_in_dim(d_tokens, offset, share_cols, 2).astype(jnp.bfloat16)
    g_norm = lax.dynamic_slice_in_dim(g_norm_full, offset, share_cols, 0)
    big_grads = (
        lax.psum_scatter(
            g_w_zx.astype(jnp.bfloat16), "seq", scatter_dimension=0, tiled=True
        ).astype(jnp.float32),
        lax.psum_scatter(
            g_w_bc.astype(jnp.bfloat16), "seq", scatter_dimension=0, tiled=True
        ).astype(jnp.float32),
        lax.psum_scatter(
            g_w_dt.astype(jnp.bfloat16), "seq", scatter_dimension=0, tiled=True
        ).astype(jnp.float32),
        lax.psum_scatter(
            g_w_out.astype(jnp.bfloat16), "seq", scatter_dimension=0, tiled=True
        ).astype(jnp.float32),
    )
    small_grads = lax.psum(
        (
            g_norm,
            g_conv_x,
            g_conv_x_bias,
            g_conv_bc,
            g_conv_bc_bias,
            g_dt_bias,
            g_a_log,
            g_skip,
            g_gate_gain,
        ),
        "seq",
    )
    return (
        layer_out,
        input_grad,
        small_grads[0],
        big_grads[0],
        big_grads[1],
        big_grads[2],
        small_grads[1],
        small_grads[2],
        small_grads[3],
        small_grads[4],
        small_grads[5],
        small_grads[6],
        small_grads[7],
        small_grads[8],
        big_grads[3],
    )


def solution(mesh):
    placed = (
        P(None, "seq", None),
        P(None, "seq"),
        P(),
        P(None, None, "head"),
        P(),
        P(None, "head"),
        P(None, "head"),
        P("head"),
        P(),
        P(),
        P("head"),
        P("head"),
        P("head"),
        P("head"),
        P(None, "head"),
        P(None, "seq", "head"),
    )
    return jax.shard_map(
        local,
        mesh=mesh,
        in_specs=placed,
        out_specs=(
            P(None, "seq", "head"),
            P(None, "seq", "head"),
            P("head"),
            P("seq", None, "head"),
            P("seq", None),
            P("seq", "head"),
            P(None, "head"),
            P("head"),
            P(),
            P(),
            P("head"),
            P("head"),
            P("head"),
            P("head"),
            P("seq", "head"),
        ),
        check_vma=False,
    )
```

profile of v0, /device:TPU:0, one launch (start us, length us, event | category | flops | bytes accessed | tf_op | source)
XLA Modules:
  0.0 1406.2 jit_solution(15101315517833822718)
XLA Ops:
  10.1 5.4 collective-permute-start.1
  15.6 4.1 multiply_reduce_fusion.7
  19.7 14.6 %reshape.667 = bf16[2048,2048,1]{1,0,2:T(8,128)(2,1)} reshape(bf16[2048,2,1024]{2,1,0:T(2,128)(2,1)} %param.29) | data formatting | bytes 16777216 | tf_op jit(solution)/shard_map/reshape | solution.py:105
  34.3 19.4 %fusion.133 = (bf16[6,256,2048]{2,1,0:T(8,128)(2,1)S(1)}, f32[6,256,2048]{2,1,0:T(8,128)}) fusion(bf16[2048,2048,1]{1,0,2:T(8,128)(2,1)} %reshape.667, f32[2048]{0:T(1024)S(1)} %copy-done.85, f32[6,256]{1,0:T(8,128)S(1)} %add_rsqrt_fusion.1, bf16[6,256,2048]{2,1,0:T(8,128)(2,1)} %param.26), kind=kOutput, calls=%fused_computation.257 | convolution fusion | flops 12900630528 | bytes 33568768 | tf_op jit(solution)/shard_map/dot_general | solution.py:106
  54.4 3.6 collective-permute-start
  60.7 3.6 collective-permute-start.2
  66.9 3.4 reduce-window.14
  70.6 4.2 slice.252
  78.2 3.6 multiply_convert_fusion.18
  81.8 8.7 multiply_convert_fusion.9
  90.6 4.7 copy.233
  95.3 4.0 add_convert_fusion.3
  101.9 26.4 %all_gather.8 = bf16[8,6,16]{2,1,0:T(8,128)(2,1)S(1)} all-gather(bf16[1,6,16]{2,1,0:T(8,128)(2,1)S(1)} %copy.239), channel_id=1, replica_groups=mesh['seq'=8,'head'=4] {'seq'}, dimensions={0}, use_global_device_ids=true | all-gather | bytes 1728 | tf_op jit(solution)/shard_map/all_gather | solution.py:24
  129.9 5.4 copy.240
  135.2 139.4 %all-gather.8.cloned.1.call-done = bf16[48,16,64,128]{3,2,1,0:T(8,128)(2,1)} async-done(((bf16[6,16,64,128]{3,2,1,0:T(8,128)(2,1)}), bf16[48,16,64,128]{3,2,1,0:T(8,128)(2,1)}) %all-gather.8.cloned.1.call-update) | async-done | bytes 12582928 | tf_op jit(solution)/shard_map/all_gather | solution.py:24
  280.1 4.1 copy-done.12
  284.2 10.5 fusion.19
  294.7 6.6 copy.241
  301.4 7.3 multiply_reduce_fusion.11
  308.6 12.2 all-gather.6.cloned.1.call-done
  320.8 13.9 multiply_reduce_fusion.6
  334.7 10.8 all-reduce.10
  345.5 19.3 %multiply_reduce_fusion.9 = (f32[1024]{0:T(1024)}, f32[6,256,1024]{2,1,0:T(8,128)}, bf16[6,256,1024]{2,1,0:T(8,128)(2,1)}, f32[1024]{0:T(1024)}) fusion(bf16[6,256,1024]{2,1,0:T(8,128)(2,1)} %get-tuple-element.267, f32[6,256,2048]{2,1,0:T(8,128)} %get-tuple-element.303, f32[6,256,1024]{2,1,0:T(8,128)} %get-tuple-element.262, ...), kind=kOutput, calls=%fused_computation.56 | convolution fusion | flops 6483343360 | bytes 41967616 | tf_op jit(solution)/shard_map/dot_general | solution.py:201
  364.8 6.6 copy.243
  371.4 4.9 add_convert_fusion.1
  376.5 5.0 convolution_bitcast_fusion.2
  382.9 17.3 %multiply_reduce_fusion.1 = (f32[6,16,256]{2,1,0:T(8,128)}, f32[6,16,256]{2,1,0:T(8,128)}, f32[6,16,256]{2,1,0:T(8,128)}, bf16[6,256,256]{2,1,0:T(8,128)(2,1)S(1)}) fusion(f32[6,16,256]{2,1,0:T(8,128)S(1)} %copy-done.47, f32[6,256,256]{2,1,0:T(8,128)} %fusion.92, f32[6,256,256]{2,1,0:T(8,128)} %and_convert_fusion, f32[6,16,256]{2,1,0:T(8,128)S(1)} %copy-done.50, ...), kind=kOutput, calls=%fused_computation.8 | convolution fusion | flops 875618304 | bytes 13860864 | tf_op jit(solution)/shard_map/sbihp,sbjhp->sbhij/dot_general | solution.py:221
  405.1 164.4 %all-gather.10.cloned.1.call-done = bf16[48,16,64,128]{3,2,1,0:T(8,128)(2,1)} async-done(((bf16[6,16,64,128]{3,2,1,0:T(8,128)(2,1)}), bf16[48,16,64,128]{3,2,1,0:T(8,128)(2,1)}) %all-gather.10.cloned.1.call-update) | async-done | bytes 12582928 | tf_op jit(solution)/shard_map/all_gather | solution.py:24
  571.5 30.8 %while.30 = (s32[]{:T(128)}, f32[6,16,64,128]{3,2,1,0:T(8,128)}, s32[]{:T(128)}, bf16[8,6,16]{2,1,0:T(8,128)(2,1)S(1)}, bf16[8,6,16,64,128]{4,3,2,1,0:T(8,128)(2...) while((s32[]{:T(128)}, f32[6,16,64,128]{3,2,1,0:T(8,128)}, s32[]{:T(128)}, ...), condition=%wide.region_11.12_spmd, body=%wide.region_10.11_spmd.sunk | while | flops 2359398 | bytes 7865427 | solution.py:39
  571.7 4.4 convert_add_fusion.6
  576.1 4.4 convert_add_fusion.6
  580.5 4.4 convert_add_fusion.6
  584.9 4.4 convert_add_fusion.6
  589.3 4.4 convert_add_fusion.6
  593.6 4.4 convert_add_fusion.6
  598.0 4.4 convert_add_fusion.6
  602.4 6.6 fusion.17
  611.1 14.9 %reduce-window.16 = f32[6,1,16,2,128]{4,2,3,1,0:T(8,128)S(1)} reduce-window(f32[6,1,16,2,128]{4,2,3,1,0:T(8,128)S(1)} %copy.248, f32[]{:T(128)} %constant.174.clone.1), window={size=1x1x1x1x128 pad=0_0x0_0x0_0x0_0x0_127}, to_apply=%region_19.20 | reduce-window | flops 3121152 | bytes 196612 | tf_op jit(solution)/shard_map/reduce-window.2
  626.2 14.5 %fusion.18 = f32[6,1,256,16,64]{2,4,3,0,1:T(8,128)} fusion(f32[6,256,16,64]{1,3,2,0:T(8,128)} %get-tuple-element.307, f32[6,1,256,16,64]{2,4,3,0,1:T(8,128)} %bitcast.242, f32[16]{0:T(128)S(1)} %copy-done.107, f32[6,256,16]{1,2,0:T(8,128)S(1)} %copy-done.37, f32[6,16,256]{2,1,0:T(8,128)S(1)} %copy-done.48, f32[6,256,256]{2,1,0:T(8,128)S(1)} %copy-done.18, ...), kind=kOutput, calls=%fused_computation.52 | convolution fusion | flops 850919424 | bytes 28606528 | tf_op jit(solution)/shard_map/sbhij,sbihp->sbjhp/dot_general | solution.py:224
  640.8 6.6 copy.245
  647.4 15.2 %fusion.9 = (f32[1024]{0:T(1024)}, f32[1024]{0:T(1024)}, f32[1024]{0:T(1024)}, f32[1024]{0:T(1024)}, f32[1024]{0:T(1024)}, /*index=5*/f32[6,256,1024]{2,1,0:T(8,128)S(1)}) fusion(f32[6,256]{1,0:T(8,128)S(1)} %copy-done.28, bf16[6,256,1024]{2,1,0:T(8,128)(2,1)} %slice.252, bf16[6,3,1024]{2,1,0:T(4,128)(2,1)} %collective-permute-done, ...), kind=kLoop, calls=%fused_computation.41 | loop fusion | flops 53472256 | bytes 25247744 | tf_op jit(solution)/shard_map/reduce_sum | solution.py:67
  662.6 5.5 multiply_multiply_fusion.4
  668.1 8.0 pad_add_fusion
  679.8 4.2 fusion.65
  691.5 17.8 %fusion.26 = f32[6,256,2048]{2,1,0:T(8,128)S(1)} fusion(bf16[2048,2048,1]{1,0,2:T(8,128)(2,1)} %reshape.667, bf16[6,256,1024]{2,1,0:T(8,128)(2,1)} %scatter-add.10, bf16[6,256,1024]{2,1,0:T(8,128)(2,1)} %get-tuple-element.271), kind=kOutput, calls=%fused_computation.80 | convolution fusion | flops 12897484800 | bytes 27262976 | tf_op jit(solution)/shard_map/dot_general | solution.py:288
  709.3 4.5 add_convert_fusion
  714.5 12.5 bitcast_convert_fusion.3
  727.1 8.0 multiply_convert_fusion.2
  735.3 110.6 %all-reduce.17.cloned.1.call-done = (bf16[6,256,256]{2,1,0:T(8,128)(2,1)}, bf16[6,256,2048]{2,1,0:T(8,128)(2,1)}) async-done(((bf16[6,256,256]{2,1,0:T(8,128)(2,1)}, bf16[6,256,2048]{2,1,0:T(8,128)(2,1)}), (bf16[6,256,256]{2,1,0:T(8,128)(2,1)}, bf16[6,256,2048]{2,1,0:T(8,128)(2,1)})) %all-reduce.17.cloned.1.call-update) | async-done | bytes 7077904 | tf_op jit(solution)/shard_map/psum | solution.py:274
  845.9 4.0 fusion.45
  861.0 6.2 fusion.35
  867.5 20.1 %bitcast_convert_fusion.2 = bf16[2048,2048]{0,1:T(8,128)(2,1)} fusion(bf16[6,256,1024]{2,1,0:T(8,128)(2,1)} %scatter-add.10, bf16[6,256,1024]{2,1,0:T(8,128)(2,1)} %get-tuple-element.271, f32[2048]{0:T(1024)S(1)} %copy-done.87, f32[6,256]{1,0:T(8,128)S(1)} %copy-done.57, bf16[6,256,2048]{2,1,0:T(8,128)(2,1)} %param.26), kind=kOutput, calls=%fused_computation.11 | convolution fusion | flops 12914262016 | bytes 20985856 | tf_op jit(solution)/shard_map/dot_general | solution.py:294
  887.6 21.5 %copy.258 = bf16[2048,2,1024]{2,1,0:T(2,128)(2,1)} copy(bf16[2048,2,1024]{0,2,1:T(8,128)(2,1)} %bitcast.256) | data formatting | bytes 16777216 | tf_op jit(solution)/shard_map/convert_element_type | solution.py:315
  909.1 8.9 convert_element_type.312
  919.3 8.8 convert_element_type.347
  928.4 9.2 reduce-scatter.11.cloned.1.call-done
  939.7 58.6 %reduce-scatter.5.cloned.1.call-done = bf16[6,256,512]{2,1,0:T(8,128)(2,1)} async-done(((bf16[6,256,2048]{2,1,0:T(8,128)(2,1)}), bf16[6,256,512]{2,1,0:T(8,128)(2,1)}) %reduce-scatter.5.cloned.1.call-update) | async-done | bytes 1572880 | tf_op jit(solution)/shard_map/reduce_scatter | solution.py:192
  998.3 4.0 add_convert_fusion.2
  1002.6 53.1 %reduce-scatter.9.cloned.1.call-done = bf16[256,16]{0,1:T(8,128)(2,1)} async-done(((bf16[2048,16]{0,1:T(8,128)(2,1)}), bf16[256,16]{0,1:T(8,128)(2,1)}) %reduce-scatter.9.cloned.1.call-update) | async-done | bytes 8208 | tf_op jit(solution)/shard_map/reduce_scatter | solution.py:320
  1057.1 13.7 multiply_reduce_fusion.4
  1070.9 36.6 %all-reduce.9 = (f32[512]{0:T(512)}, f32[4,1024]{1,0:T(4,128)}, f32[1024]{0:T(1024)}, f32[4,256]{1,0:T(4,128)}, f32[256]{0:T(256)}, /*index=5*/f32[16]{0:T(128)}, f32[16]{0:T(128)}, f32[16]{0:T(128)}, f32[1024]{0:T(1024)}) all-reduce(f32[512]{0:T(512)S(1)} %dynamic_slice.37, ...), channel_id=1, replica_groups=mesh['seq'=8,'head'=4] {'seq'}, use_global_device_ids=true, to_apply=%region_26.27 | all-reduce | flops 7984 | bytes 63872 | tf_op jit(solution)/shard_map/psum | solution.py:327
  1107.5 5.4 fusion.29
  1112.9 9.5 reduce-scatter.7.cloned.1.call-done
  1124.0 272.2 %all-reduce.15.cloned.1.call-done = bf16[2048,2,1024]{2,1,0:T(2,128)(2,1)} async-done(((bf16[2048,2,1024]{2,1,0:T(2,128)(2,1)}), bf16[2048,2,1024]{2,1,0:T(2,128)(2,1)}) %all-reduce.15.cloned.1.call-update) | async-done | bytes 8388624
  (357 shorter events, 65.1 us)
Async XLA Ops:
  7.2 50.8 %copy-start = (bf16[2048,256]{1,0:T(8,128)(2,1)S(1)}, bf16[2048,256]{1,0:T(8,128)(2,1)}, u32[]{:S(2)}) copy-start(bf16[2048,256]{1,0:T(8,128)(2,1)} %param.30) | copy-start | bytes 3145732
  7.2 267.5 %all-gather.8.cloned.1.call-start = ((), (), s32[]{:S(2)}) async-start(), calls=%async_computation.9 | async-start | bytes 14155776 | tf_op jit(solution)/shard_map/all_gather | solution.py:24
  9.5 65.9 %copy-start.68 = (bf16[6,256]{1,0:T(8,128)(2,1)}, bf16[6,256]{1,0:T(8,128)(2,1)S(1)}, u32[]{:S(2)}) copy-start(bf16[6,256]{1,0:T(8,128)(2,1)S(1)} %get-tuple-element.270) | copy-start | bytes 9220
  9.5 67.5 %copy-start.41 = (f32[6,256]{1,0:T(8,128)}, f32[6,256]{1,0:T(8,128)S(1)}, u32[]{:S(2)}) copy-start(f32[6,256]{1,0:T(8,128)S(1)} %get-tuple-element.292) | copy-start | bytes 18436
  9.5 72.3 %copy-start.25 = (f32[6,256]{1,0:T(8,128)}, f32[6,256]{1,0:T(8,128)S(1)}, u32[]{:S(2)}) copy-start(f32[6,256]{1,0:T(8,128)S(1)} %get-tuple-element.269) | copy-start | bytes 18436
  10.1 65.3 %collective-permute-start.1 = (bf16[6,3]{1,0:T(8,128)(2,1)}, bf16[6,3]{1,0:T(8,128)(2,1)}, u32[]{:S(2)}, u32[]{:S(2)}) collective-permute-start(bf16[6,3]{1,0:T(8,128)(2,1)} %slice.255), channel_id=1, source_target_pairs={{0,4},{4,8},{8,12},{12,16},{16,20},{20,24},{24,28},{1,5},{5,9},{9,... | collective-permute-start | bytes 116 | tf_op jit(solution)/shard_map/ppermute | solution.py:16
  19.6 45.2 %copy-start.55 = (f32[6,256]{1,0:T(8,128)}, f32[6,256]{1,0:T(8,128)S(1)}, u32[]{:S(2)}) copy-start(f32[6,256]{1,0:T(8,128)S(1)} %add_rsqrt_fusion.1) | copy-start | bytes 18436
  19.7 38.3 %slice-start.2 = ((s8[6291456]{0:T(1024)(128)(4,1)}), s8[2097152]{0:T(1024)(128)(4,1)S(1)}, s32[]{:S(2)}) async-start(s8[6291456]{0:T(1024)(128)(4,1)} %bitcast.246), calls=%async_computation.15 | async-start | bytes 4194304
  34.3 23.7 %slice-start.3 = ((s8[6291456]{0:T(1024)(128)(4,1)}), s8[4194304]{0:T(1024)(128)(4,1)S(1)}, s32[]{:S(2)}) async-start(s8[6291456]{0:T(1024)(128)(4,1)} %bitcast.246), calls=%async_computation.16 | async-start | bytes 8388608
  54.4 27.4 %collective-permute-start = (bf16[6,3,1024]{2,1,0:T(4,128)(2,1)}, bf16[6,3,1024]{2,1,0:T(4,128)(2,1)}, u32[]{:S(2)}, u32[]{:S(2)}) collective-permute-start(bf16[6,3,1024]{2,1,0:T(4,128)(2,1)} %slice.251), channel_id=1, source_target_pairs={{0,4},{4,8},{8,12},{12,16},{16,20},{20,24},{24,28},{1,5},{5,9},{9,... | collective-permute-start | bytes 110600 | tf_op jit(solution)/shard_map/ppermute | solution.py:16
  60.7 17.5 %collective-permute-start.2 = (bf16[6,3,256]{2,1,0:T(4,128)(2,1)}, bf16[6,3,256]{2,1,0:T(4,128)(2,1)}, u32[]{:S(2)}, u32[]{:S(2)}) collective-permute-start(bf16[6,3,256]{2,1,0:T(4,128)(2,1)} %slice.262), channel_id=1, source_target_pairs={{0,4},{4,8},{8,12},{12,16},{16,20},{20,24},{24,28},{1,5},{5,9},{9,... | collective-permute-start | bytes 27656 | tf_op jit(solution)/shard_map/ppermute | solution.py:16
  66.8 213.2 %copy-start.46 = (f32[6,16,256]{2,1,0:T(8,128)}, f32[6,16,256]{2,1,0:T(8,128)S(1)}, u32[]{:S(2)}) copy-start(f32[6,16,256]{2,1,0:T(8,128)S(1)} %get-tuple-element.284) | copy-start | bytes 294916
  75.3 15.2 %copy-start.60 = (f32[1,1024]{1,0:T(1,128)}, f32[1,1024]{1,0:T(1,128)S(1)}, u32[]{:S(2)}) copy-start(f32[1,1024]{1,0:T(1,128)S(1)} %get-tuple-element.286) | copy-start | bytes 12292
  75.3 15.2 %copy-start.62 = (f32[1,1024]{1,0:T(1,128)}, f32[1,1024]{1,0:T(1,128)S(1)}, u32[]{:S(2)}) copy-start(f32[1,1024]{1,0:T(1,128)S(1)} %get-tuple-element.287) | copy-start | bytes 12292
  75.3 15.2 %copy-start.64 = (f32[1,1024]{1,0:T(1,128)}, f32[1,1024]{1,0:T(1,128)S(1)}, u32[]{:S(2)}) copy-start(f32[1,1024]{1,0:T(1,128)S(1)} %get-tuple-element.288) | copy-start | bytes 12292
  75.3 15.2 %copy-start.66 = (f32[1,1024]{1,0:T(1,128)}, f32[1,1024]{1,0:T(1,128)S(1)}, u32[]{:S(2)}) copy-start(f32[1,1024]{1,0:T(1,128)S(1)} %get-tuple-element.289) | copy-start | bytes 12292
  76.6 294.8 %copy-start.24 = (f32[6,256,16]{1,2,0:T(8,128)}, f32[6,256,16]{1,2,0:T(8,128)S(1)}, u32[]{:S(2)}) copy-start(f32[6,256,16]{1,2,0:T(8,128)S(1)} %get-tuple-element.263) | copy-start | bytes 294916
  77.0 24.8 %copy-start.83 = (f32[6]{0:T(128)}, f32[6]{0:T(128)S(1)}, u32[]{:S(2)}) copy-start(f32[6]{0:T(128)S(1)} %slice_reduce_fusion.4) | copy-start | bytes 76
  77.1 18.1 %copy-start.36 = (f32[6,256,16]{1,2,0:T(8,128)}, f32[6,256,16]{1,2,0:T(8,128)S(1)}, u32[]{:S(2)}) copy-start(f32[6,256,16]{1,2,0:T(8,128)S(1)} %fusion.119) | copy-start | bytes 294916
  81.8 289.7 %copy-start.7 = (bf16[6,256,256]{2,1,0:T(8,128)(2,1)}, bf16[6,256,256]{2,1,0:T(8,128)(2,1)S(1)}, u32[]{:S(2)}) copy-start(bf16[6,256,256]{2,1,0:T(8,128)(2,1)S(1)} %get-tuple-element.265) | copy-start | bytes 2359300
  99.3 221.5 %all-gather.6.cloned.1.call-start = ((), (), s32[]{:S(2)}) async-start(), calls=%async_computation.5 | async-start | bytes 7864320 | tf_op jit(solution)/shard_map/all_gather | solution.py:198
  100.1 469.4 %all-gather.10.cloned.1.call-start = ((), (), s32[]{:S(2)}) async-start(), calls=%async_computation.10 | async-start | bytes 14155776 | tf_op jit(solution)/shard_map/all_gather | solution.py:24
  100.3 179.7 %copy-start.49 = (f32[6,16,256]{2,1,0:T(8,128)}, f32[6,16,256]{2,1,0:T(8,128)S(1)}, u32[]{:S(2)}) copy-start(f32[6,16,256]{2,1,0:T(8,128)S(1)} %reduce_window_sum.49) | copy-start | bytes 294916
  301.4 19.5 %copy-start.102 = (f32[1024]{0:T(1024)S(1)}, f32[1024]{0:T(1024)}, u32[]{:S(2)}) copy-start(f32[1024]{0:T(1024)} %param.39) | copy-start | bytes 12292
  345.5 19.3 %copy-start.69 = (f32[6,256]{1,0:T(8,128)}, f32[6,256]{1,0:T(8,128)S(1)}, u32[]{:S(2)}) copy-start(f32[6,256]{1,0:T(8,128)S(1)} %get-tuple-element.291) | copy-start | bytes 18436
  376.4 469.5 %all-reduce.17.cloned.1.call-start = ((), (), s32[]{:S(2)}) async-start(), calls=%async_computation.12 | async-start | bytes 14155776 | tf_op jit(solution)/shard_map/psum | solution.py:274
  376.4 26.2 %slice-start.6 = ((s8[6291456]{0:T(1024)(128)(4,1)}), s8[4194304]{0:T(1024)(128)(4,1)S(1)}, s32[]{:S(2)}) async-start(s8[6291456]{0:T(1024)(128)(4,1)} %bitcast.254), calls=%async_computation.19 | async-start | bytes 8388608
  382.9 17.3 %copy-start.8 = (bf16[6,256,256]{2,1,0:T(8,128)(2,1)S(1)}, bf16[6,256,256]{2,1,0:T(8,128)(2,1)}, u32[]{:S(2)}) copy-start(bf16[6,256,256]{2,1,0:T(8,128)(2,1)} %copy-done.7) | copy-start | bytes 2359300
  382.9 19.7 %slice-start.7 = ((s8[6291456]{0:T(1024)(128)(4,1)}), s8[2097152]{0:T(1024)(128)(4,1)S(1)}, s32[]{:S(2)}) async-start(s8[6291456]{0:T(1024)(128)(4,1)} %bitcast.254), calls=%async_computation.20 | async-start | bytes 4194304
  571.5 30.8 %copy-start.9 = (bf16[6,256,256]{2,1,0:T(8,128)(2,1)S(1)}, bf16[6,256,256]{2,1,0:T(8,128)(2,1)}, u32[]{:S(2)}) copy-start(bf16[6,256,256]{2,1,0:T(8,128)(2,1)} %copy-done.7) | copy-start | bytes 2359300
  609.0 17.2 %copy-start.18 = (f32[6,256,256]{2,1,0:T(8,128)S(1)}, f32[6,256,256]{2,1,0:T(8,128)}, u32[]{:S(2)}) copy-start(f32[6,256,256]{2,1,0:T(8,128)} %and_convert_fusion) | copy-start | bytes 4718596
  609.0 17.2 %copy-start.37 = (f32[6,256,16]{1,2,0:T(8,128)S(1)}, f32[6,256,16]{1,2,0:T(8,128)}, u32[]{:S(2)}) copy-start(f32[6,256,16]{1,2,0:T(8,128)} %copy-done.36) | copy-start | bytes 294916
  609.1 17.2 %copy-start.48 = (f32[6,16,256]{2,1,0:T(8,128)S(1)}, f32[6,16,256]{2,1,0:T(8,128)}, u32[]{:S(2)}) copy-start(f32[6,16,256]{2,1,0:T(8,128)} %copy-done.46) | copy-start | bytes 294916
  609.1 17.2 %copy-start.107 = (f32[16]{0:T(128)S(1)}, f32[16]{0:T(128)}, u32[]{:S(2)}) copy-start(f32[16]{0:T(128)} %param.38) | copy-start | bytes 196
  647.4 15.2 %copy-start.61 = (f32[1,1024]{1,0:T(1,128)S(1)}, f32[1,1024]{1,0:T(1,128)}, u32[]{:S(2)}) copy-start(f32[1,1024]{1,0:T(1,128)} %copy-done.60) | copy-start | bytes 12292
  647.4 15.2 %copy-start.63 = (f32[1,1024]{1,0:T(1,128)S(1)}, f32[1,1024]{1,0:T(1,128)}, u32[]{:S(2)}) copy-start(f32[1,1024]{1,0:T(1,128)} %copy-done.62) | copy-start | bytes 12292
  647.4 15.2 %copy-start.65 = (f32[1,1024]{1,0:T(1,128)S(1)}, f32[1,1024]{1,0:T(1,128)}, u32[]{:S(2)}) copy-start(f32[1,1024]{1,0:T(1,128)} %copy-done.64) | copy-start | bytes 12292
  647.4 15.2 %copy-start.67 = (f32[1,1024]{1,0:T(1,128)S(1)}, f32[1,1024]{1,0:T(1,128)}, u32[]{:S(2)}) copy-start(f32[1,1024]{1,0:T(1,128)} %copy-done.66) | copy-start | bytes 12292
  677.7 11.2 collective-permute-start.3
  685.4 23.8 %copy-start.39 = (bf16[6,256,16]{1,2,0:T(8,128)(2,1)}, bf16[6,256,16]{1,2,0:T(8,128)(2,1)S(1)}, u32[]{:S(2)}) copy-start(bf16[6,256,16]{1,2,0:T(8,128)(2,1)S(1)} %get-tuple-element.257) | copy-start | bytes 147460
  691.5 17.8 %copy-start.59 = (bf16[2048,16]{0,1:T(8,128)(2,1)S(1)}, bf16[2048,16]{0,1:T(8,128)(2,1)}, u32[]{:S(2)}) copy-start(bf16[2048,16]{0,1:T(8,128)(2,1)} %param.31) | copy-start | bytes 196612
  713.8 223.8 %reduce-scatter.11.cloned.1.call-start = ((), (), s32[]{:S(2)}) async-start(), calls=%async_computation.8 | async-start | bytes 4718592 | tf_op jit(solution)/shard_map/reduce_scatter | solution.py:323
  727.1 271.3 %reduce-scatter.5.cloned.1.call-start = ((), (), s32[]{:S(2)}) async-start(), calls=%async_computation.4 | async-start | bytes 7864320 | tf_op jit(solution)/shard_map/reduce_scatter | solution.py:192
  735.1 110.7 %copy-start.13 = (f32[6,256,256]{2,1,0:T(8,128)S(1)}, f32[6,256,256]{2,1,0:T(8,128)}, u32[]{:S(2)}) copy-start(f32[6,256,256]{2,1,0:T(8,128)} %get-tuple-element.266) | copy-start | bytes 4718596
  735.1 110.7 %copy-start.16 = (bf16[6,256,256]{2,1,0:T(8,128)(2,1)S(1)}, bf16[6,256,256]{2,1,0:T(8,128)(2,1)}, u32[]{:S(2)}) copy-start(bf16[6,256,256]{2,1,0:T(8,128)(2,1)} %copy-done.14) | copy-start | bytes 2359300
  735.2 110.7 %copy-start.31 = (f32[6,256]{1,0:T(8,128)S(1)}, f32[6,256]{1,0:T(8,128)}, u32[]{:S(2)}) copy-start(f32[6,256]{1,0:T(8,128)} %copy-done.29) | copy-start | bytes 18436
  735.2 110.7 %copy-start.34 = (f32[6,256]{1,0:T(8,128)S(1)}, f32[6,256]{1,0:T(8,128)}, u32[]{:S(2)}) copy-start(f32[6,256]{1,0:T(8,128)} %copy-done.32) | copy-start | bytes 18436
  735.2 114.7 %copy-start.78 = (f32[1,256]{1,0:T(1,128)S(1)}, f32[1,256]{1,0:T(1,128)}, u32[]{:S(2)}) copy-start(f32[1,256]{1,0:T(1,128)} %copy-done.77) | copy-start | bytes 3076
  735.2 114.7 %copy-start.80 = (f32[1,256]{1,0:T(1,128)S(1)}, f32[1,256]{1,0:T(1,128)}, u32[]{:S(2)}) copy-start(f32[1,256]{1,0:T(1,128)} %copy-done.79) | copy-start | bytes 3076
  735.2 320.5 %reduce-scatter.9.cloned.1.call-start = ((), (), s32[]{:S(2)}) async-start(), calls=%async_computation.7 | async-start | bytes 73728 | tf_op jit(solution)/shard_map/reduce_scatter | solution.py:320
  852.9 5.9 collective-permute-start.4
  856.6 265.8 %reduce-scatter.7.cloned.1.call-start = ((), (), s32[]{:S(2)}) async-start(), calls=%async_computation.6 | async-start | bytes 1179648 | tf_op jit(solution)/shard_map/reduce_scatter | solution.py:317
  867.3 528.9 %all-reduce.15.cloned.1.call-start = ((), (), s32[]{:S(2)}) async-start(), calls=%async_computation.11 | async-start | bytes 16777216
  928.1 74.3 %copy-start.73 = (f32[1024]{0:T(1024)S(1)}, f32[1024]{0:T(1024)}, u32[]{:S(2)}) copy-start(f32[1024]{0:T(1024)} %get-tuple-element.205) | copy-start | bytes 12292
  928.1 74.3 %copy-start.74 = (f32[1024]{0:T(1024)S(1)}, f32[1024]{0:T(1024)}, u32[]{:S(2)}) copy-start(f32[1024]{0:T(1024)} %get-tuple-element.206) | copy-start | bytes 12292
  928.1 74.3 %copy-start.75 = (f32[1024]{0:T(1024)S(1)}, f32[1024]{0:T(1024)}, u32[]{:S(2)}) copy-start(f32[1024]{0:T(1024)} %get-tuple-element.207) | copy-start | bytes 12292
  928.1 74.3 %copy-start.76 = (f32[1024]{0:T(1024)S(1)}, f32[1024]{0:T(1024)}, u32[]{:S(2)}) copy-start(f32[1024]{0:T(1024)} %get-tuple-element.211) | copy-start | bytes 12292
  928.1 74.3 %copy-start.21 = (f32[6,1,16,256]{3,2,0,1:T(8,128)S(1)}, f32[6,1,16,256]{3,2,0,1:T(8,128)}, u32[]{:S(2)}) copy-start(f32[6,1,16,256]{3,2,0,1:T(8,128)} %copy-done.20) | copy-start | bytes 294916
  928.1 74.3 %copy-start.23 = (f32[6,1,16,256]{3,2,0,1:T(8,128)S(1)}, f32[6,1,16,256]{3,2,0,1:T(8,128)}, u32[]{:S(2)}) copy-start(f32[6,1,16,256]{3,2,0,1:T(8,128)} %copy-done.22) | copy-start | bytes 294916
  928.1 74.3 %copy-start.99 = (f32[16]{0:T(128)S(1)}, f32[16]{0:T(128)}, u32[]{:S(2)}) copy-start(f32[16]{0:T(128)} %copy-done.98) | copy-start | bytes 196
  928.2 128.9 %copy-start.94 = (f32[256]{0:T(256)S(1)}, f32[256]{0:T(256)}, u32[]{:S(2)}) copy-start(f32[256]{0:T(256)} %get-tuple-element.212) | copy-start | bytes 3076
  928.2 128.9 %copy-start.95 = (f32[256]{0:T(256)S(1)}, f32[256]{0:T(256)}, u32[]{:S(2)}) copy-start(f32[256]{0:T(256)} %get-tuple-element.213) | copy-start | bytes 3076
  928.2 128.9 %copy-start.96 = (f32[256]{0:T(256)S(1)}, f32[256]{0:T(256)}, u32[]{:S(2)}) copy-start(f32[256]{0:T(256)} %get-tuple-element.214) | copy-start | bytes 3076
  928.2 128.9 %copy-start.97 = (f32[256]{0:T(256)S(1)}, f32[256]{0:T(256)}, u32[]{:S(2)}) copy-start(f32[256]{0:T(256)} %get-tuple-element.215) | copy-start | bytes 3076
  (67 other events, 535.1 us)
Sparse Core Ops, SparseCore 0:
  99.4 175.1 all-gather.7
  276.2 44.5 all-gather.5
  376.5 192.9 all-gather.9
  714.0 131.8 all-reduce.16
  849.3 88.2 reduce-scatter.10
  940.1 58.1 reduce-scatter.4
  1002.0 53.6 reduce-scatter.8
  1059.7 62.5 reduce-scatter.6
  1126.7 269.4 all-reduce.14
where the time goes:
time: 1410 us
  waiting for transfers between devices  832 us (59%)
  matrix products  207 us (15%)
  other arithmetic  165 us (12%)
  local copies, waits for them, and re-layouts  95.4 us (7%)
  blocking collectives  73.8 us (5%)
  starting transfers between devices  16.3 us (1%)
  between operations  16.2 us (1%)
    all_gather x2, waiting for transfers between devices, prefix(): lax.all_gather(a.astype(kind), axis)  304 us
    unnamed x10, waiting for transfers between devices  273 us
    psum x1, waiting for transfers between devices, local(): lax.psum(d_bc_part.astype(jnp.bfloat16), 'head').astype(jnp.float32)  111 us
    reduce_scatter x1, waiting for transfers between devices, local(): lax.psum_scatter(out_term.astype(jnp.bfloat16), 'head', scatter_dimension...  58.6 us
    reduce_scatter x1, waiting for transfers between devices, local(): lax.psum_scatter(g_w_dt.astype(jnp.bfloat16), 'seq', scatter_dimension=0,...  53.1 us
    psum x1, blocking collectives, local(): lax.psum((g_norm, g_conv_x, g_conv_x_bias, g_conv_bc, g_conv_bc_bias, g_d...  36.6 us
    add x7, other arithmetic, compose(): later[0][..., None, None] * earlier[1] + later[1]  30.6 us
  transfers between devices with their start and end apart: 14, of which 10 were waited for; matrix products, arithmetic and copies ran while one was open for 19% of the time, Pallas kernels for 0%

commit v1 on v0

v1 whole, which is shorter than its diff:
```python
import functools

import jax
import jax.numpy as jnp
from jax import lax
from jax.experimental import pallas as pl
from jax.experimental.pallas import tpu as pltpu
from jax.sharding import PartitionSpec as P

HEAD_DIM = 64
BLOCK_LEN = 256
LANES = 128
EDGE = 16
ROWS = 16
VMEM = 56 * 2**20
EPS = 1e-05
BF = jnp.bfloat16
F32 = jnp.float32
SMEM_SPEC = pl.BlockSpec(memory_space=pltpu.SMEM)


def dot(a, b, contract=((1,), (0,)), precision=None):
    return lax.dot_general(
        a, b, (contract, ((), ())), preferred_element_type=F32, precision=precision
    )


def halves(value):
    high = value.astype(BF)
    return high, (value - high.astype(F32)).astype(BF)


def widen(value, expand):
    high, low = halves(value)
    return dot(high, expand) + dot(low, expand)


def per_head(value, expand):
    high, low = halves(value)
    nt = ((1,), (1,))
    return dot(high, expand, nt) + dot(low, expand, nt)


def to_row(column):
    rows = column.shape[0]
    return jnp.transpose(jnp.broadcast_to(column, (rows, LANES)))[:8]


def sigmoid(value):
    return 1.0 / (1.0 + jnp.exp(-value))


def softplus(value):
    return jnp.maximum(value, 0.0) + jnp.log1p(jnp.exp(-jnp.abs(value)))


def triangle(span, lower):
    row = lax.broadcasted_iota(jnp.int32, (span, span), 0)
    col = lax.broadcasted_iota(jnp.int32, (span, span), 1)
    return ((col <= row) if lower else (col >= row)).astype(F32)


def running(value, lower):
    return dot(triangle(value.shape[0], lower), value, precision=lax.Precision.HIGHEST)


def doc_mask(seg_col, seg_row, lower):
    span = seg_col.shape[0]
    row = lax.broadcasted_iota(jnp.int32, (span, span), 0)
    col = lax.broadcasted_iota(jnp.int32, (span, span), 1)
    causal = (col <= row) if lower else (col >= row)
    return jnp.where(causal, (seg_col == seg_row).astype(F32), 0.0)


def back_rows(value, steps):
    return value if steps == 0 else pltpu.roll(value, steps, 0)


def ahead_rows(value, steps):
    return value if steps == 0 else pltpu.roll(value, value.shape[0] - steps, 0)


def conv_rows(extended, aux, weight):
    taps = 4
    out = weight[taps : taps + 1] + weight[taps - 1 : taps] * extended[EDGE:]
    for tap in range(taps - 1):
        window = back_rows(extended, taps - 1 - tap)[EDGE:]
        out = out + weight[tap : tap + 1] * (aux[:, tap : tap + 1] * window)
    return out


def conv_back_rows(d_conv, extended, aux, weight, grad_ref, width_at):
    taps = 4
    lanes = pl.ds(width_at, d_conv.shape[1])
    room = jnp.zeros((EDGE, d_conv.shape[1]), F32)
    total = None
    for tap in range(taps):
        steps = taps - 1 - tap
        masked = d_conv if steps == 0 else d_conv * aux[:, tap : tap + 1]
        window = back_rows(extended, steps)[EDGE:]
        grad_ref[tap : tap + 1, lanes] += jnp.sum(masked * window, axis=0, keepdims=True)
        placed = jnp.concatenate([room, masked * weight[tap : tap + 1]], axis=0)
        placed = ahead_rows(placed, steps)
        total = placed if total is None else total + placed
    grad_ref[taps : taps + 1, lanes] += jnp.sum(d_conv, axis=0, keepdims=True)
    return total


def chunk_grid(n_seq, state, own):
    across = n_seq * ROWS // state
    return across, own // across


def spread(value, scratch, outs, me, n_seq):
    across, width = chunk_grid(n_seq, value.shape[0], value.shape[1])
    for j in range(n_seq):
        a, b = j // across, j % across
        scratch[j] = value[a * ROWS : (a + 1) * ROWS, b * width : (b + 1) * width].astype(BF)
    for m in range(n_seq):
        outs[m][0] = scratch[me ^ m]


def collect(ins, scratch, me, n_seq, state, own):
    across, _ = chunk_grid(n_seq, state, own)
    for m in range(n_seq):
        scratch[me ^ m] = ins[m][0]
    rows = []
    for a in range(n_seq // across):
        rows.append(
            jnp.concatenate([scratch[a * across + b] for b in range(across)], axis=1)
            if across > 1
            else scratch[a]
        )
    return jnp.concatenate(rows, axis=0)


def front_kernel(
    seqs, n_seq, state, me_ref, tok_ref, halo_ref, gain_ref, w_ref, aux_ref, conv_ref, head_ref,
    expand_ref, normed_ref, pre_ref, pre_halo_ref, act_ref, xs_ref, dt_ref, cum_ref, *rest
):
    outs, scratch, extra = rest[:n_seq], rest[n_seq], rest[n_seq + 1]
    s = pl.program_id(0)
    me = me_ref[0]
    own = xs_ref.shape[-1]
    wide = own + 2 * state
    across, width = chunk_grid(n_seq, state, own)

    @pl.when(s == 0)
    def _():
        extra[...] = jnp.zeros_like(extra)

    @pl.when(s < seqs)
    def _():
        def norm(value):
            value = value.astype(F32)
            rstd = lax.rsqrt(jnp.mean(value * value, axis=-1, keepdims=True) + EPS)
            return (value * rstd * gain_ref[...]).astype(BF)

        normed = norm(tok_ref[0])
        normed_ref[0] = normed
        room = jnp.zeros((EDGE - halo_ref.shape[1], halo_ref.shape[2]), F32)
        ahead = jnp.concatenate([room, norm(halo_ref[0]).astype(F32)], axis=0).astype(BF)
        projected = dot(jnp.concatenate([ahead, normed], axis=0), w_ref[...])
        dt_raw = projected[EDGE:, wide:]
        dt_ref[0] = dt_raw
        pre = projected[:, :wide].astype(BF)
        pre_ref[0] = pre[EDGE:]
        pre_halo_ref[0] = pre[:EDGE]
        aux = aux_ref[0]
        conv = conv_rows(pre.astype(F32), aux, conv_ref[...])
        act = (conv * sigmoid(conv)).astype(BF)
        act_ref[0] = act
        x_float = act[:, :own].astype(F32)
        step = softplus(dt_raw + head_ref[0:1])
        log_decay = -head_ref[1:2] * step
        cum = running(log_decay, True)
        cum_ref[0] = cum
        expand = expand_ref[...]
        step_wide = widen(step, expand)
        xs_ref[0] = (x_float * step_wide).astype(BF)
        last = cum[-1:]
        tail_step = jnp.exp(last - cum) * aux[:, 3:4] * step
        loaded = (x_float * widen(tail_step, expand)).astype(BF)
        b_ssm = act[:, own : own + state]
        spread(dot(b_ssm, loaded, ((0,), (0,))), scratch, outs, me, n_seq)
        decay = jnp.broadcast_to(jnp.exp(last) * aux[-1:, 4:5], (8, LANES))
        decay_wide = widen(decay, expand)[:1]
        high = decay_wide.astype(BF).astype(F32)
        places = lax.broadcasted_iota(jnp.int32, (ROWS, 1), 0)
        extra[...] += jnp.where(places == s, high, 0.0) + jnp.where(
            places == s + seqs, decay_wide - high, 0.0
        )

    @pl.when(s == seqs)
    def _():
        for j in range(n_seq):
            b = j % across
            scratch[j] = extra[:, b * width : (b + 1) * width].astype(BF)
        for m in range(n_seq):
            outs[m][0] = scratch[me ^ m]


def scan_kernel(seqs, n_seq, me_ref, *rest):
    ins, outs = rest[:n_seq], rest[n_seq : 2 * n_seq]
    decay_ref, scratch = rest[2 * n_seq], rest[2 * n_seq + 1]
    me = me_ref[0]
    for m in range(n_seq):
        scratch[me ^ m] = ins[m][...]
    for s in range(seqs):
        entry = jnp.zeros(scratch.shape[2:], F32)
        for k in range(n_seq):
            packed = scratch[k, seqs].astype(F32)
            decay = packed[s : s + 1] + packed[s + seqs : s + seqs + 1]
            decay_ref[k, s : s + 1] = decay
            arrived = scratch[k, s].astype(F32)
            scratch[k, s] = entry.astype(BF)
            entry = decay * entry + arrived
    for m in range(n_seq):
        outs[m][...] = scratch[me ^ m, :seqs]


def scan_back_kernel(seqs, n_seq, me_ref, decay_ref, *rest):
    ins, outs, scratch = rest[:n_seq], rest[n_seq : 2 * n_seq], rest[2 * n_seq]
    me = me_ref[0]
    for m in range(n_seq):
        scratch[me ^ m] = ins[m][...]
    for s in range(seqs):
        leave = jnp.zeros(scratch.shape[2:], F32)
        for k in reversed(range(n_seq)):
            arrived = scratch[k, s].astype(F32)
            scratch[k, s] = leave.astype(BF)
            leave = decay_ref[k, s : s + 1] * leave + arrived
    for m in range(n_seq):
        outs[m][...] = scratch[me ^ m]


def inner_kernel(state, act_ref, xs_ref, cum_ref, aux_ref, seg_ref, out_ref):
    own = xs_ref.shape[-1]
    b_ssm, c_ssm = act_ref[0, :, own : own + state], act_ref[0, :, own + state :]
    cum = cum_ref[0]
    cum_t = jnp.transpose(cum)
    scores = dot(c_ssm, b_ssm, ((1,), (1,))) * doc_mask(aux_ref[0, :, 5:6], seg_ref[0, 0:1], True)
    left = lax.broadcasted_iota(jnp.int32, (1, LANES), 1) < HEAD_DIM
    for pair in range(own // LANES):
        lanes = slice(pair * LANES, (pair + 1) * LANES)
        xs = xs_ref[0, :, lanes].astype(F32)
        total = None
        for side in range(2):
            h = 2 * pair + side
            lag = jnp.minimum(cum[:, h : h + 1] - cum_t[h : h + 1], 0.0)
            weights = (scores * jnp.exp(lag)).astype(BF)
            own_xs = jnp.where(left if side == 0 else ~left, xs, 0.0).astype(BF)
            term = dot(weights, own_xs)
            total = term if total is None else total + term
        out_ref[0, :, lanes] = total


def mixer_out(state, states, act_ref, inner_ref, gate_ref, cum_ref, aux_ref, rows_ref, expand_ref):
    own = inner_ref.shape[-1]
    c_ssm = act_ref[0, :, own + state :]
    x_float = act_ref[0, :, :own].astype(F32)
    entry_wide = widen(jnp.exp(cum_ref[0]) * aux_ref[0, :, 4:5], expand_ref[...])
    mixed = inner_ref[0] + dot(c_ssm, states) * entry_wide
    y = mixed + rows_ref[1:2] * x_float
    gate = gate_ref[0].astype(F32)
    sig = sigmoid(gate)
    return mixed, y, x_float, gate, sig, entry_wide


def sums_kernel(
    n_seq, state, me_ref, act_ref, inner_ref, gate_ref, e_ref, cum_ref, aux_ref, rows_ref,
    expand_ref, *rest
):
    ins, out_ref, scratch = rest[:n_seq], rest[n_seq], rest[n_seq + 1]
    states = collect(ins, scratch, me_ref[0], n_seq, state, inner_ref.shape[-1])
    _, y, _, gate, sig, _ = mixer_out(
        state, states, act_ref, inner_ref, gate_ref, cum_ref, aux_ref, rows_ref, expand_ref
    )
    gated = y * (gate * sig)
    squares = jnp.sum(gated * gated, axis=-1, keepdims=True)
    dots = jnp.sum(e_ref[0].astype(F32) * (gated * rows_ref[0:1]), axis=-1, keepdims=True)
    out_ref[0, 0:1] = to_row(squares)[:1]
    out_ref[0, 1:2] = to_row(dots)[:1]


def gate_back_kernel(
    n_seq, state, inner_total, me_ref, act_ref, inner_ref, gate_ref, e_ref, cum_ref, aux_ref,
    rows_ref, expand_ref, sums_ref, *rest
):
    ins, rest = rest[:n_seq], rest[n_seq:]
    scaled_ref, dz_ref, dy_ref, mixed_ref, dc_ref, dot_ref, grad_ref = rest[:7]
    outs, scratch = rest[7 : 7 + n_seq], rest[7 + n_seq]
    me = me_ref[0]
    own = inner_ref.shape[-1]
    expand = expand_ref[...]
    states = collect(ins, scratch, me, n_seq, state, own)
    mixed, y, x_float, gate, sig, entry_wide = mixer_out(
        state, states, act_ref, inner_ref, gate_ref, cum_ref, aux_ref, rows_ref, expand_ref
    )
    columns = jnp.transpose(
        jnp.concatenate([sums_ref[0], jnp.zeros((LANES - 8, sums_ref.shape[2]), F32)], axis=0)
    )
    rstd = lax.rsqrt(columns[:, 0:1] / inner_total + EPS)
    slope = columns[:, 1:2] * (rstd * rstd * rstd) / inner_total
    gain = rows_ref[0:1]
    silu = gate * sig
    gated = y * silu
    scaled_ref[0] = (gated * gain * rstd).astype(BF)
    d_scaled = e_ref[0].astype(F32) * rstd
    d_gated = d_scaled * gain - slope * gated
    d_y = d_gated * silu
    dy_ref[0] = d_y.astype(BF)
    d_z = (d_gated * y * (sig * (1.0 + gate * (1.0 - sig)))).astype(BF)
    dz_ref[0] = d_z
    row = jnp.sum(d_z.astype(F32) * gate, axis=-1, keepdims=True)
    dot_ref[0] = to_row(row)
    mixed_ref[0] = per_head(d_y * mixed, expand)

    @pl.when(pl.program_id(0) == 0)
    def _():
        grad_ref[...] = jnp.zeros_like(grad_ref)

    grad_ref[0:1] += jnp.sum(d_scaled * gated, axis=0, keepdims=True)
    grad_ref[1:2] += jnp.sum(d_y * x_float, axis=0, keepdims=True)
    d_carried = (d_y * entry_wide).astype(BF)
    c_ssm = act_ref[0, :, own + state :]
    dc_ref[0] = dot(d_carried, states, ((1,), (1,)))
    spread(dot(c_ssm, d_carried, ((0,), (0,))), scratch, outs, me, n_seq)


def inner_back_kernel(
    state, act_ref, xs_ref, dy_ref, dc_ref, cum_ref, dt_ref, aux_ref, seg_ref, rows_ref, head_ref,
    expand_ref, dx_ref, dstep_ref, dbc_ref
):
    own = xs_ref.shape[-1]
    b_ssm, c_ssm = act_ref[0, :, own : own + state], act_ref[0, :, own + state :]
    cum = cum_ref[0]
    cum_t = jnp.transpose(cum)
    nt = ((1,), (1,))
    mask = doc_mask(aux_ref[0, :, 5:6], seg_ref[0, 0:1], False)
    scores = dot(b_ssm, c_ssm, nt) * mask
    left = lax.broadcasted_iota(jnp.int32, (1, LANES), 1) < HEAD_DIM
    d_scores = None
    sums = []
    for pair in range(own // LANES):
        lanes = slice(pair * LANES, (pair + 1) * LANES)
        xs = xs_ref[0, :, lanes]
        dy = dy_ref[0, :, lanes].astype(F32)
        total = None
        for side in range(2):
            h = 2 * pair + side
            lag = jnp.minimum(cum_t[h : h + 1] - cum[:, h : h + 1], 0.0)
            mixing = jnp.exp(lag)
            weights = (scores * mixing).astype(BF)
            own_dy = jnp.where(left if side == 0 else ~left, dy, 0.0).astype(BF)
            term = dot(weights, own_dy)
            total = term if total is None else total + term
            d_mixed = dot(xs, own_dy, nt) * mixing
            d_scores = d_mixed if d_scores is None else d_scores + d_mixed
        sums.append(total)
    back = jnp.concatenate(sums, axis=1)
    expand = expand_ref[...]
    x_float = act_ref[0, :, :own].astype(F32)
    dstep_ref[0] = per_head(x_float * back, expand)
    step = softplus(dt_ref[0] + head_ref[0:1])
    dy_all = dy_ref[0].astype(F32)
    dx_ref[0] = (back * widen(step, expand) + rows_ref[1:2] * dy_all).astype(BF)
    d_scores = (d_scores * mask).astype(BF)
    dbc_ref[0, :, :state] = dot(d_scores, c_ssm)
    dbc_ref[0, :, state:] = dot(d_scores, b_ssm, ((0,), (0,))) + dc_ref[0]


def leave_kernel(
    n_seq, state, me_ref, act_ref, pre_ref, pre_halo_ref, dx_ref, dstep_ref, dbc_ref, mixed_ref,
    cum_ref, dt_ref, aux_ref, conv_ref, head_ref, expand_ref, *rest
):
    in_states, in_ends, rest = rest[:n_seq], rest[n_seq : 2 * n_seq], rest[2 * n_seq :]
    dpre_ref, back_ref, dbc_out_ref, ddt_ref, dot_ref, grad_ref, small_ref, scratch = rest
    me = me_ref[0]
    own = dx_ref.shape[-1]
    expand = expand_ref[...]
    states = collect(in_states, scratch, me, n_seq, state, own)
    ends = collect(in_ends, scratch, me, n_seq, state, own)
    b_ssm = act_ref[0, :, own : own + state]
    x_float = act_ref[0, :, :own].astype(F32)
    aux = aux_ref[0]
    dt_pre = dt_ref[0] + head_ref[0:1]
    step = softplus(dt_pre)
    rate = head_ref[1:2]
    cum = cum_ref[0]
    last = cum[-1:]
    tail_decay = jnp.exp(last - cum) * aux[:, 3:4]
    tail_step = tail_decay * step
    tail_wide = widen(tail_step, expand)
    loaded = (x_float * tail_wide).astype(BF)
    d_loaded = dot(b_ssm, ends)
    dbc_out_ref[0, :, :state] = (dbc_ref[0, :, :state] + dot(loaded, ends, ((1,), (1,)))).astype(BF)
    dbc_out_ref[0, :, state:] = dbc_ref[0, :, state:].astype(BF)
    d_x = dx_ref[0].astype(F32) + d_loaded * tail_wide
    d_tail = per_head(d_loaded * x_float, expand)
    end_terms = d_tail * tail_step
    product = jnp.sum(ends.astype(F32) * states.astype(F32), axis=0, keepdims=True)
    d_decay = per_head(jnp.broadcast_to(product, (8, own)), expand)[:1]
    block_decay = jnp.exp(last) * aux[-1:, 4:5]
    d_cum = mixed_ref[0] - step * dstep_ref[0] - end_terms
    last_add = jnp.sum(end_terms, axis=0, keepdims=True) + d_decay * block_decay
    d_log = running(d_cum, False) + last_add
    d_step = dstep_ref[0] + d_tail * tail_decay - d_log * rate
    d_dt = d_step * sigmoid(dt_pre)
    ddt_ref[0] = d_dt.astype(BF)

    @pl.when(pl.program_id(0) == 0)
    def _():
        grad_ref[...] = jnp.zeros_like(grad_ref)
        small_ref[...] = jnp.zeros_like(small_ref)

    small_ref[0:1] += jnp.sum(d_dt, axis=0, keepdims=True)
    small_ref[1:2] += jnp.sum(d_log * (-rate * step), axis=0, keepdims=True)

    extended = jnp.concatenate([pre_halo_ref[0, :, :own], pre_ref[0, :, :own]], axis=0).astype(F32)
    weight = conv_ref[:, :own]
    conv = conv_rows(extended, aux, weight)
    sig = sigmoid(conv)
    d_conv = d_x * (sig * (1.0 + conv * (1.0 - sig)))
    d_ext = conv_back_rows(d_conv, extended, aux, weight, grad_ref, 0)
    d_pre = d_ext[EDGE:].astype(BF)
    dpre_ref[0] = d_pre
    back_ref[0] = d_ext[:EDGE].astype(BF)
    row = jnp.sum(d_pre.astype(F32) * extended[EDGE:], axis=-1, keepdims=True)
    row = row + jnp.sum(ddt_ref[0].astype(F32) * dt_ref[0], axis=-1, keepdims=True)
    dot_ref[0] = to_row(row)


def conv_bc_kernel(
    own, d_ref, pre_ref, pre_halo_ref, aux_ref, conv_ref, dpre_ref, back_ref, grad_ref
):
    extended = jnp.concatenate([pre_halo_ref[0], pre_ref[0]], axis=0).astype(F32)
    aux = aux_ref[0]
    weight = conv_ref[...]
    conv = conv_rows(extended, aux, weight)
    sig = sigmoid(conv)
    d_conv = d_ref[0].astype(F32) * (sig * (1.0 + conv * (1.0 - sig)))

    @pl.when(pl.program_id(0) == 0)
    def _():
        grad_ref[...] = jnp.zeros_like(grad_ref)

    d_ext = conv_back_rows(d_conv, extended, aux, weight, grad_ref, 0)
    dpre_ref[0] = d_ext[EDGE:].astype(BF)
    back_ref[0] = d_ext[:EDGE].astype(BF)


def per_seq(seqs, shape):
    zeros = (0,) * len(shape)
    return pl.BlockSpec((1, *shape), lambda s: (jnp.minimum(s, seqs - 1), *zeros))


def whole(shape):
    zeros = (0,) * len(shape)
    return pl.BlockSpec(tuple(shape), lambda s: zeros)


def call(body, grid, ins, in_specs, outs, out_specs, scratch, flops, name):
    moved = sum(v.size * v.dtype.itemsize for v in (*ins, *outs))
    return pl.pallas_call(
        body,
        grid=(grid,),
        in_specs=in_specs,
        out_specs=out_specs,
        out_shape=outs,
        scratch_shapes=scratch,
        name=name,
        compiler_params=pltpu.CompilerParams(vmem_limit_bytes=VMEM),
        cost_estimate=pl.CostEstimate(flops=int(flops), bytes_accessed=moved, transcendentals=0),
    )(*ins)


def shaped(shape, dtype):
    return jax.ShapeDtypeStruct(tuple(shape), dtype)


def swap(value, axis, mask):
    count = lax.axis_size(axis)
    return lax.ppermute(value, axis, [(i, i ^ mask) for i in range(count)])


def shift(value, axis, steps):
    count = lax.axis_size(axis)
    leading, last = (max(0, -steps), min(count, count - steps))
    return lax.ppermute(value, axis, [(i, i + steps) for i in range(leading, last)])


def exchange(chunks, axis):
    return [chunks[0]] + [swap(chunks[m], axis, m) for m in range(1, len(chunks))]


def pick(stacked, at, axis=0):
    return lax.dynamic_index_in_dim(stacked, at, axis, False)


def halving_scatter(chunks, axis):
    me = lax.axis_index(axis)
    mask = 1
    while chunks.shape[0] > 1:
        pairs = chunks.reshape(chunks.shape[0] // 2, 2, *chunks.shape[1:])
        bit = (me // mask) % 2
        chunks = pick(pairs, bit, 1) + swap(pick(pairs, 1 - bit, 1), axis, mask)
        mask *= 2
    return chunks[0]


def sum_all(value, axis):
    mask = 1
    while mask < lax.axis_size(axis):
        value = value + swap(value, axis, mask)
        mask *= 2
    return value


def pad_lanes(value, width):
    return jnp.pad(value, ((0, 0), (0, width - value.shape[1])))


def pad_rows(rows, count=8):
    stacked = jnp.concatenate([r.reshape(-1, r.shape[-1]).astype(F32) for r in rows], axis=0)
    return jnp.pad(stacked, ((0, count - stacked.shape[0]), (0, 0)))


def local(
    tokens,
    segments,
    norm_gain,
    w_zx,
    w_bc,
    w_dt,
    conv_x,
    conv_x_bias,
    conv_bc,
    conv_bc_bias,
    dt_bias,
    a_log,
    d_skip,
    gate_gain,
    w_out,
    cotangent,
):
    seqs, span, model = tokens.shape
    heads = d_skip.shape[0]
    own = heads * HEAD_DIM
    n_seq, n_head = lax.axis_size("seq"), lax.axis_size("head")
    me_head = lax.axis_index("head")
    me = lax.axis_index("seq").astype(jnp.int32).reshape(1)
    inner_total = own * n_head
    state = w_bc.shape[1] // 2
    wide = own + 2 * state
    share = model // n_head
    offset = me_head * share
    edge = conv_x.shape[0] - 1
    _, width = chunk_grid(n_seq, state, own)

    tok_halo = shift(tokens[:, -8:], "seq", 1)
    seg_halo = shift(segments[:, -8:], "seq", 1)
    cot_full = lax.all_gather(cotangent, "head", axis=2, tiled=True)

    seg_ext = jnp.concatenate([seg_halo, segments], axis=1)
    aux = [(seg_ext[:, 8 - edge + tap : 8 - edge + tap + span] == segments) for tap in range(edge)]
    aux.append(segments == segments[:, -1:])
    aux.append(segments == seg_halo[:, -1:])
    aux = [a.astype(F32) for a in aux] + [segments.astype(F32)]
    aux = jnp.stack(aux + [jnp.zeros_like(aux[0])] * 2, axis=-1)
    seg_row = jnp.broadcast_to(segments.astype(F32)[:, None], (seqs, 8, span))
    conv_w = jnp.concatenate(
        [pad_rows([conv_x, conv_x_bias]), pad_rows([conv_bc, conv_bc_bias])], axis=1
    )
    head_rows = pad_lanes(pad_rows([dt_bias, jnp.exp(a_log)]), LANES)
    wide_rows = pad_rows([gate_gain, jnp.repeat(d_skip, HEAD_DIM)])
    expand = (
        jnp.arange(LANES)[:, None] == (jnp.arange(own) // HEAD_DIM)[None, :]
    ).astype(BF)
    w_z, w_x = w_zx[:, 0, :], w_zx[:, 1, :]
    w_cat = jnp.concatenate([w_x, w_bc, pad_lanes(w_dt, LANES)], axis=1)

    seq = functools.partial(per_seq, seqs)
    chunk_spec = seq((ROWS, width))
    ins = (me, tokens, tok_halo, norm_gain.reshape(1, model), w_cat, aux, conv_w, head_rows, expand)
    outs = (
        shaped((seqs, span, model), BF),
        shaped((seqs, span, wide), BF),
        shaped((seqs, EDGE, wide), BF),
        shaped((seqs, span, wide), BF),
        shaped((seqs, span, own), BF),
        shaped((seqs, span, LANES), F32),
        shaped((seqs, span, LANES), F32),
    )
    normed, pre, pre_halo, act, xs, dt_raw, cum, *sent = call(
        functools.partial(front_kernel, seqs, n_seq, state),
        seqs + 1,
        ins,
        [SMEM_SPEC, seq(tokens.shape[1:]), seq(tok_halo.shape[1:])]
        + [whole(v.shape) for v in ins[3:5]]
        + [seq(aux.shape[1:])]
        + [whole(v.shape) for v in ins[6:]],
        outs + (shaped((seqs + 1, ROWS, width), BF),) * n_seq,
        [seq(v.shape[1:]) for v in outs]
        + [pl.BlockSpec((1, ROWS, width), lambda s: (s, 0, 0))] * n_seq,
        [pltpu.VMEM((n_seq, ROWS, width), BF), pltpu.VMEM((ROWS, own), F32)],
        2 * seqs * span * model * (wide + LANES),
        "front",
    )

    def scan(body, ins, in_specs, n_in, outs, out_specs, name):
        blocks = n_in
        return call(
            body,
            1,
            ins,
            in_specs,
            outs,
            out_specs,
            [pltpu.VMEM((n_seq, blocks, ROWS, width), BF)],
            4 * n_seq * seqs * ROWS * width,
            name,
        )

    got = exchange(sent, "seq")
    piece = shaped((seqs, ROWS, width), BF)
    decay_shape = shaped((n_seq, 8, width), F32)
    *entries, decays = scan(
        functools.partial(scan_kernel, seqs, n_seq),
        (me, *got),
        [SMEM_SPEC] + [whole(v.shape) for v in got],
        seqs + 1,
        (piece,) * n_seq + (decay_shape,),
        [whole(piece.shape)] * n_seq + [whole(decay_shape.shape)],
        "scan",
    )
    states = exchange(entries, "seq")

    gate = dot(normed, w_z, ((2,), (0,))).astype(BF)
    e_raw = dot(cot_full, w_out, ((2,), (0,))).astype(BF)
    ins = (act, xs, cum, aux, seg_row)
    (inner,) = call(
        functools.partial(inner_kernel, state),
        seqs,
        ins,
        [seq(v.shape[1:]) for v in ins],
        (shaped((seqs, span, own), F32),),
        [seq((span, own))],
        [],
        8 * seqs * heads * span * span * HEAD_DIM,
        "inner",
    )

    mixer_ins = (me, act, inner, gate, e_raw, cum, aux, wide_rows, expand)
    mixer_specs = (
        [SMEM_SPEC] + [seq(v.shape[1:]) for v in mixer_ins[1:7]] + [whole(v.shape) for v in mixer_ins[7:]]
    )
    chunk_scratch = pltpu.VMEM((n_seq, ROWS, width), BF)
    (sums,) = call(
        functools.partial(sums_kernel, n_seq, state),
        seqs,
        (*mixer_ins, *states),
        mixer_specs + [chunk_spec] * n_seq,
        (shaped((seqs, 8, span), F32),),
        [seq((8, span))],
        [chunk_scratch],
        2 * seqs * span * state * own,
        "sums",
    )
    sums = lax.psum(sums[:, :2], "head")
    sums = jnp.pad(sums, ((0, 0), (0, 6), (0, 0)))

    outs = (
        shaped((seqs, span, own), BF),
        shaped((seqs, span, own), BF),
        shaped((seqs, span, own), BF),
        shaped((seqs, span, LANES), F32),
        shaped((seqs, span, state), F32),
        shaped((seqs, 8, span), F32),
    )
    scaled, d_z, d_y, mixed, d_c, dot_z, gate_grads, *sent = call(
        functools.partial(gate_back_kernel, n_seq, state, inner_total),
        seqs,
        (*mixer_ins, sums, *states),
        mixer_specs + [seq((8, span))] + [chunk_spec] * n_seq,
        outs + (shaped((8, own), F32),) + (piece,) * n_seq,
        [seq(v.shape[1:]) for v in outs] + [whole((8, own))] + [chunk_spec] * n_seq,
        [chunk_scratch],
        6 * seqs * span * state * own,
        "gate_back",
    )

    got = exchange(sent, "seq")
    leaves = scan(
        functools.partial(scan_back_kernel, seqs, n_seq),
        (me, decays, *got),
        [SMEM_SPEC] + [whole(v.shape) for v in (decays, *got)],
        seqs,
        (piece,) * n_seq,
        [whole(piece.shape)] * n_seq,
        "scan_back",
    )
    ends = exchange(leaves, "seq")

    out_full = dot(scaled, w_out, ((2,), (1,))).astype(BF)
    own_sum = lax.psum_scatter(out_full, "head", scatter_dimension=2, tiled=True)
    tokens_own = lax.dynamic_slice_in_dim(tokens, offset, share, 2).astype(F32)
    layer_out = (tokens_own + own_sum.astype(F32)).astype(BF)
    g_w_out = dot(cot_full, scaled, ((0, 1), (0, 1))).astype(BF)
    g_w_z = dot(normed, d_z, ((0, 1), (0, 1))).astype(BF)
    early = lax.psum_scatter(
        jnp.concatenate([g_w_out, g_w_z], axis=1), "seq", scatter_dimension=0, tiled=True
    ).astype(F32)

    ins = (act, xs, d_y, d_c, cum, dt_raw, aux, seg_row, wide_rows, head_rows, expand)
    outs = (
        shaped((seqs, span, own), BF),
        shaped((seqs, span, LANES), F32),
        shaped((seqs, span, 2 * state), F32),
    )
    d_x, d_step, d_bc = call(
        functools.partial(inner_back_kernel, state),
        seqs,
        ins,
        [seq(v.shape[1:]) for v in ins[:8]] + [whole(v.shape) for v in ins[8:]],
        outs,
        [seq(v.shape[1:]) for v in outs],
        [],
        16 * seqs * heads * span * span * HEAD_DIM,
        "inner_back",
    )

    ins = (
        me, act, pre, pre_halo, d_x, d_step, d_bc, mixed, cum, dt_raw, aux, conv_w, head_rows, expand,
        *states, *ends,
    )
    outs = (
        shaped((seqs, span, own), BF),
        shaped((seqs, EDGE, own), BF),
        shaped((seqs, span, 2 * state), BF),
        shaped((seqs, span, LANES), BF),
        shaped((seqs, 8, span), F32),
    )
    d_x_pre, back_x, d_bc, d_dt, dot_x, conv_grads, head_grads = call(
        functools.partial(leave_kernel, n_seq, state),
        seqs,
        ins,
        [SMEM_SPEC]
        + [seq(v.shape[1:]) for v in ins[1:11]]
        + [whole(v.shape) for v in ins[11:14]]
        + [chunk_spec] * (2 * n_seq),
        outs + (shaped((8, own), F32), shaped((8, LANES), F32)),
        [seq(v.shape[1:]) for v in outs] + [whole((8, own)), whole((8, LANES))],
        [chunk_scratch],
        8 * seqs * span * state * own,
        "leave",
    )
    back_x = shift(back_x[:, -edge:], "seq", -1)
    d_x_pre = d_x_pre.at[:, -edge:].add(back_x)

    d_bc_all = sum_all(d_bc, "head")
    bc_pre, bc_halo = pre[..., own:], pre_halo[..., own:]
    ins = (d_bc_all, bc_pre, bc_halo, aux, conv_w[:, own:])
    outs = (shaped((seqs, span, 2 * state), BF), shaped((seqs, EDGE, 2 * state), BF))
    d_bc_pre, back_bc, bc_grads = call(
        functools.partial(conv_bc_kernel, own),
        seqs,
        ins,
        [seq(v.shape[1:]) for v in ins[:4]] + [whole(ins[4].shape)],
        outs + (shaped((8, 2 * state), F32),),
        [seq(v.shape[1:]) for v in outs] + [whole((8, 2 * state))],
        [],
        0,
        "conv_bc",
    )
    back_bc = shift(back_bc[:, -edge:], "seq", -1)
    d_bc_pre = d_bc_pre.at[:, -edge:].add(back_bc)

    g_w_x = dot(normed, d_x_pre, ((0, 1), (0, 1))).astype(BF).reshape(n_seq, -1, own)
    half = own // 2
    late_a = halving_scatter(g_w_x[..., :half], "seq").astype(F32)
    late_b = halving_scatter(g_w_x[..., half:], "seq").astype(F32)
    d_small = jnp.concatenate([d_bc_pre, d_dt], axis=-1)
    g_small = dot(normed, d_small, ((0, 1), (0, 1))).astype(BF)
    late_s = halving_scatter(g_small.reshape(n_seq, -1, 2 * state + LANES), "seq").astype(F32)

    w_dx = jnp.concatenate([w_x, pad_lanes(w_dt, LANES)], axis=1)
    part_normed = dot(d_z, w_z, ((2,), (1,))) + dot(
        jnp.concatenate([d_x_pre, d_dt], axis=-1), w_dx, ((2,), (1,))
    )
    part_normed = part_normed.astype(BF)
    by_share = jnp.stack(
        [lax.slice_in_dim(part_normed, k * share, (k + 1) * share, axis=2) for k in range(n_head)]
    )
    row_dot = dot_z[:, 0] + dot_x[:, 0]
    fix = jnp.sum(back_x.astype(F32) * pre[:, -edge:, :own].astype(F32), axis=-1)
    row_dot = row_dot + jnp.pad(fix, ((0, 0), (span - edge, 0)))
    row_dot = sum_all(row_dot, "head") + jnp.sum(
        d_bc_pre.astype(F32) * bc_pre.astype(F32), axis=-1
    )
    own_grad = halving_scatter(by_share, "head").astype(F32)
    w_bc_own = lax.dynamic_slice_in_dim(w_bc, offset, share, 0)
    own_grad = own_grad + dot(d_bc_pre, w_bc_own, ((2,), (1,)))
    tokens_f = tokens.astype(F32)
    rstd_in = lax.rsqrt(jnp.mean(tokens_f * tokens_f, axis=-1, keepdims=True) + EPS)
    unit_own = tokens_own * rstd_in
    gain_own = lax.dynamic_slice_in_dim(norm_gain, offset, share, 0)
    g_norm = jnp.sum(own_grad * unit_own, axis=(0, 1))
    d_unit = own_grad * gain_own
    input_grad = (
        rstd_in * (d_unit - unit_own * (row_dot / model)[..., None]) + cotangent.astype(F32)
    ).astype(BF)

    taps = edge + 1
    small = (
        conv_grads[:taps],
        conv_grads[taps],
        bc_grads[:taps],
        bc_grads[taps],
        head_grads[0, :heads],
        head_grads[1, :heads],
        jnp.sum(gate_grads[1].reshape(heads, HEAD_DIM), axis=-1),
        gate_grads[0],
    )
    flat = sum_all(jnp.concatenate([v.reshape(-1) for v in small]), "seq")
    summed, at = [], 0
    for v in small:
        summed.append(flat[at : at + v.size].reshape(v.shape))
        at += v.size
    g_norm = sum_all(g_norm, "seq")
    g_w_zx_own = jnp.stack([early[:, own:], jnp.concatenate([late_a, late_b], axis=1)], axis=1)
    return (
        layer_out,
        input_grad,
        g_norm,
        g_w_zx_own,
        late_s[:, : 2 * state],
        late_s[:, 2 * state : 2 * state + heads],
        *summed,
        early[:, :own],
    )


def solution(mesh):
    placed = (
        P(None, "seq", None),
        P(None, "seq"),
        P(),
        P(None, None, "head"),
        P(),
        P(None, "head"),
        P(None, "head"),
        P("head"),
        P(),
        P(),
        P("head"),
        P("head"),
        P("head"),
        P("head"),
        P(None, "head"),
        P(None, "seq", "head"),
    )
    return jax.shard_map(
        local,
        mesh=mesh,
        in_specs=placed,
        out_specs=(
            P(None, "seq", "head"),
            P(None, "seq", "head"),
            P("head"),
            P("seq", None, "head"),
            P("seq", None),
            P("seq", "head"),
            P(None, "head"),
            P("head"),
            P(),
            P(),
            P("head"),
            P("head"),
            P("head"),
            P("head"),
            P("seq", "head"),
        ),
        check_vma=False,
    )
```

time: 1410 us -> 641 us (0.45)
  waiting for transfers between devices: 832 us -> 123 us
  Pallas kernels: 0 us -> 133 us
  other arithmetic: 165 us -> 45.8 us
  starting transfers between devices: 16.3 us -> 124 us
  matrix products: 207 us -> 105 us
  blocking collectives: 73.8 us -> 10.3 us
  local copies, waits for them, and re-layouts: 95.4 us -> 75.6 us
    all_gather x2 -> x0, waiting for transfers between devices: 304 us -> none  [prefix(): lax.all_gather(a.astype(kind), axis)]
    unnamed x10 -> x3, waiting for transfers between devices: 273 us -> 0.71 us
    pallas_call x0 -> x9, Pallas kernels: none -> 133 us  [call(): pl.pallas_call(body, grid=(grid,), in_specs=in_specs, out_specs=out_specs...]
    reduce_scatter x4 -> x2, waiting for transfers between devices: 130 us -> 0.01 us  [the longest x1 0.01 us: local(): lax.psum_scatter(out_full, 'head', scatter_dimension=2, tiled=True)]
    ppermute x5 -> x53, waiting for transfers between devices: 2.1 us -> 122 us  [the longest x49 116 us: swap(): return lax.ppermute(value, axis, [(i, i ^ mask) for i in range(count)])]
    psum x1 -> x0, waiting for transfers between devices: 111 us -> none  [local(): lax.psum(d_bc_part.astype(jnp.bfloat16), 'head').astype(jnp.float32)]
    ppermute x5 -> x53, starting transfers between devices: 15.4 us -> 124 us  [the longest x49 113 us: swap(): return lax.ppermute(value, axis, [(i, i ^ mask) for i in range(count)])]
    dot_general x24 -> x10, matrix products: 207 us -> 105 us  [dot(): lax.dot_general(a, b, (contract, ((), ())), preferred_element_type=F32, p...]
  transfers between devices with their start and end apart: 14 -> 56, of which waited for: 10 -> 19; matrix products, arithmetic and copies ran while one was open for 19% -> 32% of each run, Pallas kernels for 0% -> 16%
where the time goes in v1:
time: 641 us; the launch traced here: 632 us
  Pallas kernels  133 us (21%)
  starting transfers between devices  124 us (19%)
  waiting for transfers between devices  123 us (19%)
  matrix products  105 us (16%)
  local copies, waits for them, and re-layouts  75.6 us (12%)
  other arithmetic  45.8 us (7%)
  between operations  15.1 us (2%)
  blocking collectives  10.3 us (2%)
    pallas_call x9, Pallas kernels, call(): pl.pallas_call(body, grid=(grid,), in_specs=in_specs, out_specs=out_specs...  133 us
    ppermute x49, waiting for transfers between devices, swap(): return lax.ppermute(value, axis, [(i, i ^ mask) for i in range(count)])  116 us
    ppermute x49, starting transfers between devices, swap(): return lax.ppermute(value, axis, [(i, i ^ mask) for i in range(count)])  113 us
    dot_general x10, matrix products, dot(): lax.dot_general(a, b, (contract, ((), ())), preferred_element_type=F32, p...  105 us
    slice x1, local copies, waits for them, and re-layouts, local(): w_z, w_x = (w_zx[:, 0, :], w_zx[:, 1, :])  17.4 us
    unnamed x165, local copies, waits for them, and re-layouts  15.8 us
  transfers between devices with their start and end apart: 56, of which 19 were waited for; matrix products, arithmetic and copies ran while one was open for 32% of the time, Pallas kernels for 16%

profile of v1, /device:TPU:0, one launch (start us, length us, event | category | flops | bytes accessed | tf_op | source)
XLA Modules:
  0.0 632.0 jit_solution(10458306177133046880)
XLA Ops:
  8.7 4.8 collective-permute-start.1
  14.5 4.1 collective-permute-start
  19.6 17.4 %fusion.40 = (bf16[2048,1,1024]{2,1,0:T(2,128)(2,1)}, bf16[2048,1,1024]{2,1,0:T(2,128)(2,1)S(1)}) fusion(bf16[2048,2,1024]{2,1,0:T(2,128)(2,1)} %param.23), kind=kLoop, calls=%fused_computation.128 | loop fusion | bytes 16777216 | tf_op jit(solution)/shard_map/slice | solution.py:580
  37.2 3.7 copy.201
  43.0 5.4 pad_maximum_fusion.2.w_ref
  53.5 4.0 stack.78.aux_ref
  57.5 29.3 %front.1 = (bf16[6,256,2048]{2,1,0:T(8,128)(2,1)}, bf16[6,256,1280]{2,1,0:T(8,128)(2,1)}, bf16[6,16,1280]{2,1,0:T(8,128)(2,1)}, bf16[6,256,1280]{2,1,0:T(8,128)(...) custom-call(s32[1]{0:T(128)} %bitcast.me_ref, ...), custom_call_target="tpu_custom_call" | custom-call | flops 8858370048 | bytes 33574916 | tf_op jit(solution)/shard_map/front/pallas_call | solution.py:465
  94.3 2.0 collective-permute-start.7
  96.3 7.9 %collective-permute-done.3.rest_2_ = bf16[7,16,1024]{2,1,0:T(8,128)(2,1)S(1)} collective-permute-done((bf16[7,16,1024]{2,1,0:T(8,128)(2,1)}, bf16[7,16,1024]{2,1,0:T(8,128)(2,1)S(1)}, u32[]{:S(2)}, u32[]{:S(2)}) %collective-permute-start.3) | collective-permute-done | bytes 229408 | tf_op jit(solution)/shard_map/ppermute | solution.py:484
  105.4 12.9 %convolution_convert_fusion.1.gate_ref = bf16[6,256,1024]{2,1,0:T(8,128)(2,1)} fusion(bf16[6,256,2048]{2,1,0:T(8,128)(2,1)} %get-tuple-element.102, bf16[2048,1,1024]{2,1,0:T(2,128)(2,1)} %get-tuple-element.251), kind=kOutput, calls=%fused_computation.37 | convolution fusion | flops 6444023808 | bytes 13631488 | tf_op jit(solution)/shard_map/dot_general | solution.py:23
  118.3 7.3 %collective-permute-done.6.rest_5_ = bf16[7,16,1024]{2,1,0:T(8,128)(2,1)S(1)} collective-permute-done((bf16[7,16,1024]{2,1,0:T(8,128)(2,1)}, bf16[7,16,1024]{2,1,0:T(8,128)(2,1)S(1)}, u32[]{:S(2)}, u32[]{:S(2)}) %collective-permute-start.6) | collective-permute-done | bytes 229408 | tf_op jit(solution)/shard_map/ppermute | solution.py:484
  126.6 3.5 scan.1
  130.0 7.5 %collective-permute-start.10 = (bf16[6,16,1024]{2,1,0:T(8,128)(2,1)}, bf16[6,16,1024]{2,1,0:T(8,128)(2,1)S(1)}, u32[]{:S(2)}, u32[]{:S(2)}) collective-permute-start(bf16[6,16,1024]{2,1,0:T(8,128)(2,1)} %get-tuple-element.113), channel_id=1, source_target_pairs={{0,8},{4,12},{8,0},{12,4},{16,24},{20,28},{24,16},{28,20},{1,9},{5... | collective-permute-start | bytes 589832 | tf_op jit(solution)/shard_map/ppermute | solution.py:484
  139.0 11.0 %inner.1.inner_ref = f32[6,256,1024]{2,1,0:T(8,128)} custom-call(bf16[6,256,1280]{2,1,0:T(8,128)(2,1)} %get-tuple-element.99.act_ref, bf16[6,256,1024]{2,1,0:T(8,128)(2,1)} %get-tuple-element.100.xs_ref, f32[6,256,128]{2,1,0:T(8,128)} %get-tuple-element.101.cum_ref, f32[6,256,8]{2,1,0:T(8,128)} %stack.78.aux_ref, f32[6,8,256]{2,1,0:T(8,128)} %broadcast_in_dim.4.seg_ref), custom_call_target="tpu_custom_call" | custom-call | flops 3221225472 | bytes 14254080 | tf_op jit(solution)/shard_map/inner/pallas_call | solution.py:465
  150.0 2.1 collective-permute-start.12
  153.1 2.3 collective-permute-start.14
  155.5 2.3 collective-permute-start.15
  158.6 11.2 %fusion.18.e_ref = bf16[6,256,1024]{2,1,0:T(8,128)(2,1)} fusion(bf16[6,256,2048]{2,1,0:T(8,128)(2,1)} %all-gather.2.cloned.1.call-done, bf16[2048,1024]{1,0:T(8,128)(2,1)} %param.34), kind=kOutput, calls=%fused_computation.36 | convolution fusion | flops 6444023808 | bytes 13631488 | tf_op jit(solution)/shard_map/dot_general | solution.py:23
  169.8 3.2 collective-permute-done.12.rest_4_
  172.9 4.2 collective-permute-done.13.rest_5_
  178.1 11.5 %sums.1 = f32[6,8,256]{2,1,0:T(8,128)} custom-call(s32[1]{0:T(128)} %bitcast.me_ref, bf16[6,256,1280]{2,1,0:T(8,128)(2,1)} %get-tuple-element.99.act_ref, f32[6,256,1024]{2,1,0:T(8,128)} %inner.1.inner_ref, bf16[6,256,1024]{2,1,0:T(8,128)(2,1)} %convolution_convert_fusion.1.gate_ref, bf16[6,256,1024]{2,1,0:T(8,128)(2,1)} %fusion.18.e_ref, ...), custom_call_target="tpu_custom_call" | custom-call | flops 402653184 | bytes 19267588 | tf_op jit(solution)/shard_map/sums/pallas_call | solution.py:465
  190.4 10.3 %psum.7 = f32[6,2,256]{2,1,0:T(2,128)S(1)} all-reduce(f32[6,2,256]{2,1,0:T(2,128)S(1)} %slice.226), channel_id=1, replica_groups=mesh['seq'=8,'head'=4] {'head'}, use_global_device_ids=true, to_apply=%region_0.1 | all-reduce | flops 3072 | bytes 24576 | tf_op jit(solution)/shard_map/psum | solution.py:670
  201.3 20.7 %gate_back.1 = (bf16[6,256,1024]{2,1,0:T(8,128)(2,1)}, bf16[6,256,1024]{2,1,0:T(8,128)(2,1)}, bf16[6,256,1024]{2,1,0:T(8,128)(2,1)}, f32[6,256,128]{2,1,0:T(8,12...) custom-call(s32[1]{0:T(128)} %bitcast.me_ref, ...), custom_call_target="tpu_custom_call" | custom-call | flops 1207959552 | bytes 31932420 | tf_op jit(solution)/shard_map/gate_back/pallas_call | solution.py:465
  222.0 10.6 %convolution_convert_fusion = bf16[6,256,2048]{2,1,0:T(8,128)(2,1)} fusion(bf16[6,256,1024]{2,1,0:T(8,128)(2,1)} %get-tuple-element.119, bf16[2048,1024]{1,0:T(8,128)(2,1)S(1)} %copy-done.55), kind=kOutput, calls=%fused_computation.12 | convolution fusion | flops 6445596672 | bytes 13631488 | tf_op jit(solution)/shard_map/dot_general | solution.py:23
  232.7 11.6 %fusion.11 = bf16[2048,1024]{0,1:T(8,128)(2,1)} fusion(bf16[6,256,1024]{2,1,0:T(8,128)(2,1)} %get-tuple-element.119, bf16[6,256,2048]{2,1,0:T(8,128)(2,1)} %all-gather.2.cloned.1.call-done), kind=kOutput, calls=%fused_computation.25 | convolution fusion | flops 6444548096 | bytes 13631488 | tf_op jit(solution)/shard_map/dot_general | solution.py:23
  244.3 12.0 %bitcast_convert_fusion.1 = bf16[2048,1024]{0,1:T(8,128)(2,1)} fusion(bf16[6,256,2048]{2,1,0:T(8,128)(2,1)} %get-tuple-element.102, bf16[6,256,1024]{2,1,0:T(8,128)(2,1)S(1)} %copy-done.56), kind=kOutput, calls=%fused_computation.4 | convolution fusion | flops 6444548096 | bytes 13631488 | tf_op jit(solution)/shard_map/dot_general | solution.py:23
  256.3 8.6 %pad_maximum_fusion = bf16[2048,2048]{0,1:T(8,128)(2,1)} fusion(bf16[2048,1024]{0,1:T(8,128)(2,1)} %bitcast_convert_fusion.1, bf16[2048,1024]{0,1:T(8,128)(2,1)} %fusion.11), kind=kLoop, calls=%fused_computation.2 | loop fusion | flops 16777216 | bytes 16777216 | tf_op jit(solution)/shard_map/concatenate | solution.py:712
  266.9 7.6 %collective-permute-start.17 = (bf16[6,16,1024]{2,1,0:T(8,128)(2,1)S(1)}, bf16[6,16,1024]{2,1,0:T(8,128)(2,1)S(1)}, u32[]{:S(2)}, u32[]{:S(2)}) collective-permute-start(bf16[6,16,1024]{2,1,0:T(8,128)(2,1)S(1)} %copy-done.63), channel_id=1, source_target_pairs={{0,8},{4,12},{8,0},{12,4},{16,24},{20,28},{24,16},{28,20},{1,9},{5... | collective-permute-start | bytes 589832 | tf_op jit(solution)/shard_map/ppermute | solution.py:484
  274.5 4.1 multiply_reduce_fusion
  280.3 3.0 collective-permute-start.19
  283.9 2.0 collective-permute-start.21
  285.8 2.4 collective-permute-start.22
  288.2 2.1 slice.193.pre_ref
  291.8 14.2 %collective-permute-done.19.rest_4_ = bf16[6,16,1024]{2,1,0:T(8,128)(2,1)S(1)} collective-permute-done((bf16[6,16,1024]{2,1,0:T(8,128)(2,1)S(1)}, bf16[6,16,1024]{2,1,0:T(8,128)(2,1)S(1)}, u32[]{:S(2)}, u32[]{:S(2)}) %collective-permute-start.19) | collective-permute-done | bytes 196640 | tf_op jit(solution)/shard_map/ppermute | solution.py:484
  305.9 4.6 collective-permute-done.20.rest_5_
  311.4 3.2 scan_back.1
  315.6 25.0 %collective-permute-start.24 = (bf16[6,16,1024]{2,1,0:T(8,128)(2,1)}, bf16[6,16,1024]{2,1,0:T(8,128)(2,1)S(1)}, u32[]{:S(2)}, u32[]{:S(2)}) collective-permute-start(bf16[6,16,1024]{2,1,0:T(8,128)(2,1)} %get-tuple-element.141), channel_id=1, source_target_pairs={{0,8},{4,12},{8,0},{12,4},{16,24},{20,28},{24,16},{28,20},{1,9},{5... | collective-permute-start | bytes 589832 | tf_op jit(solution)/shard_map/ppermute | solution.py:484
  340.6 18.9 %inner_back.1 = (bf16[6,256,1024]{2,1,0:T(8,128)(2,1)}, f32[6,256,128]{2,1,0:T(8,128)}, f32[6,256,256]{2,1,0:T(8,128)}) custom-call(bf16[6,256,1280]{2,1,0:T(8,128)(2,1)} %get-tuple-element.99.act_ref, bf16[6,256,1024]{2,1,0:T(8,128)(2,1)} %get-tuple-element.100.xs_ref, bf16[6,256,1024]{2,1,0:T(8,128)(2,1)} %get-tuple-element.123.dy_ref, ...), custom_call_target="tpu_custom_call" | custom-call | flops 6442450944 | bytes 18485248 | tf_op jit(solution)/shard_map/inner_back/pallas_call | solution.py:465
  359.6 3.5 collective-permute-start.26
  364.6 2.6 collective-permute-start.28
  369.6 7.1 %collective-permute-done.25.rest_11_ = bf16[6,16,1024]{2,1,0:T(8,128)(2,1)S(1)} collective-permute-done((bf16[6,16,1024]{2,1,0:T(8,128)(2,1)S(1)}, bf16[6,16,1024]{2,1,0:T(8,128)(2,1)S(1)}, u32[]{:S(2)}, u32[]{:S(2)}) %collective-permute-start.25) | collective-permute-done | bytes 196640 | tf_op jit(solution)/shard_map/ppermute | solution.py:484
  376.7 13.6 %collective-permute-done.26.rest_12_ = bf16[6,16,1024]{2,1,0:T(8,128)(2,1)S(1)} collective-permute-done((bf16[6,16,1024]{2,1,0:T(8,128)(2,1)S(1)}, bf16[6,16,1024]{2,1,0:T(8,128)(2,1)S(1)}, u32[]{:S(2)}, u32[]{:S(2)}) %collective-permute-start.26) | collective-permute-done | bytes 196640 | tf_op jit(solution)/shard_map/ppermute | solution.py:484
  390.3 20.0 %collective-permute-done.27.rest_13_ = bf16[6,16,1024]{2,1,0:T(8,128)(2,1)S(1)} collective-permute-done((bf16[6,16,1024]{2,1,0:T(8,128)(2,1)S(1)}, bf16[6,16,1024]{2,1,0:T(8,128)(2,1)S(1)}, u32[]{:S(2)}, u32[]{:S(2)}) %collective-permute-start.27) | collective-permute-done | bytes 196640 | tf_op jit(solution)/shard_map/ppermute | solution.py:484
  411.1 28.4 %leave.1 = (bf16[6,256,1024]{2,1,0:T(8,128)(2,1)}, bf16[6,16,1024]{2,1,0:T(8,128)(2,1)}, bf16[6,256,256]{2,1,0:T(8,128)(2,1)}, bf16[6,256,128]{2,1,0:T(8,128)(2,...) custom-call(s32[1]{0:T(128)} %bitcast.me_ref, bf16[6,256,1280]{2,1,0:T(8,128)(2,1)} %get-tuple-element.99.act_ref, ...), custom_call_target="tpu_custom_call" | custom-call | flops 1610612736 | bytes 24084484 | tf_op jit(solution)/shard_map/leave/pallas_call | solution.py:465
  443.4 3.1 collective-permute-done.30
  447.5 2.1 scatter-add.6
  449.6 9.8 %bitcast_convert_fusion = bf16[2048,1024]{1,0:T(8,128)(2,1)S(1)} fusion(bf16[6,256,2048]{2,1,0:T(8,128)(2,1)} %get-tuple-element.102, bf16[6,256,1024]{2,1,0:T(8,128)(2,1)} %scatter-add.6), kind=kOutput, calls=%fused_computation.3 | convolution fusion | flops 6444548096 | bytes 13631488 | tf_op jit(solution)/shard_map/dot_general | solution.py:23
  461.1 10.9 %collective-permute-start.41 = (bf16[4,256,512]{2,1,0:T(8,128)(2,1)}, bf16[4,256,512]{2,1,0:T(8,128)(2,1)}, u32[]{:S(2)}, u32[]{:S(2)}) collective-permute-start(bf16[4,256,512]{2,1,0:T(8,128)(2,1)} %dynamic-slice_bitcast_fusion.2), channel_id=1, source_target_pairs={{0,4},{4,0},{8,12},{12,8},{16,20},{20,16},{24,28},{28,24},{1,5},{5... | collective-permute-start | bytes 3145736 | tf_op jit(solution)/shard_map/ppermute | solution.py:484
  473.1 10.8 %fusion = f32[6,256,2048]{2,1,0:T(8,128)} fusion(bf16[2048,128]{1,0:T(8,128)(2,1)S(1)} %copy-done.10, bf16[2048,1024]{1,0:T(8,128)(2,1)S(1)} %bitcast.161, bf16[6,256,128]{2,1,0:T(8,128)(2,1)S(1)} %copy-done.57, bf16[6,256,1024]{2,1,0:T(8,128)(2,1)S(1)} %copy-done.52), kind=kOutput, calls=%fused_computation.9 | convolution fusion | flops 7264272384 | bytes 20840448 | tf_op jit(solution)/shard_map/dot_general | solution.py:23
  483.9 12.8 %add_convert_fusion = bf16[6,256,2048]{2,1,0:T(8,128)(2,1)S(1)} fusion(f32[6,256,2048]{2,1,0:T(8,128)} %fusion, bf16[6,256,1024]{2,1,0:T(8,128)(2,1)} %get-tuple-element.120, bf16[2048,1,1024]{2,1,0:T(2,128)(2,1)} %get-tuple-element.251), kind=kOutput, calls=%fused_computation | convolution fusion | flops 6448742400 | bytes 26214400 | tf_op jit(solution)/shard_map/dot_general | solution.py:23
  498.5 2.0 dynamic-slice_bitcast_fusion
  507.9 10.2 %collective-permute-done.44 = bf16[4,256,512]{2,1,0:T(8,128)(2,1)} collective-permute-done((bf16[4,256,512]{2,1,0:T(8,128)(2,1)}, bf16[4,256,512]{2,1,0:T(8,128)(2,1)}, u32[]{:S(2)}, u32[]{:S(2)}) %collective-permute-start.44) | collective-permute-done | bytes 1048608 | tf_op jit(solution)/shard_map/ppermute | solution.py:484
  524.1 2.2 add.241.d_ref
  526.3 6.4 %conv_bc.1 = (bf16[6,256,256]{2,1,0:T(8,128)(2,1)}, bf16[6,16,256]{2,1,0:T(8,128)(2,1)}, f32[8,256]{1,0:T(8,128)}) custom-call(bf16[6,256,256]{2,1,0:T(8,128)(2,1)} %add.241.d_ref, bf16[6,256,256]{2,1,0:T(8,128)(2,1)} %slice.193.pre_ref, bf16[6,16,256]{2,1,0:T(8,128)(2,1)} %slice.194.pre_halo_ref, f32[6,256,8]{2,1,0:T(8,128)} %stack.78.aux_ref, ...), custom_call_target="tpu_custom_call" | custom-call | bytes 2523136 | tf_op jit(solution)/shard_map/conv_bc/pallas_call | solution.py:465
  536.2 2.8 collective-permute-done.35
  539.0 8.1 %collective-permute-start.50 = (f32[7472]{0:T(1024)S(1)}, f32[7472]{0:T(1024)S(1)}, u32[]{:S(2)}, u32[]{:S(2)}) collective-permute-start(f32[7472]{0:T(1024)S(1)} %concatenate.56), channel_id=1, source_target_pairs={{0,4},{4,0},{8,12},{12,8},{16,20},{20,16},{24,28},{28,24},{1,5},{5... | collective-permute-start | bytes 89672 | tf_op jit(solution)/shard_map/ppermute | solution.py:484
  549.4 6.7 %bitcast_convert_fusion.3 = bf16[2048,384]{1,0:T(8,128)(2,1)S(1)} fusion(bf16[6,256,2048]{2,1,0:T(8,128)(2,1)} %get-tuple-element.102, bf16[6,256,128]{2,1,0:T(8,128)(2,1)} %get-tuple-element.149, bf16[6,256,256]{2,1,0:T(8,128)(2,1)} %scatter-add.9), kind=kOutput, calls=%fused_computation.34 | convolution fusion | flops 2419064832 | bytes 9043968 | tf_op jit(solution)/shard_map/dot_general | solution.py:23
  556.1 2.0 multiply_reduce_fusion.1
  561.7 2.2 bitcast_add_fusion
  572.1 9.6 %collective-permute-done.52 = f32[7472]{0:T(1024)S(1)} collective-permute-done((f32[7472]{0:T(1024)S(1)}, f32[7472]{0:T(1024)S(1)}, u32[]{:S(2)}, u32[]{:S(2)}) %collective-permute-start.52) | collective-permute-done | bytes 29920 | tf_op jit(solution)/shard_map/ppermute | solution.py:484
  588.1 6.1 collective-permute-done.48
  596.3 4.6 collective-permute-done.32
  600.9 6.7 %fusion.16 = (f32[512]{0:T(512)S(1)}, bf16[6,256,512]{2,1,0:T(8,128)(2,1)}, bf16[6,256,512]{2,1,0:T(8,128)(2,1)}) fusion(f32[6,256]{1,0:T(8,128)S(1)} %add_rsqrt_fusion, bf16[6,256,2048]{2,1,0:T(8,128)(2,1)} %tok_ref.1, s32[]{:T(128)S(6)} %select_n.125, bf16[1,6,256,512]{3,2,1,0:T(8,128)(2,1)} %collective-permute-done.32, ...), kind=kOutput, calls=%fused_computation.30 | convolution fusion | flops 418381312 | bytes 12076544 | tf_op jit(solution)/shard_map/dot_general | solution.py:23
  621.6 2.3 copy.177
  (341 shorter events, 101.8 us)
Async XLA Ops:
  7.2 151.4 %all-gather.2.cloned.1.call-start = ((), (), s32[]{:S(2)}) async-start(), calls=%async_computation.2 | async-start | bytes 7864320 | tf_op jit(solution)/shard_map/all_gather | solution.py:563
  7.9 593.0 %reduce-scatter.3.cloned.1.call-start = ((), (), s32[]{:S(2)}) async-start(), calls=%async_computation.3 | async-start | bytes 7864320 | tf_op jit(solution)/shard_map/reduce_scatter | solution.py:706
  8.7 40.3 %collective-permute-start.1 = (s32[6,8]{1,0:T(8,128)S(1)}, s32[6,8]{1,0:T(8,128)S(1)}, u32[]{:S(2)}, u32[]{:S(2)}) collective-permute-start(s32[6,8]{1,0:T(8,128)S(1)} %slice.179), channel_id=1, source_target_pairs={{0,4},{4,8},{8,12},{12,16},{16,20},{20,24},{24,28},{1,5},{5,9},{9,... | collective-permute-start | bytes 584 | tf_op jit(solution)/shard_map/ppermute | solution.py:490
  14.5 43.0 %collective-permute-start = (bf16[6,8,2048]{2,1,0:T(8,128)(2,1)S(1)}, bf16[6,8,2048]{2,1,0:T(8,128)(2,1)}, u32[]{:S(2)}, u32[]{:S(2)}) collective-permute-start(bf16[6,8,2048]{2,1,0:T(8,128)(2,1)S(1)} %slice.177), channel_id=1, source_target_pairs={{0,4},{4,8},{8,12},{12,16},{16,20},{20,24},{24,28},{1,5},{5,9},{9,... | collective-permute-start | bytes 589832 | tf_op jit(solution)/shard_map/ppermute | solution.py:490
  57.5 31.7 %copy-start.54 = (f32[16]{0:T(128)S(1)}, f32[16]{0:T(128)}, u32[]{:S(2)}) copy-start(f32[16]{0:T(128)} %param.32) | copy-start | bytes 196
  57.5 31.9 %copy-start.48 = (f32[1024]{0:T(1024)S(1)}, f32[1024]{0:T(1024)}, u32[]{:S(2)}) copy-start(f32[1024]{0:T(1024)} %param.33) | copy-start | bytes 12292
  86.8 7.5 %collective-permute-start.2 = (bf16[7,16,1024]{2,1,0:T(8,128)(2,1)}, bf16[7,16,1024]{2,1,0:T(8,128)(2,1)S(1)}, u32[]{:S(2)}, u32[]{:S(2)}) collective-permute-start(bf16[7,16,1024]{2,1,0:T(8,128)(2,1)} %get-tuple-element.104), channel_id=1, source_target_pairs={{0,4},{4,0},{8,12},{12,8},{16,20},{20,16},{24,28},{28,24},{1,5},{5... | collective-permute-start | bytes 688136 | tf_op jit(solution)/shard_map/ppermute | solution.py:484
  87.7 16.5 %collective-permute-start.3 = (bf16[7,16,1024]{2,1,0:T(8,128)(2,1)}, bf16[7,16,1024]{2,1,0:T(8,128)(2,1)S(1)}, u32[]{:S(2)}, u32[]{:S(2)}) collective-permute-start(bf16[7,16,1024]{2,1,0:T(8,128)(2,1)} %get-tuple-element.105), channel_id=1, source_target_pairs={{0,8},{4,12},{8,0},{12,4},{16,24},{20,28},{24,16},{28,20},{1,9},{5... | collective-permute-start | bytes 688136 | tf_op jit(solution)/shard_map/ppermute | solution.py:484
  90.0 28.3 %collective-permute-start.4 = (bf16[7,16,1024]{2,1,0:T(8,128)(2,1)}, bf16[7,16,1024]{2,1,0:T(8,128)(2,1)S(1)}, u32[]{:S(2)}, u32[]{:S(2)}) collective-permute-start(bf16[7,16,1024]{2,1,0:T(8,128)(2,1)} %get-tuple-element.106), channel_id=1, source_target_pairs={{0,12},{4,8},{8,4},{12,0},{16,28},{20,24},{24,20},{28,16},{1,13},{... | collective-permute-start | bytes 688136 | tf_op jit(solution)/shard_map/ppermute | solution.py:484
  91.1 27.2 %collective-permute-start.5 = (bf16[7,16,1024]{2,1,0:T(8,128)(2,1)}, bf16[7,16,1024]{2,1,0:T(8,128)(2,1)S(1)}, u32[]{:S(2)}, u32[]{:S(2)}) collective-permute-start(bf16[7,16,1024]{2,1,0:T(8,128)(2,1)} %get-tuple-element.107), channel_id=1, source_target_pairs={{0,16},{4,20},{8,24},{12,28},{16,0},{20,4},{24,8},{28,12},{1,17},{... | collective-permute-start | bytes 688136 | tf_op jit(solution)/shard_map/ppermute | solution.py:484
  93.0 32.6 %collective-permute-start.6 = (bf16[7,16,1024]{2,1,0:T(8,128)(2,1)}, bf16[7,16,1024]{2,1,0:T(8,128)(2,1)S(1)}, u32[]{:S(2)}, u32[]{:S(2)}) collective-permute-start(bf16[7,16,1024]{2,1,0:T(8,128)(2,1)} %get-tuple-element.108), channel_id=1, source_target_pairs={{0,20},{4,16},{8,28},{12,24},{16,4},{20,0},{24,12},{28,8},{1,21},{... | collective-permute-start | bytes 688136 | tf_op jit(solution)/shard_map/ppermute | solution.py:484
  94.3 31.3 %collective-permute-start.7 = (bf16[7,16,1024]{2,1,0:T(8,128)(2,1)}, bf16[7,16,1024]{2,1,0:T(8,128)(2,1)S(1)}, u32[]{:S(2)}, u32[]{:S(2)}) collective-permute-start(bf16[7,16,1024]{2,1,0:T(8,128)(2,1)} %get-tuple-element.109), channel_id=1, source_target_pairs={{0,24},{4,28},{8,16},{12,20},{16,8},{20,12},{24,0},{28,4},{1,25},{... | collective-permute-start | bytes 688136 | tf_op jit(solution)/shard_map/ppermute | solution.py:484
  104.2 21.5 %collective-permute-start.8 = (bf16[7,16,1024]{2,1,0:T(8,128)(2,1)}, bf16[7,16,1024]{2,1,0:T(8,128)(2,1)S(1)}, u32[]{:S(2)}, u32[]{:S(2)}) collective-permute-start(bf16[7,16,1024]{2,1,0:T(8,128)(2,1)} %get-tuple-element.110), channel_id=1, source_target_pairs={{0,28},{4,24},{8,20},{12,16},{16,12},{20,8},{24,4},{28,0},{1,29},{... | collective-permute-start | bytes 688136 | tf_op jit(solution)/shard_map/ppermute | solution.py:484
  130.0 25.4 %collective-permute-start.10 = (bf16[6,16,1024]{2,1,0:T(8,128)(2,1)}, bf16[6,16,1024]{2,1,0:T(8,128)(2,1)S(1)}, u32[]{:S(2)}, u32[]{:S(2)}) collective-permute-start(bf16[6,16,1024]{2,1,0:T(8,128)(2,1)} %get-tuple-element.113), channel_id=1, source_target_pairs={{0,8},{4,12},{8,0},{12,4},{16,24},{20,28},{24,16},{28,20},{1,9},{5... | collective-permute-start | bytes 589832 | tf_op jit(solution)/shard_map/ppermute | solution.py:484
  137.6 20.2 %collective-permute-start.11 = (bf16[6,16,1024]{2,1,0:T(8,128)(2,1)}, bf16[6,16,1024]{2,1,0:T(8,128)(2,1)S(1)}, u32[]{:S(2)}, u32[]{:S(2)}) collective-permute-start(bf16[6,16,1024]{2,1,0:T(8,128)(2,1)} %get-tuple-element.114), channel_id=1, source_target_pairs={{0,12},{4,8},{8,4},{12,0},{16,28},{20,24},{24,20},{28,16},{1,13},{... | collective-permute-start | bytes 589832 | tf_op jit(solution)/shard_map/ppermute | solution.py:484
  150.0 22.9 %collective-permute-start.12 = (bf16[6,16,1024]{2,1,0:T(8,128)(2,1)S(1)}, bf16[6,16,1024]{2,1,0:T(8,128)(2,1)S(1)}, u32[]{:S(2)}, u32[]{:S(2)}) collective-permute-start(bf16[6,16,1024]{2,1,0:T(8,128)(2,1)S(1)} %copy-done.74), channel_id=1, source_target_pairs={{0,16},{4,20},{8,24},{12,28},{16,0},{20,4},{24,8},{28,12},{1,17},{... | collective-permute-start | bytes 589832 | tf_op jit(solution)/shard_map/ppermute | solution.py:484
  152.1 25.0 %collective-permute-start.13 = (bf16[6,16,1024]{2,1,0:T(8,128)(2,1)S(1)}, bf16[6,16,1024]{2,1,0:T(8,128)(2,1)S(1)}, u32[]{:S(2)}, u32[]{:S(2)}) collective-permute-start(bf16[6,16,1024]{2,1,0:T(8,128)(2,1)S(1)} %copy-done.73), channel_id=1, source_target_pairs={{0,20},{4,16},{8,28},{12,24},{16,4},{20,0},{24,12},{28,8},{1,21},{... | collective-permute-start | bytes 589832 | tf_op jit(solution)/shard_map/ppermute | solution.py:484
  153.1 24.0 %collective-permute-start.14 = (bf16[6,16,1024]{2,1,0:T(8,128)(2,1)S(1)}, bf16[6,16,1024]{2,1,0:T(8,128)(2,1)S(1)}, u32[]{:S(2)}, u32[]{:S(2)}) collective-permute-start(bf16[6,16,1024]{2,1,0:T(8,128)(2,1)S(1)} %copy-done.72), channel_id=1, source_target_pairs={{0,24},{4,28},{8,16},{12,20},{16,8},{20,12},{24,0},{28,4},{1,25},{... | collective-permute-start | bytes 589832 | tf_op jit(solution)/shard_map/ppermute | solution.py:484
  155.5 21.7 %collective-permute-start.15 = (bf16[6,16,1024]{2,1,0:T(8,128)(2,1)S(1)}, bf16[6,16,1024]{2,1,0:T(8,128)(2,1)S(1)}, u32[]{:S(2)}, u32[]{:S(2)}) collective-permute-start(bf16[6,16,1024]{2,1,0:T(8,128)(2,1)S(1)} %copy-done.71), channel_id=1, source_target_pairs={{0,28},{4,24},{8,20},{12,16},{16,12},{20,8},{24,4},{28,0},{1,29},{... | collective-permute-start | bytes 589832 | tf_op jit(solution)/shard_map/ppermute | solution.py:484
  157.8 19.4 %collective-permute-start.9 = (bf16[6,16,1024]{2,1,0:T(8,128)(2,1)S(1)}, bf16[6,16,1024]{2,1,0:T(8,128)(2,1)S(1)}, u32[]{:S(2)}, u32[]{:S(2)}) collective-permute-start(bf16[6,16,1024]{2,1,0:T(8,128)(2,1)S(1)} %copy-done.69), channel_id=1, source_target_pairs={{0,4},{4,0},{8,12},{12,8},{16,20},{20,16},{24,28},{28,24},{1,5},{5... | collective-permute-start | bytes 589832 | tf_op jit(solution)/shard_map/ppermute | solution.py:484
  232.6 387.2 %reduce-scatter.5.cloned.1.call-start = ((), (), s32[]{:S(2)}) async-start(), calls=%async_computation.4 | async-start | bytes 9437184 | tf_op jit(solution)/shard_map/reduce_scatter | solution.py:711
  265.8 18.1 %collective-permute-start.16 = (bf16[6,16,1024]{2,1,0:T(8,128)(2,1)S(1)}, bf16[6,16,1024]{2,1,0:T(8,128)(2,1)S(1)}, u32[]{:S(2)}, u32[]{:S(2)}) collective-permute-start(bf16[6,16,1024]{2,1,0:T(8,128)(2,1)S(1)} %copy-done.64), channel_id=1, source_target_pairs={{0,4},{4,0},{8,12},{12,8},{16,20},{20,16},{24,28},{28,24},{1,5},{5... | collective-permute-start | bytes 589832 | tf_op jit(solution)/shard_map/ppermute | solution.py:484
  266.9 18.9 %collective-permute-start.17 = (bf16[6,16,1024]{2,1,0:T(8,128)(2,1)S(1)}, bf16[6,16,1024]{2,1,0:T(8,128)(2,1)S(1)}, u32[]{:S(2)}, u32[]{:S(2)}) collective-permute-start(bf16[6,16,1024]{2,1,0:T(8,128)(2,1)S(1)} %copy-done.63), channel_id=1, source_target_pairs={{0,8},{4,12},{8,0},{12,4},{16,24},{20,28},{24,16},{28,20},{1,9},{5... | collective-permute-start | bytes 589832 | tf_op jit(solution)/shard_map/ppermute | solution.py:484
  280.0 11.8 %collective-permute-start.18 = (bf16[6,16,1024]{2,1,0:T(8,128)(2,1)S(1)}, bf16[6,16,1024]{2,1,0:T(8,128)(2,1)S(1)}, u32[]{:S(2)}, u32[]{:S(2)}) collective-permute-start(bf16[6,16,1024]{2,1,0:T(8,128)(2,1)S(1)} %copy-done.62), channel_id=1, source_target_pairs={{0,12},{4,8},{8,4},{12,0},{16,28},{20,24},{24,20},{28,16},{1,13},{... | collective-permute-start | bytes 589832 | tf_op jit(solution)/shard_map/ppermute | solution.py:484
  280.3 25.6 %collective-permute-start.19 = (bf16[6,16,1024]{2,1,0:T(8,128)(2,1)S(1)}, bf16[6,16,1024]{2,1,0:T(8,128)(2,1)S(1)}, u32[]{:S(2)}, u32[]{:S(2)}) collective-permute-start(bf16[6,16,1024]{2,1,0:T(8,128)(2,1)S(1)} %copy-done.61), channel_id=1, source_target_pairs={{0,16},{4,20},{8,24},{12,28},{16,0},{20,4},{24,8},{28,12},{1,17},{... | collective-permute-start | bytes 589832 | tf_op jit(solution)/shard_map/ppermute | solution.py:484
  283.3 27.3 %collective-permute-start.20 = (bf16[6,16,1024]{2,1,0:T(8,128)(2,1)S(1)}, bf16[6,16,1024]{2,1,0:T(8,128)(2,1)S(1)}, u32[]{:S(2)}, u32[]{:S(2)}) collective-permute-start(bf16[6,16,1024]{2,1,0:T(8,128)(2,1)S(1)} %copy-done.60), channel_id=1, source_target_pairs={{0,20},{4,16},{8,28},{12,24},{16,4},{20,0},{24,12},{28,8},{1,21},{... | collective-permute-start | bytes 589832 | tf_op jit(solution)/shard_map/ppermute | solution.py:484
  283.9 26.7 %copy-start.30 = (bf16[6,16,1024]{2,1,0:T(8,128)(2,1)}, bf16[6,16,1024]{2,1,0:T(8,128)(2,1)S(1)}, u32[]{:S(2)}) copy-start(bf16[6,16,1024]{2,1,0:T(8,128)(2,1)S(1)} %collective-permute-done.16.rest_1_) | copy-start | bytes 589828
  283.9 26.7 %collective-permute-start.21 = (bf16[6,16,1024]{2,1,0:T(8,128)(2,1)S(1)}, bf16[6,16,1024]{2,1,0:T(8,128)(2,1)S(1)}, u32[]{:S(2)}, u32[]{:S(2)}) collective-permute-start(bf16[6,16,1024]{2,1,0:T(8,128)(2,1)S(1)} %copy-done.59), channel_id=1, source_target_pairs={{0,24},{4,28},{8,16},{12,20},{16,8},{20,12},{24,0},{28,4},{1,25},{... | collective-permute-start | bytes 589832 | tf_op jit(solution)/shard_map/ppermute | solution.py:484
  285.8 24.8 %collective-permute-start.22 = (bf16[6,16,1024]{2,1,0:T(8,128)(2,1)S(1)}, bf16[6,16,1024]{2,1,0:T(8,128)(2,1)S(1)}, u32[]{:S(2)}, u32[]{:S(2)}) collective-permute-start(bf16[6,16,1024]{2,1,0:T(8,128)(2,1)S(1)} %copy-done.58), channel_id=1, source_target_pairs={{0,28},{4,24},{8,20},{12,16},{16,12},{20,8},{24,4},{28,0},{1,29},{... | collective-permute-start | bytes 589832 | tf_op jit(solution)/shard_map/ppermute | solution.py:484
  314.6 50.1 %collective-permute-start.23 = (bf16[6,16,1024]{2,1,0:T(8,128)(2,1)}, bf16[6,16,1024]{2,1,0:T(8,128)(2,1)S(1)}, u32[]{:S(2)}, u32[]{:S(2)}) collective-permute-start(bf16[6,16,1024]{2,1,0:T(8,128)(2,1)} %get-tuple-element.140), channel_id=1, source_target_pairs={{0,4},{4,0},{8,12},{12,8},{16,20},{20,16},{24,28},{28,24},{1,5},{5... | collective-permute-start | bytes 589832 | tf_op jit(solution)/shard_map/ppermute | solution.py:484
  315.6 51.6 %collective-permute-start.24 = (bf16[6,16,1024]{2,1,0:T(8,128)(2,1)}, bf16[6,16,1024]{2,1,0:T(8,128)(2,1)S(1)}, u32[]{:S(2)}, u32[]{:S(2)}) collective-permute-start(bf16[6,16,1024]{2,1,0:T(8,128)(2,1)} %get-tuple-element.141), channel_id=1, source_target_pairs={{0,8},{4,12},{8,0},{12,4},{16,24},{20,28},{24,16},{28,20},{1,9},{5... | collective-permute-start | bytes 589832 | tf_op jit(solution)/shard_map/ppermute | solution.py:484
  340.6 26.6 %copy-start.65 = (bf16[6,16,1024]{2,1,0:T(8,128)(2,1)S(1)}, bf16[6,16,1024]{2,1,0:T(8,128)(2,1)}, u32[]{:S(2)}) copy-start(bf16[6,16,1024]{2,1,0:T(8,128)(2,1)} %get-tuple-element.146) | copy-start | bytes 589828
  359.5 17.2 %collective-permute-start.25 = (bf16[6,16,1024]{2,1,0:T(8,128)(2,1)S(1)}, bf16[6,16,1024]{2,1,0:T(8,128)(2,1)S(1)}, u32[]{:S(2)}, u32[]{:S(2)}) collective-permute-start(bf16[6,16,1024]{2,1,0:T(8,128)(2,1)S(1)} %copy-done.70), channel_id=1, source_target_pairs={{0,12},{4,8},{8,4},{12,0},{16,28},{20,24},{24,20},{28,16},{1,13},{... | collective-permute-start | bytes 589832 | tf_op jit(solution)/shard_map/ppermute | solution.py:484
  359.6 30.7 %collective-permute-start.26 = (bf16[6,16,1024]{2,1,0:T(8,128)(2,1)S(1)}, bf16[6,16,1024]{2,1,0:T(8,128)(2,1)S(1)}, u32[]{:S(2)}, u32[]{:S(2)}) collective-permute-start(bf16[6,16,1024]{2,1,0:T(8,128)(2,1)S(1)} %copy-done.68), channel_id=1, source_target_pairs={{0,16},{4,20},{8,24},{12,28},{16,0},{20,4},{24,8},{28,12},{1,17},{... | collective-permute-start | bytes 589832 | tf_op jit(solution)/shard_map/ppermute | solution.py:484
  363.2 47.1 %collective-permute-start.27 = (bf16[6,16,1024]{2,1,0:T(8,128)(2,1)S(1)}, bf16[6,16,1024]{2,1,0:T(8,128)(2,1)S(1)}, u32[]{:S(2)}, u32[]{:S(2)}) collective-permute-start(bf16[6,16,1024]{2,1,0:T(8,128)(2,1)S(1)} %copy-done.67), channel_id=1, source_target_pairs={{0,20},{4,16},{8,28},{12,24},{16,4},{20,0},{24,12},{28,8},{1,21},{... | collective-permute-start | bytes 589832 | tf_op jit(solution)/shard_map/ppermute | solution.py:484
  364.6 45.7 %copy-start.37 = (bf16[6,16,1024]{2,1,0:T(8,128)(2,1)}, bf16[6,16,1024]{2,1,0:T(8,128)(2,1)S(1)}, u32[]{:S(2)}) copy-start(bf16[6,16,1024]{2,1,0:T(8,128)(2,1)S(1)} %collective-permute-done.23.rest_9_) | copy-start | bytes 589828
  364.6 45.7 %collective-permute-start.28 = (bf16[6,16,1024]{2,1,0:T(8,128)(2,1)S(1)}, bf16[6,16,1024]{2,1,0:T(8,128)(2,1)S(1)}, u32[]{:S(2)}, u32[]{:S(2)}) collective-permute-start(bf16[6,16,1024]{2,1,0:T(8,128)(2,1)S(1)} %copy-done.66), channel_id=1, source_target_pairs={{0,24},{4,28},{8,16},{12,20},{16,8},{20,12},{24,0},{28,4},{1,25},{... | collective-permute-start | bytes 589832 | tf_op jit(solution)/shard_map/ppermute | solution.py:484
  367.2 43.1 %copy-start.38 = (bf16[6,16,1024]{2,1,0:T(8,128)(2,1)}, bf16[6,16,1024]{2,1,0:T(8,128)(2,1)S(1)}, u32[]{:S(2)}) copy-start(bf16[6,16,1024]{2,1,0:T(8,128)(2,1)S(1)} %collective-permute-done.24.rest_10_) | copy-start | bytes 589828
  367.2 43.1 %collective-permute-start.29 = (bf16[6,16,1024]{2,1,0:T(8,128)(2,1)S(1)}, bf16[6,16,1024]{2,1,0:T(8,128)(2,1)S(1)}, u32[]{:S(2)}, u32[]{:S(2)}) collective-permute-start(bf16[6,16,1024]{2,1,0:T(8,128)(2,1)S(1)} %copy-done.65), channel_id=1, source_target_pairs={{0,28},{4,24},{8,20},{12,16},{16,12},{20,8},{24,4},{28,0},{1,29},{... | collective-permute-start | bytes 589832 | tf_op jit(solution)/shard_map/ppermute | solution.py:484
  376.7 33.6 %copy-start.39 = (bf16[6,16,1024]{2,1,0:T(8,128)(2,1)}, bf16[6,16,1024]{2,1,0:T(8,128)(2,1)S(1)}, u32[]{:S(2)}) copy-start(bf16[6,16,1024]{2,1,0:T(8,128)(2,1)S(1)} %collective-permute-done.25.rest_11_) | copy-start | bytes 589828
  439.6 62.7 %collective-permute-start.33 = (bf16[6,256,256]{2,1,0:T(8,128)(2,1)}, bf16[6,256,256]{2,1,0:T(8,128)(2,1)S(1)}, u32[]{:S(2)}, u32[]{:S(2)}) collective-permute-start(bf16[6,256,256]{2,1,0:T(8,128)(2,1)} %get-tuple-element.150), channel_id=1, source_target_pairs={{0,1},{1,0},{2,3},{3,2},{4,5},{5,4},{6,7},{7,6},{8,9},{9,8},{10,11... | collective-permute-start | bytes 2359304 | tf_op jit(solution)/shard_map/ppermute | solution.py:484
  440.6 6.0 collective-permute-start.30
  461.1 45.5 %collective-permute-start.41 = (bf16[4,256,512]{2,1,0:T(8,128)(2,1)}, bf16[4,256,512]{2,1,0:T(8,128)(2,1)}, u32[]{:S(2)}, u32[]{:S(2)}) collective-permute-start(bf16[4,256,512]{2,1,0:T(8,128)(2,1)} %dynamic-slice_bitcast_fusion.2), channel_id=1, source_target_pairs={{0,4},{4,0},{8,12},{12,8},{16,20},{20,16},{24,28},{28,24},{1,5},{5... | collective-permute-start | bytes 3145736 | tf_op jit(solution)/shard_map/ppermute | solution.py:484
  473.0 45.1 %collective-permute-start.44 = (bf16[4,256,512]{2,1,0:T(8,128)(2,1)}, bf16[4,256,512]{2,1,0:T(8,128)(2,1)}, u32[]{:S(2)}, u32[]{:S(2)}) collective-permute-start(bf16[4,256,512]{2,1,0:T(8,128)(2,1)} %dynamic-slice_bitcast_fusion.1), channel_id=1, source_target_pairs={{0,4},{4,0},{8,12},{12,8},{16,20},{20,16},{24,28},{28,24},{1,5},{5... | collective-permute-start | bytes 3145736 | tf_op jit(solution)/shard_map/ppermute | solution.py:484
  500.5 61.2 %collective-permute-start.31 = (bf16[2,6,256,512]{3,2,1,0:T(8,128)(2,1)}, bf16[2,6,256,512]{3,2,1,0:T(8,128)(2,1)}, u32[]{:S(2)}, u32[]{:S(2)}) collective-permute-start(bf16[2,6,256,512]{3,2,1,0:T(8,128)(2,1)} %dynamic-slice_bitcast_fusion), channel_id=1, source_target_pairs={{0,1},{1,0},{2,3},{3,2},{4,5},{5,4},{6,7},{7,6},{8,9},{9,8},{10,11... | collective-permute-start | bytes 9437192 | tf_op jit(solution)/shard_map/ppermute | solution.py:484
  501.7 4.5 collective-permute-start.36
  502.4 21.6 %collective-permute-start.34 = (bf16[6,256,256]{2,1,0:T(8,128)(2,1)S(1)}, bf16[6,256,256]{2,1,0:T(8,128)(2,1)}, u32[]{:S(2)}, u32[]{:S(2)}) collective-permute-start(bf16[6,256,256]{2,1,0:T(8,128)(2,1)S(1)} %add.240), channel_id=1, source_target_pairs={{0,2},{1,3},{2,0},{3,1},{4,6},{5,7},{6,4},{7,5},{8,10},{9,11},{10,... | collective-permute-start | bytes 2359304 | tf_op jit(solution)/shard_map/ppermute | solution.py:484
  506.2 52.9 %collective-permute-start.37 = (f32[6,256]{1,0:T(8,128)S(1)}, f32[6,256]{1,0:T(8,128)S(1)}, u32[]{:S(2)}, u32[]{:S(2)}) collective-permute-start(f32[6,256]{1,0:T(8,128)S(1)} %add.247), channel_id=1, source_target_pairs={{0,2},{1,3},{2,0},{3,1},{4,6},{5,7},{6,4},{7,5},{8,10},{9,11},{10,... | collective-permute-start | bytes 18440 | tf_op jit(solution)/shard_map/ppermute | solution.py:484
  520.6 38.6 %collective-permute-start.42 = (bf16[2,256,512]{1,2,0:T(8,128)(2,1)}, bf16[2,256,512]{1,2,0:T(8,128)(2,1)}, u32[]{:S(2)}, u32[]{:S(2)}) collective-permute-start(bf16[2,256,512]{1,2,0:T(8,128)(2,1)} %bitcast.38), channel_id=1, source_target_pairs={{0,8},{4,12},{8,0},{12,4},{16,24},{20,28},{24,16},{28,20},{1,9},{5... | collective-permute-start | bytes 1572872 | tf_op jit(solution)/shard_map/ppermute | solution.py:484
  523.8 43.5 %collective-permute-start.45 = (bf16[2,256,512]{1,2,0:T(8,128)(2,1)}, bf16[2,256,512]{1,2,0:T(8,128)(2,1)}, u32[]{:S(2)}, u32[]{:S(2)}) collective-permute-start(bf16[2,256,512]{1,2,0:T(8,128)(2,1)} %bitcast.45), channel_id=1, source_target_pairs={{0,8},{4,12},{8,0},{12,4},{16,24},{20,28},{24,16},{28,20},{1,9},{5... | collective-permute-start | bytes 1572872 | tf_op jit(solution)/shard_map/ppermute | solution.py:484
  533.4 5.6 collective-permute-start.35
  539.0 20.1 %collective-permute-start.50 = (f32[7472]{0:T(1024)S(1)}, f32[7472]{0:T(1024)S(1)}, u32[]{:S(2)}, u32[]{:S(2)}) collective-permute-start(f32[7472]{0:T(1024)S(1)} %concatenate.56), channel_id=1, source_target_pairs={{0,4},{4,0},{8,12},{12,8},{16,20},{20,16},{24,28},{28,24},{1,5},{5... | collective-permute-start | bytes 89672 | tf_op jit(solution)/shard_map/ppermute | solution.py:484
  559.0 25.1 %collective-permute-start.47 = (bf16[4,256,384]{2,1,0:T(8,128)(2,1)}, bf16[4,256,384]{2,1,0:T(8,128)(2,1)}, u32[]{:S(2)}, u32[]{:S(2)}) collective-permute-start(bf16[4,256,384]{2,1,0:T(8,128)(2,1)} %dynamic-slice_bitcast_fusion.3), channel_id=1, source_target_pairs={{0,4},{4,0},{8,12},{12,8},{16,20},{20,16},{24,28},{28,24},{1,5},{5... | collective-permute-start | bytes 2359304 | tf_op jit(solution)/shard_map/ppermute | solution.py:484
  559.1 9.3 %collective-permute-start.51 = (f32[7472]{0:T(1024)S(1)}, f32[7472]{0:T(1024)S(1)}, u32[]{:S(2)}, u32[]{:S(2)}) collective-permute-start(f32[7472]{0:T(1024)S(1)} %add.272), channel_id=1, source_target_pairs={{0,8},{4,12},{8,0},{12,4},{16,24},{20,28},{24,16},{28,20},{1,9},{5... | collective-permute-start | bytes 89672 | tf_op jit(solution)/shard_map/ppermute | solution.py:484
  560.4 25.9 %collective-permute-start.43 = (bf16[1,256,512]{1,2,0:T(8,128)(2,1)S(1)}, bf16[1,256,512]{1,2,0:T(8,128)(2,1)}, u32[]{:S(2)}, u32[]{:S(2)}) collective-permute-start(bf16[1,256,512]{1,2,0:T(8,128)(2,1)S(1)} %constant_dynamic-slice_fusion.4), channel_id=1, source_target_pairs={{0,16},{4,20},{8,24},{12,28},{16,0},{20,4},{24,8},{28,12},{1,17},{... | collective-permute-start | bytes 786440 | tf_op jit(solution)/shard_map/ppermute | solution.py:484
  566.9 34.0 %collective-permute-start.32 = (bf16[1,6,256,512]{3,2,1,0:T(8,128)(2,1)}, bf16[1,6,256,512]{3,2,1,0:T(8,128)(2,1)}, u32[]{:S(2)}, u32[]{:S(2)}) collective-permute-start(bf16[1,6,256,512]{3,2,1,0:T(8,128)(2,1)} %constant_dynamic-slice_fusion.7), channel_id=1, source_target_pairs={{0,2},{1,3},{2,0},{3,1},{4,6},{5,7},{6,4},{7,5},{8,10},{9,11},{10,... | collective-permute-start | bytes 4718600 | tf_op jit(solution)/shard_map/ppermute | solution.py:484
  568.3 32.6 %copy-start.3 = (bf16[2,6,256,512]{3,2,1,0:T(8,128)(2,1)S(1)}, bf16[2,6,256,512]{3,2,1,0:T(8,128)(2,1)}, u32[]{:S(2)}) copy-start(bf16[2,6,256,512]{3,2,1,0:T(8,128)(2,1)} %copy-done.2) | copy-start | bytes 9437188
  568.4 13.3 %collective-permute-start.52 = (f32[7472]{0:T(1024)S(1)}, f32[7472]{0:T(1024)S(1)}, u32[]{:S(2)}, u32[]{:S(2)}) collective-permute-start(f32[7472]{0:T(1024)S(1)} %add.273), channel_id=1, source_target_pairs={{0,16},{4,20},{8,24},{12,28},{16,0},{20,4},{24,8},{28,12},{1,17},{... | collective-permute-start | bytes 89672 | tf_op jit(solution)/shard_map/ppermute | solution.py:484
  570.7 38.6 %collective-permute-start.46 = (bf16[1,256,512]{1,2,0:T(8,128)(2,1)}, bf16[1,256,512]{1,2,0:T(8,128)(2,1)}, u32[]{:S(2)}, u32[]{:S(2)}) collective-permute-start(bf16[1,256,512]{1,2,0:T(8,128)(2,1)} %constant_dynamic-slice_fusion.1), channel_id=1, source_target_pairs={{0,16},{4,20},{8,24},{12,28},{16,0},{20,4},{24,8},{28,12},{1,17},{... | collective-permute-start | bytes 786440 | tf_op jit(solution)/shard_map/ppermute | solution.py:484
  585.6 8.5 %collective-permute-start.48 = (bf16[2,256,384]{2,1,0:T(8,128)(2,1)S(1)}, bf16[2,256,384]{2,1,0:T(8,128)(2,1)S(1)}, u32[]{:S(2)}, u32[]{:S(2)}) collective-permute-start(bf16[2,256,384]{2,1,0:T(8,128)(2,1)S(1)} %dynamic-slice_bitcast_fusion.4), channel_id=1, source_target_pairs={{0,8},{4,12},{8,0},{12,4},{16,24},{20,28},{24,16},{28,20},{1,9},{5... | collective-permute-start | bytes 1179656 | tf_op jit(solution)/shard_map/ppermute | solution.py:484
  594.9 21.8 %collective-permute-start.49 = (bf16[1,256,384]{2,1,0:T(8,128)(2,1)}, bf16[1,256,384]{2,1,0:T(8,128)(2,1)}, u32[]{:S(2)}, u32[]{:S(2)}) collective-permute-start(bf16[1,256,384]{2,1,0:T(8,128)(2,1)} %constant_dynamic-slice_fusion), channel_id=1, source_target_pairs={{0,16},{4,20},{8,24},{12,28},{16,0},{20,4},{24,8},{28,12},{1,17},{... | collective-permute-start | bytes 589832 | tf_op jit(solution)/shard_map/ppermute | solution.py:484
  607.6 3.6 collective-permute-start.38
  611.2 3.6 collective-permute-start.39
  614.8 4.5 collective-permute-start.40
  (70 other events, 621.6 us)
Sparse Core Ops, SparseCore 0:
  9.6 49.0 all-gather.1
  232.7 64.2 reduce-scatter.2
  301.1 185.6 reduce-scatter.4

commit v2 on v1

v2 whole, which is shorter than its diff:
```python
import functools

import jax
import jax.numpy as jnp
from jax import lax
from jax.experimental import pallas as pl
from jax.experimental.pallas import tpu as pltpu
from jax.sharding import PartitionSpec as P

HEAD_DIM = 64
BLOCK_LEN = 256
LANES = 128
EDGE = 16
ROWS = 16
VMEM = 56 * 2**20
EPS = 1e-05
BF = jnp.bfloat16
F32 = jnp.float32
def cost(micros):
    return pl.CostEstimate(flops=int(micros * 1.15e+09), bytes_accessed=1000, transcendentals=0)


SMEM_SPEC = pl.BlockSpec(memory_space=pltpu.SMEM)


def dot(a, b, contract=((1,), (0,)), precision=None):
    return lax.dot_general(
        a, b, (contract, ((), ())), preferred_element_type=F32, precision=precision
    )


def halves(value):
    high = value.astype(BF)
    return high, (value - high.astype(F32)).astype(BF)


def widen(value, expand):
    high, low = halves(value)
    return dot(high, expand) + dot(low, expand)


def per_head(value, expand):
    high, low = halves(value)
    nt = ((1,), (1,))
    return dot(high, expand, nt) + dot(low, expand, nt)


def to_row(column):
    rows = column.shape[0]
    return jnp.transpose(jnp.broadcast_to(column, (rows, LANES)))[:8]


def sigmoid(value):
    return 0.5 * jnp.tanh(0.5 * value) + 0.5


def softplus(value):
    return jnp.maximum(value, 0.0) + jnp.log1p(jnp.exp(-jnp.abs(value)))


def triangle(span, lower):
    row = lax.broadcasted_iota(jnp.int32, (span, span), 0)
    col = lax.broadcasted_iota(jnp.int32, (span, span), 1)
    return ((col <= row) if lower else (col >= row)).astype(F32)


def running(value, lower):
    return dot(triangle(value.shape[0], lower), value, precision=lax.Precision.HIGHEST)


def doc_mask(seg_col, seg_row, lower):
    span = seg_col.shape[0]
    row = lax.broadcasted_iota(jnp.int32, (span, span), 0)
    col = lax.broadcasted_iota(jnp.int32, (span, span), 1)
    causal = (col <= row) if lower else (col >= row)
    return jnp.where(causal, (seg_col == seg_row).astype(F32), 0.0)


def back_rows(value, steps):
    return value if steps == 0 else pltpu.roll(value, steps, 0)


def ahead_rows(value, steps):
    return value if steps == 0 else pltpu.roll(value, value.shape[0] - steps, 0)


def conv_rows(extended, aux, weight):
    taps = 4
    out = weight[taps : taps + 1] + weight[taps - 1 : taps] * extended[EDGE:]
    for tap in range(taps - 1):
        window = back_rows(extended, taps - 1 - tap)[EDGE:]
        out = out + weight[tap : tap + 1] * (aux[:, tap : tap + 1] * window)
    return out


def conv_back_rows(d_conv, extended, aux, weight, grad_ref=None):
    taps = 4
    room = jnp.zeros((EDGE, d_conv.shape[1]), F32)
    total = None
    for tap in range(taps):
        steps = taps - 1 - tap
        masked = d_conv if steps == 0 else d_conv * aux[:, tap : tap + 1]
        if grad_ref is not None:
            window = back_rows(extended, steps)[EDGE:]
            grad_ref[tap : tap + 1] += jnp.sum(masked * window, axis=0, keepdims=True)
        placed = jnp.concatenate([room, masked * weight[tap : tap + 1]], axis=0)
        placed = ahead_rows(placed, steps)
        total = placed if total is None else total + placed
    if grad_ref is not None:
        grad_ref[taps : taps + 1] += jnp.sum(d_conv, axis=0, keepdims=True)
    return total


def chunk_grid(count, rows, own):
    across = count * ROWS // rows
    return across, own // across


def cut(value, scratch, at, count):
    across, width = chunk_grid(count, value.shape[0], value.shape[1])
    for j in range(count):
        a, b = j // across, j % across
        scratch[j, at] = value[a * ROWS : (a + 1) * ROWS, b * width : (b + 1) * width].astype(BF)


def uncut(scratch, at, count, rows, own):
    across, _ = chunk_grid(count, rows, own)
    return jnp.concatenate(
        [
            jnp.concatenate([scratch[a * across + b, at] for b in range(across)], axis=1)
            for a in range(count // across)
        ],
        axis=0,
    )


def both_halves(me, mine_ref, other_ref):
    mine, other = mine_ref[0], other_ref[0]
    return jnp.where(
        me % 2 == 0,
        jnp.concatenate([mine, other], axis=0),
        jnp.concatenate([other, mine], axis=0),
    )


def front_kernel(
    state, me_ref, tok_ref, halo_ref, gain_ref, w_ref, w_small_ref, seg_ref, conv_x_ref,
    conv_bc_ref, head_ref, expand_ref, normed_ref, pre_x_ref, pre_bc_ref, halo_x_ref, halo_bc_ref,
    x_ref, bc_ref, xs_ref, dt_ref, cum_ref, aux_ref, keep_ref, send_ref
):
    s = pl.program_id(0)
    seqs = pl.num_programs(0)
    odd = me_ref[0] % 2
    half = state // 2
    own = xs_ref.shape[-1]
    wide = 2 * state
    span = tok_ref.shape[1]

    def norm(value):
        value = value.astype(F32)
        rstd = lax.rsqrt(jnp.mean(value * value, axis=-1, keepdims=True) + EPS)
        return (value * rstd * gain_ref[...]).astype(BF), rstd

    normed, rstd = norm(tok_ref[0])
    normed_ref[0] = normed
    room = jnp.zeros((EDGE - halo_ref.shape[1], halo_ref.shape[2]), F32)
    ahead = jnp.concatenate([room, norm(halo_ref[0])[0].astype(F32)], axis=0).astype(BF)
    rows = jnp.concatenate([ahead, normed], axis=0)
    pre_x = dot(rows, w_ref[0]).astype(BF)
    small = dot(rows, w_small_ref[...])
    pre_bc = small[:, :wide].astype(BF)
    dt_raw = small[EDGE:, wide:]

    seg = jnp.transpose(jnp.broadcast_to(seg_ref[0, 0:1], (LANES, LANES + span)))[LANES - EDGE :]
    here = seg[EDGE:]
    lane = lax.broadcasted_iota(jnp.int32, here.shape, 1)
    columns = [(back_rows(seg, 3 - tap)[EDGE:] == here).astype(F32) for tap in range(3)]
    columns.append((here == here[-1:]).astype(F32))
    columns.append((here == seg[EDGE - 1 : EDGE]).astype(F32))
    columns.append(here)
    columns.append(jnp.broadcast_to(rstd, here.shape))
    aux = jnp.zeros(here.shape, F32)
    for at, column in enumerate(columns):
        aux = jnp.where(lane == at, column, aux)
    aux_ref[0] = aux

    dt_ref[0] = dt_raw
    pre_x_ref[0] = pre_x[EDGE:]
    halo_x_ref[0] = pre_x[:EDGE]
    pre_bc_ref[0] = pre_bc[EDGE:]
    halo_bc_ref[0] = pre_bc[:EDGE]
    conv = conv_rows(pre_bc.astype(F32), aux, conv_bc_ref[...])
    bc = (conv * sigmoid(conv)).astype(BF)
    bc_ref[0] = bc
    conv = conv_rows(pre_x.astype(F32), aux, conv_x_ref[...])
    x = (conv * sigmoid(conv)).astype(BF)
    x_ref[0] = x
    x_float = x.astype(F32)
    step = softplus(dt_raw + head_ref[0:1])
    cum = running(-head_ref[1:2] * step, True)
    cum_ref[0] = cum
    expand = expand_ref[...]
    xs_ref[0] = (x_float * widen(step, expand)).astype(BF)
    last = cum[-1:]
    tail_step = jnp.exp(last - cum) * aux[:, 3:4] * step
    loaded = (x_float * widen(tail_step, expand)).astype(BF)
    own_state = dot(bc[:, :state], loaded, ((0,), (0,)))
    low, high = own_state[:half], own_state[half:]
    at = pl.ds(pl.multiple_of(s * half, half), half)
    keep_ref[at] = jnp.where(odd == 0, low, high).astype(BF)
    send_ref[at] = jnp.where(odd == 0, high, low).astype(BF)

    decay = jnp.broadcast_to(jnp.exp(last) * aux[-1:, 4:5], (8, LANES))
    decay_wide = widen(decay, expand)[:1]
    high = decay_wide.astype(BF).astype(F32)
    places = lax.broadcasted_iota(jnp.int32, (ROWS, 1), 0)
    extra = jnp.where(places == s, high, 0.0) + jnp.where(
        places == s + seqs, decay_wide - high, 0.0
    )
    end = pl.ds(seqs * half, ROWS)

    @pl.when(s == 0)
    def _():
        keep_ref[end] = extra.astype(BF)

    @pl.when(s > 0)
    def _():
        keep_ref[end] = (keep_ref[end].astype(F32) + extra).astype(BF)

    @pl.when(s == seqs - 1)
    def _():
        send_ref[end] = keep_ref[end]


def pair_kernel(seqs, groups, half, me_ref, mine_ref, other_ref, *rest):
    outs, decay_ref, scratch = rest[:groups], rest[groups], rest[groups + 1]
    odd, place = me_ref[0] % 2, me_ref[0] // 2
    end = seqs * half
    packed = [ref[end : end + ROWS].astype(F32) for ref in (mine_ref, other_ref)]
    mine, other = [p[:seqs] + p[seqs : 2 * seqs] for p in packed]
    first = jnp.where(odd == 0, mine, other)
    second = jnp.where(odd == 0, other, mine)
    decay_ref[0:seqs] = first
    decay_ref[8 : 8 + seqs] = second
    both = first * second
    high = both.astype(BF).astype(F32)
    room = jnp.zeros((ROWS - 2 * seqs, both.shape[1]), F32)
    extra = jnp.concatenate([high, both - high, room], axis=0)
    width = scratch.shape[3]
    across, _ = chunk_grid(groups, half, both.shape[1])
    for j in range(groups):
        b = j % across
        scratch[j, seqs] = extra[:, b * width : (b + 1) * width].astype(BF)
    for s in range(seqs):
        rows = slice(s * half, (s + 1) * half)
        mine, other = mine_ref[rows].astype(F32), other_ref[rows].astype(F32)
        early = jnp.where(odd == 0, mine, other)
        late = jnp.where(odd == 0, other, mine)
        cut(second[s : s + 1] * early + late, scratch, s, groups)
    for m in range(groups):
        outs[m][...] = scratch[place ^ m]


def pair_back_kernel(seqs, groups, half, me_ref, mine_ref, other_ref, decay_ref, *rest):
    outs, scratch = rest[:groups], rest[groups]
    odd, place = me_ref[0] % 2, me_ref[0] // 2
    for s in range(seqs):
        rows = slice(s * half, (s + 1) * half)
        mine, other = mine_ref[rows].astype(F32), other_ref[rows].astype(F32)
        early = jnp.where(odd == 0, mine, other)
        late = jnp.where(odd == 0, other, mine)
        cut(decay_ref[s : s + 1] * late + early, scratch, s, groups)
    for m in range(groups):
        outs[m][...] = scratch[place ^ m]


def scan_kernel(seqs, groups, me_ref, *rest):
    ins, outs = rest[:groups], rest[groups : 2 * groups]
    decay_ref, scratch = rest[2 * groups], rest[2 * groups + 1]
    place = me_ref[0] // 2
    for m in range(groups):
        scratch[place ^ m] = ins[m][...]
    for s in range(seqs):
        entry = jnp.zeros(scratch.shape[2:], F32)
        for k in range(groups):
            packed = scratch[k, seqs].astype(F32)
            decay = packed[s : s + 1] + packed[s + seqs : s + seqs + 1]
            decay_ref[k, s : s + 1] = decay
            arrived = scratch[k, s].astype(F32)
            scratch[k, s] = entry.astype(BF)
            entry = decay * entry + arrived
    for m in range(groups):
        outs[m][...] = scratch[place ^ m, :seqs]


def scan_back_kernel(seqs, groups, me_ref, decay_ref, *rest):
    ins, outs, scratch = rest[:groups], rest[groups : 2 * groups], rest[2 * groups]
    place = me_ref[0] // 2
    for m in range(groups):
        scratch[place ^ m] = ins[m][...]
    for s in range(seqs):
        leave = jnp.zeros(scratch.shape[2:], F32)
        for k in reversed(range(groups)):
            arrived = scratch[k, s].astype(F32)
            scratch[k, s] = leave.astype(BF)
            leave = decay_ref[k, s : s + 1] * leave + arrived
    for m in range(groups):
        outs[m][...] = scratch[place ^ m]


def unpair_kernel(seqs, groups, half, forward, me_ref, mine_ref, other_ref, decay_ref, *rest):
    ins, (own_ref, send_ref, scratch) = rest[:groups], rest[groups:]
    odd, place = me_ref[0] % 2, me_ref[0] // 2
    own = own_ref.shape[-1]
    for m in range(groups):
        scratch[place ^ m] = ins[m][...]
    is_first = (odd == 0) if forward else (odd == 1)
    for s in range(seqs):
        rows = slice(s * half, (s + 1) * half)
        entry = uncut(scratch, s, groups, half, own).astype(F32)
        mine, other = mine_ref[rows].astype(F32), other_ref[rows].astype(F32)
        first = jnp.where(is_first, mine, other)
        at = s if forward else 8 + s
        later = decay_ref[at : at + 1] * entry + first
        own_ref[s] = jnp.where(is_first, entry, later).astype(BF)
        send_ref[s] = jnp.where(is_first, later, entry).astype(BF)


def inner_kernel(state, bc_ref, xs_ref, cum_ref, aux_ref, seg_ref, out_ref):
    own = xs_ref.shape[-1]
    b_ssm, c_ssm = bc_ref[0, :, :state], bc_ref[0, :, state:]
    cum = cum_ref[0]
    cum_t = jnp.transpose(cum)
    mask = doc_mask(aux_ref[0, :, 5:6], seg_ref[0, 0:1, LANES:], True)
    scores = dot(c_ssm, b_ssm, ((1,), (1,))) * mask
    left = lax.broadcasted_iota(jnp.int32, (1, LANES), 1) < HEAD_DIM
    for pair in range(own // LANES):
        lanes = slice(pair * LANES, (pair + 1) * LANES)
        xs = xs_ref[0, :, lanes].astype(F32)
        total = None
        for side in range(2):
            h = 2 * pair + side
            lag = jnp.minimum(cum[:, h : h + 1] - cum_t[h : h + 1], 0.0)
            weights = (scores * jnp.exp(lag)).astype(BF)
            own_xs = jnp.where(left if side == 0 else ~left, xs, 0.0).astype(BF)
            term = dot(weights, own_xs)
            total = term if total is None else total + term
        out_ref[0, :, lanes] = total


def mixer_out(state, states, x_ref, bc_ref, inner_ref, gate_ref, cum_ref, aux_ref, rows_ref, expand_ref):
    c_ssm = bc_ref[0, :, state:]
    x_float = x_ref[0].astype(F32)
    entry_wide = widen(jnp.exp(cum_ref[0]) * aux_ref[0, :, 4:5], expand_ref[...])
    mixed = inner_ref[0] + dot(c_ssm, states) * entry_wide
    y = mixed + rows_ref[1:2] * x_float
    gate = gate_ref[0].astype(F32)
    sig = sigmoid(gate)
    return mixed, y, x_float, gate, sig, entry_wide


def sums_kernel(
    state, me_ref, x_ref, bc_ref, inner_ref, gate_ref, e_ref, cum_ref, aux_ref, mine_ref,
    other_ref, rows_ref, expand_ref, out_ref
):
    states = both_halves(me_ref[0], mine_ref, other_ref)
    _, y, _, gate, sig, _ = mixer_out(
        state, states, x_ref, bc_ref, inner_ref, gate_ref, cum_ref, aux_ref, rows_ref, expand_ref
    )
    gated = y * (gate * sig)
    squares = jnp.sum(gated * gated, axis=-1, keepdims=True)
    dots = jnp.sum(e_ref[0].astype(F32) * (gated * rows_ref[0:1]), axis=-1, keepdims=True)
    place = lax.broadcasted_iota(jnp.int32, (8, 1), 0)
    out_ref[0] = jnp.where(place == 0, to_row(squares), jnp.where(place == 1, to_row(dots), 0.0))


def gate_back_kernel(
    state, inner_total, me_ref, x_ref, bc_ref, inner_ref, gate_ref, e_ref, cum_ref, aux_ref,
    mine_ref, other_ref, rows_ref, expand_ref, sums_ref, scaled_ref, dz_ref, dy_ref, mixed_ref,
    dc_ref, dot_ref, grad_ref, keep_ref, send_ref
):
    s = pl.program_id(0)
    odd = me_ref[0] % 2
    half = state // 2
    expand = expand_ref[...]
    states = both_halves(me_ref[0], mine_ref, other_ref)
    mixed, y, x_float, gate, sig, entry_wide = mixer_out(
        state, states, x_ref, bc_ref, inner_ref, gate_ref, cum_ref, aux_ref, rows_ref, expand_ref
    )
    columns = jnp.transpose(
        jnp.concatenate([sums_ref[0], jnp.zeros((LANES - 8, sums_ref.shape[2]), F32)], axis=0)
    )
    rstd = lax.rsqrt(columns[:, 0:1] / inner_total + EPS)
    slope = columns[:, 1:2] * (rstd * rstd * rstd) / inner_total
    gain = rows_ref[0:1]
    silu = gate * sig
    gated = y * silu
    scaled_ref[0] = (gated * gain * rstd).astype(BF)
    d_scaled = e_ref[0].astype(F32) * rstd
    d_gated = d_scaled * gain - slope * gated
    d_y = d_gated * silu
    dy_ref[0] = d_y.astype(BF)
    d_z = (d_gated * y * (sig * (1.0 + gate * (1.0 - sig)))).astype(BF)
    dz_ref[0] = d_z
    row = jnp.sum(d_z.astype(F32) * gate, axis=-1, keepdims=True)
    dot_ref[0] = to_row(row)
    mixed_ref[0] = per_head(d_y * mixed, expand)

    @pl.when(s == 0)
    def _():
        grad_ref[...] = jnp.zeros_like(grad_ref)

    grad_ref[0:1] += jnp.sum(d_scaled * gated, axis=0, keepdims=True)
    grad_ref[1:2] += jnp.sum(d_y * x_float, axis=0, keepdims=True)
    d_carried = (d_y * entry_wide).astype(BF)
    dc_ref[0] = dot(d_carried, states, ((1,), (1,)))
    grad = dot(bc_ref[0, :, state:], d_carried, ((0,), (0,)))
    low, high = grad[:half], grad[half:]
    at = pl.ds(pl.multiple_of(s * half, half), half)
    keep_ref[at] = jnp.where(odd == 0, low, high).astype(BF)
    send_ref[at] = jnp.where(odd == 0, high, low).astype(BF)


def inner_back_kernel(
    state, x_ref, bc_ref, xs_ref, dy_ref, dc_ref, cum_ref, dt_ref, aux_ref, seg_ref, rows_ref,
    head_ref, expand_ref, dx_ref, dstep_ref, dbc_ref
):
    own = xs_ref.shape[-1]
    b_ssm, c_ssm = bc_ref[0, :, :state], bc_ref[0, :, state:]
    cum = cum_ref[0]
    cum_t = jnp.transpose(cum)
    nt = ((1,), (1,))
    mask = doc_mask(aux_ref[0, :, 5:6], seg_ref[0, 0:1, LANES:], False)
    scores = dot(b_ssm, c_ssm, nt) * mask
    left = lax.broadcasted_iota(jnp.int32, (1, LANES), 1) < HEAD_DIM
    d_scores = None
    sums = []
    for pair in range(own // LANES):
        lanes = slice(pair * LANES, (pair + 1) * LANES)
        xs = xs_ref[0, :, lanes]
        dy = dy_ref[0, :, lanes].astype(F32)
        total = None
        for side in range(2):
            h = 2 * pair + side
            lag = jnp.minimum(cum_t[h : h + 1] - cum[:, h : h + 1], 0.0)
            mixing = jnp.exp(lag)
            weights = (scores * mixing).astype(BF)
            own_dy = jnp.where(left if side == 0 else ~left, dy, 0.0).astype(BF)
            term = dot(weights, own_dy)
            total = term if total is None else total + term
            d_mixed = dot(xs, own_dy, nt) * mixing
            d_scores = d_mixed if d_scores is None else d_scores + d_mixed
        sums.append(total)
    back = jnp.concatenate(sums, axis=1)
    expand = expand_ref[...]
    x_float = x_ref[0].astype(F32)
    dstep_ref[0] = per_head(x_float * back, expand)
    step = softplus(dt_ref[0] + head_ref[0:1])
    dy_all = dy_ref[0].astype(F32)
    dx_ref[0] = (back * widen(step, expand) + rows_ref[1:2] * dy_all).astype(BF)
    d_scores = (d_scores * mask).astype(BF)
    dbc_ref[0, :, :state] = dot(d_scores, c_ssm)
    dbc_ref[0, :, state:] = dot(d_scores, b_ssm, ((0,), (0,))) + dc_ref[0]


def leave_kernel(
    state, me_ref, x_ref, bc_ref, pre_ref, halo_ref, pre_bc_ref, halo_bc_ref, dx_ref, dstep_ref,
    dbc_ref, mixed_ref, cum_ref, dt_ref, aux_ref, dot_z_ref, mine_ref, other_ref, end_mine_ref,
    end_other_ref, conv_ref, conv_bc_ref, head_ref, expand_ref, dpre_ref, back_ref, back_bc_ref,
    dbc_out_ref, ddt_ref, dot_ref, grad_ref, small_ref
):
    me = me_ref[0]
    own = dx_ref.shape[-1]
    expand = expand_ref[...]
    states = both_halves(me, mine_ref, other_ref)
    ends = both_halves(me, end_mine_ref, end_other_ref)
    b_ssm = bc_ref[0, :, :state]
    x_float = x_ref[0].astype(F32)
    aux = aux_ref[0]
    dt_pre = dt_ref[0] + head_ref[0:1]
    step = softplus(dt_pre)
    rate = head_ref[1:2]
    cum = cum_ref[0]
    last = cum[-1:]
    tail_decay = jnp.exp(last - cum) * aux[:, 3:4]
    tail_step = tail_decay * step
    tail_wide = widen(tail_step, expand)
    loaded = (x_float * tail_wide).astype(BF)
    d_loaded = dot(b_ssm, ends)
    dbc_out_ref[0, :, :state] = (dbc_ref[0, :, :state] + dot(loaded, ends, ((1,), (1,)))).astype(BF)
    dbc_out_ref[0, :, state:] = dbc_ref[0, :, state:].astype(BF)
    d_bc = dbc_out_ref[0, :EDGE].astype(F32)
    extended = jnp.concatenate([halo_bc_ref[0], pre_bc_ref[0, :EDGE]], axis=0).astype(F32)
    weight = conv_bc_ref[...]
    conv = conv_rows(extended, aux[:EDGE], weight)
    sig = sigmoid(conv)
    d_conv = d_bc * (sig * (1.0 + conv * (1.0 - sig)))
    back_bc_ref[0] = conv_back_rows(d_conv, extended, aux[:EDGE], weight)[:EDGE].astype(BF)
    d_x = dx_ref[0].astype(F32) + d_loaded * tail_wide
    d_tail = per_head(d_loaded * x_float, expand)
    end_terms = d_tail * tail_step
    product = jnp.sum(ends.astype(F32) * states.astype(F32), axis=0, keepdims=True)
    d_decay = per_head(jnp.broadcast_to(product, (8, own)), expand)[:1]
    block_decay = jnp.exp(last) * aux[-1:, 4:5]
    d_cum = mixed_ref[0] - step * dstep_ref[0] - end_terms
    last_add = jnp.sum(end_terms, axis=0, keepdims=True) + d_decay * block_decay
    d_log = running(d_cum, False) + last_add
    d_step = dstep_ref[0] + d_tail * tail_decay - d_log * rate
    d_dt = d_step * sigmoid(dt_pre)
    ddt_ref[0] = d_dt.astype(BF)

    @pl.when(pl.program_id(0) == 0)
    def _():
        grad_ref[...] = jnp.zeros_like(grad_ref)
        small_ref[...] = jnp.zeros_like(small_ref)

    small_ref[0:1] += jnp.sum(d_dt, axis=0, keepdims=True)
    small_ref[1:2] += jnp.sum(d_log * (-rate * step), axis=0, keepdims=True)

    extended = jnp.concatenate([halo_ref[0], pre_ref[0]], axis=0).astype(F32)
    weight = conv_ref[...]
    conv = conv_rows(extended, aux, weight)
    sig = sigmoid(conv)
    d_conv = d_x * (sig * (1.0 + conv * (1.0 - sig)))
    d_ext = conv_back_rows(d_conv, extended, aux, weight, grad_ref)
    d_pre = d_ext[EDGE:].astype(BF)
    dpre_ref[0] = d_pre
    back_ref[0] = d_ext[:EDGE].astype(BF)
    row = jnp.sum(d_pre.astype(F32) * extended[EDGE:], axis=-1, keepdims=True)
    row = row + jnp.sum(ddt_ref[0].astype(F32) * dt_ref[0], axis=-1, keepdims=True)
    dot_ref[0] = to_row(row) + dot_z_ref[0]


def conv_bc_kernel(d_ref, pre_ref, halo_ref, aux_ref, conv_ref, dpre_ref, dot_ref, grad_ref):
    span = pre_ref.shape[1]
    extended = jnp.concatenate([halo_ref[0], pre_ref[0]], axis=0).astype(F32)
    aux = aux_ref[0]
    weight = conv_ref[...]
    conv = conv_rows(extended, aux, weight)
    sig = sigmoid(conv)
    d_conv = d_ref[0, :span].astype(F32) * (sig * (1.0 + conv * (1.0 - sig)))

    @pl.when(pl.program_id(0) == 0)
    def _():
        grad_ref[...] = jnp.zeros_like(grad_ref)

    d_pre = conv_back_rows(d_conv, extended, aux, weight, grad_ref)[EDGE:]
    ahead = d_ref[0, span : span + EDGE].astype(F32)
    d_pre = jnp.concatenate([d_pre[: span - EDGE], d_pre[span - EDGE :] + ahead], axis=0)
    d_pre = d_pre.astype(BF)
    dpre_ref[0] = d_pre
    row = jnp.sum(d_pre.astype(F32) * extended[EDGE:], axis=-1, keepdims=True)
    packed = d_ref[0, span + EDGE :].astype(F32)
    dot_ref[0] = to_row(row) + (packed[0:1] + packed[1:2])


def gram_chunk_kernel(me_ref, a_ref, b_ref, *outs):
    product = dot(a_ref[...], b_ref[...], ((0,), (0,))).astype(BF)
    width = product.shape[1] // len(outs)
    for at, out_ref in enumerate(outs):
        out_ref[0] = product[:, at * width : (at + 1) * width]


def share_kernel(terms, with_sum, me_ref, *refs):
    out_ref = refs[2 * terms + with_sum]
    nt = ((1,), (1,))
    total = None
    for t in range(terms):
        rhs = refs[2 * t + 1]
        rhs = rhs[0] if len(rhs.shape) == 3 else rhs[...]
        term = dot(refs[2 * t][...], rhs, nt)
        total = term if total is None else total + term
    out_ref[0] = total.astype(BF)
    if with_sum:
        sum_ref = refs[-1]

        @pl.when(pl.program_id(1) == 0)
        def _():
            sum_ref[...] = jnp.zeros_like(sum_ref)

        normed = refs[2 * terms][...].astype(F32)
        sum_ref[0, 0:1] += jnp.sum(total * normed, axis=0, keepdims=True)


def per_seq(seqs, shape):
    zeros = (0,) * len(shape)
    return pl.BlockSpec((1, *shape), lambda s: (jnp.minimum(s, seqs - 1), *zeros))


def whole(shape):
    zeros = (0,) * len(shape)
    return pl.BlockSpec(tuple(shape), lambda s: zeros)


def call(body, grid, ins, in_specs, outs, out_specs, scratch, flops, name, aliases={}):
    return pl.pallas_call(
        body,
        grid=(grid,),
        in_specs=in_specs,
        out_specs=out_specs,
        out_shape=outs,
        scratch_shapes=scratch,
        name=name,
        input_output_aliases=aliases,
        compiler_params=pltpu.CompilerParams(vmem_limit_bytes=VMEM),
        cost_estimate=cost(flops),
    )(*ins)


def shaped(shape, dtype):
    return jax.ShapeDtypeStruct(tuple(shape), dtype)


def swap(value, axis, mask):
    count = lax.axis_size(axis)
    return lax.ppermute(value, axis, [(i, i ^ mask) for i in range(count)])


def shift(value, axis, steps):
    count = lax.axis_size(axis)
    leading, last = (max(0, -steps), min(count, count - steps))
    return lax.ppermute(value, axis, [(i, i + steps) for i in range(leading, last)])


def exchange(chunks, masks):
    return [swap(c, "seq", mask) if mask else c for c, mask in zip(chunks, masks)]


def after(value, *others):
    return lax.optimization_barrier((value, *others))[0]


def fold_step(sides, axis, mask):
    odd, even = sides
    arrived = swap(odd, axis, mask)
    if even.shape[0] == 1:
        return (even + arrived)[0]
    return even[1::2] + arrived[1::2], even[0::2] + arrived[0::2]


def fold(sides, axis, mask=1):
    while isinstance(sides, tuple):
        sides = fold_step(sides, axis, mask)
        mask *= 2
    return sides


def pair_sides(full):
    odd = lax.axis_index("seq") % 2
    chunks = full.reshape(lax.axis_size("seq") // 2, 2, -1, full.shape[-1])
    return tuple(lax.dynamic_index_in_dim(chunks, at, 1, False) for at in (1 - odd, odd))


def pair_sum(sides):
    return sides[1] + swap(sides[0], "seq", 1)


def spread_sum(total):
    count = lax.axis_size("seq")
    return lax.psum_scatter(
        total.reshape(-1, total.shape[-1]),
        "seq",
        scatter_dimension=0,
        tiled=True,
        axis_index_groups=[[2 * z + x for z in range(count // 2)] for x in range(2)],
    )


def row_sides(full, axis):
    count = lax.axis_size(axis)
    me = lax.axis_index(axis)
    chunks = full.reshape(count, -1, full.shape[-1])

    def stacked(masks):
        return jnp.stack([lax.dynamic_index_in_dim(chunks, me ^ m, 0, False) for m in masks])

    return stacked(range(1, count, 2)), stacked(range(0, count, 2))


def sum_all(value, axis):
    mask = 1
    while mask < lax.axis_size(axis):
        value = value + swap(value, axis, mask)
        mask *= 2
    return value


def pad_lanes(value, width):
    return jnp.pad(value, ((0, 0), (0, width - value.shape[1])))


def pad_rows(rows, count=8):
    stacked = jnp.concatenate([r.reshape(-1, r.shape[-1]).astype(F32) for r in rows], axis=0)
    return jnp.pad(stacked, ((0, count - stacked.shape[0]), (0, 0)))


def local(
    tokens,
    segments,
    norm_gain,
    w_zx,
    w_bc,
    w_dt,
    conv_x,
    conv_x_bias,
    conv_bc,
    conv_bc_bias,
    dt_bias,
    a_log,
    d_skip,
    gate_gain,
    w_out,
    cotangent,
):
    seqs, span, model = tokens.shape
    rows = seqs * span
    heads = d_skip.shape[0]
    own = heads * HEAD_DIM
    n_seq, n_head = lax.axis_size("seq"), lax.axis_size("head")
    me_head = lax.axis_index("head")
    me = lax.axis_index("seq").astype(jnp.int32).reshape(1)
    head_at = me_head.astype(jnp.int32).reshape(1)
    inner_total = own * n_head
    state = w_bc.shape[1] // 2
    half = state // 2
    wide = 2 * state
    share = model // n_head
    offset = me_head * share
    edge = conv_x.shape[0] - 1
    groups = n_seq // 2
    masks = [2 * m for m in range(groups)]
    _, width = chunk_grid(groups, half, own)

    tok_halo = shift(tokens[:, -8:], "seq", 1)
    seg_halo = shift(segments[:, -8:], "seq", 1)
    cot_full = lax.all_gather(cotangent, "head", axis=2, tiled=True)

    w_in = lax.optimization_barrier(jnp.transpose(w_zx, (1, 0, 2)))
    w_dt = pad_lanes(w_dt, LANES)
    w_small = jnp.concatenate([w_bc, w_dt], axis=1)
    seg_rows = jnp.concatenate([jnp.pad(seg_halo, ((0, 0), (LANES - 8, 0))), segments], axis=1)
    seg_rows = jnp.broadcast_to(seg_rows.astype(F32)[:, None], (seqs, 8, LANES + span))
    conv_x_w = pad_rows([conv_x, conv_x_bias])
    conv_bc_w = pad_rows([conv_bc, conv_bc_bias])
    head_rows = pad_lanes(pad_rows([dt_bias, jnp.exp(a_log)]), LANES)
    wide_rows = pad_rows([gate_gain, jnp.repeat(d_skip, HEAD_DIM)])
    expand = (
        jnp.arange(LANES)[:, None] == (jnp.arange(own) // HEAD_DIM)[None, :]
    ).astype(BF)

    seq = functools.partial(per_seq, seqs)

    def seq_of(values):
        return [seq(v.shape[1:]) for v in values]

    def whole_of(values):
        return [whole(v.shape) for v in values]

    w_x_spec = pl.BlockSpec((1, model, own), lambda s: (1, 0, 0))
    ins = (
        me, tokens, tok_halo, norm_gain.reshape(1, model), w_in, w_small, seg_rows, conv_x_w,
        conv_bc_w, head_rows, expand,
    )
    per = (
        shaped((seqs, span, model), BF),
        shaped((seqs, span, own), BF),
        shaped((seqs, span, wide), BF),
        shaped((seqs, EDGE, own), BF),
        shaped((seqs, EDGE, wide), BF),
        shaped((seqs, span, own), BF),
        shaped((seqs, span, wide), BF),
        shaped((seqs, span, own), BF),
        shaped((seqs, span, LANES), F32),
        shaped((seqs, span, LANES), F32),
        shaped((seqs, span, LANES), F32),
    )
    packed = (shaped((seqs * half + ROWS, own), BF),) * 2
    normed, pre_x, pre_bc, halo_x, halo_bc, x_ssm, bc_ssm, xs, dt_raw, cum, aux, keep, send = call(
        functools.partial(front_kernel, state),
        seqs,
        ins,
        [SMEM_SPEC, *seq_of(ins[1:3]), whole(ins[3].shape), w_x_spec, whole(w_small.shape)]
        + seq_of(ins[6:7])
        + whole_of(ins[7:]),
        per + packed,
        seq_of(per) + whole_of(packed),
        [],
        30,
        "front",
    )

    def small_call(body, ins, outs, blocks, name):
        return call(
            body,
            1,
            ins,
            [SMEM_SPEC] + whole_of(ins[1:]),
            outs,
            whole_of(outs),
            [pltpu.VMEM((groups, blocks, ROWS, width), BF)],
            3,
            name,
        )

    piece = shaped((seqs, ROWS, width), BF)
    halves_out = (shaped((seqs, half, own), BF),) * 2
    other = swap(send, "seq", 1)
    *parts, pair_decay = small_call(
        functools.partial(pair_kernel, seqs, groups, half),
        (me, keep, other),
        (shaped((seqs + 1, ROWS, width), BF),) * groups + (shaped((16, own), F32),),
        seqs + 1,
        "pair",
    )
    *entries, decays = small_call(
        functools.partial(scan_kernel, seqs, groups),
        (me, *exchange(parts, masks)),
        (piece,) * groups + (shaped((groups, 8, width), F32),),
        seqs + 1,
        "scan",
    )
    state_mine, state_send = small_call(
        functools.partial(unpair_kernel, seqs, groups, half, True),
        (me, keep, other, pair_decay, *exchange(entries, masks)),
        halves_out,
        seqs,
        "unpair",
    )
    state_other = swap(state_send, "seq", 1)

    gate = dot(normed, w_in[0], ((2,), (0,))).astype(BF)
    e_raw = dot(cot_full, w_out, ((2,), (0,))).astype(BF)
    ins = (bc_ssm, xs, cum, aux, seg_rows)
    (inner,) = call(
        functools.partial(inner_kernel, state),
        seqs,
        ins,
        seq_of(ins),
        (shaped((seqs, span, own), F32),),
        [seq((span, own))],
        [],
        10.3,
        "inner",
    )

    mixer = (me, x_ssm, bc_ssm, inner, gate, e_raw, cum, aux, state_mine, state_other, wide_rows, expand)
    mixer_specs = [SMEM_SPEC] + seq_of(mixer[1:10]) + whole_of(mixer[10:])
    (sums,) = call(
        functools.partial(sums_kernel, state),
        seqs,
        mixer,
        mixer_specs,
        (shaped((seqs, 8, span), F32),),
        [seq((8, span))],
        [],
        12,
        "sums",
    )
    sums = sum_all(sums, "head")

    per = (
        shaped((seqs, span, own), BF),
        shaped((seqs, span, own), BF),
        shaped((seqs, span, own), BF),
        shaped((seqs, span, LANES), F32),
        shaped((seqs, span, state), F32),
        shaped((seqs, 8, span), F32),
    )
    fixed = (shaped((8, own), F32),) + (shaped((seqs * half, own), BF),) * 2
    scaled, d_z, d_y, mixed, d_c, dot_z, gate_grads, keep, send = call(
        functools.partial(gate_back_kernel, state, inner_total),
        seqs,
        (*mixer, sums),
        mixer_specs + [seq((8, span))],
        per + fixed,
        seq_of(per) + whole_of(fixed),
        [],
        21,
        "gate_back",
    )

    other = swap(send, "seq", 1)

    ins = (x_ssm, bc_ssm, xs, d_y, d_c, cum, dt_raw, aux, seg_rows, wide_rows, head_rows, expand)
    per = (
        shaped((seqs, span, own), BF),
        shaped((seqs, span, LANES), F32),
        shaped((seqs, span, wide), F32),
    )
    d_x, d_step, d_bc = call(
        functools.partial(inner_back_kernel, state),
        seqs,
        ins,
        seq_of(ins[:9]) + whole_of(ins[9:]),
        per,
        seq_of(per),
        [],
        18.6,
        "inner_back",
    )

    normed_rows = normed.reshape(rows, model)

    def chunk_sides(left, values, pieces, natural=False):
        tile = model // n_seq
        block = values.shape[1] // pieces
        if tile % LANES:
            full = dot(left, values, ((0,), (0,))).astype(BF)
            cuts = [full[:, at * block : (at + 1) * block] for at in range(pieces)]
            if natural:
                return [pair_sides(c) for c in cuts]
            return [row_sides(c, "seq") for c in cuts]
        sides = []
        for parity in (1, 0):
            if sides:
                values = after(values, sides[0][0])
            sides.append(
                pl.pallas_call(
                    gram_chunk_kernel,
                    grid_spec=pltpu.PrefetchScalarGridSpec(
                        num_scalar_prefetch=1,
                        grid=(groups,),
                        in_specs=[
                            pl.BlockSpec(
                                (rows, tile), lambda i, me_ref: (
                                    0,
                                    2 * i + ((parity + me_ref[0]) % 2)
                                    if natural
                                    else (2 * i + parity) ^ me_ref[0],
                                ),
                            ),
                            pl.BlockSpec(values.shape, lambda i, me_ref: (0, 0)),
                        ],
                        out_specs=[
                            pl.BlockSpec((1, tile, block), lambda i, me_ref: (i, 0, 0))
                        ] * pieces,
                    ),
                    out_shape=[shaped((groups, tile, block), BF)] * pieces,
                    name="gram_chunks",
                    compiler_params=pltpu.CompilerParams(vmem_limit_bytes=VMEM),
                    cost_estimate=pl.CostEstimate(
                        flops=rows * model * values.shape[1],
                        bytes_accessed=rows * (model + 2 * values.shape[1])
                        + model * values.shape[1],
                        transcendentals=0,
                    ),
                )(me, left, values)
            )
        return list(zip(*sides))

    def share_sum(terms, parity, summed):
        pairs = n_head // 2
        tall = rows
        def at(i, head_ref):
            return (2 * i + parity) ^ head_ref[0]

        ins, specs = [], []
        for lhs, rhs, first in terms:
            ins += [lhs, rhs]
            specs.append(pl.BlockSpec((tall, lhs.shape[1]), lambda i, s, head_ref: (s, 0)))
            if rhs.ndim == 3:
                specs.append(
                    pl.BlockSpec(
                        (1, share, rhs.shape[2]),
                        lambda i, s, head_ref, first=first: (first, at(i, head_ref), 0),
                    )
                )
            else:
                specs.append(
                    pl.BlockSpec(
                        (share, rhs.shape[1]), lambda i, s, head_ref: (at(i, head_ref), 0)
                    )
                )
        out_specs = [pl.BlockSpec((1, tall, share), lambda i, s, head_ref: (i, s, 0))]
        outs = [shaped((pairs, rows, share), BF)]
        if summed:
            ins.append(normed_rows)
            specs.append(
                pl.BlockSpec((tall, share), lambda i, s, head_ref: (s, at(i, head_ref)))
            )
            out_specs.append(pl.BlockSpec((1, 8, share), lambda i, s, head_ref: (i, 0, 0)))
            outs.append(shaped((pairs, 8, share), F32))
        depth = sum(t[0].shape[1] for t in terms)
        got = pl.pallas_call(
            functools.partial(share_kernel, len(terms), summed),
            grid_spec=pltpu.PrefetchScalarGridSpec(
                num_scalar_prefetch=1,
                grid=(pairs, rows // tall),
                in_specs=specs,
                out_specs=out_specs,
            ),
            out_shape=outs,
            name="shares",
            compiler_params=pltpu.CompilerParams(vmem_limit_bytes=VMEM),
            cost_estimate=cost(rows * model * depth / 5e8),
        )(head_at, *ins)
        return got if summed else got[0]

    scaled_rows, d_z_rows = scaled.reshape(rows, own), d_z.reshape(rows, own)
    parts = small_call(
        functools.partial(pair_back_kernel, seqs, groups, half),
        (me, after(keep, d_x), other, pair_decay),
        (piece,) * groups,
        seqs,
        "pair_back",
    )
    arrived = exchange(parts, masks)
    (out_grad,) = chunk_sides(cot_full.reshape(rows, model), after(scaled_rows, parts[0]), 1, True)
    out_total = pair_sum(out_grad)
    leaves = small_call(
        functools.partial(scan_back_kernel, seqs, groups),
        (me, after(decays, out_grad[1]), *arrived),
        (piece,) * groups,
        seqs,
        "scan_back",
    )
    arrived = exchange(leaves, masks)
    (gate_grad,) = chunk_sides(normed_rows, after(d_z_rows, leaves[0]), 1, True)
    end_mine, end_send = small_call(
        functools.partial(unpair_kernel, seqs, groups, half, False),
        (me, after(keep, gate_grad[1]), other, pair_decay, *arrived),
        halves_out,
        seqs,
        "unpair_back",
    )
    end_other = swap(end_send, "seq", 1)
    gate_total = pair_sum((after(gate_grad[0], end_other), gate_grad[1]))
    out_odd = share_sum([(after(scaled_rows, end_mine), w_out, 0)], 1, False)
    out_even = share_sum([(after(scaled_rows, out_odd), w_out, 0)], 0, False)

    ins = (
        me, after(x_ssm, out_even, out_total), bc_ssm, pre_x, halo_x, pre_bc, halo_bc, d_x, d_step, d_bc, mixed, cum,
        dt_raw, aux, dot_z, state_mine, state_other, end_mine, end_other, conv_x_w, conv_bc_w,
        head_rows, expand,
    )
    per = (
        shaped((seqs, span, own), BF),
        shaped((seqs, EDGE, own), BF),
        shaped((seqs, EDGE, wide), BF),
        shaped((seqs, span, wide), BF),
        shaped((seqs, span, LANES), BF),
        shaped((seqs, 8, span), F32),
    )
    fixed = (shaped((8, own), F32), shaped((8, LANES), F32))
    d_x_pre, back_x, back_bc, d_bc, d_dt, row_dot, conv_grads, head_grads = call(
        functools.partial(leave_kernel, state),
        seqs,
        ins,
        [SMEM_SPEC] + seq_of(ins[1:19]) + whole_of(ins[19:]),
        per + fixed,
        seq_of(per) + whole_of(fixed),
        [],
        28,
        "leave",
    )
    back = shift(jnp.concatenate([back_x, back_bc], axis=2)[:, -edge:], "seq", -1)
    back_x, back_bc = back[..., :own], back[..., own:]
    fix = jnp.sum(back_x.astype(F32) * pre_x[:, -edge:].astype(F32), axis=-1)
    row_dot = row_dot[:, 0] + jnp.pad(fix, ((0, 0), (span - edge, 0)))
    dot_high = row_dot.astype(BF)
    dot_low = (row_dot - dot_high.astype(F32)).astype(BF)
    dots = jnp.pad(jnp.stack([dot_high, dot_low], axis=1), ((0, 0), (0, EDGE - 2), (0, 0)))
    back_bc = jnp.pad(back_bc, ((0, 0), (EDGE - edge, 0), (0, 0)))
    d_bc = jnp.concatenate([d_bc, back_bc, dots], axis=1)
    d_bc = d_bc + swap(d_bc, "head", 1)
    d_x_pre = after(d_x_pre, d_bc, gate_total).at[:, -edge:].add(back_x)
    d_x_rows = d_x_pre.reshape(rows, own)
    d_dt_rows = d_dt.reshape(rows, LANES)
    (late_sides,) = chunk_sides(normed_rows, d_x_rows, 1, True)

    core, middle = me_head % 2, seqs // 2
    part = lax.dynamic_slice_in_dim(d_bc, core * middle, middle, 0)
    mask = 2
    while mask < n_head:
        part = part + swap(part, "head", mask)
        mask *= 2
    part = after(part, late_sides[1])
    part_other = swap(part, "head", 1)
    d_bc_all = jnp.where(
        core == 0,
        jnp.concatenate([part, part_other], axis=0),
        jnp.concatenate([part_other, part], axis=0),
    )
    ins = (d_bc_all, pre_bc, halo_bc, aux, conv_bc_w)
    per = (shaped((seqs, span, wide), BF), shaped((seqs, 8, span), F32))
    d_bc_pre, row_dot, bc_grads = call(
        conv_bc_kernel,
        seqs,
        ins,
        seq_of(ins[:4]) + whole_of(ins[4:]),
        per + (shaped((8, wide), F32),),
        seq_of(per) + [whole((8, wide))],
        [],
        6.3,
        "conv_bc",
    )
    d_small = jnp.concatenate([d_bc_pre.reshape(rows, wide), d_dt_rows], axis=-1)
    (small_sides,) = chunk_sides(normed_rows, d_small, 1)
    out_next = fold_step((out_odd, after(out_even, d_bc_pre)), "head", 1)
    terms = [(after(d_z_rows, small_sides[1], *out_next), w_in, 0), (d_x_rows, w_in, 1)]
    terms.append((d_dt_rows, w_dt, 0))
    grad_odd, norm_odd = share_sum(terms, 1, True)
    late_total = pair_sum((late_sides[0], after(late_sides[1], grad_odd)))
    terms[0] = (after(d_z_rows, late_total), w_in, 0)
    grad_even, norm_even = share_sum(terms, 0, True)
    grad_next = fold_step((grad_odd, grad_even), "head", 1)
    small_next = fold_step((small_sides[0], after(small_sides[1], *grad_next)), "seq", 1)
    out_next = out_next[0], after(out_next[1], *small_next)
    own_sum = fold(out_next, "head", 2).reshape(seqs, span, share)
    tokens_own = lax.dynamic_slice_in_dim(tokens, offset, share, 2).astype(F32)
    layer_out = (tokens_own + own_sum.astype(F32)).astype(BF)
    own_grad = fold(grad_next, "head", 2).reshape(seqs, span, share).astype(F32)
    late_s = fold(small_next, "seq", 2).astype(F32)
    out_grad_own = spread_sum(out_total).astype(F32)
    gate_grad_own = spread_sum(gate_total).astype(F32)
    late_a = spread_sum(late_total).astype(F32)

    row_dot = row_dot[:, 0]
    w_bc_own = lax.dynamic_slice_in_dim(w_bc, offset, share, 0)
    bc_term = dot(d_bc_pre, w_bc_own, ((2,), (1,)))
    rstd_in = aux[:, :, 6:7]
    unit_own = tokens_own * rstd_in
    gain_own = lax.dynamic_slice_in_dim(norm_gain, offset, share, 0)
    d_unit = (own_grad + bc_term) * gain_own
    input_grad = (
        rstd_in * (d_unit - unit_own * (row_dot / model)[..., None]) + cotangent.astype(F32)
    ).astype(BF)

    taps = edge + 1
    norm_part = jnp.concatenate([norm_even[:, 0], norm_odd[:, 0]], axis=0)
    norm_part = norm_part.at[0].add(gain_own * jnp.sum(bc_term * unit_own, axis=(0, 1)))
    small = (
        norm_part,
        conv_grads[:taps],
        conv_grads[taps],
        bc_grads[:taps],
        bc_grads[taps],
        head_grads[0, :heads],
        head_grads[1, :heads],
        jnp.sum(gate_grads[1].reshape(heads, HEAD_DIM), axis=-1),
        gate_grads[0],
    )
    flat = sum_all(jnp.concatenate([v.reshape(-1) for v in small]), "seq")
    summed, at = [], 0
    for v in small:
        summed.append(flat[at : at + v.size].reshape(v.shape))
        at += v.size
    norm_part = summed.pop(0)
    g_norm = fold((norm_part[n_head // 2 :], norm_part[: n_head // 2]), "head") / gain_own
    g_w_zx_own = jnp.stack([gate_grad_own, late_a], axis=1)
    return (
        layer_out,
        input_grad,
        g_norm,
        g_w_zx_own,
        late_s[:, :wide],
        late_s[:, wide : wide + heads],
        *summed,
        out_grad_own,
    )


def solution(mesh):
    placed = (
        P(None, "seq", None),
        P(None, "seq"),
        P(),
        P(None, None, "head"),
        P(),
        P(None, "head"),
        P(None, "head"),
        P("head"),
        P(),
        P(),
        P("head"),
        P("head"),
        P("head"),
        P("head"),
        P(None, "head"),
        P(None, "seq", "head"),
    )
    return jax.shard_map(
        local,
        mesh=mesh,
        in_specs=placed,
        out_specs=(
            P(None, "seq", "head"),
            P(None, "seq", "head"),
            P("head"),
            P("seq", None, "head"),
            P("seq", None),
            P("seq", "head"),
            P(None, "head"),
            P("head"),
            P(),
            P(),
            P("head"),
            P("head"),
            P("head"),
            P("head"),
            P("seq", "head"),
        ),
        check_vma=False,
    )
```

time: 641 us -> 552 us (0.86)
  Pallas kernels: 133 us -> 242 us
  matrix products: 105 us -> 23.8 us
  starting transfers between devices: 124 us -> 77.2 us
  local copies, waits for them, and re-layouts: 75.6 us -> 36.8 us
  waiting for transfers between devices: 123 us -> 99 us
  blocking collectives: 10.3 us -> 0 us
  other arithmetic: 45.8 us -> 53.1 us
    pallas_call x0 -> x12, Pallas kernels: none -> 97.1 us  [the longest x8 55.8 us: chunk_sides(): pl.pallas_call(gram_chunk_kernel, grid_spec=pltpu.PrefetchScalarGridSpec(...]
    dot_general x10 -> x3, matrix products: 105 us -> 23.8 us  [dot(): lax.dot_general(a, b, (contract, ((), ())), preferred_element_type=F32, p...]
    ppermute x49 -> x36, starting transfers between devices: 113 us -> 67.2 us  [swap(): return lax.ppermute(value, axis, [(i, i ^ mask) for i in range(count)])]
    ppermute x49 -> x36, waiting for transfers between devices: 116 us -> 89.7 us  [swap(): return lax.ppermute(value, axis, [(i, i ^ mask) for i in range(count)])]
    slice x12 -> x8, local copies, waits for them, and re-layouts: 25.1 us -> 3.4 us  [the longest x1 0.8 us: local(): row_dot = row_dot[:, 0] + jnp.pad(fix, ((0, 0), (span - edge, 0)))]
    add x11 -> x15, other arithmetic: 11.3 us -> 30.4 us  [the longest x3 10.8 us: pair_sum(): return sides[1] + swap(sides[0], 'seq', 1)]
    pallas_call x9 -> x13, Pallas kernels: 133 us -> 145 us  [call(): pl.pallas_call(body, grid=(grid,), in_specs=in_specs, out_specs=out_specs...]
    psum x1 -> x0, blocking collectives: 10.3 us -> none  [local(): sums = lax.psum(sums[:, :2], 'head')]
  transfers between devices with their start and end apart: 56 -> 43, of which waited for: 19 -> 20; matrix products, arithmetic and copies ran while one was open for 32% -> 18% of each run, Pallas kernels for 16% -> 36%
where the time goes in v2:
time: 552 us; the launch traced here: 546 us
  Pallas kernels  242 us (44%)
  waiting for transfers between devices  99 us (18%)
  starting transfers between devices  77.2 us (14%)
  other arithmetic  53.1 us (10%)
  local copies, waits for them, and re-layouts  36.8 us (7%)
  matrix products  23.8 us (4%)
  between operations  14.7 us (3%)
    pallas_call x13, Pallas kernels, call(): pl.pallas_call(body, grid=(grid,), in_specs=in_specs, out_specs=out_specs...  145 us
    ppermute x36, waiting for transfers between devices, swap(): return lax.ppermute(value, axis, [(i, i ^ mask) for i in range(count)])  89.7 us
    ppermute x36, starting transfers between devices, swap(): return lax.ppermute(value, axis, [(i, i ^ mask) for i in range(count)])  67.2 us
    pallas_call x8, Pallas kernels, chunk_sides(): pl.pallas_call(gram_chunk_kernel, grid_spec=pltpu.PrefetchScalarGridSpec(...  55.8 us
    pallas_call x4, Pallas kernels, share_sum(): pl.pallas_call(functools.partial(share_kernel, len(terms), summed), grid_...  41.3 us
    dot_general x3, matrix products, dot(): lax.dot_general(a, b, (contract, ((), ())), preferred_element_type=F32, p...  23.8 us
    unnamed x122, local copies, waits for them, and re-layouts  22 us
  transfers between devices with their start and end apart: 43, of which 20 were waited for; matrix products, arithmetic and copies ran while one was open for 18% of the time, Pallas kernels for 36%

profile of v2, /device:TPU:0, one launch (start us, length us, event | category | flops | bytes accessed | tf_op | source)
XLA Modules:
  0.0 546.4 jit_solution(11103784132810382381)
XLA Ops:
  8.7 4.8 collective-permute-start.1
  14.5 3.5 collective-permute-start
  18.1 10.4 %copy.72 = bf16[2048,2,1024]{2,0,1:T(8,128)(2,1)} copy(bf16[2048,2,1024]{2,1,0:T(2,128)(2,1)} %param.23) | data formatting | bytes 16777216 | tf_op args[3]
  33.7 30.4 %front.1 = (bf16[6,256,2048]{2,1,0:T(8,128)(2,1)}, bf16[6,256,1024]{2,1,0:T(8,128)(2,1)}, bf16[6,256,256]{2,1,0:T(8,128)(2,1)}, bf16[6,16,1024]{2,1,0:T(8,128)(2...) custom-call(s32[1]{0:T(128)} %bitcast.1.me_ref, ...), custom_call_target="tpu_custom_call" | custom-call | flops 34500001792 | bytes 1000 | tf_op jit(solution)/shard_map/front/pallas_call | solution.py:596
  66.4 17.3 %collective-permute-done.2.other_ref = bf16[400,1024]{1,0:T(8,128)(2,1)S(1)} collective-permute-done((bf16[400,1024]{1,0:T(8,128)(2,1)}, bf16[400,1024]{1,0:T(8,128)(2,1)S(1)}, u32[]{:S(2)}, u32[]{:S(2)}) %collective-permute-start.2) | collective-permute-done | bytes 819232 | tf_op jit(solution)/shard_map/ppermute | solution.py:616
  84.6 3.1 pair.1
  92.1 9.7 %fusion.15.gate_ref = bf16[6,256,1024]{2,1,0:T(8,128)(2,1)} fusion(bf16[6,256,2048]{2,1,0:T(8,128)(2,1)S(1)} %copy-done, bf16[2,2048,1024]{2,1,0:T(8,128)(2,1)} %bitcast.109), kind=kOutput, calls=%fused_computation.20 | convolution fusion | flops 6444023808 | bytes 13631488 | tf_op jit(solution)/shard_map/dot_general | solution.py:27
  101.8 6.4 %collective-permute-done.4.rest_2_ = bf16[7,16,1024]{2,1,0:T(8,128)(2,1)S(1)} collective-permute-done((bf16[7,16,1024]{2,1,0:T(8,128)(2,1)}, bf16[7,16,1024]{2,1,0:T(8,128)(2,1)S(1)}, u32[]{:S(2)}, u32[]{:S(2)}) %collective-permute-start.4) | collective-permute-done | bytes 229408 | tf_op jit(solution)/shard_map/ppermute | solution.py:616
  109.0 2.5 scan.1
  111.5 2.9 collective-permute-start.6
  117.0 10.4 %inner.1.inner_ref = f32[6,256,1024]{2,1,0:T(8,128)} custom-call(bf16[6,256,256]{2,1,0:T(8,128)(2,1)} %get-tuple-element.123.bc_ref, bf16[6,256,1024]{2,1,0:T(8,128)(2,1)} %get-tuple-element.124.xs_ref, f32[6,256,128]{2,1,0:T(8,128)} %get-tuple-element.125.cum_ref, f32[6,256,128]{2,1,0:T(8,128)} %get-tuple-element.126.aux_ref, ...), custom_call_target="tpu_custom_call" | custom-call | flops 11845000192 | bytes 1000 | tf_op jit(solution)/shard_map/inner/pallas_call | solution.py:596
  127.4 2.7 collective-permute-done.7.rest_2_
  130.9 3.6 unpair.1
  136.0 11.5 %fusion.12.e_ref = bf16[6,256,1024]{2,1,0:T(8,128)(2,1)} fusion(bf16[6,256,2048]{2,1,0:T(8,128)(2,1)} %all-gather.2.cloned.1.call-done, bf16[2048,1024]{1,0:T(8,128)(2,1)} %refs_1_.3), kind=kOutput, calls=%fused_computation.19 | convolution fusion | flops 6444023808 | bytes 13631488 | tf_op jit(solution)/shard_map/dot_general | solution.py:27
  147.5 2.0 collective-permute-done.9.other_ref
  150.4 11.9 %sums.1 = f32[6,8,256]{2,1,0:T(8,128)} custom-call(s32[1]{0:T(128)} %bitcast.1.me_ref, bf16[6,256,1024]{2,1,0:T(8,128)(2,1)} %get-tuple-element.168.x_ref, bf16[6,256,256]{2,1,0:T(8,128)(2,1)} %get-tuple-element.123.bc_ref, f32[6,256,1024]{2,1,0:T(8,128)} %inner.1.inner_ref, bf16[6,256,1024]{2,1,0:T(8,128)(2,1)} %fusion.15.gate_ref, ...), custom_call_target="tpu_custom_call" | custom-call | flops 13799999488 | bytes 1000 | tf_op jit(solution)/shard_map/sums/pallas_call | solution.py:596
  166.3 2.3 collective-permute-done.11
  169.2 20.8 %gate_back.1 = (bf16[6,256,1024]{2,1,0:T(8,128)(2,1)}, bf16[6,256,1024]{2,1,0:T(8,128)(2,1)}, bf16[6,256,1024]{2,1,0:T(8,128)(2,1)}, f32[6,256,128]{2,1,0:T(8,12...) custom-call(s32[1]{0:T(128)} %bitcast.1.me_ref, ...), custom_call_target="tpu_custom_call" | custom-call | flops 24149999616 | bytes 1000 | tf_op jit(solution)/shard_map/gate_back/pallas_call | solution.py:596
  191.6 18.6 %inner_back.1 = (bf16[6,256,1024]{2,1,0:T(8,128)(2,1)}, f32[6,256,128]{2,1,0:T(8,128)}, f32[6,256,256]{2,1,0:T(8,128)}) custom-call(bf16[6,256,1024]{2,1,0:T(8,128)(2,1)} %get-tuple-element.168.x_ref, bf16[6,256,256]{2,1,0:T(8,128)(2,1)} %get-tuple-element.123.bc_ref, bf16[6,256,1024]{2,1,0:T(8,128)(2,1)} %get-tuple-element.124.xs_ref, ...), custom_call_target="tpu_custom_call" | custom-call | flops 21390000128 | bytes 1000 | tf_op jit(solution)/shard_map/inner_back/pallas_call | solution.py:596
  211.1 2.8 pair_back.1
  214.0 7.5 %gram_chunks.8 = bf16[4,256,1024]{2,1,0:T(8,128)(2,1)} custom-call(s32[1]{0:T(128)} %bitcast.1.me_ref, bf16[1536,2048]{1,0:T(8,128)(2,1)} %bitcast.144, bf16[1536,1024]{1,0:T(8,128)(2,1)} %bitcast.150), custom_call_target="tpu_custom_call" | custom-call | flops 3221225472 | bytes 8388608 | tf_op jit(solution)/shard_map/gram_chunks/pallas_call | solution.py:918
  222.0 6.4 %collective-permute-start.13 = (bf16[6,16,1024]{2,1,0:T(8,128)(2,1)S(1)}, bf16[6,16,1024]{2,1,0:T(8,128)(2,1)S(1)}, u32[]{:S(2)}, u32[]{:S(2)}) collective-permute-start(bf16[6,16,1024]{2,1,0:T(8,128)(2,1)S(1)} %copy-done.50), channel_id=1, source_target_pairs={{0,8},{4,12},{8,0},{12,4},{16,24},{20,28},{24,16},{28,20},{1,9},{5... | collective-permute-start | bytes 589832 | tf_op jit(solution)/shard_map/ppermute | solution.py:616
  231.7 7.4 %gram_chunks.9 = bf16[4,256,1024]{2,1,0:T(8,128)(2,1)} custom-call(s32[1]{0:T(128)} %bitcast.1.me_ref, bf16[1536,2048]{1,0:T(8,128)(2,1)} %bitcast.145, bf16[1536,1024]{1,0:T(8,128)(2,1)} %bitcast.151), custom_call_target="tpu_custom_call" | custom-call | flops 3221225472 | bytes 8388608 | tf_op jit(solution)/shard_map/gram_chunks/pallas_call | solution.py:918
  239.1 5.7 %collective-permute-done.14.rest_2_ = bf16[6,16,1024]{2,1,0:T(8,128)(2,1)S(1)} collective-permute-done((bf16[6,16,1024]{2,1,0:T(8,128)(2,1)S(1)}, bf16[6,16,1024]{2,1,0:T(8,128)(2,1)S(1)}, u32[]{:S(2)}, u32[]{:S(2)}) %collective-permute-start.14) | collective-permute-done | bytes 196640 | tf_op jit(solution)/shard_map/ppermute | solution.py:616
  246.1 2.4 scan_back.1
  248.5 7.7 %gram_chunks.10 = bf16[4,256,1024]{2,1,0:T(8,128)(2,1)} custom-call(s32[1]{0:T(128)} %bitcast.1.me_ref, bf16[1536,2048]{1,0:T(8,128)(2,1)} %bitcast.97, bf16[1536,1024]{1,0:T(8,128)(2,1)} %bitcast.146), custom_call_target="tpu_custom_call" | custom-call | flops 3221225472 | bytes 8388608 | tf_op jit(solution)/shard_map/gram_chunks/pallas_call | solution.py:918
  261.5 7.4 %gram_chunks.11 = bf16[4,256,1024]{2,1,0:T(8,128)(2,1)} custom-call(s32[1]{0:T(128)} %bitcast.1.me_ref, bf16[1536,2048]{1,0:T(8,128)(2,1)} %bitcast.98, bf16[1536,1024]{1,0:T(8,128)(2,1)} %bitcast.147), custom_call_target="tpu_custom_call" | custom-call | flops 3221225472 | bytes 8388608 | tf_op jit(solution)/shard_map/gram_chunks/pallas_call | solution.py:918
  268.9 6.1 %collective-permute-done.17.rest_2_ = bf16[6,16,1024]{2,1,0:T(8,128)(2,1)S(1)} collective-permute-done((bf16[6,16,1024]{2,1,0:T(8,128)(2,1)S(1)}, bf16[6,16,1024]{2,1,0:T(8,128)(2,1)S(1)}, u32[]{:S(2)}, u32[]{:S(2)}) %collective-permute-start.17) | collective-permute-done | bytes 196640 | tf_op jit(solution)/shard_map/ppermute | solution.py:616
  276.4 3.6 unpair_back.1
  281.5 7.1 %shares.4 = bf16[2,1536,512]{2,1,0:T(8,128)(2,1)} custom-call(s32[1]{0:T(128)} %bitcast.me_ref, bf16[1536,1024]{1,0:T(8,128)(2,1)} %bitcast.152, bf16[2048,1024]{1,0:T(8,128)(2,1)} %refs_1_.3), custom_call_target="tpu_custom_call" | custom-call | flops 7408818688 | bytes 1000 | tf_op jit(solution)/shard_map/shares/pallas_call | solution.py:984
  288.5 7.2 %shares.5 = bf16[2,1536,512]{2,1,0:T(8,128)(2,1)} custom-call(s32[1]{0:T(128)} %bitcast.me_ref, bf16[1536,1024]{1,0:T(8,128)(2,1)} %bitcast.153, bf16[2048,1024]{1,0:T(8,128)(2,1)} %refs_1_.3), custom_call_target="tpu_custom_call" | custom-call | flops 7408818688 | bytes 1000 | tf_op jit(solution)/shard_map/shares/pallas_call | solution.py:984
  296.5 2.4 collective-permute-start.24
  298.9 2.3 add.148
  301.2 28.4 %leave.1 = (bf16[6,256,1024]{2,1,0:T(8,128)(2,1)}, bf16[6,16,1024]{2,1,0:T(8,128)(2,1)}, bf16[6,16,256]{2,1,0:T(8,128)(2,1)}, bf16[6,256,256]{2,1,0:T(8,128)(2,1...) custom-call(s32[1]{0:T(128)} %bitcast.1.me_ref, ...), custom_call_target="tpu_custom_call" | custom-call | flops 32199999488 | bytes 1000 | tf_op jit(solution)/shard_map/leave/pallas_call | solution.py:596
  332.8 8.6 %collective-permute-done.21 = bf16[6,3,1280]{2,1,0:T(4,128)(2,1)S(1)} collective-permute-done((bf16[6,3,1280]{2,1,0:T(4,128)(2,1)S(1)}, bf16[6,3,1280]{2,1,0:T(4,128)(2,1)S(1)}, u32[]{:S(2)}, u32[]{:S(2)}) %collective-permute-start.21) | collective-permute-done | bytes 46112 | tf_op jit(solution)/shard_map/ppermute | solution.py:622
  344.3 2.2 collective-permute-done.22
  348.6 4.6 add.153
  355.7 7.4 %gram_chunks.12 = bf16[4,256,1024]{2,1,0:T(8,128)(2,1)} custom-call(s32[1]{0:T(128)} %bitcast.1.me_ref, bf16[1536,2048]{1,0:T(8,128)(2,1)} %bitcast.99, bf16[1536,1024]{1,0:T(8,128)(2,1)} %bitcast.138), custom_call_target="tpu_custom_call" | custom-call | flops 3221225472 | bytes 8388608 | tf_op jit(solution)/shard_map/gram_chunks/pallas_call | solution.py:918
  363.2 7.4 %gram_chunks.13 = bf16[4,256,1024]{2,1,0:T(8,128)(2,1)} custom-call(s32[1]{0:T(128)} %bitcast.1.me_ref, bf16[1536,2048]{1,0:T(8,128)(2,1)} %bitcast.100, bf16[1536,1024]{1,0:T(8,128)(2,1)} %bitcast.139), custom_call_target="tpu_custom_call" | custom-call | flops 3221225472 | bytes 8388608 | tf_op jit(solution)/shard_map/gram_chunks/pallas_call | solution.py:918
  373.5 6.3 %conv_bc.1 = (bf16[6,256,256]{2,1,0:T(8,128)(2,1)}, f32[6,8,256]{2,1,0:T(8,128)}, f32[8,256]{1,0:T(8,128)}) custom-call(bf16[6,288,256]{2,1,0:T(8,128)(2,1)} %maximum_select_fusion.d_ref, bf16[6,256,256]{2,1,0:T(8,128)(2,1)} %get-tuple-element.171.pre_bc_ref.pre_ref, bf16[6,16,256]{2,1,0:T(8,128)(2,1)} %get-tuple-element.172.halo_bc_ref.halo_ref, ...), custom_call_target="tpu_custom_call" | custom-call | flops 7245000192 | bytes 1000 | tf_op jit(solution)/shard_map/conv_bc/pallas_call | solution.py:596
  379.9 2.3 pad_maximum_fusion.1.b_ref
  382.1 5.4 gram_chunks.14
  387.5 5.5 %gram_chunks.15 = bf16[4,256,384]{2,1,0:T(8,128)(2,1)} custom-call(s32[1]{0:T(128)} %bitcast.1.me_ref, bf16[1536,2048]{1,0:T(8,128)(2,1)} %bitcast.102, bf16[1536,384]{1,0:T(8,128)(2,1)} %pad_maximum_fusion.1.b_ref), custom_call_target="tpu_custom_call" | custom-call | flops 1207959552 | bytes 5111808 | tf_op jit(solution)/shard_map/gram_chunks/pallas_call | solution.py:918
  393.0 4.0 slice_add_fusion.2
  397.0 13.6 %shares.6 = (bf16[2,1536,512]{2,1,0:T(8,128)(2,1)}, f32[2,8,512]{2,1,0:T(8,128)}) custom-call(s32[1]{0:T(128)} %bitcast.me_ref, bf16[1536,1024]{1,0:T(8,128)(2,1)} %bitcast.148, bf16[2,2048,1024]{2,1,0:T(8,128)(2,1)} %bitcast.110, bf16[1536,1024]{1,0:T(8,128)(2,1)} %bitcast.140, bf16[2,2048,1024]{2,1,0:T(8,128)(2,1)} %bitcast.111, ...), custom_call_target="tpu_custom_call" | custom-call | flops 15743739904 | bytes 1000 | tf_op jit(solution)/shard_map/shares/pallas_call | solution.py:984
  413.2 2.5 fusion.9
  415.7 3.3 collective-permute-done.27
  419.1 3.9 add.157
  423.0 13.4 %shares.7 = (bf16[2,1536,512]{2,1,0:T(8,128)(2,1)}, f32[2,8,512]{2,1,0:T(8,128)}) custom-call(s32[1]{0:T(128)} %bitcast.me_ref, bf16[1536,1024]{1,0:T(8,128)(2,1)} %bitcast.149, bf16[2,2048,1024]{2,1,0:T(8,128)(2,1)} %bitcast.112, bf16[1536,1024]{1,0:T(8,128)(2,1)} %bitcast.141, bf16[2,2048,1024]{2,1,0:T(8,128)(2,1)} %bitcast.113, ...), custom_call_target="tpu_custom_call" | custom-call | flops 15743739904 | bytes 1000 | tf_op jit(solution)/shard_map/shares/pallas_call | solution.py:984
  436.5 3.2 slice_add_fusion.1
  444.4 3.0 collective-permute-done.32
  447.4 5.7 %collective-permute-start.33 = (f32[9520]{0:T(1024)S(1)}, f32[9520]{0:T(1024)S(1)}, u32[]{:S(2)}, u32[]{:S(2)}) collective-permute-start(f32[9520]{0:T(1024)S(1)} %add.169), channel_id=1, source_target_pairs={{0,8},{4,12},{8,0},{12,4},{16,24},{20,28},{24,16},{28,20},{1,9},{5... | collective-permute-start | bytes 114248 | tf_op jit(solution)/shard_map/ppermute | solution.py:616
  456.9 3.6 collective-permute-start.34
  461.8 3.4 collective-permute-done.34
  469.4 7.9 %collective-permute-done.31 = bf16[1,1536,512]{2,1,0:T(8,128)(2,1)} collective-permute-done((bf16[1,1536,512]{2,1,0:T(8,128)(2,1)}, bf16[1,1536,512]{2,1,0:T(8,128)(2,1)}, u32[]{:S(2)}, u32[]{:S(2)}) %collective-permute-start.31) | collective-permute-done | bytes 1572896 | tf_op jit(solution)/shard_map/ppermute | solution.py:616
  477.3 3.7 fusion.40
  483.0 5.8 %collective-permute-start.37 = (bf16[2,256,384]{2,1,0:T(8,128)(2,1)}, bf16[2,256,384]{2,1,0:T(8,128)(2,1)}, u32[]{:S(2)}, u32[]{:S(2)}) collective-permute-start(bf16[2,256,384]{2,1,0:T(8,128)(2,1)} %get-tuple-element.259), channel_id=1, source_target_pairs={{0,8},{4,12},{8,0},{12,4},{16,24},{20,28},{24,16},{28,20},{1,9},{5... | collective-permute-start | bytes 1179656 | tf_op jit(solution)/shard_map/ppermute | solution.py:616
  491.9 17.9 %collective-permute-done.36 = f32[1,512]{1,0:T(1,128)} collective-permute-done((f32[1,512]{1,0:T(1,128)}, f32[1,512]{1,0:T(1,128)}, u32[]{:S(2)}, u32[]{:S(2)}) %collective-permute-start.36) | collective-permute-done | bytes 2080 | tf_op jit(solution)/shard_map/ppermute | solution.py:616
  511.6 2.2 convert_element_type.111
  513.9 2.0 add.162
  516.9 7.9 %collective-permute-start.38 = (bf16[1,256,384]{2,1,0:T(8,128)(2,1)S(1)}, bf16[1,256,384]{2,1,0:T(8,128)(2,1)S(1)}, u32[]{:S(2)}, u32[]{:S(2)}) collective-permute-start(bf16[1,256,384]{2,1,0:T(8,128)(2,1)S(1)} %slice_add_fusion.6), channel_id=1, source_target_pairs={{0,16},{4,20},{8,24},{12,28},{16,0},{20,4},{24,8},{28,12},{1,17},{... | collective-permute-start | bytes 589832 | tf_op jit(solution)/shard_map/ppermute | solution.py:616
  524.9 3.8 fusion.8
  528.7 4.3 collective-permute-done.38
  536.6 2.9 copy.49
  (256 shorter events, 84.8 us)
Async XLA Ops:
  7.2 128.8 %all-gather.2.cloned.1.call-start = ((), (), s32[]{:S(2)}) async-start(), calls=%async_computation.3 | async-start | bytes 7864320 | tf_op jit(solution)/shard_map/all_gather | solution.py:736
  7.9 503.7 %reduce-scatter.8.cloned.1.call-start = ((), (), s32[]{:S(2)}) async-start(), calls=%async_computation.6 | async-start | bytes 2621440 | tf_op jit(solution)/shard_map/reduce_scatter | solution.py:660
  8.7 24.2 %collective-permute-start.1 = (s32[6,8]{1,0:T(8,128)S(1)}, s32[6,8]{1,0:T(8,128)S(1)}, u32[]{:S(2)}, u32[]{:S(2)}) collective-permute-start(s32[6,8]{1,0:T(8,128)S(1)} %slice.232), channel_id=1, source_target_pairs={{0,4},{4,8},{8,12},{12,16},{16,20},{20,24},{24,28},{1,5},{5,9},{9,... | collective-permute-start | bytes 584 | tf_op jit(solution)/shard_map/ppermute | solution.py:622
  14.5 18.5 %collective-permute-start = (bf16[6,8,2048]{2,1,0:T(8,128)(2,1)S(1)}, bf16[6,8,2048]{2,1,0:T(8,128)(2,1)S(1)}, u32[]{:S(2)}, u32[]{:S(2)}) collective-permute-start(bf16[6,8,2048]{2,1,0:T(8,128)(2,1)S(1)} %slice.231), channel_id=1, source_target_pairs={{0,4},{4,8},{8,12},{12,16},{16,20},{20,24},{24,28},{1,5},{5,9},{9,... | collective-permute-start | bytes 589832 | tf_op jit(solution)/shard_map/ppermute | solution.py:622
  18.0 10.5 %copy-start.17 = (bf16[2048,16]{0,1:T(8,128)(2,1)S(1)}, bf16[2048,16]{0,1:T(8,128)(2,1)}, u32[]{:S(2)}) copy-start(bf16[2048,16]{0,1:T(8,128)(2,1)} %param.25) | copy-start | bytes 196612
  18.0 10.9 %copy-start.25 = (f32[4,256]{1,0:T(4,128)S(1)}, f32[4,256]{1,0:T(4,128)}, u32[]{:S(2)}) copy-start(f32[4,256]{1,0:T(4,128)} %param.28) | copy-start | bytes 12292
  18.0 10.9 %copy-start.29 = (f32[256]{0:T(256)S(1)}, f32[256]{0:T(256)}, u32[]{:S(2)}) copy-start(f32[256]{0:T(256)} %param.29) | copy-start | bytes 3076
  18.0 11.6 %copy-start.22 = (f32[4,1024]{1,0:T(4,128)S(1)}, f32[4,1024]{1,0:T(4,128)}, u32[]{:S(2)}) copy-start(f32[4,1024]{1,0:T(4,128)} %param.26) | copy-start | bytes 49156
  18.0 11.6 %copy-start.27 = (f32[1024]{0:T(1024)S(1)}, f32[1024]{0:T(1024)}, u32[]{:S(2)}) copy-start(f32[1024]{0:T(1024)} %param.27) | copy-start | bytes 12292
  18.0 12.2 %copy-start.55 = (f32[16]{0:T(128)S(1)}, f32[16]{0:T(128)}, u32[]{:S(2)}) copy-start(f32[16]{0:T(128)} %param.31) | copy-start | bytes 196
  33.7 31.9 %copy-start.31 = (f32[16]{0:T(128)S(1)}, f32[16]{0:T(128)}, u32[]{:S(2)}) copy-start(f32[16]{0:T(128)} %param.32) | copy-start | bytes 196
  33.7 32.1 %copy-start.24 = (f32[1024]{0:T(1024)S(1)}, f32[1024]{0:T(1024)}, u32[]{:S(2)}) copy-start(f32[1024]{0:T(1024)} %param.33) | copy-start | bytes 12292
  64.1 19.7 %collective-permute-start.2 = (bf16[400,1024]{1,0:T(8,128)(2,1)}, bf16[400,1024]{1,0:T(8,128)(2,1)S(1)}, u32[]{:S(2)}, u32[]{:S(2)}) collective-permute-start(bf16[400,1024]{1,0:T(8,128)(2,1)} %get-tuple-element.129), channel_id=1, source_target_pairs={{0,4},{4,0},{8,12},{12,8},{16,20},{20,16},{24,28},{28,24},{1,5},{5... | collective-permute-start | bytes 2457608 | tf_op jit(solution)/shard_map/ppermute | solution.py:616
  87.8 14.1 %collective-permute-start.3 = (bf16[7,16,1024]{2,1,0:T(8,128)(2,1)}, bf16[7,16,1024]{2,1,0:T(8,128)(2,1)S(1)}, u32[]{:S(2)}, u32[]{:S(2)}) collective-permute-start(bf16[7,16,1024]{2,1,0:T(8,128)(2,1)} %get-tuple-element.132), channel_id=1, source_target_pairs={{0,8},{4,12},{8,0},{12,4},{16,24},{20,28},{24,16},{28,20},{1,9},{5... | collective-permute-start | bytes 688136 | tf_op jit(solution)/shard_map/ppermute | solution.py:616
  89.3 18.9 %collective-permute-start.4 = (bf16[7,16,1024]{2,1,0:T(8,128)(2,1)}, bf16[7,16,1024]{2,1,0:T(8,128)(2,1)S(1)}, u32[]{:S(2)}, u32[]{:S(2)}) collective-permute-start(bf16[7,16,1024]{2,1,0:T(8,128)(2,1)} %get-tuple-element.133), channel_id=1, source_target_pairs={{0,16},{4,20},{8,24},{12,28},{16,0},{20,4},{24,8},{28,12},{1,17},{... | collective-permute-start | bytes 688136 | tf_op jit(solution)/shard_map/ppermute | solution.py:616
  90.3 17.9 %collective-permute-start.5 = (bf16[7,16,1024]{2,1,0:T(8,128)(2,1)}, bf16[7,16,1024]{2,1,0:T(8,128)(2,1)S(1)}, u32[]{:S(2)}, u32[]{:S(2)}) collective-permute-start(bf16[7,16,1024]{2,1,0:T(8,128)(2,1)} %get-tuple-element.134), channel_id=1, source_target_pairs={{0,24},{4,28},{8,16},{12,20},{16,8},{20,12},{24,0},{28,4},{1,25},{... | collective-permute-start | bytes 688136 | tf_op jit(solution)/shard_map/ppermute | solution.py:616
  111.5 15.8 %collective-permute-start.6 = (bf16[6,16,1024]{2,1,0:T(8,128)(2,1)}, bf16[6,16,1024]{2,1,0:T(8,128)(2,1)S(1)}, u32[]{:S(2)}, u32[]{:S(2)}) collective-permute-start(bf16[6,16,1024]{2,1,0:T(8,128)(2,1)} %get-tuple-element.136), channel_id=1, source_target_pairs={{0,8},{4,12},{8,0},{12,4},{16,24},{20,28},{24,16},{28,20},{1,9},{5... | collective-permute-start | bytes 589832 | tf_op jit(solution)/shard_map/ppermute | solution.py:616
  114.4 15.6 %collective-permute-start.7 = (bf16[6,16,1024]{2,1,0:T(8,128)(2,1)}, bf16[6,16,1024]{2,1,0:T(8,128)(2,1)S(1)}, u32[]{:S(2)}, u32[]{:S(2)}) collective-permute-start(bf16[6,16,1024]{2,1,0:T(8,128)(2,1)} %get-tuple-element.137), channel_id=1, source_target_pairs={{0,16},{4,20},{8,24},{12,28},{16,0},{20,4},{24,8},{28,12},{1,17},{... | collective-permute-start | bytes 589832 | tf_op jit(solution)/shard_map/ppermute | solution.py:616
  115.5 14.6 %collective-permute-start.8 = (bf16[6,16,1024]{2,1,0:T(8,128)(2,1)}, bf16[6,16,1024]{2,1,0:T(8,128)(2,1)S(1)}, u32[]{:S(2)}, u32[]{:S(2)}) collective-permute-start(bf16[6,16,1024]{2,1,0:T(8,128)(2,1)} %get-tuple-element.138), channel_id=1, source_target_pairs={{0,24},{4,28},{8,16},{12,20},{16,8},{20,12},{24,0},{28,4},{1,25},{... | collective-permute-start | bytes 589832 | tf_op jit(solution)/shard_map/ppermute | solution.py:616
  134.4 15.1 %collective-permute-start.9 = (bf16[6,64,1024]{2,1,0:T(8,128)(2,1)}, bf16[6,64,1024]{2,1,0:T(8,128)(2,1)S(1)}, u32[]{:S(2)}, u32[]{:S(2)}) collective-permute-start(bf16[6,64,1024]{2,1,0:T(8,128)(2,1)} %get-tuple-element.140), channel_id=1, source_target_pairs={{0,4},{4,0},{8,12},{12,8},{16,20},{20,16},{24,28},{28,24},{1,5},{5... | collective-permute-start | bytes 2359304 | tf_op jit(solution)/shard_map/ppermute | solution.py:616
  162.3 1.4 collective-permute-start.10
  164.5 4.1 collective-permute-start.11
  190.0 20.2 %collective-permute-start.12 = (bf16[384,1024]{1,0:T(8,128)(2,1)}, bf16[384,1024]{1,0:T(8,128)(2,1)S(1)}, u32[]{:S(2)}, u32[]{:S(2)}) collective-permute-start(bf16[384,1024]{1,0:T(8,128)(2,1)} %get-tuple-element.150), channel_id=1, source_target_pairs={{0,4},{4,0},{8,12},{12,8},{16,20},{20,16},{24,28},{28,24},{1,5},{5... | collective-permute-start | bytes 2359304 | tf_op jit(solution)/shard_map/ppermute | solution.py:616
  213.9 14.4 %copy-start.46 = (bf16[6,16,1024]{2,1,0:T(8,128)(2,1)S(1)}, bf16[6,16,1024]{2,1,0:T(8,128)(2,1)}, u32[]{:S(2)}) copy-start(bf16[6,16,1024]{2,1,0:T(8,128)(2,1)} %get-tuple-element.156) | copy-start | bytes 589828
  213.9 16.2 %copy-start.41 = (bf16[6,16,1024]{2,1,0:T(8,128)(2,1)S(1)}, bf16[6,16,1024]{2,1,0:T(8,128)(2,1)}, u32[]{:S(2)}) copy-start(bf16[6,16,1024]{2,1,0:T(8,128)(2,1)} %get-tuple-element.157) | copy-start | bytes 589828
  221.5 77.4 %collective-permute-start.19 = (bf16[4,256,1024]{2,1,0:T(8,128)(2,1)}, bf16[4,256,1024]{2,1,0:T(8,128)(2,1)S(1)}, u32[]{:S(2)}, u32[]{:S(2)}) collective-permute-start(bf16[4,256,1024]{2,1,0:T(8,128)(2,1)} %gram_chunks.8), channel_id=1, source_target_pairs={{0,4},{4,0},{8,12},{12,8},{16,20},{20,16},{24,28},{28,24},{1,5},{5... | collective-permute-start | bytes 6291464 | tf_op jit(solution)/shard_map/ppermute | solution.py:616
  222.0 17.1 %collective-permute-start.13 = (bf16[6,16,1024]{2,1,0:T(8,128)(2,1)S(1)}, bf16[6,16,1024]{2,1,0:T(8,128)(2,1)S(1)}, u32[]{:S(2)}, u32[]{:S(2)}) collective-permute-start(bf16[6,16,1024]{2,1,0:T(8,128)(2,1)S(1)} %copy-done.50), channel_id=1, source_target_pairs={{0,8},{4,12},{8,0},{12,4},{16,24},{20,28},{24,16},{28,20},{1,9},{5... | collective-permute-start | bytes 589832 | tf_op jit(solution)/shard_map/ppermute | solution.py:616
  228.3 16.4 %collective-permute-start.14 = (bf16[6,16,1024]{2,1,0:T(8,128)(2,1)S(1)}, bf16[6,16,1024]{2,1,0:T(8,128)(2,1)S(1)}, u32[]{:S(2)}, u32[]{:S(2)}) collective-permute-start(bf16[6,16,1024]{2,1,0:T(8,128)(2,1)S(1)} %copy-done.46), channel_id=1, source_target_pairs={{0,16},{4,20},{8,24},{12,28},{16,0},{20,4},{24,8},{28,12},{1,17},{... | collective-permute-start | bytes 589832 | tf_op jit(solution)/shard_map/ppermute | solution.py:616
  230.2 14.6 %collective-permute-start.15 = (bf16[6,16,1024]{2,1,0:T(8,128)(2,1)S(1)}, bf16[6,16,1024]{2,1,0:T(8,128)(2,1)S(1)}, u32[]{:S(2)}, u32[]{:S(2)}) collective-permute-start(bf16[6,16,1024]{2,1,0:T(8,128)(2,1)S(1)} %copy-done.41), channel_id=1, source_target_pairs={{0,24},{4,28},{8,16},{12,20},{16,8},{20,12},{24,0},{28,4},{1,25},{... | collective-permute-start | bytes 589832 | tf_op jit(solution)/shard_map/ppermute | solution.py:616
  248.5 11.5 %copy-start.42 = (bf16[6,16,1024]{2,1,0:T(8,128)(2,1)S(1)}, bf16[6,16,1024]{2,1,0:T(8,128)(2,1)}, u32[]{:S(2)}) copy-start(bf16[6,16,1024]{2,1,0:T(8,128)(2,1)} %get-tuple-element.164) | copy-start | bytes 589828
  256.2 12.7 %collective-permute-start.16 = (bf16[6,16,1024]{2,1,0:T(8,128)(2,1)S(1)}, bf16[6,16,1024]{2,1,0:T(8,128)(2,1)S(1)}, u32[]{:S(2)}, u32[]{:S(2)}) collective-permute-start(bf16[6,16,1024]{2,1,0:T(8,128)(2,1)S(1)} %copy-done.52), channel_id=1, source_target_pairs={{0,8},{4,12},{8,0},{12,4},{16,24},{20,28},{24,16},{28,20},{1,9},{5... | collective-permute-start | bytes 589832 | tf_op jit(solution)/shard_map/ppermute | solution.py:616
  258.2 16.8 %collective-permute-start.17 = (bf16[6,16,1024]{2,1,0:T(8,128)(2,1)S(1)}, bf16[6,16,1024]{2,1,0:T(8,128)(2,1)S(1)}, u32[]{:S(2)}, u32[]{:S(2)}) collective-permute-start(bf16[6,16,1024]{2,1,0:T(8,128)(2,1)S(1)} %copy-done.47), channel_id=1, source_target_pairs={{0,16},{4,20},{8,24},{12,28},{16,0},{20,4},{24,8},{28,12},{1,17},{... | collective-permute-start | bytes 589832 | tf_op jit(solution)/shard_map/ppermute | solution.py:616
  260.1 15.0 %collective-permute-start.18 = (bf16[6,16,1024]{2,1,0:T(8,128)(2,1)S(1)}, bf16[6,16,1024]{2,1,0:T(8,128)(2,1)S(1)}, u32[]{:S(2)}, u32[]{:S(2)}) collective-permute-start(bf16[6,16,1024]{2,1,0:T(8,128)(2,1)S(1)} %copy-done.42), channel_id=1, source_target_pairs={{0,24},{4,28},{8,16},{12,20},{16,8},{20,12},{24,0},{28,4},{1,25},{... | collective-permute-start | bytes 589832 | tf_op jit(solution)/shard_map/ppermute | solution.py:616
  280.0 16.5 %collective-permute-start.20 = (bf16[6,64,1024]{2,1,0:T(8,128)(2,1)}, bf16[6,64,1024]{2,1,0:T(8,128)(2,1)S(1)}, u32[]{:S(2)}, u32[]{:S(2)}) collective-permute-start(bf16[6,64,1024]{2,1,0:T(8,128)(2,1)} %get-tuple-element.177), channel_id=1, source_target_pairs={{0,4},{4,0},{8,12},{12,8},{16,20},{20,16},{24,28},{28,24},{1,5},{5... | collective-permute-start | bytes 2359304 | tf_op jit(solution)/shard_map/ppermute | solution.py:616
  296.5 52.1 %collective-permute-start.24 = (bf16[4,256,1024]{2,1,0:T(8,128)(2,1)}, bf16[4,256,1024]{2,1,0:T(8,128)(2,1)}, u32[]{:S(2)}, u32[]{:S(2)}) collective-permute-start(bf16[4,256,1024]{2,1,0:T(8,128)(2,1)} %gram_chunks.10), channel_id=1, source_target_pairs={{0,4},{4,0},{8,12},{12,8},{16,20},{20,16},{24,28},{28,24},{1,5},{5... | collective-permute-start | bytes 6291464 | tf_op jit(solution)/shard_map/ppermute | solution.py:616
  301.2 234.1 %reduce-scatter.4.cloned.1.call-start = ((), (), s32[]{:S(2)}) async-start(), calls=%async_computation.4 | async-start | bytes 2621440 | tf_op jit(solution)/shard_map/reduce_scatter | solution.py:660
  329.7 16.9 %copy-start.5 = (bf16[6,256,256]{2,1,0:T(8,128)(2,1)S(1)}, bf16[6,256,256]{2,1,0:T(8,128)(2,1)}, u32[]{:S(2)}) copy-start(bf16[6,256,256]{2,1,0:T(8,128)(2,1)} %get-tuple-element.178) | copy-start | bytes 2359300
  330.7 10.7 %collective-permute-start.21 = (bf16[6,3,1280]{2,1,0:T(4,128)(2,1)S(1)}, bf16[6,3,1280]{2,1,0:T(4,128)(2,1)S(1)}, u32[]{:S(2)}, u32[]{:S(2)}) collective-permute-start(bf16[6,3,1280]{2,1,0:T(4,128)(2,1)S(1)} %pad_maximum_fusion.2), channel_id=1, source_target_pairs={{4,0},{8,4},{12,8},{16,12},{20,16},{24,20},{28,24},{5,1},{9,5},{13... | collective-permute-start | bytes 138248 | tf_op jit(solution)/shard_map/ppermute | solution.py:622
  343.8 2.8 collective-permute-start.22
  343.9 49.2 %collective-permute-start.26 = (bf16[2,1536,512]{2,1,0:T(8,128)(2,1)}, bf16[2,1536,512]{2,1,0:T(8,128)(2,1)}, u32[]{:S(2)}, u32[]{:S(2)}) collective-permute-start(bf16[2,1536,512]{2,1,0:T(8,128)(2,1)} %shares.4), channel_id=1, source_target_pairs={{0,1},{1,0},{2,3},{3,2},{4,5},{5,4},{6,7},{7,6},{8,9},{9,8},{10,11... | collective-permute-start | bytes 9437192 | tf_op jit(solution)/shard_map/ppermute | solution.py:616
  346.8 23.7 %collective-permute-start.23 = (bf16[3,288,256]{2,1,0:T(8,128)(2,1)S(1)}, bf16[3,288,256]{2,1,0:T(8,128)(2,1)S(1)}, u32[]{:S(2)}, u32[]{:S(2)}) collective-permute-start(bf16[3,288,256]{2,1,0:T(8,128)(2,1)S(1)} %constant_dynamic-slice_fusion), channel_id=1, source_target_pairs={{0,2},{1,3},{2,0},{3,1},{4,6},{5,7},{6,4},{7,5},{8,10},{9,11},{10,... | collective-permute-start | bytes 1327112 | tf_op jit(solution)/shard_map/ppermute | solution.py:616
  370.6 1.9 collective-permute-start.25
  370.7 48.4 %collective-permute-start.27 = (bf16[4,256,1024]{2,1,0:T(8,128)(2,1)}, bf16[4,256,1024]{2,1,0:T(8,128)(2,1)}, u32[]{:S(2)}, u32[]{:S(2)}) collective-permute-start(bf16[4,256,1024]{2,1,0:T(8,128)(2,1)} %gram_chunks.12), channel_id=1, source_target_pairs={{0,4},{4,0},{8,12},{12,8},{16,20},{20,16},{24,28},{28,24},{1,5},{5... | collective-permute-start | bytes 6291464 | tf_op jit(solution)/shard_map/ppermute | solution.py:616
  371.7 163.6 %reduce-scatter.6.cloned.1.call-start = ((), (), s32[]{:S(2)}) async-start(), calls=%async_computation.5 | async-start | bytes 2621440 | tf_op jit(solution)/shard_map/reduce_scatter | solution.py:660
  397.0 13.8 %copy-start.11 = (f32[6,256,128]{2,1,0:T(8,128)S(1)}, f32[6,256,128]{2,1,0:T(8,128)}, u32[]{:S(2)}) copy-start(f32[6,256,128]{2,1,0:T(8,128)} %get-tuple-element.126.aux_ref) | copy-start | bytes 2359300
  397.0 15.4 %copy-start.23 = (f32[8,1024]{1,0:T(8,128)S(1)}, f32[8,1024]{1,0:T(8,128)}, u32[]{:S(2)}) copy-start(f32[8,1024]{1,0:T(8,128)} %get-tuple-element.201) | copy-start | bytes 98308
  410.6 25.8 %collective-permute-start.28 = (bf16[2,1536,512]{2,1,0:T(8,128)(2,1)}, bf16[2,1536,512]{2,1,0:T(8,128)(2,1)}, u32[]{:S(2)}, u32[]{:S(2)}) collective-permute-start(bf16[2,1536,512]{2,1,0:T(8,128)(2,1)} %get-tuple-element.192), channel_id=1, source_target_pairs={{0,1},{1,0},{2,3},{3,2},{4,5},{5,4},{6,7},{7,6},{8,9},{9,8},{10,11... | collective-permute-start | bytes 9437192 | tf_op jit(solution)/shard_map/ppermute | solution.py:616
  439.7 37.6 %collective-permute-start.31 = (bf16[1,1536,512]{2,1,0:T(8,128)(2,1)}, bf16[1,1536,512]{2,1,0:T(8,128)(2,1)}, u32[]{:S(2)}, u32[]{:S(2)}) collective-permute-start(bf16[1,1536,512]{2,1,0:T(8,128)(2,1)} %slice_add_fusion.1), channel_id=1, source_target_pairs={{0,2},{1,3},{2,0},{3,1},{4,6},{5,7},{6,4},{7,5},{8,10},{9,11},{10,... | collective-permute-start | bytes 4718600 | tf_op jit(solution)/shard_map/ppermute | solution.py:616
  443.4 4.0 collective-permute-start.32
  447.4 9.5 %collective-permute-start.33 = (f32[9520]{0:T(1024)S(1)}, f32[9520]{0:T(1024)S(1)}, u32[]{:S(2)}, u32[]{:S(2)}) collective-permute-start(f32[9520]{0:T(1024)S(1)} %add.169), channel_id=1, source_target_pairs={{0,8},{4,12},{8,0},{12,4},{16,24},{20,28},{24,16},{28,20},{1,9},{5... | collective-permute-start | bytes 114248 | tf_op jit(solution)/shard_map/ppermute | solution.py:616
  453.1 27.9 %collective-permute-start.29 = (bf16[4,256,384]{2,1,0:T(8,128)(2,1)}, bf16[4,256,384]{2,1,0:T(8,128)(2,1)}, u32[]{:S(2)}, u32[]{:S(2)}) collective-permute-start(bf16[4,256,384]{2,1,0:T(8,128)(2,1)} %gram_chunks.14), channel_id=1, source_target_pairs={{0,4},{4,0},{8,12},{12,8},{16,20},{20,16},{24,28},{28,24},{1,5},{5... | collective-permute-start | bytes 2359304 | tf_op jit(solution)/shard_map/ppermute | solution.py:616
  453.4 60.5 %collective-permute-start.30 = (bf16[1,1536,512]{2,1,0:T(8,128)(2,1)}, bf16[1,1536,512]{2,1,0:T(8,128)(2,1)}, u32[]{:S(2)}, u32[]{:S(2)}) collective-permute-start(bf16[1,1536,512]{2,1,0:T(8,128)(2,1)} %get-tuple-element.256), channel_id=1, source_target_pairs={{0,2},{1,3},{2,0},{3,1},{4,6},{5,7},{6,4},{7,5},{8,10},{9,11},{10,... | collective-permute-start | bytes 4718600 | tf_op jit(solution)/shard_map/ppermute | solution.py:616
  456.9 8.4 %collective-permute-start.34 = (f32[9520]{0:T(1024)S(1)}, f32[9520]{0:T(1024)S(1)}, u32[]{:S(2)}, u32[]{:S(2)}) collective-permute-start(f32[9520]{0:T(1024)S(1)} %add.170), channel_id=1, source_target_pairs={{0,16},{4,20},{8,24},{12,28},{16,0},{20,4},{24,8},{28,12},{1,17},{... | collective-permute-start | bytes 114248 | tf_op jit(solution)/shard_map/ppermute | solution.py:616
  465.3 15.7 %copy-start.13 = (f32[9520]{0:T(1024)}, f32[9520]{0:T(1024)S(1)}, u32[]{:S(2)}) copy-start(f32[9520]{0:T(1024)S(1)} %add.171) | copy-start | bytes 114244
  465.9 1.2 collective-permute-start.35
  467.7 13.3 %copy-start.4 = (bf16[4,256,384]{2,1,0:T(8,128)(2,1)S(1)}, bf16[4,256,384]{2,1,0:T(8,128)(2,1)}, u32[]{:S(2)}) copy-start(bf16[4,256,384]{2,1,0:T(8,128)(2,1)} %gram_chunks.15) | copy-start | bytes 2359300
  467.7 42.0 %collective-permute-start.36 = (f32[1,512]{1,0:T(1,128)}, f32[1,512]{1,0:T(1,128)}, u32[]{:S(2)}, u32[]{:S(2)}) collective-permute-start(f32[1,512]{1,0:T(1,128)} %slice_add_fusion.9), channel_id=1, source_target_pairs={{0,2},{1,3},{2,0},{3,1},{4,6},{5,7},{6,4},{7,5},{8,10},{9,11},{10,... | collective-permute-start | bytes 6152 | tf_op jit(solution)/shard_map/ppermute | solution.py:616
  483.0 32.9 %collective-permute-start.37 = (bf16[2,256,384]{2,1,0:T(8,128)(2,1)}, bf16[2,256,384]{2,1,0:T(8,128)(2,1)}, u32[]{:S(2)}, u32[]{:S(2)}) collective-permute-start(bf16[2,256,384]{2,1,0:T(8,128)(2,1)} %get-tuple-element.259), channel_id=1, source_target_pairs={{0,8},{4,12},{8,0},{12,4},{16,24},{20,28},{24,16},{28,20},{1,9},{5... | collective-permute-start | bytes 1179656 | tf_op jit(solution)/shard_map/ppermute | solution.py:616
  513.9 10.9 %copy-start.2 = (bf16[6,256,512]{2,1,0:T(8,128)(2,1)S(1)}, bf16[6,256,512]{2,1,0:T(8,128)(2,1)}, u32[]{:S(2)}) copy-start(bf16[6,256,512]{2,1,0:T(8,128)(2,1)} %param.35) | copy-start | bytes 4718596
  513.9 10.9 %copy-start.3 = (bf16[1,1536,512]{2,1,0:T(8,128)(2,1)S(1)}, bf16[1,1536,512]{2,1,0:T(8,128)(2,1)}, u32[]{:S(2)}) copy-start(bf16[1,1536,512]{2,1,0:T(8,128)(2,1)} %fusion.40) | copy-start | bytes 4718596
  513.9 10.9 %copy-start.16 = (f32[6,256]{1,0:T(8,128)S(1)}, f32[6,256]{1,0:T(8,128)}, u32[]{:S(2)}) copy-start(f32[6,256]{1,0:T(8,128)} %copy-done.15) | copy-start | bytes 18436
  513.9 10.9 %copy-start.19 = (f32[6,1,256]{2,0,1:T(8,128)S(1)}, f32[6,1,256]{2,0,1:T(8,128)}, u32[]{:S(2)}) copy-start(f32[6,1,256]{2,0,1:T(8,128)} %copy.74) | copy-start | bytes 18436
  513.9 11.0 %copy-start.21 = (f32[512]{0:T(512)S(1)}, f32[512]{0:T(512)}, u32[]{:S(2)}) copy-start(f32[512]{0:T(512)} %get-tuple-element.251) | copy-start | bytes 6148
  516.9 16.0 %collective-permute-start.38 = (bf16[1,256,384]{2,1,0:T(8,128)(2,1)S(1)}, bf16[1,256,384]{2,1,0:T(8,128)(2,1)S(1)}, u32[]{:S(2)}, u32[]{:S(2)}) collective-permute-start(bf16[1,256,384]{2,1,0:T(8,128)(2,1)S(1)} %slice_add_fusion.6), channel_id=1, source_target_pairs={{0,16},{4,20},{8,24},{12,28},{16,0},{20,4},{24,8},{28,12},{1,17},{... | collective-permute-start | bytes 589832 | tf_op jit(solution)/shard_map/ppermute | solution.py:616
  (36 other events, 139.4 us)
Sparse Core Ops, SparseCore 0:
  9.6 49.0 all-gather.1
  301.3 46.9 reduce-scatter.7
  371.8 48.0 reduce-scatter.3
  423.1 49.1 reduce-scatter.5

commit v3 on v2

--- a/solution.py
+++ b/solution.py
@@ -40,9 +40,16 @@
 
 
 def per_head(value, expand):
-    high, low = halves(value)
-    nt = ((1,), (1,))
-    return dot(high, expand, nt) + dot(low, expand, nt)
+    lane = lax.broadcasted_iota(jnp.int32, (1, LANES), 1)
+    left = lane < HEAD_DIM
+    total = None
+    for pair in range(value.shape[1] // LANES):
+        both = value[:, pair * LANES : (pair + 1) * LANES]
+        low = jnp.sum(jnp.where(left, both, 0.0), axis=1, keepdims=True)
+        high = jnp.sum(jnp.where(left, 0.0, both), axis=1, keepdims=True)
+        placed = jnp.where(lane == 2 * pair, low, jnp.where(lane == 2 * pair + 1, high, 0.0))
+        total = placed if total is None else total + placed
+    return total
 
 
 def to_row(column):
@@ -65,7 +72,12 @@
 
 
 def running(value, lower):
-    return dot(triangle(value.shape[0], lower), value, precision=lax.Precision.HIGHEST)
+    width = value.shape[1]
+    high, low = halves(value)
+    lowest = (value - high.astype(F32) - low.astype(F32)).astype(BF)
+    parts = jnp.concatenate([high, low, lowest], axis=1)
+    sums = dot(triangle(value.shape[0], lower).astype(BF), parts)
+    return sums[:, :width] + sums[:, width : 2 * width] + sums[:, 2 * width :]
 
 
 def doc_mask(seg_col, seg_row, lower):
@@ -410,8 +422,8 @@
     def _():
         grad_ref[...] = jnp.zeros_like(grad_ref)
 
-    grad_ref[0:1] += jnp.sum(d_scaled * gated, axis=0, keepdims=True)
-    grad_ref[1:2] += jnp.sum(d_y * x_float, axis=0, keepdims=True)
+    grad_ref[5:6] += jnp.sum(d_scaled * gated, axis=0, keepdims=True)
+    grad_ref[6:7] += jnp.sum(d_y * x_float, axis=0, keepdims=True)
     d_carried = (d_y * entry_wide).astype(BF)
     dc_ref[0] = dot(d_carried, states, ((1,), (1,)))
     grad = dot(bc_ref[0, :, state:], d_carried, ((0,), (0,)))
@@ -531,7 +543,9 @@
     dot_ref[0] = to_row(row) + dot_z_ref[0]
 
 
-def conv_bc_kernel(d_ref, pre_ref, halo_ref, aux_ref, conv_ref, dpre_ref, dot_ref, grad_ref):
+def conv_bc_kernel(
+    d_ref, pre_ref, halo_ref, aux_ref, ddt_ref, conv_ref, dpre_ref, dot_ref, grad_ref
+):
     span = pre_ref.shape[1]
     extended = jnp.concatenate([halo_ref[0], pre_ref[0]], axis=0).astype(F32)
     aux = aux_ref[0]
@@ -548,21 +562,28 @@
     ahead = d_ref[0, span : span + EDGE].astype(F32)
     d_pre = jnp.concatenate([d_pre[: span - EDGE], d_pre[span - EDGE :] + ahead], axis=0)
     d_pre = d_pre.astype(BF)
-    dpre_ref[0] = d_pre
+    dpre_ref[0, :, : d_pre.shape[1]] = d_pre
+    dpre_ref[0, :, d_pre.shape[1] :] = ddt_ref[0]
     row = jnp.sum(d_pre.astype(F32) * extended[EDGE:], axis=-1, keepdims=True)
     packed = d_ref[0, span + EDGE :].astype(F32)
     dot_ref[0] = to_row(row) + (packed[0:1] + packed[1:2])
 
 
-def gram_chunk_kernel(me_ref, a_ref, b_ref, *outs):
+def gram_kernel(a_ref, b_ref, out_ref):
+    out_ref[...] = dot(a_ref[...], b_ref[...], ((0,), (0,))).astype(BF)
+
+
+def gram_pair_kernel(me_ref, a_ref, b_ref, odd_ref, even_ref):
     product = dot(a_ref[...], b_ref[...], ((0,), (0,))).astype(BF)
-    width = product.shape[1] // len(outs)
-    for at, out_ref in enumerate(outs):
-        out_ref[0] = product[:, at * width : (at + 1) * width]
+    tile = product.shape[0] // 2
+    low, high = product[:tile], product[tile:]
+    same = me_ref[0] % 2 == 0
+    odd_ref[0] = jnp.where(same, high, low)
+    even_ref[0] = jnp.where(same, low, high)
 
 
 def share_kernel(terms, with_sum, me_ref, *refs):
-    out_ref = refs[2 * terms + with_sum]
+    odd_ref, even_ref = refs[2 * terms + with_sum : 2 * terms + with_sum + 2]
     nt = ((1,), (1,))
     total = None
     for t in range(terms):
@@ -570,7 +591,16 @@
         rhs = rhs[0] if len(rhs.shape) == 3 else rhs[...]
         term = dot(refs[2 * t][...], rhs, nt)
         total = term if total is None else total + term
-    out_ref[0] = total.astype(BF)
+    total_low = total.astype(BF)
+
+    @pl.when(pl.program_id(0) < pl.num_programs(0) // 2)
+    def _():
+        odd_ref[0] = total_low
+
+    @pl.when(pl.program_id(0) >= pl.num_programs(0) // 2)
+    def _():
+        even_ref[0] = total_low
+
     if with_sum:
         sum_ref = refs[-1]
 
@@ -643,6 +673,10 @@
         sides = fold_step(sides, axis, mask)
         mask *= 2
     return sides
+
+
+def core_sum(odd, even):
+    return even + swap(odd, "head", 1)
 
 
 def pair_sides(full):
@@ -731,15 +765,17 @@
     masks = [2 * m for m in range(groups)]
     _, width = chunk_grid(groups, half, own)
 
-    tok_halo = shift(tokens[:, -8:], "seq", 1)
-    seg_halo = shift(segments[:, -8:], "seq", 1)
+    seg_lanes = jnp.broadcast_to(segments[:, -8:, None].astype(BF), (seqs, 8, LANES))
+    halo = shift(jnp.concatenate([tokens[:, -8:], seg_lanes], axis=2), "seq", 1)
+    tok_halo, seg_halo = halo[..., :model], halo[..., model]
     cot_full = lax.all_gather(cotangent, "head", axis=2, tiled=True)
 
     w_in = lax.optimization_barrier(jnp.transpose(w_zx, (1, 0, 2)))
     w_dt = pad_lanes(w_dt, LANES)
     w_small = jnp.concatenate([w_bc, w_dt], axis=1)
-    seg_rows = jnp.concatenate([jnp.pad(seg_halo, ((0, 0), (LANES - 8, 0))), segments], axis=1)
-    seg_rows = jnp.broadcast_to(seg_rows.astype(F32)[:, None], (seqs, 8, LANES + span))
+    seg_rows = [jnp.pad(seg_halo.astype(F32), ((0, 0), (LANES - 8, 0))), segments.astype(F32)]
+    seg_rows = jnp.concatenate(seg_rows, axis=1)
+    seg_rows = jnp.broadcast_to(seg_rows[:, None], (seqs, 8, LANES + span))
     conv_x_w = pad_rows([conv_x, conv_x_bias])
     conv_bc_w = pad_rows([conv_bc, conv_bc_bias])
     head_rows = pad_lanes(pad_rows([dt_bias, jnp.exp(a_log)]), LANES)
@@ -881,78 +917,58 @@
 
     other = swap(send, "seq", 1)
 
-    ins = (x_ssm, bc_ssm, xs, d_y, d_c, cum, dt_raw, aux, seg_rows, wide_rows, head_rows, expand)
-    per = (
-        shaped((seqs, span, own), BF),
-        shaped((seqs, span, LANES), F32),
-        shaped((seqs, span, wide), F32),
-    )
-    d_x, d_step, d_bc = call(
-        functools.partial(inner_back_kernel, state),
-        seqs,
-        ins,
-        seq_of(ins[:9]) + whole_of(ins[9:]),
-        per,
-        seq_of(per),
-        [],
-        18.6,
-        "inner_back",
-    )
-
     normed_rows = normed.reshape(rows, model)
 
-    def chunk_sides(left, values, pieces, natural=False):
+    def gram(left, values):
+        tile = 4 * LANES
+        return call(
+            gram_kernel,
+            model // tile,
+            (left, values),
+            [pl.BlockSpec((rows, tile), lambda i: (0, i)), whole(values.shape)],
+            (shaped((model, values.shape[1]), BF),),
+            [pl.BlockSpec((tile, values.shape[1]), lambda i: (i, 0))],
+            [],
+            10.8,
+            "gram",
+        )[0]
+
+    def chunk_pair(left, values, natural):
         tile = model // n_seq
-        block = values.shape[1] // pieces
         if tile % LANES:
             full = dot(left, values, ((0,), (0,))).astype(BF)
-            cuts = [full[:, at * block : (at + 1) * block] for at in range(pieces)]
-            if natural:
-                return [pair_sides(c) for c in cuts]
-            return [row_sides(c, "seq") for c in cuts]
-        sides = []
-        for parity in (1, 0):
-            if sides:
-                values = after(values, sides[0][0])
-            sides.append(
-                pl.pallas_call(
-                    gram_chunk_kernel,
-                    grid_spec=pltpu.PrefetchScalarGridSpec(
-                        num_scalar_prefetch=1,
-                        grid=(groups,),
-                        in_specs=[
-                            pl.BlockSpec(
-                                (rows, tile), lambda i, me_ref: (
-                                    0,
-                                    2 * i + ((parity + me_ref[0]) % 2)
-                                    if natural
-                                    else (2 * i + parity) ^ me_ref[0],
-                                ),
-                            ),
-                            pl.BlockSpec(values.shape, lambda i, me_ref: (0, 0)),
-                        ],
-                        out_specs=[
-                            pl.BlockSpec((1, tile, block), lambda i, me_ref: (i, 0, 0))
-                        ] * pieces,
-                    ),
-                    out_shape=[shaped((groups, tile, block), BF)] * pieces,
-                    name="gram_chunks",
-                    compiler_params=pltpu.CompilerParams(vmem_limit_bytes=VMEM),
-                    cost_estimate=pl.CostEstimate(
-                        flops=rows * model * values.shape[1],
-                        bytes_accessed=rows * (model + 2 * values.shape[1])
-                        + model * values.shape[1],
-                        transcendentals=0,
-                    ),
-                )(me, left, values)
-            )
-        return list(zip(*sides))
+            return pair_sides(full) if natural else row_sides(full, "seq")
+        block = (tile, values.shape[1])
+
+        def at(i, me_ref):
+            return i if natural else i ^ (me_ref[0] // 2)
+
+        return tuple(
+            pl.pallas_call(
+                gram_pair_kernel,
+                grid_spec=pltpu.PrefetchScalarGridSpec(
+                    num_scalar_prefetch=1,
+                    grid=(groups,),
+                    in_specs=[
+                        pl.BlockSpec((rows, 2 * tile), lambda i, me_ref: (0, at(i, me_ref))),
+                        pl.BlockSpec(values.shape, lambda i, me_ref: (0, 0)),
+                    ],
+                    out_specs=[pl.BlockSpec((1, *block), lambda i, me_ref: (i, 0, 0))] * 2,
+                ),
+                out_shape=[shaped((groups, *block), BF)] * 2,
+                name="gram_pair",
+                compiler_params=pltpu.CompilerParams(vmem_limit_bytes=VMEM),
+                cost_estimate=cost(rows * model * values.shape[1] / 3e8),
+            )(me, left, values)
+        )
 
     def share_sum(terms, parity, summed):
         pairs = n_head // 2
+        quads = pairs // 2
         tall = rows
         def at(i, head_ref):
-            return (2 * i + parity) ^ head_ref[0]
+            core = 1 - i // quads
+            return (4 * (i % quads) + 2 * parity + core) ^ head_ref[0]
 
         ins, specs = [], []
         for lhs, rhs, first in terms:
@@ -971,8 +987,15 @@
                         (share, rhs.shape[1]), lambda i, s, head_ref: (at(i, head_ref), 0)
                     )
                 )
-        out_specs = [pl.BlockSpec((1, tall, share), lambda i, s, head_ref: (i, s, 0))]
-        outs = [shaped((pairs, rows, share), BF)]
+        out_specs = [
+            pl.BlockSpec(
+                (1, tall, share), lambda i, s, head_ref: (jnp.minimum(i, quads - 1), s, 0)
+            ),
+            pl.BlockSpec(
+                (1, tall, share), lambda i, s, head_ref: (jnp.maximum(i - quads, 0), s, 0)
+            ),
+        ]
+        outs = [shaped((quads, rows, share), BF)] * 2
         if summed:
             ins.append(normed_rows)
             specs.append(
@@ -994,42 +1017,64 @@
             compiler_params=pltpu.CompilerParams(vmem_limit_bytes=VMEM),
             cost_estimate=cost(rows * model * depth / 5e8),
         )(head_at, *ins)
-        return got if summed else got[0]
+        return (got[:2], got[2]) if summed else got
 
     scaled_rows, d_z_rows = scaled.reshape(rows, own), d_z.reshape(rows, own)
+    out_grad = chunk_pair(cot_full.reshape(rows, model), scaled_rows, True)
+    out_far = share_sum([(after(scaled_rows, out_grad[1]), w_out, 0)], 1, False)
     parts = small_call(
         functools.partial(pair_back_kernel, seqs, groups, half),
-        (me, after(keep, d_x), other, pair_decay),
+        (me, after(keep, out_far[1]), other, pair_decay),
         (piece,) * groups,
         seqs,
         "pair_back",
     )
     arrived = exchange(parts, masks)
-    (out_grad,) = chunk_sides(cot_full.reshape(rows, model), after(scaled_rows, parts[0]), 1, True)
-    out_total = pair_sum(out_grad)
+    ins = (
+        x_ssm, bc_ssm, xs, after(d_y, parts[0]), d_c, cum, dt_raw, aux, seg_rows, wide_rows, head_rows, expand,
+    )
+    per = (
+        shaped((seqs, span, own), BF),
+        shaped((seqs, span, LANES), F32),
+        shaped((seqs, span, wide), F32),
+    )
+    d_x, d_step, d_bc = call(
+        functools.partial(inner_back_kernel, state),
+        seqs,
+        ins,
+        seq_of(ins[:9]) + whole_of(ins[9:]),
+        per,
+        seq_of(per),
+        [],
+        18.6,
+        "inner_back",
+    )
+
     leaves = small_call(
         functools.partial(scan_back_kernel, seqs, groups),
-        (me, after(decays, out_grad[1]), *arrived),
+        (me, after(decays, d_x), *arrived),
         (piece,) * groups,
         seqs,
         "scan_back",
     )
     arrived = exchange(leaves, masks)
-    (gate_grad,) = chunk_sides(normed_rows, after(d_z_rows, leaves[0]), 1, True)
+    gate_grad = gram(normed_rows, after(d_z_rows, leaves[0]))
     end_mine, end_send = small_call(
         functools.partial(unpair_kernel, seqs, groups, half, False),
-        (me, after(keep, gate_grad[1]), other, pair_decay, *arrived),
+        (me, after(keep, gate_grad), other, pair_decay, *arrived),
         halves_out,
         seqs,
         "unpair_back",
     )
     end_other = swap(end_send, "seq", 1)
-    gate_total = pair_sum((after(gate_grad[0], end_other), gate_grad[1]))
+    gate_total = spread_sum(gate_grad).reshape(2, -1, own)
+    gate_total = spread_sum(gate_grad).reshape(2, -1, own)
     out_odd = share_sum([(after(scaled_rows, end_mine), w_out, 0)], 1, False)
     out_even = share_sum([(after(scaled_rows, out_odd), w_out, 0)], 0, False)
 
+    out_total = pair_sum((out_grad[0], after(out_grad[1], end_mine)))
     ins = (
-        me, after(x_ssm, out_even, out_total), bc_ssm, pre_x, halo_x, pre_bc, halo_bc, d_x, d_step, d_bc, mixed, cum,
+        me, after(x_ssm, out_total), bc_ssm, pre_x, halo_x, pre_bc, halo_bc, d_x, d_step, d_bc, mixed, cum,
         dt_raw, aux, dot_z, state_mine, state_other, end_mine, end_other, conv_x_w, conv_bc_w,
         head_rows, expand,
     )
@@ -1053,7 +1098,10 @@
         28,
         "leave",
     )
+    out_near = share_sum([(after(scaled_rows, d_x_pre), w_out, 0)], 0, False)
+    out_far = core_sum(out_far[0], after(out_far[1], out_near[1]))
     back = shift(jnp.concatenate([back_x, back_bc], axis=2)[:, -edge:], "seq", -1)
+    back = after(back, out_near[1])
     back_x, back_bc = back[..., :own], back[..., own:]
     fix = jnp.sum(back_x.astype(F32) * pre_x[:, -edge:].astype(F32), axis=-1)
     row_dot = row_dot[:, 0] + jnp.pad(fix, ((0, 0), (span - edge, 0)))
@@ -1063,10 +1111,10 @@
     back_bc = jnp.pad(back_bc, ((0, 0), (EDGE - edge, 0), (0, 0)))
     d_bc = jnp.concatenate([d_bc, back_bc, dots], axis=1)
     d_bc = d_bc + swap(d_bc, "head", 1)
-    d_x_pre = after(d_x_pre, d_bc, gate_total).at[:, -edge:].add(back_x)
+    d_x_pre = after(d_x_pre, d_bc, out_far).at[:, -edge:].add(back_x)
     d_x_rows = d_x_pre.reshape(rows, own)
     d_dt_rows = d_dt.reshape(rows, LANES)
-    (late_sides,) = chunk_sides(normed_rows, d_x_rows, 1, True)
+    late_sides = chunk_pair(normed_rows, d_x_rows, True)
 
     core, middle = me_head % 2, seqs // 2
     part = lax.dynamic_slice_in_dim(d_bc, core * middle, middle, 0)
@@ -1081,43 +1129,46 @@
         jnp.concatenate([part, part_other], axis=0),
         jnp.concatenate([part_other, part], axis=0),
     )
-    ins = (d_bc_all, pre_bc, halo_bc, aux, conv_bc_w)
-    per = (shaped((seqs, span, wide), BF), shaped((seqs, 8, span), F32))
-    d_bc_pre, row_dot, bc_grads = call(
+    ins = (d_bc_all, pre_bc, halo_bc, aux, d_dt, conv_bc_w)
+    per = (shaped((seqs, span, wide + LANES), BF), shaped((seqs, 8, span), F32))
+    d_small, row_dot, bc_grads = call(
         conv_bc_kernel,
         seqs,
         ins,
-        seq_of(ins[:4]) + whole_of(ins[4:]),
+        seq_of(ins[:5]) + whole_of(ins[5:]),
         per + (shaped((8, wide), F32),),
         seq_of(per) + [whole((8, wide))],
         [],
         6.3,
         "conv_bc",
     )
-    d_small = jnp.concatenate([d_bc_pre.reshape(rows, wide), d_dt_rows], axis=-1)
-    (small_sides,) = chunk_sides(normed_rows, d_small, 1)
-    out_next = fold_step((out_odd, after(out_even, d_bc_pre)), "head", 1)
-    terms = [(after(d_z_rows, small_sides[1], *out_next), w_in, 0), (d_x_rows, w_in, 1)]
+    small_sides = chunk_pair(normed_rows, d_small.reshape(rows, -1), False)
+    out_near = core_sum(out_near[0], after(out_near[1], d_small))
+    terms = [(after(d_z_rows, small_sides[1], out_near), w_in, 0), (d_x_rows, w_in, 1)]
     terms.append((d_dt_rows, w_dt, 0))
-    grad_odd, norm_odd = share_sum(terms, 1, True)
-    late_total = pair_sum((late_sides[0], after(late_sides[1], grad_odd)))
-    terms[0] = (after(d_z_rows, late_total), w_in, 0)
-    grad_even, norm_even = share_sum(terms, 0, True)
-    grad_next = fold_step((grad_odd, grad_even), "head", 1)
-    small_next = fold_step((small_sides[0], after(small_sides[1], *grad_next)), "seq", 1)
-    out_next = out_next[0], after(out_next[1], *small_next)
-    own_sum = fold(out_next, "head", 2).reshape(seqs, span, share)
+    grad_far, norm_far = share_sum(terms, 1, True)
+    late_total = pair_sum((late_sides[0], after(late_sides[1], grad_far[1])))
+    grad_far = core_sum(grad_far[0], after(grad_far[1], late_total))
+    own_sum = fold((out_far, after(out_near, grad_far)), "head", 2)
+    own_sum = own_sum.reshape(seqs, span, share)
+    terms[0] = (after(d_z_rows, grad_far), w_in, 0)
+    grad_near, norm_near = share_sum(terms, 0, True)
+    grad_near = core_sum(grad_near[0], after(grad_near[1], own_sum))
+    small_next = fold_step((small_sides[0], after(small_sides[1], grad_near)), "seq", 1)
     tokens_own = lax.dynamic_slice_in_dim(tokens, offset, share, 2).astype(F32)
     layer_out = (tokens_own + own_sum.astype(F32)).astype(BF)
-    own_grad = fold(grad_next, "head", 2).reshape(seqs, span, share).astype(F32)
+    own_grad = fold((grad_far, grad_near), "head", 2).reshape(seqs, span, share).astype(F32)
     late_s = fold(small_next, "seq", 2).astype(F32)
     out_grad_own = spread_sum(out_total).astype(F32)
-    gate_grad_own = spread_sum(gate_total).astype(F32)
+    x_at = lax.axis_index("seq") % 2
+    gate_own = lax.dynamic_index_in_dim(gate_total, x_at, 0, False)
+    gate_sent = lax.dynamic_index_in_dim(gate_total, 1 - x_at, 0, False)
+    gate_grad_own = (gate_own + swap(gate_sent, "seq", 1)).astype(F32)
     late_a = spread_sum(late_total).astype(F32)
 
     row_dot = row_dot[:, 0]
-    w_bc_own = lax.dynamic_slice_in_dim(w_bc, offset, share, 0)
-    bc_term = dot(d_bc_pre, w_bc_own, ((2,), (1,)))
+    w_bc_own = pad_lanes(lax.dynamic_slice_in_dim(w_bc, offset, share, 0), wide + LANES)
+    bc_term = dot(d_small, w_bc_own, ((2,), (1,)))
     rstd_in = aux[:, :, 6:7]
     unit_own = tokens_own * rstd_in
     gain_own = lax.dynamic_slice_in_dim(norm_gain, offset, share, 0)
@@ -1127,26 +1178,31 @@
     ).astype(BF)
 
     taps = edge + 1
-    norm_part = jnp.concatenate([norm_even[:, 0], norm_odd[:, 0]], axis=0)
-    norm_part = norm_part.at[0].add(gain_own * jnp.sum(bc_term * unit_own, axis=(0, 1)))
-    small = (
-        norm_part,
-        conv_grads[:taps],
-        conv_grads[taps],
-        bc_grads[:taps],
-        bc_grads[taps],
-        head_grads[0, :heads],
-        head_grads[1, :heads],
-        jnp.sum(gate_grads[1].reshape(heads, HEAD_DIM), axis=-1),
-        gate_grads[0],
-    )
-    flat = sum_all(jnp.concatenate([v.reshape(-1) for v in small]), "seq")
-    summed, at = [], 0
-    for v in small:
-        summed.append(flat[at : at + v.size].reshape(v.shape))
-        at += v.size
-    norm_part = summed.pop(0)
-    g_norm = fold((norm_part[n_head // 2 :], norm_part[: n_head // 2]), "head") / gain_own
+    quads = n_head // 4
+    norm_odd, norm_even = [
+        jnp.stack([norm_near[at, 0], norm_far[at, 0]], axis=1).reshape(-1, share)
+        for at in (slice(0, quads), slice(quads, 2 * quads))
+    ]
+    norm_even = norm_even.at[0].add(gain_own * jnp.sum(bc_term * unit_own, axis=(0, 1)))
+    narrow = jnp.concatenate([norm_odd, norm_even, jnp.zeros((8 - 4 * quads, share), F32)], axis=0)
+    narrow = jnp.concatenate([bc_grads, head_grads, narrow], axis=1)
+    wide_sums = conv_grads + gate_grads
+    lanes = max(own, narrow.shape[1])
+    sums = sum_all(
+        jnp.concatenate([pad_lanes(wide_sums, lanes), pad_lanes(narrow, lanes)], axis=0), "seq"
+    )
+    norm_sums = sums[8 : 8 + 4 * quads, wide + LANES : wide + LANES + share]
+    g_norm = fold((norm_sums[: 2 * quads], norm_sums[2 * quads :]), "head") / gain_own
+    summed = (
+        sums[:taps, :own],
+        sums[taps, :own],
+        sums[8 : 8 + taps, :wide],
+        sums[8 + taps, :wide],
+        sums[8, wide : wide + heads],
+        sums[9, wide : wide + heads],
+        jnp.sum(sums[6, :own].reshape(heads, HEAD_DIM), axis=-1),
+        sums[5, :own],
+    )
     g_w_zx_own = jnp.stack([gate_grad_own, late_a], axis=1)
     return (
         layer_out,

time: 552 us -> 503 us (0.911)
  waiting for transfers between devices: 99 us -> 76 us
  Pallas kernels: 242 us -> 223 us
  starting transfers between devices: 77.2 us -> 67.6 us
    pallas_call x8 -> x3, Pallas kernels: 55.8 us -> 28.7 us  [chunk_pair(): pl.pallas_call(gram_pair_kernel, grid_spec=pltpu.PrefetchScalarGridSpec(n...]
    ppermute x36 -> x38, waiting for transfers between devices: 89.7 us -> 75.2 us  [swap(): return lax.ppermute(value, axis, [(i, i ^ mask) for i in range(count)])]
    add x2 -> x6, other arithmetic: 2.24 us -> 11.8 us  [the longest x3 9.46 us: core_sum(): return even + swap(odd, 'head', 1)]
    ppermute x3 -> x2, waiting for transfers between devices: 8.57 us -> 0.01 us  [shift(): lax.ppermute(value, axis, [(i, i + steps) for i in range(leading, last)])]
    add x5 -> x3, other arithmetic: 10.7 us -> 3.05 us  [fold_step(): return (even[1::2] + arrived[1::2], even[0::2] + arrived[0::2])]
    ppermute x36 -> x38, starting transfers between devices: 67.2 us -> 61.2 us  [swap(): return lax.ppermute(value, axis, [(i, i ^ mask) for i in range(count)])]
    pallas_call x13 -> x14, Pallas kernels: 145 us -> 149 us  [call(): pl.pallas_call(body, grid=(grid,), in_specs=in_specs, out_specs=out_specs...]
    unnamed x122 -> x95, local copies, waits for them, and re-layouts: 22 us -> 23.7 us
  transfers between devices with their start and end apart: 43 -> 44, of which waited for: 20 -> 16; matrix products, arithmetic and copies ran while one was open for 18% -> 20% of each run, Pallas kernels for 36% -> 39%
where the time goes in v3:
time: 503 us; the launch traced here: 498 us
  Pallas kernels  223 us (44%)
  waiting for transfers between devices  76 us (15%)
  starting transfers between devices  67.6 us (13%)
  other arithmetic  52.5 us (10%)
  local copies, waits for them, and re-layouts  38.5 us (8%)
  matrix products  25.3 us (5%)
  between operations  14.6 us (3%)
    pallas_call x14, Pallas kernels, call(): pl.pallas_call(body, grid=(grid,), in_specs=in_specs, out_specs=out_specs...  149 us
    ppermute x38, waiting for transfers between devices, swap(): return lax.ppermute(value, axis, [(i, i ^ mask) for i in range(count)])  75.2 us
    ppermute x38, starting transfers between devices, swap(): return lax.ppermute(value, axis, [(i, i ^ mask) for i in range(count)])  61.2 us
    pallas_call x4, Pallas kernels, share_sum(): pl.pallas_call(functools.partial(share_kernel, len(terms), summed), grid_...  45.5 us
    pallas_call x3, Pallas kernels, chunk_pair(): pl.pallas_call(gram_pair_kernel, grid_spec=pltpu.PrefetchScalarGridSpec(n...  28.7 us
    dot_general x3, matrix products, dot(): lax.dot_general(a, b, (contract, ((), ())), preferred_element_type=F32, p...  25.3 us
    unnamed x95, local copies, waits for them, and re-layouts  23.7 us
  transfers between devices with their start and end apart: 44, of which 16 were waited for; matrix products, arithmetic and copies ran while one was open for 20% of the time, Pallas kernels for 39%

profile of v3, /device:TPU:0, one launch (start us, length us, event | category | flops | bytes accessed | tf_op | source)
XLA Modules:
  0.0 497.9 jit_solution(17749299528346365275)
XLA Ops:
  8.8 4.9 collective-permute-start
  13.8 10.2 %copy.63 = bf16[2048,2,1024]{2,0,1:T(8,128)(2,1)} copy(bf16[2048,2,1024]{2,1,0:T(2,128)(2,1)} %param.23) | data formatting | bytes 16777216 | tf_op args[3]
  29.9 28.3 %front.1 = (bf16[6,256,2048]{2,1,0:T(8,128)(2,1)}, bf16[6,256,1024]{2,1,0:T(8,128)(2,1)}, bf16[6,256,256]{2,1,0:T(8,128)(2,1)}, bf16[6,16,1024]{2,1,0:T(8,128)(2...) custom-call(s32[1]{0:T(128)} %bitcast.1.me_ref, ...), custom_call_target="tpu_custom_call" | custom-call | flops 34500001792 | bytes 1000 | tf_op jit(solution)/shard_map/front/pallas_call | solution.py:626
  58.2 1.7 collective-permute-start.1
  60.8 17.7 %collective-permute-done.1.other_ref = bf16[400,1024]{1,0:T(8,128)(2,1)S(1)} collective-permute-done((bf16[400,1024]{1,0:T(8,128)(2,1)}, bf16[400,1024]{1,0:T(8,128)(2,1)S(1)}, u32[]{:S(2)}, u32[]{:S(2)}) %collective-permute-start.1) | collective-permute-done | bytes 819232 | tf_op jit(solution)/shard_map/ppermute | solution.py:646
  79.4 3.0 pair.1
  84.0 2.6 collective-permute-start.3
  86.7 11.2 %fusion.15.gate_ref = bf16[6,256,1024]{2,1,0:T(8,128)(2,1)} fusion(bf16[6,256,2048]{2,1,0:T(8,128)(2,1)} %get-tuple-element.139, bf16[2,2048,1024]{2,1,0:T(8,128)(2,1)} %bitcast.94), kind=kOutput, calls=%fused_computation.20 | convolution fusion | flops 6444023808 | bytes 13631488 | tf_op jit(solution)/shard_map/dot_general | solution.py:27
  97.9 5.5 %collective-permute-done.3.rest_2_ = bf16[7,16,1024]{2,1,0:T(8,128)(2,1)S(1)} collective-permute-done((bf16[7,16,1024]{2,1,0:T(8,128)(2,1)}, bf16[7,16,1024]{2,1,0:T(8,128)(2,1)S(1)}, u32[]{:S(2)}, u32[]{:S(2)}) %collective-permute-start.3) | collective-permute-done | bytes 229408 | tf_op jit(solution)/shard_map/ppermute | solution.py:646
  104.2 2.5 scan.1
  106.7 3.0 collective-permute-start.5
  112.2 10.4 %inner.1.inner_ref = f32[6,256,1024]{2,1,0:T(8,128)} custom-call(bf16[6,256,256]{2,1,0:T(8,128)(2,1)} %get-tuple-element.135.bc_ref, bf16[6,256,1024]{2,1,0:T(8,128)(2,1)} %get-tuple-element.136.xs_ref, f32[6,256,128]{2,1,0:T(8,128)} %get-tuple-element.137.cum_ref, f32[6,256,128]{2,1,0:T(8,128)} %get-tuple-element.138.aux_ref, ...), custom_call_target="tpu_custom_call" | custom-call | flops 11845000192 | bytes 1000 | tf_op jit(solution)/shard_map/inner/pallas_call | solution.py:626
  122.6 2.9 collective-permute-done.6.rest_2_
  126.3 3.6 unpair.1
  131.5 11.4 %fusion.12.e_ref = bf16[6,256,1024]{2,1,0:T(8,128)(2,1)} fusion(bf16[6,256,2048]{2,1,0:T(8,128)(2,1)} %all-gather.2.cloned.1.call-done, bf16[2048,1024]{1,0:T(8,128)(2,1)} %refs_1_.3), kind=kOutput, calls=%fused_computation.19 | convolution fusion | flops 6444023808 | bytes 13631488 | tf_op jit(solution)/shard_map/dot_general | solution.py:27
  142.9 1.9 collective-permute-done.8.other_ref
  145.7 11.9 %sums.1 = f32[6,8,256]{2,1,0:T(8,128)} custom-call(s32[1]{0:T(128)} %bitcast.1.me_ref, bf16[6,256,1024]{2,1,0:T(8,128)(2,1)} %get-tuple-element.181.x_ref, bf16[6,256,256]{2,1,0:T(8,128)(2,1)} %get-tuple-element.135.bc_ref, f32[6,256,1024]{2,1,0:T(8,128)} %inner.1.inner_ref, bf16[6,256,1024]{2,1,0:T(8,128)(2,1)} %fusion.15.gate_ref, ...), custom_call_target="tpu_custom_call" | custom-call | flops 13799999488 | bytes 1000 | tf_op jit(solution)/shard_map/sums/pallas_call | solution.py:626
  161.2 2.7 collective-permute-done.10
  164.5 19.4 %gate_back.1 = (bf16[6,256,1024]{2,1,0:T(8,128)(2,1)}, bf16[6,256,1024]{2,1,0:T(8,128)(2,1)}, bf16[6,256,1024]{2,1,0:T(8,128)(2,1)}, f32[6,256,128]{2,1,0:T(8,12...) custom-call(s32[1]{0:T(128)} %bitcast.1.me_ref, ...), custom_call_target="tpu_custom_call" | custom-call | flops 24149999616 | bytes 1000 | tf_op jit(solution)/shard_map/gate_back/pallas_call | solution.py:626
  185.5 10.7 %gram_pair.3 = (bf16[4,256,1024]{2,1,0:T(8,128)(2,1)}, bf16[4,256,1024]{2,1,0:T(8,128)(2,1)}) custom-call(s32[1]{0:T(128)} %bitcast.1.me_ref, bf16[1536,2048]{1,0:T(8,128)(2,1)} %bitcast.120, bf16[1536,1024]{1,0:T(8,128)(2,1)} %bitcast.129), custom_call_target="tpu_custom_call" | custom-call | flops 12348030976 | bytes 1000 | tf_op jit(solution)/shard_map/gram_pair/pallas_call | solution.py:947
  196.2 7.9 %shares.4 = (bf16[1,1536,512]{2,1,0:T(8,128)(2,1)}, bf16[1,1536,512]{2,1,0:T(8,128)(2,1)}) custom-call(s32[1]{0:T(128)} %bitcast.me_ref, bf16[1536,1024]{1,0:T(8,128)(2,1)} %bitcast.130, bf16[2048,1024]{1,0:T(8,128)(2,1)} %refs_1_.3), custom_call_target="tpu_custom_call" | custom-call | flops 7408818688 | bytes 1000 | tf_op jit(solution)/shard_map/shares/pallas_call | solution.py:1007
  205.5 2.9 pair_back.1
  208.4 6.1 %collective-permute-start.12 = (bf16[6,16,1024]{2,1,0:T(8,128)(2,1)}, bf16[6,16,1024]{2,1,0:T(8,128)(2,1)S(1)}, u32[]{:S(2)}, u32[]{:S(2)}) collective-permute-start(bf16[6,16,1024]{2,1,0:T(8,128)(2,1)} %get-tuple-element.169), channel_id=1, source_target_pairs={{0,8},{4,12},{8,0},{12,4},{16,24},{20,28},{24,16},{28,20},{1,9},{5... | collective-permute-start | bytes 589832 | tf_op jit(solution)/shard_map/ppermute | solution.py:646
  214.6 1.8 collective-permute-start.13
  217.8 18.7 %inner_back.1 = (bf16[6,256,1024]{2,1,0:T(8,128)(2,1)}, f32[6,256,128]{2,1,0:T(8,128)}, f32[6,256,256]{2,1,0:T(8,128)}) custom-call(bf16[6,256,1024]{2,1,0:T(8,128)(2,1)} %get-tuple-element.181.x_ref, bf16[6,256,256]{2,1,0:T(8,128)(2,1)} %get-tuple-element.135.bc_ref, bf16[6,256,1024]{2,1,0:T(8,128)(2,1)} %get-tuple-element.136.xs_ref, ...), custom_call_target="tpu_custom_call" | custom-call | flops 21390000128 | bytes 1000 | tf_op jit(solution)/shard_map/inner_back/pallas_call | solution.py:626
  237.9 2.4 scan_back.1
  240.9 2.4 collective-permute-start.16
  244.7 10.7 %gram.1 = bf16[2048,1024]{1,0:T(8,128)(2,1)} custom-call(bf16[1536,2048]{1,0:T(8,128)(2,1)} %bitcast.121, bf16[1536,1024]{1,0:T(8,128)(2,1)} %bitcast.126), custom_call_target="tpu_custom_call" | custom-call | flops 12419999744 | bytes 1000 | tf_op jit(solution)/shard_map/gram/pallas_call | solution.py:626
  258.3 3.6 unpair_back.1
  261.9 2.3 add.165
  266.9 13.5 %collective-permute-done.19.end_other_ref = bf16[6,64,1024]{2,1,0:T(8,128)(2,1)S(1)} collective-permute-done((bf16[6,64,1024]{2,1,0:T(8,128)(2,1)S(1)}, bf16[6,64,1024]{2,1,0:T(8,128)(2,1)S(1)}, u32[]{:S(2)}, u32[]{:S(2)}) %collective-permute-start.19) | collective-permute-done | bytes 786464 | tf_op jit(solution)/shard_map/ppermute | solution.py:646
  281.2 25.3 %leave.1 = (bf16[6,256,1024]{2,1,0:T(8,128)(2,1)}, bf16[6,16,1024]{2,1,0:T(8,128)(2,1)}, bf16[6,16,256]{2,1,0:T(8,128)(2,1)}, bf16[6,256,256]{2,1,0:T(8,128)(2,1...) custom-call(s32[1]{0:T(128)} %bitcast.1.me_ref, ...), custom_call_target="tpu_custom_call" | custom-call | flops 32199999488 | bytes 1000 | tf_op jit(solution)/shard_map/leave/pallas_call | solution.py:626
  308.9 8.1 %shares.5 = (bf16[1,1536,512]{2,1,0:T(8,128)(2,1)}, bf16[1,1536,512]{2,1,0:T(8,128)(2,1)}) custom-call(s32[1]{0:T(128)} %bitcast.me_ref, bf16[1536,1024]{1,0:T(8,128)(2,1)} %bitcast.131, bf16[2048,1024]{1,0:T(8,128)(2,1)} %refs_1_.3), custom_call_target="tpu_custom_call" | custom-call | flops 7408818688 | bytes 1000 | tf_op jit(solution)/shard_map/shares/pallas_call | solution.py:1007
  319.8 3.0 add.171
  326.6 1.6 scatter-add.6
  328.3 10.7 %gram_pair.4 = (bf16[4,256,1024]{2,1,0:T(8,128)(2,1)}, bf16[4,256,1024]{2,1,0:T(8,128)(2,1)}) custom-call(s32[1]{0:T(128)} %bitcast.1.me_ref, bf16[1536,2048]{1,0:T(8,128)(2,1)} %bitcast.122, bf16[1536,1024]{1,0:T(8,128)(2,1)} %bitcast.115), custom_call_target="tpu_custom_call" | custom-call | flops 12348030976 | bytes 1000 | tf_op jit(solution)/shard_map/gram_pair/pallas_call | solution.py:947
  339.1 2.7 collective-permute-start.26
  342.9 6.5 %conv_bc.1 = (bf16[6,256,384]{2,1,0:T(8,128)(2,1)}, f32[6,8,256]{2,1,0:T(8,128)}, f32[8,256]{1,0:T(8,128)}) custom-call(bf16[6,288,256]{2,1,0:T(8,128)(2,1)} %maximum_select_fusion.d_ref, bf16[6,256,256]{2,1,0:T(8,128)(2,1)} %get-tuple-element.184.pre_bc_ref.pre_ref, bf16[6,16,256]{2,1,0:T(8,128)(2,1)} %get-tuple-element.185.halo_bc_ref.halo_ref, ...), custom_call_target="tpu_custom_call" | custom-call | flops 7245000192 | bytes 1000 | tf_op jit(solution)/shard_map/conv_bc/pallas_call | solution.py:626
  349.4 3.0 add.173
  352.4 7.3 %gram_pair.5 = (bf16[4,256,384]{2,1,0:T(8,128)(2,1)}, bf16[4,256,384]{2,1,0:T(8,128)(2,1)}) custom-call(s32[1]{0:T(128)} %bitcast.1.me_ref, bf16[1536,2048]{1,0:T(8,128)(2,1)} %bitcast.123, bf16[1536,384]{1,0:T(8,128)(2,1)} %bitcast.101), custom_call_target="tpu_custom_call" | custom-call | flops 4630511616 | bytes 1000 | tf_op jit(solution)/shard_map/gram_pair/pallas_call | solution.py:947
  359.7 15.0 %shares.6 = (bf16[1,1536,512]{2,1,0:T(8,128)(2,1)}, bf16[1,1536,512]{2,1,0:T(8,128)(2,1)}, f32[2,8,512]{2,1,0:T(8,128)}) custom-call(s32[1]{0:T(128)} %bitcast.me_ref, bf16[1536,1024]{1,0:T(8,128)(2,1)} %bitcast.127, bf16[2,2048,1024]{2,1,0:T(8,128)(2,1)} %bitcast.95, bf16[1536,1024]{1,0:T(8,128)(2,1)} %bitcast.116, bf16[2,2048,1024]{2,1,0:T(8,128)(2,1)} %bitcast.96, ...), custom_call_target="tpu_custom_call" | custom-call | flops 15743739904 | bytes 1000 | tf_op jit(solution)/shard_map/shares/pallas_call | solution.py:1007
  377.7 2.8 fusion.9
  380.5 7.9 %collective-permute-done.26 = bf16[4,256,1024]{2,1,0:T(8,128)(2,1)} collective-permute-done((bf16[4,256,1024]{2,1,0:T(8,128)(2,1)}, bf16[4,256,1024]{2,1,0:T(8,128)(2,1)}, u32[]{:S(2)}, u32[]{:S(2)}) %collective-permute-start.26) | collective-permute-done | bytes 2097184 | tf_op jit(solution)/shard_map/ppermute | solution.py:646
  388.4 3.9 add.174
  392.3 3.5 add.175
  396.3 14.5 %shares.7 = (bf16[1,1536,512]{2,1,0:T(8,128)(2,1)}, bf16[1,1536,512]{2,1,0:T(8,128)(2,1)}, f32[2,8,512]{2,1,0:T(8,128)}) custom-call(s32[1]{0:T(128)} %bitcast.me_ref, bf16[1536,1024]{1,0:T(8,128)(2,1)} %bitcast.128, bf16[2,2048,1024]{2,1,0:T(8,128)(2,1)} %bitcast.97, bf16[1536,1024]{1,0:T(8,128)(2,1)} %bitcast.117, bf16[2,2048,1024]{2,1,0:T(8,128)(2,1)} %bitcast.98, ...), custom_call_target="tpu_custom_call" | custom-call | flops 15743739904 | bytes 1000 | tf_op jit(solution)/shard_map/shares/pallas_call | solution.py:1007
  413.1 1.8 collective-permute-start.31
  415.0 2.8 collective-permute-done.31
  417.7 4.7 collective-permute-start.32
  422.4 1.7 collective-permute-start.37
  424.1 4.9 collective-permute-done.32
  429.1 3.8 collective-permute-start.33
  434.3 3.6 add.176
  437.9 2.4 collective-permute-done.33
  443.6 3.6 collective-permute-done.30
  447.2 3.3 fusion.45
  451.3 4.1 collective-permute-start.38
  461.1 2.1 convert_element_type.116
  464.6 1.6 slice_add_fusion.2
  466.3 4.7 collective-permute-start.39
  471.0 1.9 dynamic-slice_bitcast_fusion
  473.5 4.9 fusion.8
  482.2 3.7 collective-permute-done.36
  488.2 2.9 copy.46
  (230 shorter events, 71.3 us)
Async XLA Ops:
  7.2 124.3 %all-gather.2.cloned.1.call-start = ((), (), s32[]{:S(2)}) async-start(), calls=%async_computation.3 | async-start | bytes 7864320 | tf_op jit(solution)/shard_map/all_gather | solution.py:771
  7.9 453.2 %reduce-scatter.8.cloned.1.call-start = ((), (), s32[]{:S(2)}) async-start(), calls=%async_computation.6 | async-start | bytes 2621440 | tf_op jit(solution)/shard_map/reduce_scatter | solution.py:694
  8.8 19.6 %collective-permute-start = (bf16[6,8,2176]{2,1,0:T(8,128)(2,1)S(1)}, bf16[6,8,2176]{2,1,0:T(8,128)(2,1)S(1)}, u32[]{:S(2)}, u32[]{:S(2)}) collective-permute-start(bf16[6,8,2176]{2,1,0:T(8,128)(2,1)S(1)} %pad_maximum_fusion.1), channel_id=1, source_target_pairs={{0,4},{4,8},{8,12},{12,16},{16,20},{20,24},{24,28},{1,5},{5,9},{9,... | collective-permute-start | bytes 626696 | tf_op jit(solution)/shard_map/ppermute | solution.py:652
  13.7 10.3 %copy-start.12 = (bf16[2048,16]{0,1:T(8,128)(2,1)S(1)}, bf16[2048,16]{0,1:T(8,128)(2,1)}, u32[]{:S(2)}) copy-start(bf16[2048,16]{0,1:T(8,128)(2,1)} %param.25) | copy-start | bytes 196612
  13.7 10.6 %copy-start.44 = (f32[16]{0:T(128)S(1)}, f32[16]{0:T(128)}, u32[]{:S(2)}) copy-start(f32[16]{0:T(128)} %param.31) | copy-start | bytes 196
  13.8 10.7 %copy-start.25 = (f32[16]{0:T(128)S(1)}, f32[16]{0:T(128)}, u32[]{:S(2)}) copy-start(f32[16]{0:T(128)} %param.30) | copy-start | bytes 196
  13.8 11.3 %copy-start.20 = (f32[4,256]{1,0:T(4,128)S(1)}, f32[4,256]{1,0:T(4,128)}, u32[]{:S(2)}) copy-start(f32[4,256]{1,0:T(4,128)} %param.28) | copy-start | bytes 12292
  13.8 11.3 %copy-start.24 = (f32[256]{0:T(256)S(1)}, f32[256]{0:T(256)}, u32[]{:S(2)}) copy-start(f32[256]{0:T(256)} %param.29) | copy-start | bytes 3076
  13.8 11.9 %copy-start.17 = (f32[4,1024]{1,0:T(4,128)S(1)}, f32[4,1024]{1,0:T(4,128)}, u32[]{:S(2)}) copy-start(f32[4,1024]{1,0:T(4,128)} %param.26) | copy-start | bytes 49156
  13.8 11.9 %copy-start.22 = (f32[1024]{0:T(1024)S(1)}, f32[1024]{0:T(1024)}, u32[]{:S(2)}) copy-start(f32[1024]{0:T(1024)} %param.27) | copy-start | bytes 12292
  29.9 30.1 %copy-start.26 = (f32[16]{0:T(128)S(1)}, f32[16]{0:T(128)}, u32[]{:S(2)}) copy-start(f32[16]{0:T(128)} %param.32) | copy-start | bytes 196
  29.9 30.2 %copy-start.19 = (f32[1024]{0:T(1024)S(1)}, f32[1024]{0:T(1024)}, u32[]{:S(2)}) copy-start(f32[1024]{0:T(1024)} %param.33) | copy-start | bytes 12292
  58.2 20.2 %collective-permute-start.1 = (bf16[400,1024]{1,0:T(8,128)(2,1)}, bf16[400,1024]{1,0:T(8,128)(2,1)S(1)}, u32[]{:S(2)}, u32[]{:S(2)}) collective-permute-start(bf16[400,1024]{1,0:T(8,128)(2,1)} %get-tuple-element.141), channel_id=1, source_target_pairs={{0,4},{4,0},{8,12},{12,8},{16,20},{20,16},{24,28},{28,24},{1,5},{5... | collective-permute-start | bytes 2457608 | tf_op jit(solution)/shard_map/ppermute | solution.py:646
  82.3 15.6 %collective-permute-start.2 = (bf16[7,16,1024]{2,1,0:T(8,128)(2,1)}, bf16[7,16,1024]{2,1,0:T(8,128)(2,1)S(1)}, u32[]{:S(2)}, u32[]{:S(2)}) collective-permute-start(bf16[7,16,1024]{2,1,0:T(8,128)(2,1)} %get-tuple-element.144), channel_id=1, source_target_pairs={{0,8},{4,12},{8,0},{12,4},{16,24},{20,28},{24,16},{28,20},{1,9},{5... | collective-permute-start | bytes 688136 | tf_op jit(solution)/shard_map/ppermute | solution.py:646
  84.0 19.5 %collective-permute-start.3 = (bf16[7,16,1024]{2,1,0:T(8,128)(2,1)}, bf16[7,16,1024]{2,1,0:T(8,128)(2,1)S(1)}, u32[]{:S(2)}, u32[]{:S(2)}) collective-permute-start(bf16[7,16,1024]{2,1,0:T(8,128)(2,1)} %get-tuple-element.145), channel_id=1, source_target_pairs={{0,16},{4,20},{8,24},{12,28},{16,0},{20,4},{24,8},{28,12},{1,17},{... | collective-permute-start | bytes 688136 | tf_op jit(solution)/shard_map/ppermute | solution.py:646
  86.6 16.9 %collective-permute-start.4 = (bf16[7,16,1024]{2,1,0:T(8,128)(2,1)}, bf16[7,16,1024]{2,1,0:T(8,128)(2,1)S(1)}, u32[]{:S(2)}, u32[]{:S(2)}) collective-permute-start(bf16[7,16,1024]{2,1,0:T(8,128)(2,1)} %get-tuple-element.146), channel_id=1, source_target_pairs={{0,24},{4,28},{8,16},{12,20},{16,8},{20,12},{24,0},{28,4},{1,25},{... | collective-permute-start | bytes 688136 | tf_op jit(solution)/shard_map/ppermute | solution.py:646
  106.7 15.9 %collective-permute-start.5 = (bf16[6,16,1024]{2,1,0:T(8,128)(2,1)}, bf16[6,16,1024]{2,1,0:T(8,128)(2,1)S(1)}, u32[]{:S(2)}, u32[]{:S(2)}) collective-permute-start(bf16[6,16,1024]{2,1,0:T(8,128)(2,1)} %get-tuple-element.148), channel_id=1, source_target_pairs={{0,8},{4,12},{8,0},{12,4},{16,24},{20,28},{24,16},{28,20},{1,9},{5... | collective-permute-start | bytes 589832 | tf_op jit(solution)/shard_map/ppermute | solution.py:646
  109.7 15.8 %collective-permute-start.6 = (bf16[6,16,1024]{2,1,0:T(8,128)(2,1)}, bf16[6,16,1024]{2,1,0:T(8,128)(2,1)S(1)}, u32[]{:S(2)}, u32[]{:S(2)}) collective-permute-start(bf16[6,16,1024]{2,1,0:T(8,128)(2,1)} %get-tuple-element.149), channel_id=1, source_target_pairs={{0,16},{4,20},{8,24},{12,28},{16,0},{20,4},{24,8},{28,12},{1,17},{... | collective-permute-start | bytes 589832 | tf_op jit(solution)/shard_map/ppermute | solution.py:646
  110.8 14.8 %collective-permute-start.7 = (bf16[6,16,1024]{2,1,0:T(8,128)(2,1)}, bf16[6,16,1024]{2,1,0:T(8,128)(2,1)S(1)}, u32[]{:S(2)}, u32[]{:S(2)}) collective-permute-start(bf16[6,16,1024]{2,1,0:T(8,128)(2,1)} %get-tuple-element.150), channel_id=1, source_target_pairs={{0,24},{4,28},{8,16},{12,20},{16,8},{20,12},{24,0},{28,4},{1,25},{... | collective-permute-start | bytes 589832 | tf_op jit(solution)/shard_map/ppermute | solution.py:646
  129.9 14.9 %collective-permute-start.8 = (bf16[6,64,1024]{2,1,0:T(8,128)(2,1)}, bf16[6,64,1024]{2,1,0:T(8,128)(2,1)S(1)}, u32[]{:S(2)}, u32[]{:S(2)}) collective-permute-start(bf16[6,64,1024]{2,1,0:T(8,128)(2,1)} %get-tuple-element.152), channel_id=1, source_target_pairs={{0,4},{4,0},{8,12},{12,8},{16,20},{20,16},{24,28},{28,24},{1,5},{5... | collective-permute-start | bytes 2359304 | tf_op jit(solution)/shard_map/ppermute | solution.py:646
  157.5 1.4 collective-permute-start.9
  159.8 4.1 collective-permute-start.10
  183.9 20.7 %collective-permute-start.11 = (bf16[384,1024]{1,0:T(8,128)(2,1)}, bf16[384,1024]{1,0:T(8,128)(2,1)S(1)}, u32[]{:S(2)}, u32[]{:S(2)}) collective-permute-start(bf16[384,1024]{1,0:T(8,128)(2,1)} %get-tuple-element.162), channel_id=1, source_target_pairs={{0,4},{4,0},{8,12},{12,8},{16,20},{20,16},{24,28},{28,24},{1,5},{5... | collective-permute-start | bytes 2359304 | tf_op jit(solution)/shard_map/ppermute | solution.py:646
  204.1 57.9 %collective-permute-start.18 = (bf16[4,256,1024]{2,1,0:T(8,128)(2,1)}, bf16[4,256,1024]{2,1,0:T(8,128)(2,1)S(1)}, u32[]{:S(2)}, u32[]{:S(2)}) collective-permute-start(bf16[4,256,1024]{2,1,0:T(8,128)(2,1)} %get-tuple-element.180), channel_id=1, source_target_pairs={{0,4},{4,0},{8,12},{12,8},{16,20},{20,16},{24,28},{28,24},{1,5},{5... | collective-permute-start | bytes 6291464 | tf_op jit(solution)/shard_map/ppermute | solution.py:646
  208.4 28.1 %collective-permute-start.12 = (bf16[6,16,1024]{2,1,0:T(8,128)(2,1)}, bf16[6,16,1024]{2,1,0:T(8,128)(2,1)S(1)}, u32[]{:S(2)}, u32[]{:S(2)}) collective-permute-start(bf16[6,16,1024]{2,1,0:T(8,128)(2,1)} %get-tuple-element.169), channel_id=1, source_target_pairs={{0,8},{4,12},{8,0},{12,4},{16,24},{20,28},{24,16},{28,20},{1,9},{5... | collective-permute-start | bytes 589832 | tf_op jit(solution)/shard_map/ppermute | solution.py:646
  214.6 21.9 %collective-permute-start.13 = (bf16[6,16,1024]{2,1,0:T(8,128)(2,1)}, bf16[6,16,1024]{2,1,0:T(8,128)(2,1)S(1)}, u32[]{:S(2)}, u32[]{:S(2)}) collective-permute-start(bf16[6,16,1024]{2,1,0:T(8,128)(2,1)} %get-tuple-element.170), channel_id=1, source_target_pairs={{0,16},{4,20},{8,24},{12,28},{16,0},{20,4},{24,8},{28,12},{1,17},{... | collective-permute-start | bytes 589832 | tf_op jit(solution)/shard_map/ppermute | solution.py:646
  216.4 20.2 %collective-permute-start.14 = (bf16[6,16,1024]{2,1,0:T(8,128)(2,1)}, bf16[6,16,1024]{2,1,0:T(8,128)(2,1)S(1)}, u32[]{:S(2)}, u32[]{:S(2)}) collective-permute-start(bf16[6,16,1024]{2,1,0:T(8,128)(2,1)} %get-tuple-element.171), channel_id=1, source_target_pairs={{0,24},{4,28},{8,16},{12,20},{16,8},{20,12},{24,0},{28,4},{1,25},{... | collective-permute-start | bytes 589832 | tf_op jit(solution)/shard_map/ppermute | solution.py:646
  240.3 15.1 %collective-permute-start.15 = (bf16[6,16,1024]{2,1,0:T(8,128)(2,1)}, bf16[6,16,1024]{2,1,0:T(8,128)(2,1)S(1)}, u32[]{:S(2)}, u32[]{:S(2)}) collective-permute-start(bf16[6,16,1024]{2,1,0:T(8,128)(2,1)} %get-tuple-element.175), channel_id=1, source_target_pairs={{0,8},{4,12},{8,0},{12,4},{16,24},{20,28},{24,16},{28,20},{1,9},{5... | collective-permute-start | bytes 589832 | tf_op jit(solution)/shard_map/ppermute | solution.py:646
  240.9 16.1 %collective-permute-start.16 = (bf16[6,16,1024]{2,1,0:T(8,128)(2,1)}, bf16[6,16,1024]{2,1,0:T(8,128)(2,1)S(1)}, u32[]{:S(2)}, u32[]{:S(2)}) collective-permute-start(bf16[6,16,1024]{2,1,0:T(8,128)(2,1)} %get-tuple-element.176), channel_id=1, source_target_pairs={{0,16},{4,20},{8,24},{12,28},{16,0},{20,4},{24,8},{28,12},{1,17},{... | collective-permute-start | bytes 589832 | tf_op jit(solution)/shard_map/ppermute | solution.py:646
  243.2 13.7 %collective-permute-start.17 = (bf16[6,16,1024]{2,1,0:T(8,128)(2,1)}, bf16[6,16,1024]{2,1,0:T(8,128)(2,1)S(1)}, u32[]{:S(2)}, u32[]{:S(2)}) collective-permute-start(bf16[6,16,1024]{2,1,0:T(8,128)(2,1)} %get-tuple-element.177), channel_id=1, source_target_pairs={{0,24},{4,28},{8,16},{12,20},{16,8},{20,12},{24,0},{28,4},{1,25},{... | collective-permute-start | bytes 589832 | tf_op jit(solution)/shard_map/ppermute | solution.py:646
  264.3 206.8 %reduce-scatter.4.cloned.1.call-start = ((), (), s32[]{:S(2)}) async-start(), calls=%async_computation.4 | async-start | bytes 5242880 | tf_op jit(solution)/shard_map/reduce_scatter | solution.py:694
  265.4 15.0 %collective-permute-start.19 = (bf16[6,64,1024]{2,1,0:T(8,128)(2,1)S(1)}, bf16[6,64,1024]{2,1,0:T(8,128)(2,1)S(1)}, u32[]{:S(2)}, u32[]{:S(2)}) collective-permute-start(bf16[6,64,1024]{2,1,0:T(8,128)(2,1)S(1)} %copy-done.31), channel_id=1, source_target_pairs={{0,4},{4,0},{8,12},{12,8},{16,20},{20,16},{24,28},{28,24},{1,5},{5... | collective-permute-start | bytes 2359304 | tf_op jit(solution)/shard_map/ppermute | solution.py:646
  266.8 53.0 %collective-permute-start.23 = (bf16[1,1536,512]{2,1,0:T(8,128)(2,1)}, bf16[1,1536,512]{2,1,0:T(8,128)(2,1)}, u32[]{:S(2)}, u32[]{:S(2)}) collective-permute-start(bf16[1,1536,512]{2,1,0:T(8,128)(2,1)} %get-tuple-element.200), channel_id=1, source_target_pairs={{0,1},{1,0},{2,3},{3,2},{4,5},{5,4},{6,7},{7,6},{8,9},{9,8},{10,11... | collective-permute-start | bytes 4718600 | tf_op jit(solution)/shard_map/ppermute | solution.py:646
  266.8 220.1 %reduce-scatter.6.cloned.1.call-start = ((), (), s32[]{:S(2)}) async-start(), calls=%async_computation.5 | async-start | bytes 2621440 | tf_op jit(solution)/shard_map/reduce_scatter | solution.py:694
  307.5 11.7 %copy-start = (bf16[6,256,256]{2,1,0:T(8,128)(2,1)S(1)}, bf16[6,256,256]{2,1,0:T(8,128)(2,1)}, u32[]{:S(2)}) copy-start(bf16[6,256,256]{2,1,0:T(8,128)(2,1)} %get-tuple-element.194) | copy-start | bytes 2359300
  307.5 10.5 %collective-permute-start.20 = (bf16[6,3,1280]{2,1,0:T(4,128)(2,1)S(1)}, bf16[6,3,1280]{2,1,0:T(4,128)(2,1)S(1)}, u32[]{:S(2)}, u32[]{:S(2)}) collective-permute-start(bf16[6,3,1280]{2,1,0:T(4,128)(2,1)S(1)} %pad_maximum_fusion.3), channel_id=1, source_target_pairs={{4,0},{8,4},{12,8},{16,12},{20,16},{24,20},{28,24},{5,1},{9,5},{13... | collective-permute-start | bytes 138248 | tf_op jit(solution)/shard_map/ppermute | solution.py:652
  319.2 3.6 collective-permute-start.21
  319.3 30.0 %collective-permute-start.25 = (bf16[1,1536,512]{2,1,0:T(8,128)(2,1)}, bf16[1,1536,512]{2,1,0:T(8,128)(2,1)}, u32[]{:S(2)}, u32[]{:S(2)}) collective-permute-start(bf16[1,1536,512]{2,1,0:T(8,128)(2,1)} %get-tuple-element.207), channel_id=1, source_target_pairs={{0,1},{1,0},{2,3},{3,2},{4,5},{5,4},{6,7},{7,6},{8,9},{9,8},{10,11... | collective-permute-start | bytes 4718600 | tf_op jit(solution)/shard_map/ppermute | solution.py:646
  324.2 14.7 %collective-permute-start.22 = (bf16[3,288,256]{2,1,0:T(8,128)(2,1)S(1)}, bf16[3,288,256]{2,1,0:T(8,128)(2,1)S(1)}, u32[]{:S(2)}, u32[]{:S(2)}) collective-permute-start(bf16[3,288,256]{2,1,0:T(8,128)(2,1)S(1)} %constant_dynamic-slice_fusion.1), channel_id=1, source_target_pairs={{0,2},{1,3},{2,0},{3,1},{4,6},{5,7},{6,4},{7,5},{8,10},{9,11},{10,... | collective-permute-start | bytes 1327112 | tf_op jit(solution)/shard_map/ppermute | solution.py:646
  339.0 2.8 collective-permute-start.24
  339.1 49.3 %collective-permute-start.26 = (bf16[4,256,1024]{2,1,0:T(8,128)(2,1)}, bf16[4,256,1024]{2,1,0:T(8,128)(2,1)}, u32[]{:S(2)}, u32[]{:S(2)}) collective-permute-start(bf16[4,256,1024]{2,1,0:T(8,128)(2,1)} %get-tuple-element.212), channel_id=1, source_target_pairs={{0,4},{4,0},{8,12},{12,8},{16,20},{20,16},{24,28},{28,24},{1,5},{5... | collective-permute-start | bytes 6291464 | tf_op jit(solution)/shard_map/ppermute | solution.py:646
  359.7 16.1 %copy-start.9 = (f32[6,256,128]{2,1,0:T(8,128)S(1)}, f32[6,256,128]{2,1,0:T(8,128)}, u32[]{:S(2)}) copy-start(f32[6,256,128]{2,1,0:T(8,128)} %get-tuple-element.138.aux_ref) | copy-start | bytes 2359300
  359.7 17.2 %copy-start.13 = (f32[8,1024]{1,0:T(8,128)S(1)}, f32[8,1024]{1,0:T(8,128)}, u32[]{:S(2)}) copy-start(f32[8,1024]{1,0:T(8,128)} %get-tuple-element.222) | copy-start | bytes 98308
  359.7 17.2 %copy-start.14 = (f32[8,1024]{1,0:T(8,128)S(1)}, f32[8,1024]{1,0:T(8,128)}, u32[]{:S(2)}) copy-start(f32[8,1024]{1,0:T(8,128)} %get-tuple-element.221) | copy-start | bytes 98308
  374.7 17.5 %collective-permute-start.27 = (bf16[1,1536,512]{2,1,0:T(8,128)(2,1)}, bf16[1,1536,512]{2,1,0:T(8,128)(2,1)}, u32[]{:S(2)}, u32[]{:S(2)}) collective-permute-start(bf16[1,1536,512]{2,1,0:T(8,128)(2,1)} %get-tuple-element.214), channel_id=1, source_target_pairs={{0,1},{1,0},{2,3},{3,2},{4,5},{5,4},{6,7},{7,6},{8,9},{9,8},{10,11... | collective-permute-start | bytes 4718600 | tf_op jit(solution)/shard_map/ppermute | solution.py:646
  376.4 57.9 %collective-permute-start.28 = (bf16[1,1536,512]{2,1,0:T(8,128)(2,1)}, bf16[1,1536,512]{2,1,0:T(8,128)(2,1)}, u32[]{:S(2)}, u32[]{:S(2)}) collective-permute-start(bf16[1,1536,512]{2,1,0:T(8,128)(2,1)} %add.171), channel_id=1, source_target_pairs={{0,2},{1,3},{2,0},{3,1},{4,6},{5,7},{6,4},{7,5},{8,10},{9,11},{10,... | collective-permute-start | bytes 4718600 | tf_op jit(solution)/shard_map/ppermute | solution.py:646
  377.7 10.7 %copy-start.2 = (bf16[4,256,1024]{2,1,0:T(8,128)(2,1)S(1)}, bf16[4,256,1024]{2,1,0:T(8,128)(2,1)}, u32[]{:S(2)}) copy-start(bf16[4,256,1024]{2,1,0:T(8,128)(2,1)} %get-tuple-element.211) | copy-start | bytes 6291460
  395.7 17.4 %copy-start.18 = (f32[8,256]{1,0:T(8,128)S(1)}, f32[8,256]{1,0:T(8,128)}, u32[]{:S(2)}) copy-start(f32[8,256]{1,0:T(8,128)} %get-tuple-element.223) | copy-start | bytes 24580
  395.7 17.4 %copy-start.23 = (f32[8,128]{1,0:T(8,128)S(1)}, f32[8,128]{1,0:T(8,128)}, u32[]{:S(2)}) copy-start(f32[8,128]{1,0:T(8,128)} %get-tuple-element.224) | copy-start | bytes 12292
  395.7 51.5 %collective-permute-start.30 = (bf16[1,1536,512]{2,1,0:T(8,128)(2,1)}, bf16[1,1536,512]{2,1,0:T(8,128)(2,1)}, u32[]{:S(2)}, u32[]{:S(2)}) collective-permute-start(bf16[1,1536,512]{2,1,0:T(8,128)(2,1)} %add.175), channel_id=1, source_target_pairs={{0,2},{1,3},{2,0},{3,1},{4,6},{5,7},{6,4},{7,5},{8,10},{9,11},{10,... | collective-permute-start | bytes 4718600 | tf_op jit(solution)/shard_map/ppermute | solution.py:646
  410.9 32.8 %collective-permute-start.29 = (bf16[1,1536,512]{2,1,0:T(8,128)(2,1)}, bf16[1,1536,512]{2,1,0:T(8,128)(2,1)}, u32[]{:S(2)}, u32[]{:S(2)}) collective-permute-start(bf16[1,1536,512]{2,1,0:T(8,128)(2,1)} %get-tuple-element.219), channel_id=1, source_target_pairs={{0,1},{1,0},{2,3},{3,2},{4,5},{5,4},{6,7},{7,6},{8,9},{9,8},{10,11... | collective-permute-start | bytes 4718600 | tf_op jit(solution)/shard_map/ppermute | solution.py:646
  413.1 4.6 collective-permute-start.31
  417.7 11.4 %collective-permute-start.32 = (f32[16,1024]{1,0:T(8,128)S(1)}, f32[16,1024]{1,0:T(8,128)S(1)}, u32[]{:S(2)}, u32[]{:S(2)}) collective-permute-start(f32[16,1024]{1,0:T(8,128)S(1)} %fusion.43), channel_id=1, source_target_pairs={{0,8},{4,12},{8,0},{12,4},{16,24},{20,28},{24,16},{28,20},{1,9},{5... | collective-permute-start | bytes 196616 | tf_op jit(solution)/shard_map/ppermute | solution.py:646
  422.4 28.1 %collective-permute-start.37 = (bf16[4,256,384]{2,1,0:T(8,128)(2,1)}, bf16[4,256,384]{2,1,0:T(8,128)(2,1)S(1)}, u32[]{:S(2)}, u32[]{:S(2)}) collective-permute-start(bf16[4,256,384]{2,1,0:T(8,128)(2,1)} %get-tuple-element.228), channel_id=1, source_target_pairs={{0,4},{4,0},{8,12},{12,8},{16,20},{20,16},{24,28},{28,24},{1,5},{5... | collective-permute-start | bytes 2359304 | tf_op jit(solution)/shard_map/ppermute | solution.py:646
  429.1 11.2 %collective-permute-start.33 = (f32[16,1024]{1,0:T(8,128)S(1)}, f32[16,1024]{1,0:T(8,128)S(1)}, u32[]{:S(2)}, u32[]{:S(2)}) collective-permute-start(f32[16,1024]{1,0:T(8,128)S(1)} %add.186), channel_id=1, source_target_pairs={{0,16},{4,20},{8,24},{12,28},{16,0},{20,4},{24,8},{28,12},{1,17},{... | collective-permute-start | bytes 196616 | tf_op jit(solution)/shard_map/ppermute | solution.py:646
  434.3 12.9 %copy-start.6 = (bf16[1,1536,512]{2,1,0:T(8,128)(2,1)S(1)}, bf16[1,1536,512]{2,1,0:T(8,128)(2,1)}, u32[]{:S(2)}) copy-start(bf16[1,1536,512]{2,1,0:T(8,128)(2,1)} %get-tuple-element.218) | copy-start | bytes 4718596
  440.3 16.8 %copy-start.11 = (f32[16,1024]{1,0:T(8,128)}, f32[16,1024]{1,0:T(8,128)S(1)}, u32[]{:S(2)}) copy-start(f32[16,1024]{1,0:T(8,128)S(1)} %add.187) | copy-start | bytes 196612
  440.4 1.3 collective-permute-start.34
  441.6 8.8 %copy-start.21 = (f32[2,512]{1,0:T(2,128)}, f32[2,512]{1,0:T(2,128)S(1)}, u32[]{:S(2)}) copy-start(f32[2,512]{1,0:T(2,128)S(1)} %collective-permute-done.34) | copy-start | bytes 12292
  442.2 16.9 %collective-permute-start.35 = (f32[1,512]{1,0:T(1,128)}, f32[1,512]{1,0:T(1,128)}, u32[]{:S(2)}, u32[]{:S(2)}) collective-permute-start(f32[1,512]{1,0:T(1,128)} %slice_add_fusion.5), channel_id=1, source_target_pairs={{0,2},{1,3},{2,0},{3,1},{4,6},{5,7},{6,4},{7,5},{8,10},{9,11},{10,... | collective-permute-start | bytes 6152 | tf_op jit(solution)/shard_map/ppermute | solution.py:646
  451.3 13.3 %collective-permute-start.38 = (bf16[2,256,384]{2,1,0:T(8,128)(2,1)}, bf16[2,256,384]{2,1,0:T(8,128)(2,1)}, u32[]{:S(2)}, u32[]{:S(2)}) collective-permute-start(bf16[2,256,384]{2,1,0:T(8,128)(2,1)} %get-tuple-element.281), channel_id=1, source_target_pairs={{0,8},{4,12},{8,0},{12,4},{16,24},{20,28},{24,16},{28,20},{1,9},{5... | collective-permute-start | bytes 1179656 | tf_op jit(solution)/shard_map/ppermute | solution.py:646
  459.1 14.4 %copy-start.15 = (f32[6,1,256]{2,0,1:T(8,128)S(1)}, f32[6,1,256]{2,0,1:T(8,128)}, u32[]{:S(2)}) copy-start(f32[6,1,256]{2,0,1:T(8,128)} %copy.64) | copy-start | bytes 18436
  466.3 13.4 %collective-permute-start.39 = (bf16[1,256,384]{2,1,0:T(8,128)(2,1)}, bf16[1,256,384]{2,1,0:T(8,128)(2,1)}, u32[]{:S(2)}, u32[]{:S(2)}) collective-permute-start(bf16[1,256,384]{2,1,0:T(8,128)(2,1)} %slice_add_fusion.2), channel_id=1, source_target_pairs={{0,16},{4,20},{8,24},{12,28},{16,0},{20,4},{24,8},{28,12},{1,17},{... | collective-permute-start | bytes 589832 | tf_op jit(solution)/shard_map/ppermute | solution.py:646
  472.9 13.0 %collective-permute-start.36 = (bf16[256,1024]{1,0:T(8,128)(2,1)}, bf16[256,1024]{1,0:T(8,128)(2,1)}, u32[]{:S(2)}, u32[]{:S(2)}) collective-permute-start(bf16[256,1024]{1,0:T(8,128)(2,1)} %dynamic-slice_bitcast_fusion), channel_id=1, source_target_pairs={{0,4},{4,0},{8,12},{12,8},{16,20},{20,16},{24,28},{28,24},{1,5},{5... | collective-permute-start | bytes 1572872 | tf_op jit(solution)/shard_map/ppermute | solution.py:646
  (26 other events, 65.0 us)
Sparse Core Ops, SparseCore 0:
  9.6 49.0 all-gather.1
  264.4 44.7 reduce-scatter.7
  311.5 76.0 reduce-scatter.3
  392.4 50.7 reduce-scatter.5

commit v4 on v3

--- a/solution.py
+++ b/solution.py
@@ -766,11 +766,12 @@
     _, width = chunk_grid(groups, half, own)
 
     seg_lanes = jnp.broadcast_to(segments[:, -8:, None].astype(BF), (seqs, 8, LANES))
-    halo = shift(jnp.concatenate([tokens[:, -8:], seg_lanes], axis=2), "seq", 1)
+    cot_full = lax.all_gather(cotangent, "head", axis=2, tiled=True)
+
+    w_in = lax.optimization_barrier(jnp.transpose(w_zx, (1, 0, 2)))
+    halo = jnp.concatenate([after(tokens, w_in)[:, -8:], seg_lanes], axis=2)
+    halo = shift(halo, "seq", 1)
     tok_halo, seg_halo = halo[..., :model], halo[..., model]
-    cot_full = lax.all_gather(cotangent, "head", axis=2, tiled=True)
-
-    w_in = lax.optimization_barrier(jnp.transpose(w_zx, (1, 0, 2)))
     w_dt = pad_lanes(w_dt, LANES)
     w_small = jnp.concatenate([w_bc, w_dt], axis=1)
     seg_rows = [jnp.pad(seg_halo.astype(F32), ((0, 0), (LANES - 8, 0))), segments.astype(F32)]
@@ -1147,18 +1148,20 @@
     terms = [(after(d_z_rows, small_sides[1], out_near), w_in, 0), (d_x_rows, w_in, 1)]
     terms.append((d_dt_rows, w_dt, 0))
     grad_far, norm_far = share_sum(terms, 1, True)
-    late_total = pair_sum((late_sides[0], after(late_sides[1], grad_far[1])))
+    own_sum = fold((out_far, after(out_near, grad_far[1])), "head", 2)
+    own_sum = own_sum.reshape(seqs, span, share)
+    late_total = pair_sum((late_sides[0], after(late_sides[1], own_sum)))
     grad_far = core_sum(grad_far[0], after(grad_far[1], late_total))
-    own_sum = fold((out_far, after(out_near, grad_far)), "head", 2)
-    own_sum = own_sum.reshape(seqs, span, share)
     terms[0] = (after(d_z_rows, grad_far), w_in, 0)
     grad_near, norm_near = share_sum(terms, 0, True)
     grad_near = core_sum(grad_near[0], after(grad_near[1], own_sum))
-    small_next = fold_step((small_sides[0], after(small_sides[1], grad_near)), "seq", 1)
+    small_sum = after(small_sides[1], grad_near) + swap(small_sides[0], "seq", 1)
     tokens_own = lax.dynamic_slice_in_dim(tokens, offset, share, 2).astype(F32)
     layer_out = (tokens_own + own_sum.astype(F32)).astype(BF)
     own_grad = fold((grad_far, grad_near), "head", 2).reshape(seqs, span, share).astype(F32)
-    late_s = fold(small_next, "seq", 2).astype(F32)
+    late_s = small_sum[0].astype(F32)
+    for m in range(1, groups):
+        late_s = late_s + swap(small_sum[m], "seq", 2 * m).astype(F32)
     out_grad_own = spread_sum(out_total).astype(F32)
     x_at = lax.axis_index("seq") % 2
     gate_own = lax.dynamic_index_in_dim(gate_total, x_at, 0, False)

time: 503 us -> 492 us (0.978)
    ppermute x38 -> x39, starting transfers between devices: 61.2 us -> 56.9 us  [swap(): return lax.ppermute(value, axis, [(i, i ^ mask) for i in range(count)])]
    ppermute x38 -> x39, waiting for transfers between devices: 75.2 us -> 73.1 us  [swap(): return lax.ppermute(value, axis, [(i, i ^ mask) for i in range(count)])]
  transfers between devices with their start and end apart: 44 -> 45, of which waited for: 16 -> 15; matrix products, arithmetic and copies ran while one was open for 20% -> 19% of each run, Pallas kernels for 39% -> 39%
where the time goes in v4:
time: 492 us; the launch traced here: 487 us
  Pallas kernels  223 us (45%)
  waiting for transfers between devices  73.8 us (15%)
  starting transfers between devices  63.6 us (13%)
  other arithmetic  47.8 us (10%)
  local copies, waits for them, and re-layouts  38.8 us (8%)
  matrix products  25 us (5%)
  between operations  14.7 us (3%)
    pallas_call x14, Pallas kernels, call(): pl.pallas_call(body, grid=(grid,), in_specs=in_specs, out_specs=out_specs...  149 us
    ppermute x39, waiting for transfers between devices, swap(): return lax.ppermute(value, axis, [(i, i ^ mask) for i in range(count)])  73.1 us
    ppermute x39, starting transfers between devices, swap(): return lax.ppermute(value, axis, [(i, i ^ mask) for i in range(count)])  56.9 us
    pallas_call x4, Pallas kernels, share_sum(): pl.pallas_call(functools.partial(share_kernel, len(terms), summed), grid_...  45.6 us
    pallas_call x3, Pallas kernels, chunk_pair(): pl.pallas_call(gram_pair_kernel, grid_spec=pltpu.PrefetchScalarGridSpec(n...  28.8 us
    dot_general x3, matrix products, dot(): lax.dot_general(a, b, (contract, ((), ())), preferred_element_type=F32, p...  25 us
    unnamed x95, local copies, waits for them, and re-layouts  23.2 us
  transfers between devices with their start and end apart: 45, of which 15 were waited for; matrix products, arithmetic and copies ran while one was open for 19% of the time, Pallas kernels for 39%

profile of v4, /device:TPU:0, one launch (start us, length us, event | category | flops | bytes accessed | tf_op | source)
XLA Modules:
  0.0 487.1 jit_solution(6051180273304710768)
XLA Ops:
  8.0 9.5 %copy.63 = bf16[2048,2,1024]{2,0,1:T(8,128)(2,1)} copy(bf16[2048,2,1024]{2,1,0:T(2,128)(2,1)} %param.23) | data formatting | bytes 16777216 | tf_op args[3]
  17.7 5.2 %collective-permute-start = (bf16[6,8,2176]{2,1,0:T(8,128)(2,1)S(1)}, bf16[6,8,2176]{2,1,0:T(8,128)(2,1)S(1)}, u32[]{:S(2)}, u32[]{:S(2)}) collective-permute-start(bf16[6,8,2176]{2,1,0:T(8,128)(2,1)S(1)} %pad_maximum_fusion.1), channel_id=1, source_target_pairs={{0,4},{4,8},{8,12},{12,16},{16,20},{20,24},{24,28},{1,5},{5,9},{9,... | collective-permute-start | bytes 626696 | tf_op jit(solution)/shard_map/ppermute | solution.py:652
  28.8 28.1 %front.1 = (bf16[6,256,2048]{2,1,0:T(8,128)(2,1)}, bf16[6,256,1024]{2,1,0:T(8,128)(2,1)}, bf16[6,256,256]{2,1,0:T(8,128)(2,1)}, bf16[6,16,1024]{2,1,0:T(8,128)(2...) custom-call(s32[1]{0:T(128)} %bitcast.1.me_ref, ...), custom_call_target="tpu_custom_call" | custom-call | flops 34500001792 | bytes 1000 | tf_op jit(solution)/shard_map/front/pallas_call | solution.py:626
  57.0 2.3 collective-permute-start.1
  60.1 16.9 %collective-permute-done.1.other_ref = bf16[400,1024]{1,0:T(8,128)(2,1)S(1)} collective-permute-done((bf16[400,1024]{1,0:T(8,128)(2,1)}, bf16[400,1024]{1,0:T(8,128)(2,1)S(1)}, u32[]{:S(2)}, u32[]{:S(2)}) %collective-permute-start.1) | collective-permute-done | bytes 819232 | tf_op jit(solution)/shard_map/ppermute | solution.py:646
  77.8 3.0 pair.1
  80.8 2.6 collective-permute-start.2
  83.5 2.6 collective-permute-start.3
  86.1 11.2 %fusion.15.gate_ref = bf16[6,256,1024]{2,1,0:T(8,128)(2,1)} fusion(bf16[6,256,2048]{2,1,0:T(8,128)(2,1)} %get-tuple-element.141, bf16[2,2048,1024]{2,1,0:T(8,128)(2,1)} %bitcast.100), kind=kOutput, calls=%fused_computation.20 | convolution fusion | flops 6444023808 | bytes 13631488 | tf_op jit(solution)/shard_map/dot_general | solution.py:27
  97.2 4.9 collective-permute-done.3.rest_2_
  102.9 2.5 scan.1
  105.4 2.9 collective-permute-start.5
  110.8 10.4 %inner.1.inner_ref = f32[6,256,1024]{2,1,0:T(8,128)} custom-call(bf16[6,256,256]{2,1,0:T(8,128)(2,1)} %get-tuple-element.137.bc_ref, bf16[6,256,1024]{2,1,0:T(8,128)(2,1)} %get-tuple-element.138.xs_ref, f32[6,256,128]{2,1,0:T(8,128)} %get-tuple-element.139.cum_ref, f32[6,256,128]{2,1,0:T(8,128)} %get-tuple-element.140.aux_ref, ...), custom_call_target="tpu_custom_call" | custom-call | flops 11845000192 | bytes 1000 | tf_op jit(solution)/shard_map/inner/pallas_call | solution.py:626
  121.2 2.7 collective-permute-done.6.rest_2_
  124.6 3.6 unpair.1
  129.1 11.4 %fusion.12.e_ref = bf16[6,256,1024]{2,1,0:T(8,128)(2,1)} fusion(bf16[6,256,2048]{2,1,0:T(8,128)(2,1)} %all-gather.2.cloned.1.call-done, bf16[2048,1024]{1,0:T(8,128)(2,1)} %refs_1_.3), kind=kOutput, calls=%fused_computation.19 | convolution fusion | flops 6444023808 | bytes 13631488 | tf_op jit(solution)/shard_map/dot_general | solution.py:27
  140.5 2.8 collective-permute-done.8.other_ref
  144.2 11.9 %sums.1 = f32[6,8,256]{2,1,0:T(8,128)} custom-call(s32[1]{0:T(128)} %bitcast.1.me_ref, bf16[6,256,1024]{2,1,0:T(8,128)(2,1)} %get-tuple-element.183.x_ref, bf16[6,256,256]{2,1,0:T(8,128)(2,1)} %get-tuple-element.137.bc_ref, f32[6,256,1024]{2,1,0:T(8,128)} %inner.1.inner_ref, bf16[6,256,1024]{2,1,0:T(8,128)(2,1)} %fusion.15.gate_ref, ...), custom_call_target="tpu_custom_call" | custom-call | flops 13799999488 | bytes 1000 | tf_op jit(solution)/shard_map/sums/pallas_call | solution.py:626
  158.3 1.7 collective-permute-start.10
  159.9 2.4 collective-permute-done.10
  163.0 19.4 %gate_back.1 = (bf16[6,256,1024]{2,1,0:T(8,128)(2,1)}, bf16[6,256,1024]{2,1,0:T(8,128)(2,1)}, bf16[6,256,1024]{2,1,0:T(8,128)(2,1)}, f32[6,256,128]{2,1,0:T(8,12...) custom-call(s32[1]{0:T(128)} %bitcast.1.me_ref, ...), custom_call_target="tpu_custom_call" | custom-call | flops 24149999616 | bytes 1000 | tf_op jit(solution)/shard_map/gate_back/pallas_call | solution.py:626
  183.4 10.7 %gram_pair.3 = (bf16[4,256,1024]{2,1,0:T(8,128)(2,1)}, bf16[4,256,1024]{2,1,0:T(8,128)(2,1)}) custom-call(s32[1]{0:T(128)} %bitcast.1.me_ref, bf16[1536,2048]{1,0:T(8,128)(2,1)} %bitcast.126, bf16[1536,1024]{1,0:T(8,128)(2,1)} %bitcast.135), custom_call_target="tpu_custom_call" | custom-call | flops 12348030976 | bytes 1000 | tf_op jit(solution)/shard_map/gram_pair/pallas_call | solution.py:948
  194.1 7.9 %shares.4 = (bf16[1,1536,512]{2,1,0:T(8,128)(2,1)}, bf16[1,1536,512]{2,1,0:T(8,128)(2,1)}) custom-call(s32[1]{0:T(128)} %bitcast.me_ref, bf16[1536,1024]{1,0:T(8,128)(2,1)} %bitcast.136, bf16[2048,1024]{1,0:T(8,128)(2,1)} %refs_1_.3), custom_call_target="tpu_custom_call" | custom-call | flops 7408818688 | bytes 1000 | tf_op jit(solution)/shard_map/shares/pallas_call | solution.py:1008
  204.0 2.9 pair_back.1
  206.9 6.4 %collective-permute-start.12 = (bf16[6,16,1024]{2,1,0:T(8,128)(2,1)}, bf16[6,16,1024]{2,1,0:T(8,128)(2,1)S(1)}, u32[]{:S(2)}, u32[]{:S(2)}) collective-permute-start(bf16[6,16,1024]{2,1,0:T(8,128)(2,1)} %get-tuple-element.171), channel_id=1, source_target_pairs={{0,8},{4,12},{8,0},{12,4},{16,24},{20,28},{24,16},{28,20},{1,9},{5... | collective-permute-start | bytes 589832 | tf_op jit(solution)/shard_map/ppermute | solution.py:646
  213.3 1.8 collective-permute-start.13
  216.6 18.7 %inner_back.1 = (bf16[6,256,1024]{2,1,0:T(8,128)(2,1)}, f32[6,256,128]{2,1,0:T(8,128)}, f32[6,256,256]{2,1,0:T(8,128)}) custom-call(bf16[6,256,1024]{2,1,0:T(8,128)(2,1)} %get-tuple-element.183.x_ref, bf16[6,256,256]{2,1,0:T(8,128)(2,1)} %get-tuple-element.137.bc_ref, bf16[6,256,1024]{2,1,0:T(8,128)(2,1)} %get-tuple-element.138.xs_ref, ...), custom_call_target="tpu_custom_call" | custom-call | flops 21390000128 | bytes 1000 | tf_op jit(solution)/shard_map/inner_back/pallas_call | solution.py:626
  236.7 2.4 scan_back.1
  239.6 2.4 collective-permute-start.16
  243.4 10.7 %gram.1 = bf16[2048,1024]{1,0:T(8,128)(2,1)} custom-call(bf16[1536,2048]{1,0:T(8,128)(2,1)} %bitcast.127, bf16[1536,1024]{1,0:T(8,128)(2,1)} %bitcast.132), custom_call_target="tpu_custom_call" | custom-call | flops 12419999744 | bytes 1000 | tf_op jit(solution)/shard_map/gram/pallas_call | solution.py:626
  257.1 3.6 unpair_back.1
  260.7 2.3 add.162
  265.1 14.1 %collective-permute-done.19.end_other_ref = bf16[6,64,1024]{2,1,0:T(8,128)(2,1)S(1)} collective-permute-done((bf16[6,64,1024]{2,1,0:T(8,128)(2,1)S(1)}, bf16[6,64,1024]{2,1,0:T(8,128)(2,1)S(1)}, u32[]{:S(2)}, u32[]{:S(2)}) %collective-permute-start.19) | collective-permute-done | bytes 786464 | tf_op jit(solution)/shard_map/ppermute | solution.py:646
  280.0 25.3 %leave.1 = (bf16[6,256,1024]{2,1,0:T(8,128)(2,1)}, bf16[6,16,1024]{2,1,0:T(8,128)(2,1)}, bf16[6,16,256]{2,1,0:T(8,128)(2,1)}, bf16[6,256,256]{2,1,0:T(8,128)(2,1...) custom-call(s32[1]{0:T(128)} %bitcast.1.me_ref, ...), custom_call_target="tpu_custom_call" | custom-call | flops 32199999488 | bytes 1000 | tf_op jit(solution)/shard_map/leave/pallas_call | solution.py:626
  307.7 8.2 %shares.5 = (bf16[1,1536,512]{2,1,0:T(8,128)(2,1)}, bf16[1,1536,512]{2,1,0:T(8,128)(2,1)}) custom-call(s32[1]{0:T(128)} %bitcast.me_ref, bf16[1536,1024]{1,0:T(8,128)(2,1)} %bitcast.137, bf16[2048,1024]{1,0:T(8,128)(2,1)} %refs_1_.3), custom_call_target="tpu_custom_call" | custom-call | flops 7408818688 | bytes 1000 | tf_op jit(solution)/shard_map/shares/pallas_call | solution.py:1008
  318.6 3.1 add.168
  323.1 1.8 collective-permute-start.22
  327.4 10.8 %gram_pair.4 = (bf16[4,256,1024]{2,1,0:T(8,128)(2,1)}, bf16[4,256,1024]{2,1,0:T(8,128)(2,1)}) custom-call(s32[1]{0:T(128)} %bitcast.1.me_ref, bf16[1536,2048]{1,0:T(8,128)(2,1)} %bitcast.128, bf16[1536,1024]{1,0:T(8,128)(2,1)} %bitcast.121), custom_call_target="tpu_custom_call" | custom-call | flops 12348030976 | bytes 1000 | tf_op jit(solution)/shard_map/gram_pair/pallas_call | solution.py:948
  339.8 2.6 collective-permute-start.27
  343.4 6.5 %conv_bc.1 = (bf16[6,256,384]{2,1,0:T(8,128)(2,1)}, f32[6,8,256]{2,1,0:T(8,128)}, f32[8,256]{1,0:T(8,128)}) custom-call(bf16[6,288,256]{2,1,0:T(8,128)(2,1)} %maximum_select_fusion.d_ref, bf16[6,256,256]{2,1,0:T(8,128)(2,1)} %get-tuple-element.186.pre_bc_ref.pre_ref, bf16[6,16,256]{2,1,0:T(8,128)(2,1)} %get-tuple-element.187.halo_bc_ref.halo_ref, ...), custom_call_target="tpu_custom_call" | custom-call | flops 7245000192 | bytes 1000 | tf_op jit(solution)/shard_map/conv_bc/pallas_call | solution.py:626
  350.0 1.8 add.170
  351.8 7.3 %gram_pair.5 = (bf16[4,256,384]{2,1,0:T(8,128)(2,1)}, bf16[4,256,384]{2,1,0:T(8,128)(2,1)}) custom-call(s32[1]{0:T(128)} %bitcast.1.me_ref, bf16[1536,2048]{1,0:T(8,128)(2,1)} %bitcast.129, bf16[1536,384]{1,0:T(8,128)(2,1)} %bitcast.107), custom_call_target="tpu_custom_call" | custom-call | flops 4630511616 | bytes 1000 | tf_op jit(solution)/shard_map/gram_pair/pallas_call | solution.py:948
  359.1 15.0 %shares.6 = (bf16[1,1536,512]{2,1,0:T(8,128)(2,1)}, bf16[1,1536,512]{2,1,0:T(8,128)(2,1)}, f32[2,8,512]{2,1,0:T(8,128)}) custom-call(s32[1]{0:T(128)} %bitcast.me_ref, bf16[1536,1024]{1,0:T(8,128)(2,1)} %bitcast.133, bf16[2,2048,1024]{2,1,0:T(8,128)(2,1)} %bitcast.101, bf16[1536,1024]{1,0:T(8,128)(2,1)} %bitcast.122, bf16[2,2048,1024]{2,1,0:T(8,128)(2,1)} %bitcast.102, ...), custom_call_target="tpu_custom_call" | custom-call | flops 15743739904 | bytes 1000 | tf_op jit(solution)/shard_map/shares/pallas_call | solution.py:1008
  376.8 3.1 add.171
  380.6 2.4 fusion.9
  383.1 5.6 %collective-permute-done.27 = bf16[4,256,1024]{2,1,0:T(8,128)(2,1)} collective-permute-done((bf16[4,256,1024]{2,1,0:T(8,128)(2,1)}, bf16[4,256,1024]{2,1,0:T(8,128)(2,1)}, u32[]{:S(2)}, u32[]{:S(2)}) %collective-permute-start.27) | collective-permute-done | bytes 2097184 | tf_op jit(solution)/shard_map/ppermute | solution.py:646
  388.6 3.9 add.173
  392.6 3.5 add.174
  396.0 1.8 collective-permute-start.30
  397.8 14.5 %shares.7 = (bf16[1,1536,512]{2,1,0:T(8,128)(2,1)}, bf16[1,1536,512]{2,1,0:T(8,128)(2,1)}, f32[2,8,512]{2,1,0:T(8,128)}) custom-call(s32[1]{0:T(128)} %bitcast.me_ref, bf16[1536,1024]{1,0:T(8,128)(2,1)} %bitcast.134, bf16[2,2048,1024]{2,1,0:T(8,128)(2,1)} %bitcast.103, bf16[1536,1024]{1,0:T(8,128)(2,1)} %bitcast.123, bf16[2,2048,1024]{2,1,0:T(8,128)(2,1)} %bitcast.104, ...), custom_call_target="tpu_custom_call" | custom-call | flops 15743739904 | bytes 1000 | tf_op jit(solution)/shard_map/shares/pallas_call | solution.py:1008
  414.0 1.8 collective-permute-start.31
  415.8 2.7 collective-permute-done.31
  418.6 4.6 collective-permute-start.32
  423.2 1.7 collective-permute-start.37
  424.9 4.7 collective-permute-done.32
  429.6 3.1 collective-permute-start.33
  433.5 7.4 %collective-permute-done.33 = f32[16,1024]{1,0:T(8,128)S(1)} collective-permute-done((f32[16,1024]{1,0:T(8,128)S(1)}, f32[16,1024]{1,0:T(8,128)S(1)}, u32[]{:S(2)}, u32[]{:S(2)}) %collective-permute-start.33) | collective-permute-done | bytes 65568 | tf_op jit(solution)/shard_map/ppermute | solution.py:646
  446.3 2.2 convert_element_type.128
  448.6 3.3 fusion.44
  455.0 2.9 collective-permute-start.39
  459.4 1.9 dynamic-slice_bitcast_fusion
  462.6 4.9 %fusion.8 = (bf16[6,256,512]{2,1,0:T(8,128)(2,1)}, bf16[6,256,512]{2,1,0:T(8,128)(2,1)}) fusion(f32[6,256,512]{2,1,0:T(8,128)S(1)} %get-tuple-element.297, bf16[6,256,512]{2,1,0:T(8,128)(2,1)} %bitcast.106, bf16[6,256,512]{2,1,0:T(8,128)(2,1)} %param.35, f32[6,256]{1,0:T(8,128)S(1)} %bitcast.111, f32[512]{0:T(512)} %copy-done.17, ...), kind=kLoop, calls=%fused_computation.12 | loop fusion | flops 11010048 | bytes 12597252 | tf_op jit(solution)/shard_map/convert_element_type | solution.py:1181
  467.5 4.9 %collective-permute-done.39 = bf16[256,384]{1,0:T(8,128)(2,1)} collective-permute-done((bf16[256,384]{1,0:T(8,128)(2,1)}, bf16[256,384]{1,0:T(8,128)(2,1)}, u32[]{:S(2)}, u32[]{:S(2)}) %collective-permute-start.39) | collective-permute-done | bytes 196640 | tf_op jit(solution)/shard_map/ppermute | solution.py:646
  477.4 2.9 copy.46
  (232 shorter events, 64.6 us)
Async XLA Ops:
  7.2 121.9 %all-gather.2.cloned.1.call-start = ((), (), s32[]{:S(2)}) async-start(), calls=%async_computation.3 | async-start | bytes 7864320 | tf_op jit(solution)/shard_map/all_gather | solution.py:769
  7.9 9.6 %copy-start.16 = (s32[6,256]{1,0:T(8,128)S(1)}, s32[6,256]{1,0:T(8,128)}, u32[]{:S(2)}) copy-start(s32[6,256]{1,0:T(8,128)} %param.21) | copy-start | bytes 18436
  7.9 9.7 %slice-start = ((bf16[6,256,2048]{2,1,0:T(8,128)(2,1)}), bf16[6,8,2048]{2,1,0:T(8,128)(2,1)S(1)}, s32[]{:S(2)}) async-start(bf16[6,256,2048]{2,1,0:T(8,128)(2,1)} %tok_ref.1), calls=%async_computation.7 | async-start | bytes 393216 | tf_op jit(solution)/shard_map/slice | solution.py:772
  7.9 14.9 %copy-start.13 = (bf16[2048,16]{0,1:T(8,128)(2,1)S(1)}, bf16[2048,16]{0,1:T(8,128)(2,1)}, u32[]{:S(2)}) copy-start(bf16[2048,16]{0,1:T(8,128)(2,1)} %param.25) | copy-start | bytes 196612
  7.9 438.4 %reduce-scatter.8.cloned.1.call-start = ((), (), s32[]{:S(2)}) async-start(), calls=%async_computation.6 | async-start | bytes 2621440 | tf_op jit(solution)/shard_map/reduce_scatter | solution.py:694
  17.5 6.5 %copy-start.24 = (f32[256]{0:T(256)S(1)}, f32[256]{0:T(256)}, u32[]{:S(2)}) copy-start(f32[256]{0:T(256)} %param.29) | copy-start | bytes 3076
  17.5 7.2 %copy-start.18 = (f32[4,1024]{1,0:T(4,128)S(1)}, f32[4,1024]{1,0:T(4,128)}, u32[]{:S(2)}) copy-start(f32[4,1024]{1,0:T(4,128)} %param.26) | copy-start | bytes 49156
  17.5 7.1 %copy-start.22 = (f32[1024]{0:T(1024)S(1)}, f32[1024]{0:T(1024)}, u32[]{:S(2)}) copy-start(f32[1024]{0:T(1024)} %param.27) | copy-start | bytes 12292
  17.5 7.8 %copy-start.5 = (bf16[2048,256]{1,0:T(8,128)(2,1)S(1)}, bf16[2048,256]{1,0:T(8,128)(2,1)}, u32[]{:S(2)}) copy-start(bf16[2048,256]{1,0:T(8,128)(2,1)} %param.24) | copy-start | bytes 3145732
  17.7 9.6 %collective-permute-start = (bf16[6,8,2176]{2,1,0:T(8,128)(2,1)S(1)}, bf16[6,8,2176]{2,1,0:T(8,128)(2,1)S(1)}, u32[]{:S(2)}, u32[]{:S(2)}) collective-permute-start(bf16[6,8,2176]{2,1,0:T(8,128)(2,1)S(1)} %pad_maximum_fusion.1), channel_id=1, source_target_pairs={{0,4},{4,8},{8,12},{12,16},{16,20},{20,24},{24,28},{1,5},{5,9},{9,... | collective-permute-start | bytes 626696 | tf_op jit(solution)/shard_map/ppermute | solution.py:652
  28.8 30.4 %copy-start.26 = (f32[16]{0:T(128)S(1)}, f32[16]{0:T(128)}, u32[]{:S(2)}) copy-start(f32[16]{0:T(128)} %param.32) | copy-start | bytes 196
  28.8 30.6 %copy-start.20 = (f32[1024]{0:T(1024)S(1)}, f32[1024]{0:T(1024)}, u32[]{:S(2)}) copy-start(f32[1024]{0:T(1024)} %param.33) | copy-start | bytes 12292
  57.0 20.0 %collective-permute-start.1 = (bf16[400,1024]{1,0:T(8,128)(2,1)}, bf16[400,1024]{1,0:T(8,128)(2,1)S(1)}, u32[]{:S(2)}, u32[]{:S(2)}) collective-permute-start(bf16[400,1024]{1,0:T(8,128)(2,1)} %get-tuple-element.143), channel_id=1, source_target_pairs={{0,4},{4,0},{8,12},{12,8},{16,20},{20,16},{24,28},{28,24},{1,5},{5... | collective-permute-start | bytes 2457608 | tf_op jit(solution)/shard_map/ppermute | solution.py:646
  80.8 16.4 %collective-permute-start.2 = (bf16[7,16,1024]{2,1,0:T(8,128)(2,1)}, bf16[7,16,1024]{2,1,0:T(8,128)(2,1)S(1)}, u32[]{:S(2)}, u32[]{:S(2)}) collective-permute-start(bf16[7,16,1024]{2,1,0:T(8,128)(2,1)} %get-tuple-element.146), channel_id=1, source_target_pairs={{0,8},{4,12},{8,0},{12,4},{16,24},{20,28},{24,16},{28,20},{1,9},{5... | collective-permute-start | bytes 688136 | tf_op jit(solution)/shard_map/ppermute | solution.py:646
  83.5 18.6 %collective-permute-start.3 = (bf16[7,16,1024]{2,1,0:T(8,128)(2,1)}, bf16[7,16,1024]{2,1,0:T(8,128)(2,1)S(1)}, u32[]{:S(2)}, u32[]{:S(2)}) collective-permute-start(bf16[7,16,1024]{2,1,0:T(8,128)(2,1)} %get-tuple-element.147), channel_id=1, source_target_pairs={{0,16},{4,20},{8,24},{12,28},{16,0},{20,4},{24,8},{28,12},{1,17},{... | collective-permute-start | bytes 688136 | tf_op jit(solution)/shard_map/ppermute | solution.py:646
  86.0 16.1 %collective-permute-start.4 = (bf16[7,16,1024]{2,1,0:T(8,128)(2,1)}, bf16[7,16,1024]{2,1,0:T(8,128)(2,1)S(1)}, u32[]{:S(2)}, u32[]{:S(2)}) collective-permute-start(bf16[7,16,1024]{2,1,0:T(8,128)(2,1)} %get-tuple-element.148), channel_id=1, source_target_pairs={{0,24},{4,28},{8,16},{12,20},{16,8},{20,12},{24,0},{28,4},{1,25},{... | collective-permute-start | bytes 688136 | tf_op jit(solution)/shard_map/ppermute | solution.py:646
  105.4 15.8 %collective-permute-start.5 = (bf16[6,16,1024]{2,1,0:T(8,128)(2,1)}, bf16[6,16,1024]{2,1,0:T(8,128)(2,1)S(1)}, u32[]{:S(2)}, u32[]{:S(2)}) collective-permute-start(bf16[6,16,1024]{2,1,0:T(8,128)(2,1)} %get-tuple-element.150), channel_id=1, source_target_pairs={{0,8},{4,12},{8,0},{12,4},{16,24},{20,28},{24,16},{28,20},{1,9},{5... | collective-permute-start | bytes 589832 | tf_op jit(solution)/shard_map/ppermute | solution.py:646
  108.3 15.5 %collective-permute-start.6 = (bf16[6,16,1024]{2,1,0:T(8,128)(2,1)}, bf16[6,16,1024]{2,1,0:T(8,128)(2,1)S(1)}, u32[]{:S(2)}, u32[]{:S(2)}) collective-permute-start(bf16[6,16,1024]{2,1,0:T(8,128)(2,1)} %get-tuple-element.151), channel_id=1, source_target_pairs={{0,16},{4,20},{8,24},{12,28},{16,0},{20,4},{24,8},{28,12},{1,17},{... | collective-permute-start | bytes 589832 | tf_op jit(solution)/shard_map/ppermute | solution.py:646
  109.4 14.5 %collective-permute-start.7 = (bf16[6,16,1024]{2,1,0:T(8,128)(2,1)}, bf16[6,16,1024]{2,1,0:T(8,128)(2,1)S(1)}, u32[]{:S(2)}, u32[]{:S(2)}) collective-permute-start(bf16[6,16,1024]{2,1,0:T(8,128)(2,1)} %get-tuple-element.152), channel_id=1, source_target_pairs={{0,24},{4,28},{8,16},{12,20},{16,8},{20,12},{24,0},{28,4},{1,25},{... | collective-permute-start | bytes 589832 | tf_op jit(solution)/shard_map/ppermute | solution.py:646
  128.2 15.1 %collective-permute-start.8 = (bf16[6,64,1024]{2,1,0:T(8,128)(2,1)}, bf16[6,64,1024]{2,1,0:T(8,128)(2,1)S(1)}, u32[]{:S(2)}, u32[]{:S(2)}) collective-permute-start(bf16[6,64,1024]{2,1,0:T(8,128)(2,1)} %get-tuple-element.154), channel_id=1, source_target_pairs={{0,4},{4,0},{8,12},{12,8},{16,20},{20,16},{24,28},{28,24},{1,5},{5... | collective-permute-start | bytes 2359304 | tf_op jit(solution)/shard_map/ppermute | solution.py:646
  156.0 1.4 collective-permute-start.9
  158.3 4.1 collective-permute-start.10
  182.4 20.7 %collective-permute-start.11 = (bf16[384,1024]{1,0:T(8,128)(2,1)}, bf16[384,1024]{1,0:T(8,128)(2,1)S(1)}, u32[]{:S(2)}, u32[]{:S(2)}) collective-permute-start(bf16[384,1024]{1,0:T(8,128)(2,1)} %get-tuple-element.164), channel_id=1, source_target_pairs={{0,4},{4,0},{8,12},{12,8},{16,20},{20,16},{24,28},{28,24},{1,5},{5... | collective-permute-start | bytes 2359304 | tf_op jit(solution)/shard_map/ppermute | solution.py:646
  202.0 58.7 %collective-permute-start.18 = (bf16[4,256,1024]{2,1,0:T(8,128)(2,1)}, bf16[4,256,1024]{2,1,0:T(8,128)(2,1)S(1)}, u32[]{:S(2)}, u32[]{:S(2)}) collective-permute-start(bf16[4,256,1024]{2,1,0:T(8,128)(2,1)} %get-tuple-element.182), channel_id=1, source_target_pairs={{0,4},{4,0},{8,12},{12,8},{16,20},{20,16},{24,28},{28,24},{1,5},{5... | collective-permute-start | bytes 6291464 | tf_op jit(solution)/shard_map/ppermute | solution.py:646
  206.9 28.4 %collective-permute-start.12 = (bf16[6,16,1024]{2,1,0:T(8,128)(2,1)}, bf16[6,16,1024]{2,1,0:T(8,128)(2,1)S(1)}, u32[]{:S(2)}, u32[]{:S(2)}) collective-permute-start(bf16[6,16,1024]{2,1,0:T(8,128)(2,1)} %get-tuple-element.171), channel_id=1, source_target_pairs={{0,8},{4,12},{8,0},{12,4},{16,24},{20,28},{24,16},{28,20},{1,9},{5... | collective-permute-start | bytes 589832 | tf_op jit(solution)/shard_map/ppermute | solution.py:646
  213.3 22.0 %collective-permute-start.13 = (bf16[6,16,1024]{2,1,0:T(8,128)(2,1)}, bf16[6,16,1024]{2,1,0:T(8,128)(2,1)S(1)}, u32[]{:S(2)}, u32[]{:S(2)}) collective-permute-start(bf16[6,16,1024]{2,1,0:T(8,128)(2,1)} %get-tuple-element.172), channel_id=1, source_target_pairs={{0,16},{4,20},{8,24},{12,28},{16,0},{20,4},{24,8},{28,12},{1,17},{... | collective-permute-start | bytes 589832 | tf_op jit(solution)/shard_map/ppermute | solution.py:646
  215.1 20.2 %collective-permute-start.14 = (bf16[6,16,1024]{2,1,0:T(8,128)(2,1)}, bf16[6,16,1024]{2,1,0:T(8,128)(2,1)S(1)}, u32[]{:S(2)}, u32[]{:S(2)}) collective-permute-start(bf16[6,16,1024]{2,1,0:T(8,128)(2,1)} %get-tuple-element.173), channel_id=1, source_target_pairs={{0,24},{4,28},{8,16},{12,20},{16,8},{20,12},{24,0},{28,4},{1,25},{... | collective-permute-start | bytes 589832 | tf_op jit(solution)/shard_map/ppermute | solution.py:646
  239.0 15.1 %collective-permute-start.15 = (bf16[6,16,1024]{2,1,0:T(8,128)(2,1)}, bf16[6,16,1024]{2,1,0:T(8,128)(2,1)S(1)}, u32[]{:S(2)}, u32[]{:S(2)}) collective-permute-start(bf16[6,16,1024]{2,1,0:T(8,128)(2,1)} %get-tuple-element.177), channel_id=1, source_target_pairs={{0,8},{4,12},{8,0},{12,4},{16,24},{20,28},{24,16},{28,20},{1,9},{5... | collective-permute-start | bytes 589832 | tf_op jit(solution)/shard_map/ppermute | solution.py:646
  239.6 16.1 %collective-permute-start.16 = (bf16[6,16,1024]{2,1,0:T(8,128)(2,1)}, bf16[6,16,1024]{2,1,0:T(8,128)(2,1)S(1)}, u32[]{:S(2)}, u32[]{:S(2)}) collective-permute-start(bf16[6,16,1024]{2,1,0:T(8,128)(2,1)} %get-tuple-element.178), channel_id=1, source_target_pairs={{0,16},{4,20},{8,24},{12,28},{16,0},{20,4},{24,8},{28,12},{1,17},{... | collective-permute-start | bytes 589832 | tf_op jit(solution)/shard_map/ppermute | solution.py:646
  242.0 13.7 %collective-permute-start.17 = (bf16[6,16,1024]{2,1,0:T(8,128)(2,1)}, bf16[6,16,1024]{2,1,0:T(8,128)(2,1)S(1)}, u32[]{:S(2)}, u32[]{:S(2)}) collective-permute-start(bf16[6,16,1024]{2,1,0:T(8,128)(2,1)} %get-tuple-element.179), channel_id=1, source_target_pairs={{0,24},{4,28},{8,16},{12,20},{16,8},{20,12},{24,0},{28,4},{1,25},{... | collective-permute-start | bytes 589832 | tf_op jit(solution)/shard_map/ppermute | solution.py:646
  254.1 6.6 %copy-start.2 = (bf16[4,256,1024]{2,1,0:T(8,128)(2,1)S(1)}, bf16[4,256,1024]{2,1,0:T(8,128)(2,1)}, u32[]{:S(2)}) copy-start(bf16[4,256,1024]{2,1,0:T(8,128)(2,1)} %get-tuple-element.181) | copy-start | bytes 6291460
  263.0 196.4 %reduce-scatter.4.cloned.1.call-start = ((), (), s32[]{:S(2)}) async-start(), calls=%async_computation.4 | async-start | bytes 5242880 | tf_op jit(solution)/shard_map/reduce_scatter | solution.py:694
  264.1 15.0 %collective-permute-start.19 = (bf16[6,64,1024]{2,1,0:T(8,128)(2,1)S(1)}, bf16[6,64,1024]{2,1,0:T(8,128)(2,1)S(1)}, u32[]{:S(2)}, u32[]{:S(2)}) collective-permute-start(bf16[6,64,1024]{2,1,0:T(8,128)(2,1)S(1)} %copy-done.31), channel_id=1, source_target_pairs={{0,4},{4,0},{8,12},{12,8},{16,20},{20,16},{24,28},{28,24},{1,5},{5... | collective-permute-start | bytes 2359304 | tf_op jit(solution)/shard_map/ppermute | solution.py:646
  265.0 53.6 %collective-permute-start.23 = (bf16[1,1536,512]{2,1,0:T(8,128)(2,1)}, bf16[1,1536,512]{2,1,0:T(8,128)(2,1)}, u32[]{:S(2)}, u32[]{:S(2)}) collective-permute-start(bf16[1,1536,512]{2,1,0:T(8,128)(2,1)} %get-tuple-element.202), channel_id=1, source_target_pairs={{0,1},{1,0},{2,3},{3,2},{4,5},{5,4},{6,7},{7,6},{8,9},{9,8},{10,11... | collective-permute-start | bytes 4718600 | tf_op jit(solution)/shard_map/ppermute | solution.py:646
  265.0 211.2 %reduce-scatter.6.cloned.1.call-start = ((), (), s32[]{:S(2)}) async-start(), calls=%async_computation.5 | async-start | bytes 2621440 | tf_op jit(solution)/shard_map/reduce_scatter | solution.py:694
  306.2 11.7 %copy-start = (bf16[6,256,256]{2,1,0:T(8,128)(2,1)S(1)}, bf16[6,256,256]{2,1,0:T(8,128)(2,1)}, u32[]{:S(2)}) copy-start(bf16[6,256,256]{2,1,0:T(8,128)(2,1)} %get-tuple-element.196) | copy-start | bytes 2359300
  306.3 10.5 %collective-permute-start.20 = (bf16[6,3,1280]{2,1,0:T(4,128)(2,1)S(1)}, bf16[6,3,1280]{2,1,0:T(4,128)(2,1)S(1)}, u32[]{:S(2)}, u32[]{:S(2)}) collective-permute-start(bf16[6,3,1280]{2,1,0:T(4,128)(2,1)S(1)} %pad_maximum_fusion.3), channel_id=1, source_target_pairs={{4,0},{8,4},{12,8},{16,12},{20,16},{24,20},{28,24},{5,1},{9,5},{13... | collective-permute-start | bytes 138248 | tf_op jit(solution)/shard_map/ppermute | solution.py:652
  318.0 3.6 collective-permute-start.21
  318.1 31.8 %collective-permute-start.25 = (bf16[1,1536,512]{2,1,0:T(8,128)(2,1)}, bf16[1,1536,512]{2,1,0:T(8,128)(2,1)}, u32[]{:S(2)}, u32[]{:S(2)}) collective-permute-start(bf16[1,1536,512]{2,1,0:T(8,128)(2,1)} %get-tuple-element.209), channel_id=1, source_target_pairs={{0,1},{1,0},{2,3},{3,2},{4,5},{5,4},{6,7},{7,6},{8,9},{9,8},{10,11... | collective-permute-start | bytes 4718600 | tf_op jit(solution)/shard_map/ppermute | solution.py:646
  323.1 15.2 %collective-permute-start.22 = (bf16[3,288,256]{2,1,0:T(8,128)(2,1)S(1)}, bf16[3,288,256]{2,1,0:T(8,128)(2,1)}, u32[]{:S(2)}, u32[]{:S(2)}) collective-permute-start(bf16[3,288,256]{2,1,0:T(8,128)(2,1)S(1)} %constant_dynamic-slice_fusion.1), channel_id=1, source_target_pairs={{0,2},{1,3},{2,0},{3,1},{4,6},{5,7},{6,4},{7,5},{8,10},{9,11},{10,... | collective-permute-start | bytes 1327112 | tf_op jit(solution)/shard_map/ppermute | solution.py:646
  327.4 12.0 %copy-start.9 = (bf16[1,1536,512]{2,1,0:T(8,128)(2,1)S(1)}, bf16[1,1536,512]{2,1,0:T(8,128)(2,1)}, u32[]{:S(2)}) copy-start(bf16[1,1536,512]{2,1,0:T(8,128)(2,1)} %add.168) | copy-start | bytes 4718596
  339.4 3.0 collective-permute-start.24
  339.4 37.4 %collective-permute-start.26 = (bf16[1,1536,512]{2,1,0:T(8,128)(2,1)S(1)}, bf16[1,1536,512]{2,1,0:T(8,128)(2,1)}, u32[]{:S(2)}, u32[]{:S(2)}) collective-permute-start(bf16[1,1536,512]{2,1,0:T(8,128)(2,1)S(1)} %copy-done.9), channel_id=1, source_target_pairs={{0,2},{1,3},{2,0},{3,1},{4,6},{5,7},{6,4},{7,5},{8,10},{9,11},{10,... | collective-permute-start | bytes 4718600 | tf_op jit(solution)/shard_map/ppermute | solution.py:646
  339.8 48.8 %collective-permute-start.27 = (bf16[4,256,1024]{2,1,0:T(8,128)(2,1)}, bf16[4,256,1024]{2,1,0:T(8,128)(2,1)}, u32[]{:S(2)}, u32[]{:S(2)}) collective-permute-start(bf16[4,256,1024]{2,1,0:T(8,128)(2,1)} %get-tuple-element.215), channel_id=1, source_target_pairs={{0,4},{4,0},{8,12},{12,8},{16,20},{20,16},{24,28},{28,24},{1,5},{5... | collective-permute-start | bytes 6291464 | tf_op jit(solution)/shard_map/ppermute | solution.py:646
  359.1 17.7 %copy-start.14 = (f32[8,1024]{1,0:T(8,128)S(1)}, f32[8,1024]{1,0:T(8,128)}, u32[]{:S(2)}) copy-start(f32[8,1024]{1,0:T(8,128)} %get-tuple-element.224) | copy-start | bytes 98308
  359.1 17.7 %copy-start.15 = (f32[8,1024]{1,0:T(8,128)S(1)}, f32[8,1024]{1,0:T(8,128)}, u32[]{:S(2)}) copy-start(f32[8,1024]{1,0:T(8,128)} %get-tuple-element.223) | copy-start | bytes 98308
  374.0 18.5 %collective-permute-start.28 = (bf16[1,1536,512]{2,1,0:T(8,128)(2,1)}, bf16[1,1536,512]{2,1,0:T(8,128)(2,1)}, u32[]{:S(2)}, u32[]{:S(2)}) collective-permute-start(bf16[1,1536,512]{2,1,0:T(8,128)(2,1)} %get-tuple-element.217), channel_id=1, source_target_pairs={{0,1},{1,0},{2,3},{3,2},{4,5},{5,4},{6,7},{7,6},{8,9},{9,8},{10,11... | collective-permute-start | bytes 4718600 | tf_op jit(solution)/shard_map/ppermute | solution.py:646
  380.6 8.0 %copy-start.3 = (bf16[4,256,1024]{2,1,0:T(8,128)(2,1)S(1)}, bf16[4,256,1024]{2,1,0:T(8,128)(2,1)}, u32[]{:S(2)}) copy-start(bf16[4,256,1024]{2,1,0:T(8,128)(2,1)} %get-tuple-element.214) | copy-start | bytes 6291460
  396.0 17.9 %copy-start.19 = (f32[8,256]{1,0:T(8,128)S(1)}, f32[8,256]{1,0:T(8,128)}, u32[]{:S(2)}) copy-start(f32[8,256]{1,0:T(8,128)} %get-tuple-element.225) | copy-start | bytes 24580
  396.0 17.9 %copy-start.23 = (f32[8,128]{1,0:T(8,128)S(1)}, f32[8,128]{1,0:T(8,128)}, u32[]{:S(2)}) copy-start(f32[8,128]{1,0:T(8,128)} %get-tuple-element.226) | copy-start | bytes 12292
  396.0 52.6 %collective-permute-start.30 = (bf16[1,1536,512]{2,1,0:T(8,128)(2,1)}, bf16[1,1536,512]{2,1,0:T(8,128)(2,1)}, u32[]{:S(2)}, u32[]{:S(2)}) collective-permute-start(bf16[1,1536,512]{2,1,0:T(8,128)(2,1)} %add.174), channel_id=1, source_target_pairs={{0,2},{1,3},{2,0},{3,1},{4,6},{5,7},{6,4},{7,5},{8,10},{9,11},{10,... | collective-permute-start | bytes 4718600 | tf_op jit(solution)/shard_map/ppermute | solution.py:646
  412.3 36.3 %collective-permute-start.29 = (bf16[1,1536,512]{2,1,0:T(8,128)(2,1)}, bf16[1,1536,512]{2,1,0:T(8,128)(2,1)}, u32[]{:S(2)}, u32[]{:S(2)}) collective-permute-start(bf16[1,1536,512]{2,1,0:T(8,128)(2,1)} %get-tuple-element.221), channel_id=1, source_target_pairs={{0,1},{1,0},{2,3},{3,2},{4,5},{5,4},{6,7},{7,6},{8,9},{9,8},{10,11... | collective-permute-start | bytes 4718600 | tf_op jit(solution)/shard_map/ppermute | solution.py:646
  413.9 38.0 %copy-start.17 = (f32[512]{0:T(512)}, f32[512]{0:T(512)S(1)}, u32[]{:S(2)}) copy-start(f32[512]{0:T(512)S(1)} %get-tuple-element.277) | copy-start | bytes 6148
  414.0 4.6 collective-permute-start.31
  418.6 11.0 %collective-permute-start.32 = (f32[16,1024]{1,0:T(8,128)S(1)}, f32[16,1024]{1,0:T(8,128)S(1)}, u32[]{:S(2)}, u32[]{:S(2)}) collective-permute-start(f32[16,1024]{1,0:T(8,128)S(1)} %fusion.42), channel_id=1, source_target_pairs={{0,8},{4,12},{8,0},{12,4},{16,24},{20,28},{24,16},{28,20},{1,9},{5... | collective-permute-start | bytes 196616 | tf_op jit(solution)/shard_map/ppermute | solution.py:646
  423.2 28.7 %collective-permute-start.37 = (bf16[4,256,384]{2,1,0:T(8,128)(2,1)}, bf16[4,256,384]{2,1,0:T(8,128)(2,1)}, u32[]{:S(2)}, u32[]{:S(2)}) collective-permute-start(bf16[4,256,384]{2,1,0:T(8,128)(2,1)} %get-tuple-element.230), channel_id=1, source_target_pairs={{0,4},{4,0},{8,12},{12,8},{16,20},{20,16},{24,28},{28,24},{1,5},{5... | collective-permute-start | bytes 2359304 | tf_op jit(solution)/shard_map/ppermute | solution.py:646
  429.6 11.3 %collective-permute-start.33 = (f32[16,1024]{1,0:T(8,128)S(1)}, f32[16,1024]{1,0:T(8,128)S(1)}, u32[]{:S(2)}, u32[]{:S(2)}) collective-permute-start(f32[16,1024]{1,0:T(8,128)S(1)} %add.183), channel_id=1, source_target_pairs={{0,16},{4,20},{8,24},{12,28},{16,0},{20,4},{24,8},{28,12},{1,17},{... | collective-permute-start | bytes 196616 | tf_op jit(solution)/shard_map/ppermute | solution.py:646
  440.9 1.2 collective-permute-start.34
  442.2 3.6 collective-permute-start.35
  455.0 12.5 %collective-permute-start.38 = (bf16[256,384]{1,0:T(8,128)(2,1)}, bf16[256,384]{1,0:T(8,128)(2,1)S(1)}, u32[]{:S(2)}, u32[]{:S(2)}) collective-permute-start(bf16[256,384]{1,0:T(8,128)(2,1)} %get-tuple-element.282), channel_id=1, source_target_pairs={{0,8},{4,12},{8,0},{12,4},{16,24},{20,28},{24,16},{28,20},{1,9},{5... | collective-permute-start | bytes 589832 | tf_op jit(solution)/shard_map/ppermute | solution.py:646
  455.0 17.4 %collective-permute-start.39 = (bf16[256,384]{1,0:T(8,128)(2,1)}, bf16[256,384]{1,0:T(8,128)(2,1)}, u32[]{:S(2)}, u32[]{:S(2)}) collective-permute-start(bf16[256,384]{1,0:T(8,128)(2,1)} %get-tuple-element.284), channel_id=1, source_target_pairs={{0,16},{4,20},{8,24},{12,28},{16,0},{20,4},{24,8},{28,12},{1,17},{... | collective-permute-start | bytes 589832 | tf_op jit(solution)/shard_map/ppermute | solution.py:646
  457.9 14.5 %collective-permute-start.40 = (bf16[256,384]{1,0:T(8,128)(2,1)S(1)}, bf16[256,384]{1,0:T(8,128)(2,1)}, u32[]{:S(2)}, u32[]{:S(2)}) collective-permute-start(bf16[256,384]{1,0:T(8,128)(2,1)S(1)} %get-tuple-element.283), channel_id=1, source_target_pairs={{0,24},{4,28},{8,16},{12,20},{16,8},{20,12},{24,0},{28,4},{1,25},{... | collective-permute-start | bytes 589832 | tf_op jit(solution)/shard_map/ppermute | solution.py:646
  461.3 13.8 %collective-permute-start.36 = (bf16[256,1024]{1,0:T(8,128)(2,1)}, bf16[256,1024]{1,0:T(8,128)(2,1)}, u32[]{:S(2)}, u32[]{:S(2)}) collective-permute-start(bf16[256,1024]{1,0:T(8,128)(2,1)} %dynamic-slice_bitcast_fusion), channel_id=1, source_target_pairs={{0,4},{4,0},{8,12},{12,8},{16,20},{20,16},{24,28},{28,24},{1,5},{5... | collective-permute-start | bytes 1572872 | tf_op jit(solution)/shard_map/ppermute | solution.py:646
  467.5 7.6 %copy-start.11 = (bf16[512,1024]{1,0:T(8,128)(2,1)S(1)}, bf16[512,1024]{1,0:T(8,128)(2,1)}, u32[]{:S(2)}) copy-start(bf16[512,1024]{1,0:T(8,128)(2,1)} %reduce-scatter.4.cloned.1.call-done) | copy-start | bytes 3145732
  (27 other events, 59.9 us)
Sparse Core Ops, SparseCore 0:
  9.6 49.0 all-gather.1
  263.1 44.0 reduce-scatter.7
  309.6 76.0 reduce-scatter.3
  392.7 50.8 reduce-scatter.5

commit v5 on v4

--- a/solution.py
+++ b/solution.py
@@ -158,13 +158,12 @@
 def front_kernel(
     state, me_ref, tok_ref, halo_ref, gain_ref, w_ref, w_small_ref, seg_ref, conv_x_ref,
     conv_bc_ref, head_ref, expand_ref, normed_ref, pre_x_ref, pre_bc_ref, halo_x_ref, halo_bc_ref,
-    x_ref, bc_ref, xs_ref, dt_ref, cum_ref, aux_ref, keep_ref, send_ref
+    x_ref, bc_ref, dt_ref, cum_ref, aux_ref, keep_ref, send_ref
 ):
     s = pl.program_id(0)
     seqs = pl.num_programs(0)
     odd = me_ref[0] % 2
     half = state // 2
-    own = xs_ref.shape[-1]
     wide = 2 * state
     span = tok_ref.shape[1]
 
@@ -212,7 +211,6 @@
     cum = running(-head_ref[1:2] * step, True)
     cum_ref[0] = cum
     expand = expand_ref[...]
-    xs_ref[0] = (x_float * widen(step, expand)).astype(BF)
     last = cum[-1:]
     tail_step = jnp.exp(last - cum) * aux[:, 3:4] * step
     loaded = (x_float * widen(tail_step, expand)).astype(BF)
@@ -338,8 +336,13 @@
         send_ref[s] = jnp.where(is_first, later, entry).astype(BF)
 
 
-def inner_kernel(state, bc_ref, xs_ref, cum_ref, aux_ref, seg_ref, out_ref):
+def inner_kernel(
+    state, bc_ref, x_ref, cum_ref, dt_ref, aux_ref, seg_ref, head_ref, expand_ref, out_ref, xs_ref
+):
     own = xs_ref.shape[-1]
+    step = softplus(dt_ref[0] + head_ref[0:1])
+    xs_all = (x_ref[0].astype(F32) * widen(step, expand_ref[...])).astype(BF)
+    xs_ref[0] = xs_all
     b_ssm, c_ssm = bc_ref[0, :, :state], bc_ref[0, :, state:]
     cum = cum_ref[0]
     cum_t = jnp.transpose(cum)
@@ -348,7 +351,7 @@
     left = lax.broadcasted_iota(jnp.int32, (1, LANES), 1) < HEAD_DIM
     for pair in range(own // LANES):
         lanes = slice(pair * LANES, (pair + 1) * LANES)
-        xs = xs_ref[0, :, lanes].astype(F32)
+        xs = xs_all[:, lanes].astype(F32)
         total = None
         for side in range(2):
             h = 2 * pair + side
@@ -544,7 +547,8 @@
 
 
 def conv_bc_kernel(
-    d_ref, pre_ref, halo_ref, aux_ref, ddt_ref, conv_ref, dpre_ref, dot_ref, grad_ref
+    n_head, head_ref, d_ref, pre_ref, halo_ref, aux_ref, ddt_ref, conv_ref, dpre_ref, cut_ref,
+    dot_ref, grad_ref
 ):
     span = pre_ref.shape[1]
     extended = jnp.concatenate([halo_ref[0], pre_ref[0]], axis=0).astype(F32)
@@ -562,8 +566,15 @@
     ahead = d_ref[0, span : span + EDGE].astype(F32)
     d_pre = jnp.concatenate([d_pre[: span - EDGE], d_pre[span - EDGE :] + ahead], axis=0)
     d_pre = d_pre.astype(BF)
-    dpre_ref[0, :, : d_pre.shape[1]] = d_pre
-    dpre_ref[0, :, d_pre.shape[1] :] = ddt_ref[0]
+    dpre_ref[0] = d_pre
+    part = d_pre.shape[1] // n_head
+    steps = ddt_ref[0].astype(F32)[:, : LANES - part]
+    columns = d_pre.astype(F32)
+    cut_out = None
+    for head in range(n_head):
+        own = jnp.concatenate([columns[:, head * part : (head + 1) * part], steps], axis=1)
+        cut_out = own if cut_out is None else jnp.where(head_ref[0] == head, own, cut_out)
+    cut_ref[0] = cut_out.astype(BF)
     row = jnp.sum(d_pre.astype(F32) * extended[EDGE:], axis=-1, keepdims=True)
     packed = d_ref[0, span + EDGE :].astype(F32)
     dot_ref[0] = to_row(row) + (packed[0:1] + packed[1:2])
@@ -806,13 +817,12 @@
         shaped((seqs, EDGE, wide), BF),
         shaped((seqs, span, own), BF),
         shaped((seqs, span, wide), BF),
-        shaped((seqs, span, own), BF),
         shaped((seqs, span, LANES), F32),
         shaped((seqs, span, LANES), F32),
         shaped((seqs, span, LANES), F32),
     )
     packed = (shaped((seqs * half + ROWS, own), BF),) * 2
-    normed, pre_x, pre_bc, halo_x, halo_bc, x_ssm, bc_ssm, xs, dt_raw, cum, aux, keep, send = call(
+    normed, pre_x, pre_bc, halo_x, halo_bc, x_ssm, bc_ssm, dt_raw, cum, aux, keep, send = call(
         functools.partial(front_kernel, state),
         seqs,
         ins,
@@ -867,16 +877,16 @@
 
     gate = dot(normed, w_in[0], ((2,), (0,))).astype(BF)
     e_raw = dot(cot_full, w_out, ((2,), (0,))).astype(BF)
-    ins = (bc_ssm, xs, cum, aux, seg_rows)
-    (inner,) = call(
+    ins = (bc_ssm, x_ssm, cum, dt_raw, aux, seg_rows, head_rows, expand)
+    inner, xs = call(
         functools.partial(inner_kernel, state),
         seqs,
         ins,
-        seq_of(ins),
-        (shaped((seqs, span, own), F32),),
-        [seq((span, own))],
+        seq_of(ins[:6]) + whole_of(ins[6:]),
+        (shaped((seqs, span, own), F32), shaped((seqs, span, own), BF)),
+        [seq((span, own))] * 2,
         [],
-        10.3,
+        12,
         "inner",
     )
 
@@ -1130,13 +1140,17 @@
         jnp.concatenate([part, part_other], axis=0),
         jnp.concatenate([part_other, part], axis=0),
     )
-    ins = (d_bc_all, pre_bc, halo_bc, aux, d_dt, conv_bc_w)
-    per = (shaped((seqs, span, wide + LANES), BF), shaped((seqs, 8, span), F32))
-    d_small, row_dot, bc_grads = call(
-        conv_bc_kernel,
+    ins = (head_at, d_bc_all, pre_bc, halo_bc, aux, d_dt, conv_bc_w)
+    per = (
+        shaped((seqs, span, wide), BF),
+        shaped((seqs, span, LANES), BF),
+        shaped((seqs, 8, span), F32),
+    )
+    d_bc_pre, d_small, row_dot, bc_grads = call(
+        functools.partial(conv_bc_kernel, n_head),
         seqs,
         ins,
-        seq_of(ins[:5]) + whole_of(ins[5:]),
+        [SMEM_SPEC] + seq_of(ins[1:6]) + whole_of(ins[6:]),
         per + (shaped((8, wide), F32),),
         seq_of(per) + [whole((8, wide))],
         [],
@@ -1162,6 +1176,16 @@
     late_s = small_sum[0].astype(F32)
     for m in range(1, groups):
         late_s = late_s + swap(small_sum[m], "seq", 2 * m).astype(F32)
+    part = wide // n_head
+    g_w_bc, mask = late_s[:, :part], 1
+    while mask < n_head:
+        arrived = swap(g_w_bc, "head", mask)
+        g_w_bc = jnp.where(
+            (me_head // mask) % 2 == 0,
+            jnp.concatenate([g_w_bc, arrived], axis=1),
+            jnp.concatenate([arrived, g_w_bc], axis=1),
+        )
+        mask *= 2
     out_grad_own = spread_sum(out_total).astype(F32)
     x_at = lax.axis_index("seq") % 2
     gate_own = lax.dynamic_index_in_dim(gate_total, x_at, 0, False)
@@ -1170,12 +1194,12 @@
     late_a = spread_sum(late_total).astype(F32)
 
     row_dot = row_dot[:, 0]
-    w_bc_own = pad_lanes(lax.dynamic_slice_in_dim(w_bc, offset, share, 0), wide + LANES)
-    bc_term = dot(d_small, w_bc_own, ((2,), (1,)))
+    w_bc_own = lax.dynamic_slice_in_dim(w_bc, offset, share, 0)
+    bc_term = dot(d_bc_pre, w_bc_own, ((2,), (1,)))
     rstd_in = aux[:, :, 6:7]
     unit_own = tokens_own * rstd_in
     gain_own = lax.dynamic_slice_in_dim(norm_gain, offset, share, 0)
-    d_unit = (own_grad + bc_term) * gain_own
+    d_unit = (after(own_grad, gate_grad_own) + bc_term) * gain_own
     input_grad = (
         rstd_in * (d_unit - unit_own * (row_dot / model)[..., None]) + cotangent.astype(F32)
     ).astype(BF)
@@ -1212,8 +1236,8 @@
         input_grad,
         g_norm,
         g_w_zx_own,
-        late_s[:, :wide],
-        late_s[:, wide : wide + heads],
+        g_w_bc,
+        late_s[:, part : part + heads],
         *summed,
         out_grad_own,
     )

time: 492 us -> 492 us (level)
  other arithmetic: 47.8 us -> 54 us
    ppermute x39 -> x41, waiting for transfers between devices: 73.1 us -> 69.1 us  [swap(): return lax.ppermute(value, axis, [(i, i ^ mask) for i in range(count)])]
    ppermute x39 -> x41, starting transfers between devices: 56.9 us -> 58.2 us  [swap(): return lax.ppermute(value, axis, [(i, i ^ mask) for i in range(count)])]
    unnamed x95 -> x101, local copies, waits for them, and re-layouts: 23.2 us -> 22.7 us
  transfers between devices with their start and end apart: 45 -> 47, of which waited for: 15 -> 15; matrix products, arithmetic and copies ran while one was open for 19% -> 20% of each run, Pallas kernels for 39% -> 39%
where the time goes in v5:
time: 492 us; the launch traced here: 487 us
  Pallas kernels  222 us (45%)
  waiting for transfers between devices  69.8 us (14%)
  starting transfers between devices  64.9 us (13%)
  other arithmetic  54 us (11%)
  local copies, waits for them, and re-layouts  38.3 us (8%)
  matrix products  23.4 us (5%)
  between operations  14.7 us (3%)
    pallas_call x14, Pallas kernels, call(): pl.pallas_call(body, grid=(grid,), in_specs=in_specs, out_specs=out_specs...  149 us
    ppermute x41, waiting for transfers between devices, swap(): return lax.ppermute(value, axis, [(i, i ^ mask) for i in range(count)])  69.1 us
    ppermute x41, starting transfers between devices, swap(): return lax.ppermute(value, axis, [(i, i ^ mask) for i in range(count)])  58.2 us
    pallas_call x4, Pallas kernels, share_sum(): pl.pallas_call(functools.partial(share_kernel, len(terms), summed), grid_...  45.8 us
    pallas_call x3, Pallas kernels, chunk_pair(): pl.pallas_call(gram_pair_kernel, grid_spec=pltpu.PrefetchScalarGridSpec(n...  27.1 us
    dot_general x3, matrix products, dot(): lax.dot_general(a, b, (contract, ((), ())), preferred_element_type=F32, p...  23.4 us
    unnamed x101, local copies, waits for them, and re-layouts  22.7 us
  transfers between devices with their start and end apart: 47, of which 15 were waited for; matrix products, arithmetic and copies ran while one was open for 20% of the time, Pallas kernels for 39%

profile of v5, /device:TPU:0, one launch (start us, length us, event | category | flops | bytes accessed | tf_op | source)
XLA Modules:
  0.0 487.2 jit_solution(10328798249951936726)
XLA Ops:
  8.0 9.4 %copy.63 = bf16[2048,2,1024]{2,0,1:T(8,128)(2,1)} copy(bf16[2048,2,1024]{2,1,0:T(2,128)(2,1)} %param.23) | data formatting | bytes 16777216 | tf_op args[3]
  17.7 5.2 %collective-permute-start = (bf16[6,8,2176]{2,1,0:T(8,128)(2,1)S(1)}, bf16[6,8,2176]{2,1,0:T(8,128)(2,1)S(1)}, u32[]{:S(2)}, u32[]{:S(2)}) collective-permute-start(bf16[6,8,2176]{2,1,0:T(8,128)(2,1)S(1)} %pad_maximum_fusion.2), channel_id=1, source_target_pairs={{0,4},{4,8},{8,12},{12,16},{16,20},{20,24},{24,28},{1,5},{5,9},{9,... | collective-permute-start | bytes 626696 | tf_op jit(solution)/shard_map/ppermute | solution.py:663
  28.8 27.2 %front.1 = (bf16[6,256,2048]{2,1,0:T(8,128)(2,1)}, bf16[6,256,1024]{2,1,0:T(8,128)(2,1)}, bf16[6,256,256]{2,1,0:T(8,128)(2,1)}, bf16[6,16,1024]{2,1,0:T(8,128)(2...) custom-call(s32[1]{0:T(128)} %bitcast.1.me_ref, ...), custom_call_target="tpu_custom_call" | custom-call | flops 34500001792 | bytes 1000 | tf_op jit(solution)/shard_map/front/pallas_call | solution.py:637
  56.0 2.3 collective-permute-start.1
  59.1 16.9 %collective-permute-done.1.other_ref = bf16[400,1024]{1,0:T(8,128)(2,1)S(1)} collective-permute-done((bf16[400,1024]{1,0:T(8,128)(2,1)}, bf16[400,1024]{1,0:T(8,128)(2,1)S(1)}, u32[]{:S(2)}, u32[]{:S(2)}) %collective-permute-start.1) | collective-permute-done | bytes 819232 | tf_op jit(solution)/shard_map/ppermute | solution.py:657
  76.9 3.1 pair.1
  80.0 2.6 collective-permute-start.2
  82.6 2.6 collective-permute-start.3
  85.2 9.7 %fusion.14.gate_ref = bf16[6,256,1024]{2,1,0:T(8,128)(2,1)} fusion(bf16[6,256,2048]{2,1,0:T(8,128)(2,1)S(1)} %copy-done.1, bf16[2,2048,1024]{2,1,0:T(8,128)(2,1)} %bitcast.102), kind=kOutput, calls=%fused_computation.18 | convolution fusion | flops 6444023808 | bytes 13631488 | tf_op jit(solution)/shard_map/dot_general | solution.py:27
  94.9 6.4 %collective-permute-done.3.rest_2_ = bf16[7,16,1024]{2,1,0:T(8,128)(2,1)S(1)} collective-permute-done((bf16[7,16,1024]{2,1,0:T(8,128)(2,1)}, bf16[7,16,1024]{2,1,0:T(8,128)(2,1)S(1)}, u32[]{:S(2)}, u32[]{:S(2)}) %collective-permute-start.3) | collective-permute-done | bytes 229408 | tf_op jit(solution)/shard_map/ppermute | solution.py:657
  102.0 2.5 scan.1
  104.6 2.9 collective-permute-start.5
  110.0 11.4 %inner.1 = (f32[6,256,1024]{2,1,0:T(8,128)}, bf16[6,256,1024]{2,1,0:T(8,128)(2,1)}) custom-call(bf16[6,256,256]{2,1,0:T(8,128)(2,1)} %get-tuple-element.140.bc_ref, bf16[6,256,1024]{2,1,0:T(8,128)(2,1)} %get-tuple-element.187.x_ref, f32[6,256,128]{2,1,0:T(8,128)} %get-tuple-element.141.cum_ref, f32[6,256,128]{2,1,0:T(8,128)} %get-tuple-element.142.dt_ref, ...), custom_call_target="tpu_custom_call" | custom-call | flops 13799999488 | bytes 1000 | tf_op jit(solution)/shard_map/inner/pallas_call | solution.py:637
  123.8 3.6 unpair.1
  128.3 11.4 %fusion.11.e_ref = bf16[6,256,1024]{2,1,0:T(8,128)(2,1)} fusion(bf16[6,256,2048]{2,1,0:T(8,128)(2,1)} %all-gather.2.cloned.1.call-done, bf16[2048,1024]{1,0:T(8,128)(2,1)} %refs_1_.3), kind=kOutput, calls=%fused_computation.17 | convolution fusion | flops 6444023808 | bytes 13631488 | tf_op jit(solution)/shard_map/dot_general | solution.py:27
  139.7 3.4 collective-permute-done.8.other_ref
  143.9 11.9 %sums.1 = f32[6,8,256]{2,1,0:T(8,128)} custom-call(s32[1]{0:T(128)} %bitcast.1.me_ref, bf16[6,256,1024]{2,1,0:T(8,128)(2,1)} %get-tuple-element.187.x_ref, bf16[6,256,256]{2,1,0:T(8,128)(2,1)} %get-tuple-element.140.bc_ref, f32[6,256,1024]{2,1,0:T(8,128)} %get-tuple-element.144.inner_ref, bf16[6,256,1024]{2,1,0:T(8,128)(2,1)} %fusion.14.gate_ref, ...), custom_call_target="tpu_custom_call" | custom-call | flops 13799999488 | bytes 1000 | tf_op jit(solution)/shard_map/sums/pallas_call | solution.py:637
  159.7 2.4 collective-permute-done.10
  162.8 19.4 %gate_back.1 = (bf16[6,256,1024]{2,1,0:T(8,128)(2,1)}, bf16[6,256,1024]{2,1,0:T(8,128)(2,1)}, bf16[6,256,1024]{2,1,0:T(8,128)(2,1)}, f32[6,256,128]{2,1,0:T(8,12...) custom-call(s32[1]{0:T(128)} %bitcast.1.me_ref, ...), custom_call_target="tpu_custom_call" | custom-call | flops 24149999616 | bytes 1000 | tf_op jit(solution)/shard_map/gate_back/pallas_call | solution.py:637
  183.1 10.7 %gram_pair.3 = (bf16[4,256,1024]{2,1,0:T(8,128)(2,1)}, bf16[4,256,1024]{2,1,0:T(8,128)(2,1)}) custom-call(s32[1]{0:T(128)} %bitcast.1.me_ref, bf16[1536,2048]{1,0:T(8,128)(2,1)} %bitcast.135, bf16[1536,1024]{1,0:T(8,128)(2,1)} %bitcast.139), custom_call_target="tpu_custom_call" | custom-call | flops 12348030976 | bytes 1000 | tf_op jit(solution)/shard_map/gram_pair/pallas_call | solution.py:958
  193.8 7.9 %shares.4 = (bf16[1,1536,512]{2,1,0:T(8,128)(2,1)}, bf16[1,1536,512]{2,1,0:T(8,128)(2,1)}) custom-call(s32[1]{0:T(128)} %bitcast.me_ref.head_ref, bf16[1536,1024]{1,0:T(8,128)(2,1)} %bitcast.140, bf16[2048,1024]{1,0:T(8,128)(2,1)} %refs_1_.3), custom_call_target="tpu_custom_call" | custom-call | flops 7408818688 | bytes 1000 | tf_op jit(solution)/shard_map/shares/pallas_call | solution.py:1018
  203.8 2.9 pair_back.1
  206.7 5.8 %collective-permute-start.12 = (bf16[6,16,1024]{2,1,0:T(8,128)(2,1)}, bf16[6,16,1024]{2,1,0:T(8,128)(2,1)S(1)}, u32[]{:S(2)}, u32[]{:S(2)}) collective-permute-start(bf16[6,16,1024]{2,1,0:T(8,128)(2,1)} %get-tuple-element.175), channel_id=1, source_target_pairs={{0,8},{4,12},{8,0},{12,4},{16,24},{20,28},{24,16},{28,20},{1,9},{5... | collective-permute-start | bytes 589832 | tf_op jit(solution)/shard_map/ppermute | solution.py:657
  212.5 1.8 collective-permute-start.13
  215.8 18.7 %inner_back.1 = (bf16[6,256,1024]{2,1,0:T(8,128)(2,1)}, f32[6,256,128]{2,1,0:T(8,128)}, f32[6,256,256]{2,1,0:T(8,128)}) custom-call(bf16[6,256,1024]{2,1,0:T(8,128)(2,1)} %get-tuple-element.187.x_ref, bf16[6,256,256]{2,1,0:T(8,128)(2,1)} %get-tuple-element.140.bc_ref, bf16[6,256,1024]{2,1,0:T(8,128)(2,1)} %get-tuple-element.164.xs_ref, ...), custom_call_target="tpu_custom_call" | custom-call | flops 21390000128 | bytes 1000 | tf_op jit(solution)/shard_map/inner_back/pallas_call | solution.py:637
  235.9 2.4 scan_back.1
  238.8 2.4 collective-permute-start.16
  242.7 10.7 %gram.1 = bf16[2048,1024]{1,0:T(8,128)(2,1)} custom-call(bf16[1536,2048]{1,0:T(8,128)(2,1)} %bitcast.107, bf16[1536,1024]{1,0:T(8,128)(2,1)} %bitcast.136), custom_call_target="tpu_custom_call" | custom-call | flops 12419999744 | bytes 1000 | tf_op jit(solution)/shard_map/gram/pallas_call | solution.py:637
  256.3 3.6 unpair_back.1
  261.5 3.9 add.166
  265.3 9.8 %collective-permute-done.19.end_other_ref = bf16[6,64,1024]{2,1,0:T(8,128)(2,1)S(1)} collective-permute-done((bf16[6,64,1024]{2,1,0:T(8,128)(2,1)}, bf16[6,64,1024]{2,1,0:T(8,128)(2,1)S(1)}, u32[]{:S(2)}, u32[]{:S(2)}) %collective-permute-start.19) | collective-permute-done | bytes 786464 | tf_op jit(solution)/shard_map/ppermute | solution.py:657
  276.0 25.4 %leave.1 = (bf16[6,256,1024]{2,1,0:T(8,128)(2,1)}, bf16[6,16,1024]{2,1,0:T(8,128)(2,1)}, bf16[6,16,256]{2,1,0:T(8,128)(2,1)}, bf16[6,256,256]{2,1,0:T(8,128)(2,1...) custom-call(s32[1]{0:T(128)} %bitcast.1.me_ref, ...), custom_call_target="tpu_custom_call" | custom-call | flops 32199999488 | bytes 1000 | tf_op jit(solution)/shard_map/leave/pallas_call | solution.py:637
  303.8 8.1 %shares.5 = (bf16[1,1536,512]{2,1,0:T(8,128)(2,1)}, bf16[1,1536,512]{2,1,0:T(8,128)(2,1)}) custom-call(s32[1]{0:T(128)} %bitcast.me_ref.head_ref, bf16[1536,1024]{1,0:T(8,128)(2,1)} %bitcast.141, bf16[2048,1024]{1,0:T(8,128)(2,1)} %refs_1_.3), custom_call_target="tpu_custom_call" | custom-call | flops 7408818688 | bytes 1000 | tf_op jit(solution)/shard_map/shares/pallas_call | solution.py:1018
  315.5 3.0 add.172
  319.1 1.7 collective-permute-start.22
  323.4 10.7 %gram_pair.4 = (bf16[4,256,1024]{2,1,0:T(8,128)(2,1)}, bf16[4,256,1024]{2,1,0:T(8,128)(2,1)}) custom-call(s32[1]{0:T(128)} %bitcast.1.me_ref, bf16[1536,2048]{1,0:T(8,128)(2,1)} %bitcast.108, bf16[1536,1024]{1,0:T(8,128)(2,1)} %bitcast.130), custom_call_target="tpu_custom_call" | custom-call | flops 12348030976 | bytes 1000 | tf_op jit(solution)/shard_map/gram_pair/pallas_call | solution.py:958
  336.1 3.6 collective-permute-start.27
  340.8 6.6 %conv_bc.1 = (bf16[6,256,256]{2,1,0:T(8,128)(2,1)}, bf16[6,256,128]{2,1,0:T(8,128)(2,1)}, f32[6,8,256]{2,1,0:T(8,128)}, f32[8,256]{1,0:T(8,128)}) custom-call(s32[1]{0:T(128)} %bitcast.me_ref.head_ref, bf16[6,288,256]{2,1,0:T(8,128)(2,1)} %maximum_select_fusion.d_ref, bf16[6,256,256]{2,1,0:T(8,128)(2,1)} %get-tuple-element.190.pre_bc_ref.pre_ref, ...), custom_call_target="tpu_custom_call" | custom-call | flops 7245000192 | bytes 1000 | tf_op jit(solution)/shard_map/conv_bc/pallas_call | solution.py:637
  347.4 1.9 add.174
  349.3 5.7 %gram_pair.5 = (bf16[4,256,128]{2,1,0:T(8,128)(2,1)}, bf16[4,256,128]{2,1,0:T(8,128)(2,1)}) custom-call(s32[1]{0:T(128)} %bitcast.1.me_ref, bf16[1536,2048]{1,0:T(8,128)(2,1)} %bitcast.109, bf16[1536,128]{1,0:T(8,128)(2,1)} %bitcast.119), custom_call_target="tpu_custom_call" | custom-call | flops 1543503872 | bytes 1000 | tf_op jit(solution)/shard_map/gram_pair/pallas_call | solution.py:958
  355.0 14.6 %shares.6 = (bf16[1,1536,512]{2,1,0:T(8,128)(2,1)}, bf16[1,1536,512]{2,1,0:T(8,128)(2,1)}, f32[2,8,512]{2,1,0:T(8,128)}) custom-call(s32[1]{0:T(128)} %bitcast.me_ref.head_ref, bf16[1536,1024]{1,0:T(8,128)(2,1)} %bitcast.137, bf16[2,2048,1024]{2,1,0:T(8,128)(2,1)} %bitcast.103, bf16[1536,1024]{1,0:T(8,128)(2,1)} %bitcast.131, ...), custom_call_target="tpu_custom_call" | custom-call | flops 15743739904 | bytes 1000 | tf_op jit(solution)/shard_map/shares/pallas_call | solution.py:1018
  372.4 3.0 add.175
  376.2 2.3 fusion.9
  378.5 7.5 %collective-permute-done.27 = bf16[4,256,1024]{2,1,0:T(8,128)(2,1)} collective-permute-done((bf16[4,256,1024]{2,1,0:T(8,128)(2,1)}, bf16[4,256,1024]{2,1,0:T(8,128)(2,1)}, u32[]{:S(2)}, u32[]{:S(2)}) %collective-permute-start.27) | collective-permute-done | bytes 2097184 | tf_op jit(solution)/shard_map/ppermute | solution.py:657
  386.0 3.9 add.177
  389.9 3.5 add.178
  395.0 15.1 %shares.7 = (bf16[1,1536,512]{2,1,0:T(8,128)(2,1)}, bf16[1,1536,512]{2,1,0:T(8,128)(2,1)}, f32[2,8,512]{2,1,0:T(8,128)}) custom-call(s32[1]{0:T(128)} %bitcast.me_ref.head_ref, bf16[1536,1024]{1,0:T(8,128)(2,1)} %bitcast.138, bf16[2,2048,1024]{2,1,0:T(8,128)(2,1)} %bitcast.105, bf16[1536,1024]{1,0:T(8,128)(2,1)} %bitcast.132, ...), custom_call_target="tpu_custom_call" | custom-call | flops 15743739904 | bytes 1000 | tf_op jit(solution)/shard_map/shares/pallas_call | solution.py:1018
  412.4 1.8 collective-permute-start.32
  414.1 2.8 collective-permute-done.32
  416.9 3.2 collective-permute-start.33
  420.1 1.7 collective-permute-start.37
  421.8 4.0 collective-permute-done.33
  425.9 2.9 collective-permute-start.34
  429.6 7.4 %collective-permute-done.34 = f32[16,1024]{1,0:T(8,128)S(1)} collective-permute-done((f32[16,1024]{1,0:T(8,128)S(1)}, f32[16,1024]{1,0:T(8,128)S(1)}, u32[]{:S(2)}, u32[]{:S(2)}) %collective-permute-start.34) | collective-permute-done | bytes 65568 | tf_op jit(solution)/shard_map/ppermute | solution.py:657
  438.3 3.8 fusion.43
  442.8 2.0 collective-permute-start.39
  444.8 2.4 collective-permute-start.40
  456.6 1.9 dynamic-slice_bitcast_fusion
  461.9 2.2 convert_element_type.131
  464.1 2.1 convert.10
  467.0 1.7 maximum_select_fusion.1
  469.9 2.4 collective-permute-done.31
  473.8 2.9 copy.46
  476.8 3.6 fusion.8
  (244 shorter events, 72.5 us)
Async XLA Ops:
  7.2 121.1 %all-gather.2.cloned.1.call-start = ((), (), s32[]{:S(2)}) async-start(), calls=%async_computation.3 | async-start | bytes 7864320 | tf_op jit(solution)/shard_map/all_gather | solution.py:780
  7.9 9.6 %copy-start.20 = (s32[6,256]{1,0:T(8,128)S(1)}, s32[6,256]{1,0:T(8,128)}, u32[]{:S(2)}) copy-start(s32[6,256]{1,0:T(8,128)} %param.21) | copy-start | bytes 18436
  7.9 9.7 %slice-start = ((bf16[6,256,2048]{2,1,0:T(8,128)(2,1)}), bf16[6,8,2048]{2,1,0:T(8,128)(2,1)S(1)}, s32[]{:S(2)}) async-start(bf16[6,256,2048]{2,1,0:T(8,128)(2,1)} %tok_ref.1), calls=%async_computation.7 | async-start | bytes 393216 | tf_op jit(solution)/shard_map/slice | solution.py:783
  7.9 14.9 %copy-start.16 = (bf16[2048,16]{0,1:T(8,128)(2,1)S(1)}, bf16[2048,16]{0,1:T(8,128)(2,1)}, u32[]{:S(2)}) copy-start(bf16[2048,16]{0,1:T(8,128)(2,1)} %param.25) | copy-start | bytes 196612
  7.9 15.2 %copy-start.47 = (f32[16]{0:T(128)S(1)}, f32[16]{0:T(128)}, u32[]{:S(2)}) copy-start(f32[16]{0:T(128)} %param.31) | copy-start | bytes 196
  8.0 15.2 %copy-start.29 = (f32[16]{0:T(128)S(1)}, f32[16]{0:T(128)}, u32[]{:S(2)}) copy-start(f32[16]{0:T(128)} %param.30) | copy-start | bytes 196
  8.0 448.6 %reduce-scatter.4.cloned.1.call-start = ((), (), s32[]{:S(2)}) async-start(), calls=%async_computation.4 | async-start | bytes 5242880 | tf_op jit(solution)/shard_map/reduce_scatter | solution.py:705
  17.5 7.2 %copy-start.26 = (f32[1024]{0:T(1024)S(1)}, f32[1024]{0:T(1024)}, u32[]{:S(2)}) copy-start(f32[1024]{0:T(1024)} %param.27) | copy-start | bytes 12292
  17.5 7.8 %copy-start.9 = (bf16[2048,256]{1,0:T(8,128)(2,1)S(1)}, bf16[2048,256]{1,0:T(8,128)(2,1)}, u32[]{:S(2)}) copy-start(bf16[2048,256]{1,0:T(8,128)(2,1)} %param.24) | copy-start | bytes 3145732
  17.7 9.7 %collective-permute-start = (bf16[6,8,2176]{2,1,0:T(8,128)(2,1)S(1)}, bf16[6,8,2176]{2,1,0:T(8,128)(2,1)S(1)}, u32[]{:S(2)}, u32[]{:S(2)}) collective-permute-start(bf16[6,8,2176]{2,1,0:T(8,128)(2,1)S(1)} %pad_maximum_fusion.2), channel_id=1, source_target_pairs={{0,4},{4,8},{8,12},{12,16},{16,20},{20,24},{24,28},{1,5},{5,9},{9,... | collective-permute-start | bytes 626696 | tf_op jit(solution)/shard_map/ppermute | solution.py:663
  28.8 29.4 %copy-start.30 = (f32[16]{0:T(128)S(1)}, f32[16]{0:T(128)}, u32[]{:S(2)}) copy-start(f32[16]{0:T(128)} %param.32) | copy-start | bytes 196
  28.8 29.6 %copy-start.24 = (f32[1024]{0:T(1024)S(1)}, f32[1024]{0:T(1024)}, u32[]{:S(2)}) copy-start(f32[1024]{0:T(1024)} %param.33) | copy-start | bytes 12292
  56.0 20.0 %collective-permute-start.1 = (bf16[400,1024]{1,0:T(8,128)(2,1)}, bf16[400,1024]{1,0:T(8,128)(2,1)S(1)}, u32[]{:S(2)}, u32[]{:S(2)}) collective-permute-start(bf16[400,1024]{1,0:T(8,128)(2,1)} %get-tuple-element.147), channel_id=1, source_target_pairs={{0,4},{4,0},{8,12},{12,8},{16,20},{20,16},{24,28},{28,24},{1,5},{5... | collective-permute-start | bytes 2457608 | tf_op jit(solution)/shard_map/ppermute | solution.py:657
  76.9 8.3 %copy-start.1 = (bf16[6,256,2048]{2,1,0:T(8,128)(2,1)S(1)}, bf16[6,256,2048]{2,1,0:T(8,128)(2,1)}, u32[]{:S(2)}) copy-start(bf16[6,256,2048]{2,1,0:T(8,128)(2,1)} %get-tuple-element.145) | copy-start | bytes 18874372
  80.0 14.9 %collective-permute-start.2 = (bf16[7,16,1024]{2,1,0:T(8,128)(2,1)}, bf16[7,16,1024]{2,1,0:T(8,128)(2,1)S(1)}, u32[]{:S(2)}, u32[]{:S(2)}) collective-permute-start(bf16[7,16,1024]{2,1,0:T(8,128)(2,1)} %get-tuple-element.150), channel_id=1, source_target_pairs={{0,8},{4,12},{8,0},{12,4},{16,24},{20,28},{24,16},{28,20},{1,9},{5... | collective-permute-start | bytes 688136 | tf_op jit(solution)/shard_map/ppermute | solution.py:657
  82.6 18.6 %collective-permute-start.3 = (bf16[7,16,1024]{2,1,0:T(8,128)(2,1)}, bf16[7,16,1024]{2,1,0:T(8,128)(2,1)S(1)}, u32[]{:S(2)}, u32[]{:S(2)}) collective-permute-start(bf16[7,16,1024]{2,1,0:T(8,128)(2,1)} %get-tuple-element.151), channel_id=1, source_target_pairs={{0,16},{4,20},{8,24},{12,28},{16,0},{20,4},{24,8},{28,12},{1,17},{... | collective-permute-start | bytes 688136 | tf_op jit(solution)/shard_map/ppermute | solution.py:657
  85.2 16.1 %collective-permute-start.4 = (bf16[7,16,1024]{2,1,0:T(8,128)(2,1)}, bf16[7,16,1024]{2,1,0:T(8,128)(2,1)S(1)}, u32[]{:S(2)}, u32[]{:S(2)}) collective-permute-start(bf16[7,16,1024]{2,1,0:T(8,128)(2,1)} %get-tuple-element.152), channel_id=1, source_target_pairs={{0,24},{4,28},{8,16},{12,20},{16,8},{20,12},{24,0},{28,4},{1,25},{... | collective-permute-start | bytes 688136 | tf_op jit(solution)/shard_map/ppermute | solution.py:657
  104.6 16.8 %collective-permute-start.5 = (bf16[6,16,1024]{2,1,0:T(8,128)(2,1)}, bf16[6,16,1024]{2,1,0:T(8,128)(2,1)S(1)}, u32[]{:S(2)}, u32[]{:S(2)}) collective-permute-start(bf16[6,16,1024]{2,1,0:T(8,128)(2,1)} %get-tuple-element.154), channel_id=1, source_target_pairs={{0,8},{4,12},{8,0},{12,4},{16,24},{20,28},{24,16},{28,20},{1,9},{5... | collective-permute-start | bytes 589832 | tf_op jit(solution)/shard_map/ppermute | solution.py:657
  107.5 15.5 %collective-permute-start.6 = (bf16[6,16,1024]{2,1,0:T(8,128)(2,1)}, bf16[6,16,1024]{2,1,0:T(8,128)(2,1)S(1)}, u32[]{:S(2)}, u32[]{:S(2)}) collective-permute-start(bf16[6,16,1024]{2,1,0:T(8,128)(2,1)} %get-tuple-element.155), channel_id=1, source_target_pairs={{0,16},{4,20},{8,24},{12,28},{16,0},{20,4},{24,8},{28,12},{1,17},{... | collective-permute-start | bytes 589832 | tf_op jit(solution)/shard_map/ppermute | solution.py:657
  108.5 14.5 %collective-permute-start.7 = (bf16[6,16,1024]{2,1,0:T(8,128)(2,1)}, bf16[6,16,1024]{2,1,0:T(8,128)(2,1)S(1)}, u32[]{:S(2)}, u32[]{:S(2)}) collective-permute-start(bf16[6,16,1024]{2,1,0:T(8,128)(2,1)} %get-tuple-element.156), channel_id=1, source_target_pairs={{0,24},{4,28},{8,16},{12,20},{16,8},{20,12},{24,0},{28,4},{1,25},{... | collective-permute-start | bytes 589832 | tf_op jit(solution)/shard_map/ppermute | solution.py:657
  127.4 15.7 %collective-permute-start.8 = (bf16[6,64,1024]{2,1,0:T(8,128)(2,1)}, bf16[6,64,1024]{2,1,0:T(8,128)(2,1)S(1)}, u32[]{:S(2)}, u32[]{:S(2)}) collective-permute-start(bf16[6,64,1024]{2,1,0:T(8,128)(2,1)} %get-tuple-element.158), channel_id=1, source_target_pairs={{0,4},{4,0},{8,12},{12,8},{16,20},{20,16},{24,28},{28,24},{1,5},{5... | collective-permute-start | bytes 2359304 | tf_op jit(solution)/shard_map/ppermute | solution.py:657
  155.8 1.4 collective-permute-start.9
  158.0 4.1 collective-permute-start.10
  182.2 20.7 %collective-permute-start.11 = (bf16[384,1024]{1,0:T(8,128)(2,1)}, bf16[384,1024]{1,0:T(8,128)(2,1)S(1)}, u32[]{:S(2)}, u32[]{:S(2)}) collective-permute-start(bf16[384,1024]{1,0:T(8,128)(2,1)} %get-tuple-element.169), channel_id=1, source_target_pairs={{0,4},{4,0},{8,12},{12,8},{16,20},{20,16},{24,28},{28,24},{1,5},{5... | collective-permute-start | bytes 2359304 | tf_op jit(solution)/shard_map/ppermute | solution.py:657
  201.8 59.1 %collective-permute-start.18 = (bf16[4,256,1024]{2,1,0:T(8,128)(2,1)}, bf16[4,256,1024]{2,1,0:T(8,128)(2,1)}, u32[]{:S(2)}, u32[]{:S(2)}) collective-permute-start(bf16[4,256,1024]{2,1,0:T(8,128)(2,1)} %get-tuple-element.186), channel_id=1, source_target_pairs={{0,4},{4,0},{8,12},{12,8},{16,20},{20,16},{24,28},{28,24},{1,5},{5... | collective-permute-start | bytes 6291464 | tf_op jit(solution)/shard_map/ppermute | solution.py:657
  206.7 27.8 %collective-permute-start.12 = (bf16[6,16,1024]{2,1,0:T(8,128)(2,1)}, bf16[6,16,1024]{2,1,0:T(8,128)(2,1)S(1)}, u32[]{:S(2)}, u32[]{:S(2)}) collective-permute-start(bf16[6,16,1024]{2,1,0:T(8,128)(2,1)} %get-tuple-element.175), channel_id=1, source_target_pairs={{0,8},{4,12},{8,0},{12,4},{16,24},{20,28},{24,16},{28,20},{1,9},{5... | collective-permute-start | bytes 589832 | tf_op jit(solution)/shard_map/ppermute | solution.py:657
  212.5 22.0 %collective-permute-start.13 = (bf16[6,16,1024]{2,1,0:T(8,128)(2,1)}, bf16[6,16,1024]{2,1,0:T(8,128)(2,1)S(1)}, u32[]{:S(2)}, u32[]{:S(2)}) collective-permute-start(bf16[6,16,1024]{2,1,0:T(8,128)(2,1)} %get-tuple-element.176), channel_id=1, source_target_pairs={{0,16},{4,20},{8,24},{12,28},{16,0},{20,4},{24,8},{28,12},{1,17},{... | collective-permute-start | bytes 589832 | tf_op jit(solution)/shard_map/ppermute | solution.py:657
  214.3 20.2 %collective-permute-start.14 = (bf16[6,16,1024]{2,1,0:T(8,128)(2,1)}, bf16[6,16,1024]{2,1,0:T(8,128)(2,1)S(1)}, u32[]{:S(2)}, u32[]{:S(2)}) collective-permute-start(bf16[6,16,1024]{2,1,0:T(8,128)(2,1)} %get-tuple-element.177), channel_id=1, source_target_pairs={{0,24},{4,28},{8,16},{12,20},{16,8},{20,12},{24,0},{28,4},{1,25},{... | collective-permute-start | bytes 589832 | tf_op jit(solution)/shard_map/ppermute | solution.py:657
  238.3 15.1 %collective-permute-start.15 = (bf16[6,16,1024]{2,1,0:T(8,128)(2,1)}, bf16[6,16,1024]{2,1,0:T(8,128)(2,1)S(1)}, u32[]{:S(2)}, u32[]{:S(2)}) collective-permute-start(bf16[6,16,1024]{2,1,0:T(8,128)(2,1)} %get-tuple-element.181), channel_id=1, source_target_pairs={{0,8},{4,12},{8,0},{12,4},{16,24},{20,28},{24,16},{28,20},{1,9},{5... | collective-permute-start | bytes 589832 | tf_op jit(solution)/shard_map/ppermute | solution.py:657
  238.8 16.1 %collective-permute-start.16 = (bf16[6,16,1024]{2,1,0:T(8,128)(2,1)}, bf16[6,16,1024]{2,1,0:T(8,128)(2,1)S(1)}, u32[]{:S(2)}, u32[]{:S(2)}) collective-permute-start(bf16[6,16,1024]{2,1,0:T(8,128)(2,1)} %get-tuple-element.182), channel_id=1, source_target_pairs={{0,16},{4,20},{8,24},{12,28},{16,0},{20,4},{24,8},{28,12},{1,17},{... | collective-permute-start | bytes 589832 | tf_op jit(solution)/shard_map/ppermute | solution.py:657
  241.2 13.8 %collective-permute-start.17 = (bf16[6,16,1024]{2,1,0:T(8,128)(2,1)}, bf16[6,16,1024]{2,1,0:T(8,128)(2,1)S(1)}, u32[]{:S(2)}, u32[]{:S(2)}) collective-permute-start(bf16[6,16,1024]{2,1,0:T(8,128)(2,1)} %get-tuple-element.183), channel_id=1, source_target_pairs={{0,24},{4,28},{8,16},{12,20},{16,8},{20,12},{24,0},{28,4},{1,25},{... | collective-permute-start | bytes 589832 | tf_op jit(solution)/shard_map/ppermute | solution.py:657
  259.9 15.2 %collective-permute-start.19 = (bf16[6,64,1024]{2,1,0:T(8,128)(2,1)}, bf16[6,64,1024]{2,1,0:T(8,128)(2,1)S(1)}, u32[]{:S(2)}, u32[]{:S(2)}) collective-permute-start(bf16[6,64,1024]{2,1,0:T(8,128)(2,1)} %get-tuple-element.196), channel_id=1, source_target_pairs={{0,4},{4,0},{8,12},{12,8},{16,20},{20,16},{24,28},{28,24},{1,5},{5... | collective-permute-start | bytes 2359304 | tf_op jit(solution)/shard_map/ppermute | solution.py:657
  260.8 201.1 %reduce-scatter.8.cloned.1.call-start = ((), (), s32[]{:S(2)}) async-start(), calls=%async_computation.6 | async-start | bytes 2621440 | tf_op jit(solution)/shard_map/reduce_scatter | solution.py:705
  260.8 54.7 %collective-permute-start.23 = (bf16[1,1536,512]{2,1,0:T(8,128)(2,1)}, bf16[1,1536,512]{2,1,0:T(8,128)(2,1)}, u32[]{:S(2)}, u32[]{:S(2)}) collective-permute-start(bf16[1,1536,512]{2,1,0:T(8,128)(2,1)} %get-tuple-element.206), channel_id=1, source_target_pairs={{0,1},{1,0},{2,3},{3,2},{4,5},{5,4},{6,7},{7,6},{8,9},{9,8},{10,11... | collective-permute-start | bytes 4718600 | tf_op jit(solution)/shard_map/ppermute | solution.py:657
  302.3 11.6 %copy-start.5 = (bf16[6,256,256]{2,1,0:T(8,128)(2,1)S(1)}, bf16[6,256,256]{2,1,0:T(8,128)(2,1)}, u32[]{:S(2)}) copy-start(bf16[6,256,256]{2,1,0:T(8,128)(2,1)} %get-tuple-element.200) | copy-start | bytes 2359300
  302.3 10.5 %collective-permute-start.20 = (bf16[6,3,1280]{2,1,0:T(4,128)(2,1)S(1)}, bf16[6,3,1280]{2,1,0:T(4,128)(2,1)S(1)}, u32[]{:S(2)}, u32[]{:S(2)}) collective-permute-start(bf16[6,3,1280]{2,1,0:T(4,128)(2,1)S(1)} %pad_maximum_fusion.4), channel_id=1, source_target_pairs={{4,0},{8,4},{12,8},{16,12},{20,16},{24,20},{28,24},{5,1},{9,5},{13... | collective-permute-start | bytes 138248 | tf_op jit(solution)/shard_map/ppermute | solution.py:663
  315.0 3.9 collective-permute-start.21
  315.0 32.4 %collective-permute-start.25 = (bf16[1,1536,512]{2,1,0:T(8,128)(2,1)}, bf16[1,1536,512]{2,1,0:T(8,128)(2,1)}, u32[]{:S(2)}, u32[]{:S(2)}) collective-permute-start(bf16[1,1536,512]{2,1,0:T(8,128)(2,1)} %get-tuple-element.213), channel_id=1, source_target_pairs={{0,1},{1,0},{2,3},{3,2},{4,5},{5,4},{6,7},{7,6},{8,9},{9,8},{10,11... | collective-permute-start | bytes 4718600 | tf_op jit(solution)/shard_map/ppermute | solution.py:657
  319.1 15.0 %collective-permute-start.22 = (bf16[3,288,256]{2,1,0:T(8,128)(2,1)S(1)}, bf16[3,288,256]{2,1,0:T(8,128)(2,1)}, u32[]{:S(2)}, u32[]{:S(2)}) collective-permute-start(bf16[3,288,256]{2,1,0:T(8,128)(2,1)S(1)} %constant_dynamic-slice_fusion), channel_id=1, source_target_pairs={{0,2},{1,3},{2,0},{3,1},{4,6},{5,7},{6,4},{7,5},{8,10},{9,11},{10,... | collective-permute-start | bytes 1327112 | tf_op jit(solution)/shard_map/ppermute | solution.py:657
  335.3 4.4 collective-permute-start.24
  335.4 133.3 %reduce-scatter.6.cloned.1.call-start = ((), (), s32[]{:S(2)}) async-start(), calls=%async_computation.5 | async-start | bytes 2621440 | tf_op jit(solution)/shard_map/reduce_scatter | solution.py:705
  335.7 36.8 %collective-permute-start.26 = (bf16[1,1536,512]{2,1,0:T(8,128)(2,1)S(1)}, bf16[1,1536,512]{2,1,0:T(8,128)(2,1)}, u32[]{:S(2)}, u32[]{:S(2)}) collective-permute-start(bf16[1,1536,512]{2,1,0:T(8,128)(2,1)S(1)} %copy-done.12), channel_id=1, source_target_pairs={{0,2},{1,3},{2,0},{3,1},{4,6},{5,7},{6,4},{7,5},{8,10},{9,11},{10,... | collective-permute-start | bytes 4718600 | tf_op jit(solution)/shard_map/ppermute | solution.py:657
  336.1 49.8 %collective-permute-start.27 = (bf16[4,256,1024]{2,1,0:T(8,128)(2,1)}, bf16[4,256,1024]{2,1,0:T(8,128)(2,1)}, u32[]{:S(2)}, u32[]{:S(2)}) collective-permute-start(bf16[4,256,1024]{2,1,0:T(8,128)(2,1)} %get-tuple-element.219), channel_id=1, source_target_pairs={{0,4},{4,0},{8,12},{12,8},{16,20},{20,16},{24,28},{28,24},{1,5},{5... | collective-permute-start | bytes 6291464 | tf_op jit(solution)/shard_map/ppermute | solution.py:657
  355.0 16.4 %copy-start.18 = (f32[8,1024]{1,0:T(8,128)S(1)}, f32[8,1024]{1,0:T(8,128)}, u32[]{:S(2)}) copy-start(f32[8,1024]{1,0:T(8,128)} %get-tuple-element.230) | copy-start | bytes 98308
  355.0 16.4 %copy-start.19 = (f32[8,1024]{1,0:T(8,128)S(1)}, f32[8,1024]{1,0:T(8,128)}, u32[]{:S(2)}) copy-start(f32[8,1024]{1,0:T(8,128)} %get-tuple-element.229) | copy-start | bytes 98308
  369.6 20.2 %collective-permute-start.28 = (bf16[1,1536,512]{2,1,0:T(8,128)(2,1)}, bf16[1,1536,512]{2,1,0:T(8,128)(2,1)}, u32[]{:S(2)}, u32[]{:S(2)}) collective-permute-start(bf16[1,1536,512]{2,1,0:T(8,128)(2,1)} %get-tuple-element.221), channel_id=1, source_target_pairs={{0,1},{1,0},{2,3},{3,2},{4,5},{5,4},{6,7},{7,6},{8,9},{9,8},{10,11... | collective-permute-start | bytes 4718600 | tf_op jit(solution)/shard_map/ppermute | solution.py:657
  376.2 9.8 %copy-start.7 = (bf16[4,256,1024]{2,1,0:T(8,128)(2,1)S(1)}, bf16[4,256,1024]{2,1,0:T(8,128)(2,1)}, u32[]{:S(2)}) copy-start(bf16[4,256,1024]{2,1,0:T(8,128)(2,1)} %get-tuple-element.218) | copy-start | bytes 6291460
  393.3 19.0 %copy-start.23 = (f32[8,256]{1,0:T(8,128)S(1)}, f32[8,256]{1,0:T(8,128)}, u32[]{:S(2)}) copy-start(f32[8,256]{1,0:T(8,128)} %get-tuple-element.231) | copy-start | bytes 24580
  393.3 19.0 %copy-start.27 = (f32[8,128]{1,0:T(8,128)S(1)}, f32[8,128]{1,0:T(8,128)}, u32[]{:S(2)}) copy-start(f32[8,128]{1,0:T(8,128)} %get-tuple-element.232) | copy-start | bytes 12292
  393.3 44.9 %collective-permute-start.30 = (bf16[1,1536,512]{2,1,0:T(8,128)(2,1)}, bf16[1,1536,512]{2,1,0:T(8,128)(2,1)}, u32[]{:S(2)}, u32[]{:S(2)}) collective-permute-start(bf16[1,1536,512]{2,1,0:T(8,128)(2,1)} %add.178), channel_id=1, source_target_pairs={{0,2},{1,3},{2,0},{3,1},{4,6},{5,7},{6,4},{7,5},{8,10},{9,11},{10,... | collective-permute-start | bytes 4718600 | tf_op jit(solution)/shard_map/ppermute | solution.py:657
  410.1 28.1 %collective-permute-start.29 = (bf16[1,1536,512]{2,1,0:T(8,128)(2,1)}, bf16[1,1536,512]{2,1,0:T(8,128)(2,1)}, u32[]{:S(2)}, u32[]{:S(2)}) collective-permute-start(bf16[1,1536,512]{2,1,0:T(8,128)(2,1)} %get-tuple-element.225), channel_id=1, source_target_pairs={{0,1},{1,0},{2,3},{3,2},{4,5},{5,4},{6,7},{7,6},{8,9},{9,8},{10,11... | collective-permute-start | bytes 4718600 | tf_op jit(solution)/shard_map/ppermute | solution.py:657
  412.4 4.6 collective-permute-start.32
  416.9 8.9 %collective-permute-start.33 = (f32[16,1024]{1,0:T(8,128)S(1)}, f32[16,1024]{1,0:T(8,128)S(1)}, u32[]{:S(2)}, u32[]{:S(2)}) collective-permute-start(f32[16,1024]{1,0:T(8,128)S(1)} %fusion.41), channel_id=1, source_target_pairs={{0,8},{4,12},{8,0},{12,4},{16,24},{20,28},{24,16},{28,20},{1,9},{5... | collective-permute-start | bytes 196616 | tf_op jit(solution)/shard_map/ppermute | solution.py:657
  420.1 22.0 %collective-permute-start.37 = (bf16[4,256,128]{2,1,0:T(8,128)(2,1)}, bf16[4,256,128]{2,1,0:T(8,128)(2,1)S(1)}, u32[]{:S(2)}, u32[]{:S(2)}) collective-permute-start(bf16[4,256,128]{2,1,0:T(8,128)(2,1)} %get-tuple-element.236), channel_id=1, source_target_pairs={{0,4},{4,0},{8,12},{12,8},{16,20},{20,16},{24,28},{28,24},{1,5},{5... | collective-permute-start | bytes 786440 | tf_op jit(solution)/shard_map/ppermute | solution.py:657
  425.9 11.2 %collective-permute-start.34 = (f32[16,1024]{1,0:T(8,128)S(1)}, f32[16,1024]{1,0:T(8,128)S(1)}, u32[]{:S(2)}, u32[]{:S(2)}) collective-permute-start(f32[16,1024]{1,0:T(8,128)S(1)} %add.191), channel_id=1, source_target_pairs={{0,16},{4,20},{8,24},{12,28},{16,0},{20,4},{24,8},{28,12},{1,17},{... | collective-permute-start | bytes 196616 | tf_op jit(solution)/shard_map/ppermute | solution.py:657
  437.0 12.5 %copy-start.15 = (f32[16,1024]{1,0:T(8,128)}, f32[16,1024]{1,0:T(8,128)S(1)}, u32[]{:S(2)}) copy-start(f32[16,1024]{1,0:T(8,128)S(1)} %add.192) | copy-start | bytes 196612
  442.8 8.7 %collective-permute-start.38 = (bf16[256,128]{1,0:T(8,128)(2,1)}, bf16[256,128]{1,0:T(8,128)(2,1)S(1)}, u32[]{:S(2)}, u32[]{:S(2)}) collective-permute-start(bf16[256,128]{1,0:T(8,128)(2,1)} %get-tuple-element.288), channel_id=1, source_target_pairs={{0,8},{4,12},{8,0},{12,4},{16,24},{20,28},{24,16},{28,20},{1,9},{5... | collective-permute-start | bytes 196616 | tf_op jit(solution)/shard_map/ppermute | solution.py:657
  442.8 8.7 %collective-permute-start.39 = (bf16[256,128]{1,0:T(8,128)(2,1)}, bf16[256,128]{1,0:T(8,128)(2,1)}, u32[]{:S(2)}, u32[]{:S(2)}) collective-permute-start(bf16[256,128]{1,0:T(8,128)(2,1)} %get-tuple-element.290), channel_id=1, source_target_pairs={{0,16},{4,20},{8,24},{12,28},{16,0},{20,4},{24,8},{28,12},{1,17},{... | collective-permute-start | bytes 196616 | tf_op jit(solution)/shard_map/ppermute | solution.py:657
  444.8 7.3 %collective-permute-start.40 = (bf16[256,128]{1,0:T(8,128)(2,1)}, bf16[256,128]{1,0:T(8,128)(2,1)}, u32[]{:S(2)}, u32[]{:S(2)}) collective-permute-start(bf16[256,128]{1,0:T(8,128)(2,1)} %get-tuple-element.289), channel_id=1, source_target_pairs={{0,24},{4,28},{8,16},{12,20},{16,8},{20,12},{24,0},{28,4},{1,25},{... | collective-permute-start | bytes 196616 | tf_op jit(solution)/shard_map/ppermute | solution.py:657
  450.1 3.5 collective-permute-start.35
  453.1 2.6 collective-permute-start.41
  454.4 5.6 %collective-permute-start.36 = (f32[1,512]{1,0:T(1,128)S(1)}, f32[1,512]{1,0:T(1,128)S(1)}, u32[]{:S(2)}, u32[]{:S(2)}) collective-permute-start(f32[1,512]{1,0:T(1,128)S(1)} %slice_add_fusion.1), channel_id=1, source_target_pairs={{0,2},{1,3},{2,0},{3,1},{4,6},{5,7},{6,4},{7,5},{8,10},{9,11},{10,... | collective-permute-start | bytes 6152 | tf_op jit(solution)/shard_map/ppermute | solution.py:657
  455.8 11.2 %collective-permute-start.42 = (f32[256,128]{1,0:T(8,128)S(1)}, f32[256,128]{1,0:T(8,128)}, u32[]{:S(2)}, u32[]{:S(2)}) collective-permute-start(f32[256,128]{1,0:T(8,128)S(1)} %maximum_select_fusion.2), channel_id=1, source_target_pairs={{0,2},{1,3},{2,0},{3,1},{4,6},{5,7},{6,4},{7,5},{8,10},{9,11},{10,... | collective-permute-start | bytes 393224 | tf_op jit(solution)/shard_map/ppermute | solution.py:657
  458.5 13.8 %collective-permute-start.31 = (bf16[256,1024]{1,0:T(8,128)(2,1)}, bf16[256,1024]{1,0:T(8,128)(2,1)}, u32[]{:S(2)}, u32[]{:S(2)}) collective-permute-start(bf16[256,1024]{1,0:T(8,128)(2,1)} %dynamic-slice_bitcast_fusion), channel_id=1, source_target_pairs={{0,4},{4,0},{8,12},{12,8},{16,20},{20,16},{24,28},{28,24},{1,5},{5... | collective-permute-start | bytes 1572872 | tf_op jit(solution)/shard_map/ppermute | solution.py:657
  (32 other events, 78.3 us)
Sparse Core Ops, SparseCore 0:
  9.6 49.0 all-gather.1
  260.9 78.7 reduce-scatter.3
  342.0 43.4 reduce-scatter.7
  390.0 49.5 reduce-scatter.5
